TPU v7x, 32 devices: a whole 2x2x4 slice. The times are simulated.
32 devices in a mesh: head: 4 (over z), batch: 8 (over y, x, core).
Axes of the slice: x: 2, y: 2, z: 4, core: 2. Of those that a mesh axis runs over, the one named last changes fastest.
Arguments:
- layer_input: bfloat16 [16384, 1024], P('batch', 'head'), may hold values from -6 to 6
- cotangent: bfloat16 [16384, 1024], P('batch', 'head'), may hold values from -6 to 6
- positions: int32 [16384], P('batch'), may hold values from 0 to 2047, as said below
- w_qkv: float32 [1024, 3, 1024], P('batch', None, 'head'), may hold values from -2 to 2
- w_out: float32 [1024, 1024], P('head', 'batch'), may hold values from -2 to 2
- w_up: float32 [1024, 2, 4096], P('batch', None, 'head'), may hold values from -2 to 2
- w_down: float32 [4096, 1024], P('head', 'batch'), may hold values from -2 to 2
- moment_qkv: float32 [1024, 3, 1024], P('batch', None, 'head'), may hold values from -12 to 12
- moment_out: float32 [1024, 1024], P('head', 'batch'), may hold values from -12 to 12
- moment_up: float32 [1024, 2, 4096], P('batch', None, 'head'), may hold values from -12 to 12
- moment_down: float32 [4096, 1024], P('head', 'batch'), may hold values from -12 to 12
- square_qkv: float32 [1024, 3, 1024], P('batch', None, 'head'), may hold values from 16 to 256
- square_out: float32 [1024, 1024], P('head', 'batch'), may hold values from 16 to 256
- square_up: float32 [1024, 2, 4096], P('batch', None, 'head'), may hold values from 8 to 128
- square_down: float32 [4096, 1024], P('head', 'batch'), may hold values from 16 to 256
- s_qk: float32 [1024], P('head'), may hold values from 0.7 to 1.4
- alpha_attn: float32 [1024], replicated, may hold values from 0.15 to 0.6
- alpha_mlp: float32 [1024], replicated, may hold values from 0.15 to 0.6
- s_uv: float32 [2, 4096], P(None, 'head'), may hold values from 0.5 to 2
Outputs:
- hidden: float32 [16384, 1024], P('batch', 'head')
- input_grad: float32 [16384, 1024], P('batch', 'head')
- grad_qkv: float32 [1024, 3, 1024], P('batch', None, 'head')
- grad_out: float32 [1024, 1024], P('head', 'batch')
- grad_up: float32 [1024, 2, 4096], P('batch', None, 'head')
- grad_down: float32 [4096, 1024], P('head', 'batch')
- moment_qkv_new: float32 [1024, 3, 1024], P('batch', None, 'head')
- moment_out_new: float32 [1024, 1024], P('head', 'batch')
- moment_up_new: float32 [1024, 2, 4096], P('batch', None, 'head')
- moment_down_new: float32 [4096, 1024], P('head', 'batch')
- square_qkv_new: float32 [1024, 3, 1024], P('batch', None, 'head')
- square_out_new: float32 [1024, 1024], P('head', 'batch')
- square_up_new: float32 [1024, 2, 4096], P('batch', None, 'head')
- square_down_new: float32 [4096, 1024], P('head', 'batch')
- new_qkv: float32 [1024, 3, 1024], P('batch', None, 'head')
- new_out: float32 [1024, 1024], P('head', 'batch')
- new_up: float32 [1024, 2, 4096], P('batch', None, 'head')
- new_down: float32 [4096, 1024], P('head', 'batch')
- grad_s_qk: float32 [1024], P(('head', 'batch'))
- grad_alpha_attn: float32 [1024], P(('head', 'batch'))
- grad_alpha_mlp: float32 [1024], P(('head', 'batch'))
- grad_s_uv: float32 [2, 4096], P(None, ('head', 'batch'))
Inputs may be any that keep to these rules, and one draw needn't show every extreme that they name: Each block of 2048 tokens (one index of batch) holds either one sequence of 2048 tokens or sequences of 1024 tokens that fill it; positions count 0, 1, 2 within each sequence; exactly 4 blocks hold a long sequence.
All inputs are finite; a program needn't handle non-finite values.
Results may differ from a plain program's by a relative error of at most 0.017.
Values may be sent and summed in bfloat16 or wider, within the bound.
No kernel may reach another device: no remote copies, remote signals or barrier semaphores. Data moves between devices by JAX's collectives and lax.ppermute only.
A program may use at most 256 MiB of HBM per device.

v0:
```python
import math

import jax
import jax.numpy as jnp
from jax import lax
from jax.sharding import PartitionSpec as P

HEAD_DIM = 64


layer_eps = 1e-06
learn_rate = 0.008
beta_one = 0.9
beta_two = 0.95
adam_eps = 1e-08
bias_one = 1.0 - math.exp(100.0 * math.log(0.9))
bias_two = 1.0 - math.exp(100.0 * math.log(0.95))
score_scale = 8.0


def rotate(value, cosine, sine):
    half = value.shape[-1] // 2
    first = value[..., :half]
    second = value[..., half:]
    return jnp.concatenate(
        [first * cosine - second * sine, second * cosine + first * sine], axis=-1
    )


def angles(places, head_dim):
    freqs = jnp.exp(
        jnp.arange(head_dim // 2, dtype=jnp.float32) * (-2.0 * math.log(10000.0) / head_dim)
    )
    phase = places.astype(jnp.float32)[:, None] * freqs[None, :]
    return (jnp.cos(phase)[:, None, :], jnp.sin(phase)[:, None, :])


def row_total(values):
    return lax.psum(jnp.sum(values * values, axis=1), "head")


def row_inner(left, right):
    return lax.psum(jnp.sum(left * right, axis=1), "head")


def adam_step(weight, grad, first, second):
    first_new = beta_one * first + (1.0 - beta_one) * grad
    second_new = beta_two * second + (1.0 - beta_two) * grad * grad
    moved = weight - learn_rate * (first_new / bias_one) / (
        jnp.sqrt(second_new / bias_two) + adam_eps
    )
    return (first_new, second_new, moved)


def per_device(
    layer_input,
    cotangent,
    positions,
    w_qkv,
    w_out,
    w_up,
    w_down,
    moment_qkv,
    moment_out,
    moment_up,
    moment_down,
    square_qkv,
    square_out,
    square_up,
    square_down,
    s_qk,
    alpha_attn,
    alpha_mlp,
    s_uv,
):
    rows = layer_input.shape[0]
    local_cols = layer_input.shape[1]
    width = local_cols * lax.axis_size("head")
    head_dim = HEAD_DIM
    local_heads = local_cols // head_dim
    column_start = lax.axis_index("head") * local_cols
    attn_gain = lax.dynamic_slice_in_dim(alpha_attn, column_start, local_cols)
    mlp_gain = lax.dynamic_slice_in_dim(alpha_mlp, column_start, local_cols)
    qkv_full, out_full, up_full, down_full = (
        lax.all_gather(w_qkv.astype(jnp.bfloat16), "batch", axis=0, tiled=True),
        lax.all_gather(w_out.astype(jnp.bfloat16), "batch", axis=1, tiled=True),
        lax.all_gather(w_up.astype(jnp.bfloat16), "batch", axis=0, tiled=True),
        lax.all_gather(w_down.astype(jnp.bfloat16), "batch", axis=1, tiled=True),
    )
    tokens_full = lax.all_gather(layer_input, "head", axis=1, tiled=True)
    start = layer_input.astype(jnp.float32)
    proj = jnp.einsum("td,dcn->tcn", tokens_full, qkv_full, preferred_element_type=jnp.float32)
    cosine, sine = angles(positions, head_dim)
    query_rot = rotate(proj[:, 0].reshape(rows, local_heads, head_dim), cosine, sine)
    key_rot = rotate(proj[:, 1].reshape(rows, local_heads, head_dim), cosine, sine)
    values_b = proj[:, 2].astype(jnp.bfloat16).reshape(rows, local_heads, head_dim)
    query_scale = lax.rsqrt(jnp.sum(query_rot * query_rot, axis=-1, keepdims=True) + layer_eps)
    key_scale = lax.rsqrt(jnp.sum(key_rot * key_rot, axis=-1, keepdims=True) + layer_eps)
    query_unit = query_rot * query_scale
    key_unit = key_rot * key_scale
    qk_gain = s_qk.reshape(local_heads, head_dim)
    query_b = (query_unit * qk_gain).astype(jnp.bfloat16)
    key_b = (key_unit * qk_gain).astype(jnp.bfloat16)
    block = min(512, rows)
    count = rows // block
    row_ids = jnp.arange(rows, dtype=jnp.int32)
    first_ids = row_ids - positions

    def scores_of(index):
        low_row = index * block
        end = low_row + block
        query_ids = row_ids[low_row:end]
        key_ids = row_ids[:end]
        allowed = (key_ids[None, :] <= query_ids[:, None]) & (
            key_ids[None, :] >= first_ids[low_row:end][:, None]
        )
        raw = score_scale * jnp.einsum(
            "qhd,khd->hqk", query_b[low_row:end], key_b[:end], preferred_element_type=jnp.float32
        )
        return jnp.where(allowed[None], raw, -1e30)

    outputs = []
    totals = []
    for index in range(count):
        end = (index + 1) * block
        scores = scores_of(index)
        top = jnp.max(scores, axis=-1, keepdims=True)
        expo = jnp.exp(scores - top)
        mass = jnp.sum(expo, axis=-1, keepdims=True)
        probs_b = (expo / mass).astype(jnp.bfloat16)
        totals.append(top + jnp.log(mass))
        outputs.append(
            jnp.einsum(
                "hqk,khd->qhd", probs_b, values_b[:end], preferred_element_type=jnp.float32
            ).reshape(block, local_cols)
        )
    attended_b = jnp.concatenate(outputs, axis=0).astype(jnp.bfloat16)
    out_part = jnp.dot(attended_b, out_full, preferred_element_type=jnp.float32)
    out_sum = lax.psum_scatter(out_part, "head", scatter_dimension=1, tiled=True)
    attn_norm = lax.rsqrt(row_total(out_sum)[:, None] / width + layer_eps)
    attn_hidden = out_sum * attn_norm
    mixed = start + attn_gain * (attn_hidden - start)
    first_norm = lax.rsqrt(row_total(mixed)[:, None] / width + layer_eps)
    first_hidden = mixed * first_norm
    first_b_full = lax.all_gather(first_hidden.astype(jnp.bfloat16), "head", axis=1, tiled=True)
    up_gate = jnp.einsum("td,dcf->tcf", first_b_full, up_full, preferred_element_type=jnp.float32)
    up_val = up_gate[:, 0]
    gate_val = up_gate[:, 1]
    lifted = s_uv[0] * up_val
    gated = s_uv[1] * gate_val
    sigma = jax.nn.sigmoid(gated)
    act_b = (lifted * gated * sigma).astype(jnp.bfloat16)
    mlp_part = jnp.dot(act_b, down_full, preferred_element_type=jnp.float32)
    mlp_sum = lax.psum_scatter(mlp_part, "head", scatter_dimension=1, tiled=True)
    mlp_norm = lax.rsqrt(row_total(mlp_sum)[:, None] / width + layer_eps)
    mlp_hidden = mlp_sum * mlp_norm
    mixed_two = first_hidden + mlp_gain * (mlp_hidden - first_hidden)
    last_norm = lax.rsqrt(row_total(mixed_two)[:, None] / width + layer_eps)
    hidden = mixed_two * last_norm

    def norm_back(scale, result, grad):
        return scale * (grad - result * (row_inner(grad, result)[:, None] / width))

    grad_mixed_two = norm_back(last_norm, hidden, cotangent.astype(jnp.float32))
    grad_alpha_mlp = jnp.sum(grad_mixed_two * (mlp_hidden - first_hidden), axis=0)
    grad_mlp_sum = norm_back(mlp_norm, mlp_hidden, mlp_gain * grad_mixed_two)
    grad_mlp_full = lax.all_gather(grad_mlp_sum.astype(jnp.bfloat16), "head", axis=1, tiled=True)
    grad_down = jnp.einsum("tf,td->fd", act_b, grad_mlp_full, preferred_element_type=jnp.float32)
    grad_act = jnp.einsum("td,fd->tf", grad_mlp_full, down_full, preferred_element_type=jnp.float32)
    grad_lifted = grad_act * gated * sigma
    grad_gated = grad_act * lifted * sigma * (1.0 + gated * (1.0 - sigma))
    grad_suv = jnp.stack(
        [jnp.sum(grad_lifted * up_val, axis=0), jnp.sum(grad_gated * gate_val, axis=0)], axis=0
    )
    grad_uv = jnp.stack([grad_lifted * s_uv[0], grad_gated * s_uv[1]], axis=1).astype(jnp.bfloat16)
    grad_up = jnp.einsum("td,tcf->dcf", first_b_full, grad_uv, preferred_element_type=jnp.float32)
    back_part = jnp.einsum("tcf,dcf->td", grad_uv, up_full, preferred_element_type=jnp.float32)
    grad_first = (1.0 - mlp_gain) * grad_mixed_two + lax.psum_scatter(
        back_part, "head", scatter_dimension=1, tiled=True
    )
    grad_mixed = norm_back(first_norm, first_hidden, grad_first)
    grad_alpha_attn = jnp.sum(grad_mixed * (attn_hidden - start), axis=0)
    grad_attn_sum = norm_back(attn_norm, attn_hidden, attn_gain * grad_mixed)
    grad_attn_full = lax.all_gather(grad_attn_sum.astype(jnp.bfloat16), "head", axis=1, tiled=True)
    grad_out = jnp.einsum(
        "tj,td->jd", attended_b, grad_attn_full, preferred_element_type=jnp.float32
    )
    grad_attended = (
        jnp.einsum("td,jd->tj", grad_attn_full, out_full, preferred_element_type=jnp.float32)
        .astype(jnp.bfloat16)
        .reshape(rows, local_heads, head_dim)
    )
    grad_query_blocks = []
    grad_keys = jnp.zeros((rows, local_heads, head_dim), jnp.float32)
    grad_values = jnp.zeros((rows, local_heads, head_dim), jnp.float32)
    for index in range(count):
        low_row = index * block
        end = low_row + block
        scores = scores_of(index)
        probs = jnp.exp(scores - totals[index])
        probs_b = probs.astype(jnp.bfloat16)
        grad_block = grad_attended[low_row:end]
        grad_probs = jnp.einsum(
            "qhd,khd->hqk", grad_block, values_b[:end], preferred_element_type=jnp.float32
        )
        grad_values = grad_values.at[:end].add(
            jnp.einsum("hqk,qhd->khd", probs_b, grad_block, preferred_element_type=jnp.float32)
        )
        inner = jnp.sum(probs * grad_probs, axis=-1, keepdims=True)
        grad_scores = (probs * (grad_probs - inner)).astype(jnp.bfloat16)
        grad_query_blocks.append(
            score_scale
            * jnp.einsum(
                "hqk,khd->qhd", grad_scores, key_b[:end], preferred_element_type=jnp.float32
            )
        )
        grad_keys = grad_keys.at[:end].add(
            score_scale
            * jnp.einsum(
                "hqk,qhd->khd",
                grad_scores,
                query_b[low_row:end],
                preferred_element_type=jnp.float32,
            )
        )
    grad_query = jnp.concatenate(grad_query_blocks, axis=0)
    grad_sqk = jnp.sum(grad_query * query_unit + grad_keys * key_unit, axis=0).reshape(local_cols)
    grad_unit_q = grad_query * qk_gain
    grad_unit_k = grad_keys * qk_gain
    grad_rot_q = query_scale * (
        grad_unit_q - query_unit * jnp.sum(grad_unit_q * query_unit, axis=-1, keepdims=True)
    )
    grad_rot_k = key_scale * (
        grad_unit_k - key_unit * jnp.sum(grad_unit_k * key_unit, axis=-1, keepdims=True)
    )
    grad_q = rotate(grad_rot_q, cosine, -sine).reshape(rows, local_cols).astype(jnp.bfloat16)
    grad_k = rotate(grad_rot_k, cosine, -sine).reshape(rows, local_cols).astype(jnp.bfloat16)
    grad_v = grad_values.reshape(rows, local_cols).astype(jnp.bfloat16)
    grad_proj = jnp.stack([grad_q, grad_k, grad_v], axis=1)
    grad_qkv = jnp.einsum("td,tcn->dcn", tokens_full, grad_proj, preferred_element_type=jnp.float32)
    input_part = jnp.einsum("tcn,dcn->td", grad_proj, qkv_full, preferred_element_type=jnp.float32)
    input_grad = (1.0 - attn_gain) * grad_mixed + lax.psum_scatter(
        input_part, "head", scatter_dimension=1, tiled=True
    )
    sum_qkv, sum_out, sum_up, sum_down, sum_sqk, sum_attn, sum_mlp, sum_suv = (
        lax.psum_scatter(grad_qkv, "batch", scatter_dimension=0, tiled=True),
        lax.psum_scatter(grad_out, "batch", scatter_dimension=1, tiled=True),
        lax.psum_scatter(grad_up, "batch", scatter_dimension=0, tiled=True),
        lax.psum_scatter(grad_down, "batch", scatter_dimension=1, tiled=True),
        lax.psum_scatter(grad_sqk, "batch", scatter_dimension=0, tiled=True),
        lax.psum_scatter(grad_alpha_attn, "batch", scatter_dimension=0, tiled=True),
        lax.psum_scatter(grad_alpha_mlp, "batch", scatter_dimension=0, tiled=True),
        lax.psum_scatter(grad_suv, "batch", scatter_dimension=1, tiled=True),
    )
    first_a, second_a, moved_a = adam_step(w_qkv, sum_qkv, moment_qkv, square_qkv)
    first_b, second_b, moved_b = adam_step(w_out, sum_out, moment_out, square_out)
    first_c, second_c, moved_c = adam_step(w_up, sum_up, moment_up, square_up)
    first_d, second_d, moved_d = adam_step(w_down, sum_down, moment_down, square_down)
    norm_a, norm_b, norm_c, norm_d = lax.psum(
        (
            jnp.sum(moved_a * moved_a, axis=0),
            jnp.sum(moved_b * moved_b, axis=1),
            jnp.sum(moved_c * moved_c, axis=0),
            jnp.sum(moved_d * moved_d, axis=1),
        ),
        "batch",
    )
    new_qkv = moved_a * lax.rsqrt(norm_a / width + layer_eps)[None]
    new_out = moved_b * lax.rsqrt(norm_b / width + layer_eps)[:, None]
    new_up = moved_c * lax.rsqrt(norm_c / width + layer_eps)[None]
    new_down = moved_d * lax.rsqrt(norm_d / width + layer_eps)[:, None]
    return (
        hidden,
        input_grad,
        sum_qkv,
        sum_out,
        sum_up,
        sum_down,
        first_a,
        first_b,
        first_c,
        first_d,
        second_a,
        second_b,
        second_c,
        second_d,
        new_qkv,
        new_out,
        new_up,
        new_down,
        sum_sqk,
        sum_attn,
        sum_mlp,
        sum_suv,
    )


def solution(mesh):
    return jax.shard_map(
        per_device,
        mesh=mesh,
        in_specs=(
            P("batch", "head"),
            P("batch", "head"),
            P("batch"),
            P("batch", None, "head"),
            P("head", "batch"),
            P("batch", None, "head"),
            P("head", "batch"),
            P("batch", None, "head"),
            P("head", "batch"),
            P("batch", None, "head"),
            P("head", "batch"),
            P("batch", None, "head"),
            P("head", "batch"),
            P("batch", None, "head"),
            P("head", "batch"),
            P("head"),
            P(),
            P(),
            P(None, "head"),
        ),
        out_specs=(
            P("batch", "head"),
            P("batch", "head"),
            P("batch", None, "head"),
            P("head", "batch"),
            P("batch", None, "head"),
            P("head", "batch"),
            P("batch", None, "head"),
            P("head", "batch"),
            P("batch", None, "head"),
            P("head", "batch"),
            P("batch", None, "head"),
            P("head", "batch"),
            P("batch", None, "head"),
            P("head", "batch"),
            P("batch", None, "head"),
            P("head", "batch"),
            P("batch", None, "head"),
            P("head", "batch"),
            P(("head", "batch")),
            P(("head", "batch")),
            P(("head", "batch")),
            P(None, ("head", "batch")),
        ),
        check_vma=False,
    )
```

profile of v0, /device:TPU:0, one launch (start us, length us, event | category | flops | bytes accessed | tf_op | source)
XLA Modules:
  0.0 1461.8 jit_solution(8556918816213938743)
XLA Ops:
  11.7 12.5 all_gather.26
  39.1 82.2 %all-gather.8.cloned.1.call-done = bf16[2048,1024]{1,0:T(8,128)(2,1)} async-done(((bf16[2048,256]{1,0:T(8,128)(2,1)}), bf16[2048,1024]{1,0:T(8,128)(2,1)}) %all-gather.8.cloned.1.call-update) | async-done | bytes 4194320 | tf_op jit(solution)/shard_map/all_gather | solution.py:90
  181.5 139.1 %reduce-scatter.12.cloned.1.call-done = f32[2048,256]{1,0:T(8,128)} async-done(((f32[2048,1024]{1,0:T(8,128)}), f32[2048,256]{1,0:T(8,128)}) %reduce-scatter.12.cloned.1.call-update) | async-done | bytes 2097168 | tf_op jit(solution)/shard_map/reduce_scatter | solution.py:139
  322.5 11.3 psum.84
  336.3 8.7 psum.85
  348.3 12.1 all-gather.14.cloned.1.call-done
  360.4 82.6 %all-gather.12.cloned.1.call-done = bf16[2048,1024]{1,0:T(8,128)(2,1)} async-done(((bf16[2048,256]{1,0:T(8,128)(2,1)}), bf16[2048,1024]{1,0:T(8,128)(2,1)}) %all-gather.12.cloned.1.call-update) | async-done | bytes 4194320 | tf_op jit(solution)/shard_map/all_gather | solution.py:145
  443.0 15.0 %fusion.26 = f32[2048,2,1024]{2,0,1:T(8,128)S(1)} fusion(bf16[1024,2,1024]{2,0,1:T(8,128)(2,1)} %all-gather.14.cloned.1.call-done, bf16[2048,1024]{1,0:T(8,128)(2,1)} %all-gather.12.cloned.1.call-done), kind=kOutput, calls=%fused_computation.53 | convolution fusion | flops 8589934592 | bytes 25165824 | tf_op jit(solution)/shard_map/td,dcf->tcf/dot_general | solution.py:146
  471.7 10.6 fusion.154
  483.2 143.8 %reduce-scatter.14.cloned.1.call-done = f32[2048,256]{1,0:T(8,128)} async-done(((f32[2048,1024]{1,0:T(8,128)}), f32[2048,256]{1,0:T(8,128)}) %reduce-scatter.14.cloned.1.call-update) | async-done | bytes 2097168 | tf_op jit(solution)/shard_map/reduce_scatter | solution.py:154
  629.0 11.3 psum.86
  642.5 8.5 psum.87
  655.0 10.5 psum.88
  670.3 8.5 psum.89
  682.2 80.5 %all-gather.18.cloned.1.call-done = bf16[2048,1024]{1,0:T(8,128)(2,1)} async-done(((bf16[2048,256]{1,0:T(8,128)(2,1)}), bf16[2048,1024]{1,0:T(8,128)(2,1)}) %all-gather.18.cloned.1.call-update) | async-done | bytes 4194320 | tf_op jit(solution)/shard_map/all_gather | solution.py:167
  762.7 15.9 %multiply_reduce_fusion.3 = (f32[1024]{0:T(1024)S(1)}, f32[1024]{0:T(1024)S(1)}, f32[2048,1024]{1,0:T(8,128)S(1)}, bf16[2048,1,1024]{2,0,1:T(8,128)(2,1)}) fusion(f32[2048,2,1024]{2,0,1:T(8,128)} %copy-done.15, f32[1024]{0:T(1024)S(1)} %bitcast.215, f32[1024]{0:T(1024)S(1)} %bitcast.218, bf16[2048,1024]{1,0:T(8,128)(2,1)} %all-gather.18.cloned.1.call-done, ...), kind=kOutput, calls=%fused_computation.23 | convolution fusion | flops 4334811136 | bytes 35667968 | tf_op jit(solution)/shard_map/td,fd->tf/dot_general | solution.py:169
  782.0 12.8 fusion.20
  794.9 142.8 %reduce-scatter.16.cloned.1.call-done = f32[2048,256]{1,0:T(8,128)} async-done(((f32[2048,1024]{1,0:T(8,128)}), f32[2048,256]{1,0:T(8,128)}) %reduce-scatter.16.cloned.1.call-update) | async-done | bytes 2097168 | tf_op jit(solution)/shard_map/reduce_scatter | solution.py:178
  940.6 11.3 psum.90
  957.1 8.5 psum.91
  970.2 10.0 fusion.155
  981.0 14.8 %fusion.18 = f32[1024,2,1024]{2,0,1:T(8,128)} fusion(bf16[2048,1,1024]{2,0,1:T(8,128)(2,1)} %copy-done.22, bf16[2048,1,1024]{2,0,1:T(8,128)(2,1)} %get-tuple-element.218, bf16[2048,1024]{1,0:T(8,128)(2,1)} %all-gather.12.cloned.1.call-done), kind=kOutput, calls=%fused_computation.45 | convolution fusion | flops 8606711808 | bytes 20971520 | tf_op jit(solution)/shard_map/td,tcf->dcf/dot_general | solution.py:176
  995.8 53.7 %all-gather.20.cloned.1.call-done = bf16[2048,1024]{1,0:T(8,128)(2,1)} async-done(((bf16[2048,256]{1,0:T(8,128)(2,1)}), bf16[2048,1024]{1,0:T(8,128)(2,1)}) %all-gather.20.cloned.1.call-update) | async-done | bytes 4194320 | tf_op jit(solution)/shard_map/all_gather | solution.py:184
  1077.9 9.9 multiply_convert_fusion.1
  1093.1 10.8 multiply_reduce_fusion
  1103.9 10.9 multiply_convert_fusion
  1148.2 10.1 fusion.63
  1185.5 29.8 %reduce-scatter.24.cloned.1.call-done = f32[128,2,1024]{2,0,1:T(8,128)} async-done(((f32[1024,2,1024]{2,0,1:T(8,128)}), f32[128,2,1024]{2,0,1:T(8,128)}) %reduce-scatter.24.cloned.1.call-update) | async-done | bytes 1048592 | tf_op jit(solution)/shard_map/reduce_scatter | solution.py:248
  1224.0 31.3 %reduce-scatter.22.cloned.1.call-done = f32[256,128]{1,0:T(8,128)} async-done(((f32[256,1024]{1,0:T(8,128)}), f32[256,128]{1,0:T(8,128)}) %reduce-scatter.22.cloned.1.call-update) | async-done | bytes 131088 | tf_op jit(solution)/shard_map/reduce_scatter | solution.py:247
  1257.0 48.2 %reduce-scatter.20.cloned.1.call-done = f32[128,3,256]{0,2,1:T(8,128)} async-done(((f32[1024,3,256]{0,2,1:T(8,128)}), f32[128,3,256]{0,2,1:T(8,128)}) %reduce-scatter.20.cloned.1.call-update) | async-done | bytes 393232 | tf_op jit(solution)/shard_map/reduce_scatter | solution.py:246
  1307.4 23.8 %all-reduce.5 = (f32[3,256]{1,0:T(4,128)S(1)}, f32[256]{0:T(256)}, f32[2,1024]{1,0:T(2,128)S(1)}, f32[1024]{0:T(1024)S(1)}, f32[256]{0:T(256)}, /*index=5*/f32[256]{0:T(256)}, f32[256]{0:T(256)}) all-reduce(f32[3,256]{1,0:T(4,128)S(1)} %get-tuple-element.204, ...), channel_id=1, replica_groups=mesh['head'=4,'batch'=8] {'batch'}, use_global_device_ids=true, to_apply=%region_41.42 | all-reduce | flops 4864 | bytes 38912 | tf_op jit(solution)/shard_map/psum | solution.py:259
  1343.9 108.0 %reduce-scatter.18.cloned.1.call-done = f32[2048,256]{1,0:T(8,128)} async-done(((f32[2048,1024]{1,0:T(8,128)}), f32[2048,256]{1,0:T(8,128)}) %reduce-scatter.18.cloned.1.call-update) | async-done | bytes 2097168 | tf_op jit(solution)/shard_map/reduce_scatter | solution.py:242
  (392 shorter events, 255.6 us)
Async XLA Ops:
  7.2 31.9 %all-gather.10.cloned.1.call-start = ((), (), s32[]{:S(2)}) async-start(), calls=%async_computation.10 | async-start | bytes 1769472 | tf_op jit(solution)/shard_map/all_gather | solution.py:85
  8.4 118.6 %copy-start.26 = (f32[128,3,256]{0,2,1:T(8,128)}, f32[128,3,256]{0,2,1:T(8,128)S(1)}, u32[]{:S(2)}) copy-start(f32[128,3,256]{0,2,1:T(8,128)S(1)} %copy.67) | copy-start | bytes 1179652
  9.2 112.1 %all-gather.8.cloned.1.call-start = ((), (), s32[]{:S(2)}) async-start(), calls=%async_computation.9 | async-start | bytes 5242880 | tf_op jit(solution)/shard_map/all_gather | solution.py:90
  9.9 310.7 %reduce-scatter.12.cloned.1.call-start = ((), (), s32[]{:S(2)}) async-start(), calls=%async_computation.11 | async-start | bytes 10485760 | tf_op jit(solution)/shard_map/reduce_scatter | solution.py:139
  10.8 120.1 %copy-start.89 = (f32[4,64]{1,0:T(4,128)}, f32[4,64]{1,0:T(4,128)S(1)}, u32[]{:S(2)}) copy-start(f32[4,64]{1,0:T(4,128)S(1)} %mul.741) | copy-start | bytes 3076
  28.3 101.3 %copy-start.37 = (f32[2048,32]{0,1:T(8,128)}, f32[2048,32]{0,1:T(8,128)S(1)}, u32[]{:S(2)}) copy-start(f32[2048,32]{0,1:T(8,128)S(1)} %get-tuple-element.239) | copy-start | bytes 786436
  127.6 38.0 %copy-start.14 = (bf16[2048,1,256]{0,2,1:T(8,128)(2,1)}, bf16[2048,1,256]{0,2,1:T(8,128)(2,1)S(1)}, u32[]{:S(2)}) copy-start(bf16[2048,1,256]{0,2,1:T(8,128)(2,1)S(1)} %slice.518) | copy-start | bytes 3145732
  177.8 156.1 %copy-start.20 = (bf16[2048,256]{1,0:T(8,128)(2,1)S(1)}, bf16[2048,256]{1,0:T(8,128)(2,1)}, u32[]{:S(2)}) copy-start(bf16[2048,256]{1,0:T(8,128)(2,1)} %param.39) | copy-start | bytes 3145732
  177.8 182.6 %all-gather.14.cloned.1.call-start = ((), (), s32[]{:S(2)}) async-start(), calls=%async_computation.13 | async-start | bytes 4718592 | tf_op jit(solution)/shard_map/all_gather | solution.py:87
  180.1 262.9 %all-gather.12.cloned.1.call-start = ((), (), s32[]{:S(2)}) async-start(), calls=%async_computation.12 | async-start | bytes 5242880 | tf_op jit(solution)/shard_map/all_gather | solution.py:145
  346.4 125.3 %all-gather.16.cloned.1.call-start = ((), (), s32[]{:S(2)}) async-start(), calls=%async_computation.14 | async-start | bytes 2359296 | tf_op jit(solution)/shard_map/all_gather | solution.py:88
  348.3 278.8 %reduce-scatter.14.cloned.1.call-start = ((), (), s32[]{:S(2)}) async-start(), calls=%async_computation.15 | async-start | bytes 10485760 | tf_op jit(solution)/shard_map/reduce_scatter | solution.py:154
  482.4 280.3 %all-gather.18.cloned.1.call-start = ((), (), s32[]{:S(2)}) async-start(), calls=%async_computation.16 | async-start | bytes 5242880 | tf_op jit(solution)/shard_map/all_gather | solution.py:167
  682.1 255.5 %reduce-scatter.16.cloned.1.call-start = ((), (), s32[]{:S(2)}) async-start(), calls=%async_computation.17 | async-start | bytes 10485760 | tf_op jit(solution)/shard_map/reduce_scatter | solution.py:178
  794.9 254.7 %all-gather.20.cloned.1.call-start = ((), (), s32[]{:S(2)}) async-start(), calls=%async_computation.18 | async-start | bytes 5242880 | tf_op jit(solution)/shard_map/all_gather | solution.py:184
  969.0 212.5 %reduce-scatter.28.cloned.1.call-start = ((), (), s32[]{:S(2)}) async-start(), calls=%async_computation.24 | async-start | bytes 589824
  970.1 212.8 %reduce-scatter.26.cloned.1.call-start = ((), (), s32[]{:S(2)}) async-start(), calls=%async_computation.23 | async-start | bytes 4718592 | tf_op jit(solution)/shard_map/reduce_scatter | solution.py:249
  980.2 235.1 %reduce-scatter.24.cloned.1.call-start = ((), (), s32[]{:S(2)}) async-start(), calls=%async_computation.22 | async-start | bytes 9437184 | tf_op jit(solution)/shard_map/reduce_scatter | solution.py:248
  995.8 53.8 %copy-start.41 = (bf16[256,1024]{1,0:T(8,128)(2,1)S(1)}, bf16[256,1024]{1,0:T(8,128)(2,1)}, u32[]{:S(2)}) copy-start(bf16[256,1024]{1,0:T(8,128)(2,1)} %all_gather.26) | copy-start | bytes 1572868
  995.8 58.3 %copy-start.55 = (bf16[512,1,256]{0,2,1:T(8,128)(2,1)S(1)}, bf16[512,1,256]{0,2,1:T(8,128)(2,1)}, u32[]{:S(2)}) copy-start(bf16[512,1,256]{0,2,1:T(8,128)(2,1)} %copy-done.54) | copy-start | bytes 786436
  995.8 259.5 %reduce-scatter.22.cloned.1.call-start = ((), (), s32[]{:S(2)}) async-start(), calls=%async_computation.21 | async-start | bytes 1179648 | tf_op jit(solution)/shard_map/reduce_scatter | solution.py:247
  1148.2 157.0 %reduce-scatter.20.cloned.1.call-start = ((), (), s32[]{:S(2)}) async-start(), calls=%async_computation.20 | async-start | bytes 3538944 | tf_op jit(solution)/shard_map/reduce_scatter | solution.py:246
  1168.1 283.8 %reduce-scatter.18.cloned.1.call-start = ((), (), s32[]{:S(2)}) async-start(), calls=%async_computation.19 | async-start | bytes 10485760 | tf_op jit(solution)/shard_map/reduce_scatter | solution.py:242
  1177.8 37.4 %copy-start.24 = (f32[128,2,1024]{2,1,0:T(2,128)S(1)}, f32[128,2,1024]{2,1,0:T(2,128)}, u32[]{:S(2)}) copy-start(f32[128,2,1024]{2,1,0:T(2,128)} %param.44) | copy-start | bytes 3145732
  1218.5 36.8 %copy-start.63 = (f32[256,128]{1,0:T(8,128)S(1)}, f32[256,128]{1,0:T(8,128)}, u32[]{:S(2)}) copy-start(f32[256,128]{1,0:T(8,128)} %param.43) | copy-start | bytes 393220
  1218.5 36.7 %copy-start.75 = (f32[256,128]{1,0:T(8,128)S(1)}, f32[256,128]{1,0:T(8,128)}, u32[]{:S(2)}) copy-start(f32[256,128]{1,0:T(8,128)} %param.51) | copy-start | bytes 393220
  1218.5 36.7 %copy-start.76 = (f32[256,128]{1,0:T(8,128)S(1)}, f32[256,128]{1,0:T(8,128)}, u32[]{:S(2)}) copy-start(f32[256,128]{1,0:T(8,128)} %param.47) | copy-start | bytes 393220
  1218.5 86.6 %copy-start.27 = (f32[128,3,256]{0,2,1:T(8,128)S(1)}, f32[128,3,256]{0,2,1:T(8,128)}, u32[]{:S(2)}) copy-start(f32[128,3,256]{0,2,1:T(8,128)} %copy-done.26) | copy-start | bytes 1179652
  1222.1 85.3 %copy-start.93 = (f32[256]{0:T(256)S(1)}, f32[256]{0:T(256)}, u32[]{:S(2)}) copy-start(f32[256]{0:T(256)} %get-tuple-element.180) | copy-start | bytes 3076
  1222.1 85.3 %copy-start.94 = (f32[256]{0:T(256)S(1)}, f32[256]{0:T(256)}, u32[]{:S(2)}) copy-start(f32[256]{0:T(256)} %get-tuple-element.182) | copy-start | bytes 3076
  1333.2 118.7 %copy-start.13 = (f32[2048,256]{1,0:T(8,128)S(1)}, f32[2048,256]{1,0:T(8,128)}, u32[]{:S(2)}) copy-start(f32[2048,256]{1,0:T(8,128)} %get-tuple-element.210) | copy-start | bytes 6291460
  1333.2 118.7 %copy-start.95 = (f32[256]{0:T(256)S(1)}, f32[256]{0:T(256)}, u32[]{:S(2)}) copy-start(f32[256]{0:T(256)} %get-tuple-element.208) | copy-start | bytes 3076
  (94 other events, 585.7 us)
Sparse Core Ops, SparseCore 0:
  10.5 28.5 all-gather.9
  40.7 80.5 all-gather.7
  177.9 142.6 reduce-scatter.11
  322.9 37.4 all-gather.13
  362.4 80.5 all-gather.11
  445.3 26.3 all-gather.15
  482.5 144.4 reduce-scatter.13
  682.3 80.3 all-gather.17
  795.0 142.6 reduce-scatter.15
  969.1 80.3 all-gather.19
  1052.6 32.3 reduce-scatter.27
  1089.2 51.3 reduce-scatter.25
  1144.0 71.2 reduce-scatter.23
  1219.2 36.0 reduce-scatter.21
  1258.9 46.2 reduce-scatter.19
  1307.3 144.4 reduce-scatter.17
where the time goes:
time: 1470 us; the launch traced here: 1460 us
  waiting for transfers between devices  967 us (66%)
  matrix products  208 us (14%)
  blocking collectives  115 us (8%)
  other arithmetic  107 us (7%)
  local copies, waits for them, and re-layouts  48.1 us (3%)
  between operations  16.5 us (1%)
    reduce_scatter x1, waiting for transfers between devices, per_device(): lax.psum_scatter(mlp_part, 'head', scatter_dimension=1, tiled=True)  144 us
    reduce_scatter x1, waiting for transfers between devices, per_device(): lax.psum_scatter(back_part, 'head', scatter_dimension=1, tiled=True)  143 us
    reduce_scatter x1, waiting for transfers between devices, per_device(): lax.psum_scatter(out_part, 'head', scatter_dimension=1, tiled=True)  139 us
    reduce_scatter x1, waiting for transfers between devices, per_device(): lax.psum_scatter(input_part, 'head', scatter_dimension=1, tiled=True)  108 us
    all_gather x1, waiting for transfers between devices, per_device(): lax.all_gather(first_hidden.astype(jnp.bfloat16), 'head', axis=1, tiled=T...  82.6 us
    all_gather x1, waiting for transfers between devices, per_device(): tokens_full = lax.all_gather(layer_input, 'head', axis=1, tiled=True)  82.2 us
    all_gather x1, waiting for transfers between devices, per_device(): lax.all_gather(grad_mlp_sum.astype(jnp.bfloat16), 'head', axis=1, tiled=T...  80.5 us
    all_gather x1, waiting for transfers between devices, per_device(): lax.all_gather(grad_attn_sum.astype(jnp.bfloat16), 'head', axis=1, tiled=...  53.7 us
  transfers between devices with their start and end apart: 16, of which 14 were waited for; matrix products, arithmetic and copies ran while one was open for 15% of the time, Pallas kernels for 0%

commit v1 on v0

v1 whole, which is shorter than its diff:
```python
import functools
import math

import jax
import jax.numpy as jnp
from jax import lax
from jax.experimental import pallas as pl
from jax.experimental.pallas import tpu as pltpu
from jax.sharding import PartitionSpec as P

HEAD_DIM = 64
SHORT = 1024

layer_eps = 1e-06
learn_rate = 0.008
beta_one = 0.9
beta_two = 0.95
adam_eps = 1e-08
bias_one = 1.0 - math.exp(100.0 * math.log(0.9))
bias_two = 1.0 - math.exp(100.0 * math.log(0.95))
score_scale = 8.0
LOG2E = math.log2(math.e)
LN2 = math.log(2.0)

bf16 = jnp.bfloat16
f32 = jnp.float32
VMEM_LIMIT = 56 * 1024 * 1024


def dot(a, b):
    return jnp.dot(a, b, preferred_element_type=f32)


def dot_t(a, b):
    return lax.dot_general(a, b, (((1,), (1,)), ((), ())), preferred_element_type=f32)


def t_dot(a, b):
    return lax.dot_general(a, b, (((0,), (0,)), ((), ())), preferred_element_type=f32)


def params():
    return pltpu.CompilerParams(vmem_limit_bytes=VMEM_LIMIT)


def full_spec(shape):
    return pl.BlockSpec(shape, lambda *_: (0,) * len(shape))


def head_sum(value, ones):
    high = value.astype(bf16)
    low = (value - high.astype(f32)).astype(bf16)
    return dot(high, ones) + dot(low, ones)


def swap_halves(value):
    cols = value.shape[-1]
    half = HEAD_DIM // 2
    lane = lax.broadcasted_iota(jnp.int32, value.shape, 1)
    first = (lane % HEAD_DIM) < half
    up = pltpu.roll(value, cols - half, 1)
    down = pltpu.roll(value, half, 1)
    return jnp.where(first, up, down)


def qkv_kernel(z_ref, *refs, parts):
    lefts = refs[: parts - 1]
    own_ref = refs[parts - 1]
    rights = refs[parts : 2 * parts - 1]
    w_ref, cos_ref, sin_ref, gain_ref, ones_ref, x_ref, q_ref, k_ref, v_ref, rq_ref, rk_ref = refs[2 * parts - 1 :]
    cols = v_ref.shape[1]
    z = z_ref[0]
    for s in range(parts):
        value = own_ref[...]
        for at in range(parts):
            if at != s:
                other = lefts[s - at - 1] if s > at else rights[at - s - 1]
                value = jnp.where(z == at, other[...], value)
        x_ref[:, s * cols : (s + 1) * cols] = value
    proj = dot(x_ref[...], w_ref[...])
    cosine = cos_ref[...]
    sine = sin_ref[...]
    ones = ones_ref[...]
    gain = gain_ref[...]
    for c, (out, rho_ref, scale) in enumerate(
        ((q_ref, rq_ref, score_scale * LOG2E), (k_ref, rk_ref, 1.0))
    ):
        part = proj[:, c * cols : (c + 1) * cols]
        rho = lax.rsqrt(head_sum(part * part, ones) + layer_eps)
        rot = part * cosine + swap_halves(part) * sine
        out[...] = (rot * rho * (gain * scale)).astype(bf16)
        rho_ref[...] = rho
    v_ref[...] = proj[:, 2 * cols :].astype(bf16)


def qkv_project(z, lefts, own, rights, w, cosine, sine, gain, ones):
    rows, cols = own.shape
    parts = len(lefts) + 1
    width = parts * cols
    blk = 512
    row = lambda n: pl.BlockSpec((blk, n), lambda i, s: (i, 0))
    return pl.pallas_call(
        functools.partial(qkv_kernel, parts=parts),
        grid_spec=pltpu.PrefetchScalarGridSpec(
            num_scalar_prefetch=1,
            grid=(rows // blk,),
            in_specs=[row(cols)] * (2 * parts - 1)
            + [full_spec((width, 3 * cols)), row(cols), row(cols)]
            + [full_spec((1, cols)), full_spec((cols, cols))],
            out_specs=[row(width)] + [row(cols)] * 5,
        ),
        out_shape=[jax.ShapeDtypeStruct((rows, width), bf16)]
        + [jax.ShapeDtypeStruct((rows, cols), bf16)] * 3
        + [jax.ShapeDtypeStruct((rows, cols), f32)] * 2,
        compiler_params=params(),
    )(z, *lefts, own, *rights, w, cosine, sine, gain, ones)


def head_masks(cols, heads):
    lane = lax.broadcasted_iota(jnp.int32, (1, cols), 1) // HEAD_DIM
    return [(lane == h) for h in range(heads)]


def masked(value, mask):
    return jnp.where(mask, value, jnp.zeros_like(value))


def attn_fwd_kernel(long_ref, q_ref, k_ref, v_ref, y_ref, l_ref, acc, mass, *, heads, blk, sub):
    i = pl.program_id(0)
    cols = q_ref.shape[1]
    masks = head_masks(cols, heads)
    per = SHORT // blk
    low = jnp.where(long_ref[0] != 0, 0, (i // per) * per)
    acc[...] = jnp.zeros_like(acc)
    mass[...] = jnp.zeros_like(mass)

    def lanes(p):
        total = p[:, 0:128]
        for n in range(1, p.shape[1] // 128):
            total = total + p[:, n * 128 : (n + 1) * 128]
        return total

    def body(j, carry):
        start = pl.multiple_of(j * blk, blk)
        keys = k_ref[pl.ds(start, blk), :]
        vals = v_ref[pl.ds(start, blk), :]
        q = q_ref[...]
        total = jnp.zeros(acc.shape, f32)
        for h in range(heads):
            p = jnp.exp2(dot_t(masked(q, masks[h]), keys))
            mass[h] += lanes(p)
            total += dot(p.astype(bf16), masked(vals, masks[h]))
        acc[...] += total
        return carry

    lax.fori_loop(low, i, body, 0)
    start = pl.multiple_of(i * blk, blk)
    causal = lax.broadcasted_iota(jnp.int32, (sub, sub), 0) >= lax.broadcasted_iota(
        jnp.int32, (sub, sub), 1
    )
    for a in range(blk // sub):
        rows = slice(a * sub, (a + 1) * sub)
        q = q_ref[rows, :]
        for b in range(a + 1):
            at = pl.multiple_of(start + b * sub, sub)
            keys = k_ref[pl.ds(at, sub), :]
            vals = v_ref[pl.ds(at, sub), :]
            total = jnp.zeros((sub, cols), f32)
            for h in range(heads):
                p = jnp.exp2(dot_t(masked(q, masks[h]), keys))
                if a == b:
                    p = jnp.where(causal, p, 0.0)
                mass[h, rows, :] += lanes(p)
                total += dot(p.astype(bf16), masked(vals, masks[h]))
            acc[rows, :] += total
    inverse = jnp.zeros(acc.shape, f32)
    logs = jnp.zeros(l_ref.shape, f32)
    lane = lax.broadcasted_iota(jnp.int32, l_ref.shape, 1)
    for h in range(heads):
        column = jnp.sum(mass[h], axis=1, keepdims=True)
        inverse = jnp.where(masks[h], 1.0 / column, inverse)
        logs = jnp.where(lane == h, jnp.log2(column), logs)
    y_ref[...] = (acc[...] * inverse).astype(bf16)
    l_ref[...] = logs


def attn_fwd(is_long, q, k, v):
    rows, cols = q.shape
    heads = cols // HEAD_DIM
    blk, sub = 512, 256
    row = lambda n: pl.BlockSpec((blk, n), lambda i, s: (i, 0))
    return pl.pallas_call(
        functools.partial(attn_fwd_kernel, heads=heads, blk=blk, sub=sub),
        grid_spec=pltpu.PrefetchScalarGridSpec(
            num_scalar_prefetch=1,
            grid=(rows // blk,),
            in_specs=[row(cols), full_spec((rows, cols)), full_spec((rows, cols))],
            out_specs=[row(cols), row(128)],
            scratch_shapes=[pltpu.VMEM((blk, cols), f32), pltpu.VMEM((heads, blk, 128), f32)],
        ),
        out_shape=[
            jax.ShapeDtypeStruct((rows, cols), bf16),
            jax.ShapeDtypeStruct((rows, 128), f32),
        ],
        compiler_params=params(),
    )(is_long, q, k, v)


def attn_bwd_kernel(
    long_ref, q_ref, qk_ref, dy_ref, y_ref, l_ref, k_ref, v_ref, rq_ref, rk_ref, cos_ref, sin_ref, gain_ref,
    ones_ref, dk_in, dv_in, out_ref, dk_out, dv_out, s_ref, acc, dk_acc, dv_acc, stats, *, heads, blk, sub, first, count
):
    step = pl.program_id(0)
    local = count - 1 - step
    i = first + local
    cols = q_ref.shape[1]
    masks = head_masks(cols, heads)
    per = SHORT // blk
    low = jnp.where(long_ref[0] != 0, 0, (i // per) * per)
    ones = ones_ref[...]
    gain = gain_ref[...]

    @pl.when(step == 0)
    def _():
        dk_acc[...] = jnp.zeros_like(dk_acc)
        dv_acc[...] = jnp.zeros_like(dv_acc)
        s_ref[...] = jnp.zeros_like(s_ref)
        if dk_in is not None:
            dk_acc[...] = dk_in[...]
            dv_acc[...] = dv_in[...]

    acc[...] = jnp.zeros_like(acc)
    prod = dy_ref[...].astype(f32) * y_ref[...].astype(f32)
    high = prod.astype(bf16)
    rest = (prod - high.astype(f32)).astype(bf16)
    pickers = (
        lax.broadcasted_iota(jnp.int32, (8, cols), 1) // HEAD_DIM
        == lax.broadcasted_iota(jnp.int32, (8, cols), 0)
    ).astype(bf16)
    stats[0:8, :] = dot_t(pickers, high) + dot_t(pickers, rest)
    stats[8:16, :] = l_ref[...].T[0:8, :]

    def piece(at, size, rows, causal):
        keys = k_ref[pl.ds(at, size), :]
        vals = v_ref[pl.ds(at, size), :]
        q = q_ref[rows, :]
        dy = dy_ref[rows, :]
        total_q = jnp.zeros(q.shape, f32)
        total_k = jnp.zeros(keys.shape, f32)
        total_v = jnp.zeros(keys.shape, f32)
        for h in range(heads):
            qm = masked(q, masks[h])
            dym = masked(dy, masks[h])
            p = jnp.exp2(dot_t(keys, qm) - stats[8 + h : 9 + h, rows])
            if causal is not None:
                p = jnp.where(causal, p, 0.0)
            ds = (p * (dot_t(vals, dym) - stats[h : h + 1, rows])).astype(bf16)
            total_v += dot(p.astype(bf16), dym)
            total_k += dot(ds, qm)
            total_q += t_dot(ds, masked(keys, masks[h]))
        acc[rows, :] += total_q
        dk_acc[pl.ds(at, size), :] += total_k
        dv_acc[pl.ds(at, size), :] += total_v

    def body(j, carry):
        piece(pl.multiple_of(j * blk, blk), blk, slice(0, blk), None)
        return carry

    lax.fori_loop(low, i, body, 0)
    start = pl.multiple_of(i * blk, blk)
    causal = lax.broadcasted_iota(jnp.int32, (sub, sub), 0) <= lax.broadcasted_iota(
        jnp.int32, (sub, sub), 1
    )
    for a in range(blk // sub):
        for b in range(a + 1):
            piece(
                pl.multiple_of(start + b * sub, sub),
                sub,
                slice(a * sub, (a + 1) * sub),
                causal if a == b else None,
            )
    cosine = cos_ref[...]
    sine = sin_ref[...]
    total = jnp.zeros((1, cols), f32)
    here = pl.ds(start, blk)
    for c, (value, unit, rho_ref, up, scale) in enumerate(
        (
            (acc[...], q_ref[...], rq_ref, score_scale, score_scale * LOG2E),
            (dk_acc[here, :], k_ref[here, :], rk_ref, LN2, 1.0),
        )
    ):
        grad = value * up
        unit = unit.astype(f32) * (1.0 / (gain * scale))
        total += jnp.sum(grad * unit, axis=0, keepdims=True)
        grad = grad * gain
        back = rho_ref[...] * (grad - unit * head_sum(grad * unit, ones))
        turned = back * cosine - swap_halves(back) * sine
        out_ref[:, c * cols : (c + 1) * cols] = turned.astype(bf16)
    out_ref[:, 2 * cols :] = dv_acc[here, :].astype(bf16)
    s_ref[0:1, :] += total
    if dk_out is not None:
        @pl.when(step == count - 1)
        def _():
            dk_out[...] = dk_acc[0 : first * blk, :]
            dv_out[...] = dv_acc[0 : first * blk, :]


def attn_bwd(is_long, q, k, v, dy, y, logs, rq, rk, cosine, sine, gain, ones, first, count, carry):
    rows, cols = q.shape
    heads = cols // HEAD_DIM
    blk, sub = 512, 256
    top = (first + count) * blk
    at = lambda s: first + count - 1 - s
    row = lambda n: pl.BlockSpec((blk, n), lambda s, m: (at(s), 0))
    whole = pl.BlockSpec((top, cols), lambda s, m: (0, 0))
    ins = [q, k, dy, y, logs, k, v, rq, rk, cosine, sine, gain, ones]
    in_specs = [row(cols)] * 4 + [row(128), whole, whole] + [row(cols)] * 4
    in_specs += [full_spec((1, cols)), full_spec((cols, cols))]
    body = functools.partial(
        attn_bwd_kernel, heads=heads, blk=blk, sub=sub, first=first, count=count
    )
    outs = [jax.ShapeDtypeStruct((count * blk, 3 * cols), bf16)]
    out_specs = [pl.BlockSpec((blk, 3 * cols), lambda s, m: (count - 1 - s, 0))]
    if first:
        outs += [jax.ShapeDtypeStruct((first * blk, cols), f32)] * 2
        out_specs += [full_spec((first * blk, cols))] * 2
        inner = lambda *r: body(*r[:14], None, None, *r[14:])
    else:
        ins += carry
        in_specs += [full_spec((top, cols))] * 2
        inner = lambda *r: body(*r[:17], None, None, *r[17:])
    outs.append(jax.ShapeDtypeStruct((8, cols), f32))
    out_specs.append(full_spec((8, cols)))
    return pl.pallas_call(
        inner,
        grid_spec=pltpu.PrefetchScalarGridSpec(
            num_scalar_prefetch=1,
            grid=(count,),
            in_specs=in_specs,
            out_specs=out_specs,
            scratch_shapes=[
                pltpu.VMEM((blk, cols), f32),
                pltpu.VMEM((top, cols), f32),
                pltpu.VMEM((top, cols), f32),
                pltpu.VMEM((16, blk), f32),
            ],
        ),
        out_shape=outs,
        compiler_params=params(),
    )(is_long, *ins)


def row_norm(value):
    return lax.rsqrt(jnp.mean(value * value, axis=1, keepdims=True) + layer_eps)


def norm_back(scale, result, grad):
    return scale * (grad - result * jnp.mean(grad * result, axis=1, keepdims=True))


def pack_kernel(core_ref, up_ref, down_ref, out_ref, qkv_ref, mine_ref, theirs_ref, q_ref, o_ref):
    half = up_ref.shape[2] // 2
    low = core_ref[0] == 0
    down = down_ref[...].astype(bf16).T
    o_ref[...] = out_ref[...].astype(bf16).T
    for ref, first in ((mine_ref, low), (theirs_ref, jnp.logical_not(low))):
        for c in range(2):
            ref[:, c * half : (c + 1) * half] = jnp.where(
                first, up_ref[:, c, :half], up_ref[:, c, half:]
            ).astype(bf16)
        ref[:, 2 * half : 3 * half] = jnp.where(first, down[:, :half], down[:, half:])
    cols = qkv_ref.shape[2]
    for c in range(3):
        q_ref[:, c * cols : (c + 1) * cols] = qkv_ref[:, c, :].astype(bf16)


def pack(core, w_up, w_down, w_out, w_qkv):
    span, _, hid = w_up.shape
    cols = w_qkv.shape[2]
    vmem = pl.BlockSpec(memory_space=pltpu.VMEM)
    return pl.pallas_call(
        pack_kernel,
        in_specs=[pl.BlockSpec(memory_space=pltpu.SMEM)] + [vmem] * 4,
        out_specs=[vmem] * 4,
        out_shape=[jax.ShapeDtypeStruct((span, 3 * hid // 2), bf16)] * 2
        + [jax.ShapeDtypeStruct((span, 3 * cols), bf16), jax.ShapeDtypeStruct((span, cols), bf16)],
        compiler_params=params(),
    )(core, w_up, w_down, w_out, w_qkv)


def attn_out_kernel(place_ref, *refs, parts, chips):
    ys = refs[:parts]
    w_ref, x_ref, alpha_ref, ha_ref, h1_ref, hb_ref, stat_ref, acc = refs[parts:]
    z, chip = place_ref[0], place_ref[1]
    chunk = x_ref.shape[1] // chips
    for r in range(chips):
        at = pl.ds(pl.multiple_of((r ^ chip) * chunk, chunk), chunk)
        part = jnp.zeros((x_ref.shape[0], chunk), f32)
        for k in range(parts):
            part += dot_t(ys[k][...], w_ref[lax.rem(z + k, parts), at, :])
        acc[:, r * chunk : (r + 1) * chunk] = part
    total = acc[...]
    norm = row_norm(total)
    hidden = total * norm
    start = x_ref[...].astype(f32)
    mixed = start + alpha_ref[...] * (hidden - start)
    first_norm = row_norm(mixed)
    out = mixed * first_norm
    ha_ref[...] = hidden
    h1_ref[...] = out
    hb_ref[...] = out.astype(bf16)
    lane = lax.broadcasted_iota(jnp.int32, stat_ref.shape, 1)
    stat_ref[...] = jnp.where(lane == 0, norm, first_norm)


def attn_out(place, ys, w, x, alpha, chips):
    rows, width = x.shape
    cols = ys[0].shape[1]
    blk = 256
    row = lambda n: pl.BlockSpec((blk, n), lambda i, s: (i, 0))
    return pl.pallas_call(
        functools.partial(attn_out_kernel, parts=len(ys), chips=chips),
        grid_spec=pltpu.PrefetchScalarGridSpec(
            num_scalar_prefetch=1,
            grid=(rows // blk,),
            in_specs=[row(cols)] * len(ys)
            + [full_spec(w.shape), row(width), full_spec((1, width))],
            out_specs=[row(width)] * 3 + [row(128)],
            scratch_shapes=[pltpu.VMEM((blk, width), f32)],
        ),
        out_shape=[jax.ShapeDtypeStruct((rows, width), d) for d in (f32, f32, bf16)]
        + [jax.ShapeDtypeStruct((rows, 128), f32)],
        compiler_params=params(),
    )(place, *ys, w, x, alpha)


def loss_kernel(own_ref, got_ref, h1_ref, cot_ref, alpha_ref, hidden_ref, dmo_ref, base_ref, ga_ref):
    total = own_ref[...] + got_ref[...].astype(f32)
    alpha = alpha_ref[...]
    norm = row_norm(total)
    inner = total * norm
    h1 = h1_ref[...]
    mixed = h1 + alpha * (inner - h1)
    last = row_norm(mixed)
    hidden = mixed * last
    grad = norm_back(last, hidden, cot_ref[...].astype(f32))
    hidden_ref[...] = hidden.astype(bf16)
    base_ref[...] = (1.0 - alpha) * grad
    dmo_ref[...] = norm_back(norm, inner, alpha * grad).astype(bf16)

    @pl.when(pl.program_id(0) == 0)
    def _():
        ga_ref[...] = jnp.zeros_like(ga_ref)

    ga_ref[0:1, :] += jnp.sum(grad * (inner - h1), axis=0, keepdims=True)


def loss(own, got, h1, cot, alpha):
    rows, width = own.shape
    blk = 256
    row = pl.BlockSpec((blk, width), lambda i: (i, 0))
    return pl.pallas_call(
        loss_kernel,
        grid=(rows // blk,),
        in_specs=[row] * 4 + [full_spec((1, width))],
        out_specs=[row] * 3 + [full_spec((8, width))],
        out_shape=[jax.ShapeDtypeStruct((rows, width), d) for d in (bf16, bf16, f32)]
        + [jax.ShapeDtypeStruct((8, width), f32)],
        compiler_params=params(),
    )(own, got, h1, cot, alpha)


def first_back_kernel(place_ref, own_ref, got_ref, base_ref, h1_ref, ha_ref, x_ref, stat_ref, alpha_ref, w_ref, *outs, parts, chips):
    do_ref, through_ref, ga_ref = outs[:3]
    dys = outs[3:]
    z, chip = place_ref[0], place_ref[1]
    alpha = alpha_ref[...]
    grad = base_ref[...] + own_ref[...] + got_ref[...].astype(f32)
    grad = norm_back(stat_ref[:, 1:2], h1_ref[...], grad)
    ha = ha_ref[...]
    through_ref[...] = ((1.0 - alpha) * grad).astype(bf16)
    back = norm_back(stat_ref[:, 0:1], ha, alpha * grad).astype(bf16)
    do_ref[...] = back
    chunk = back.shape[1] // chips
    for k in range(parts):
        part = jnp.zeros(dys[k].shape, f32)
        for r in range(chips):
            at = pl.ds(pl.multiple_of((r ^ chip) * chunk, chunk), chunk)
            part += dot(
                do_ref[:, r * chunk : (r + 1) * chunk], w_ref[lax.rem(z + k, parts), at, :]
            )
        dys[k][...] = part.astype(bf16)

    @pl.when(pl.program_id(0) == 0)
    def _():
        ga_ref[...] = jnp.zeros_like(ga_ref)

    ga_ref[0:1, :] += jnp.sum(grad * (ha - x_ref[...].astype(f32)), axis=0, keepdims=True)


def first_back(place, own, got, base, h1, ha, x, stat, alpha, w, chips):
    rows, width = own.shape
    parts, _, cols = w.shape
    blk = 256
    row = lambda n: pl.BlockSpec((blk, n), lambda i, s: (i, 0))
    return pl.pallas_call(
        functools.partial(first_back_kernel, parts=parts, chips=chips),
        grid_spec=pltpu.PrefetchScalarGridSpec(
            num_scalar_prefetch=1,
            grid=(rows // blk,),
            in_specs=[row(width)] * 6
            + [row(128), full_spec((1, width)), full_spec(w.shape)],
            out_specs=[row(width)] * 2 + [full_spec((8, width))] + [row(cols)] * parts,
        ),
        out_shape=[jax.ShapeDtypeStruct((rows, width), bf16)] * 2
        + [jax.ShapeDtypeStruct((8, width), f32)]
        + [jax.ShapeDtypeStruct((rows, cols), bf16)] * parts,
        compiler_params=params(),
    )(place, own, got, base, h1, ha, x, stat, alpha, w)


def fetch_weights(q, slots, wbuf, sems):
    def copies(j):
        at = 0
        found = []
        for p, piece in enumerate(slots[j]):
            size = piece.shape[0]
            found.append(
                pltpu.make_async_copy(
                    piece, wbuf.at[j % 2, at : at + size, :], sems.at[j % 2, p]
                )
            )
            at += size
        return found

    for j in range(len(slots)):

        @pl.when(q == j)
        def _(j=j):
            if j == 0:
                for copy in copies(0):
                    copy.start()
            if j + 1 < len(slots):
                for copy in copies(j + 1):
                    copy.start()
            for copy in copies(j):
                copy.wait()


def mlp_fwd_kernel(*refs, half, counts, carried):
    total = sum(counts)
    flat, refs = refs[:total], refs[total:]
    slots, at = [], 0
    for n in counts:
        slots.append(flat[at : at + n])
        at += n
    ha_ref, hb_ref, suv_ref = refs[:3]
    refs = refs[3:]
    if carried:
        own_in, got_in = refs[:2]
        refs = refs[4:]
    act_ref, uv_ref, own_ref, got_ref, wbuf, sems = refs
    rows = ha_ref.shape[0]
    q = pl.program_id(0)

    @pl.when(q == 0)
    def _():
        if carried:
            own_ref[...] = own_in[...]
            got_ref[...] = got_in[...]
        else:
            own_ref[...] = jnp.zeros_like(own_ref)
            got_ref[...] = jnp.zeros_like(got_ref)

    fetch_weights(q, slots, wbuf, sems)
    w = wbuf.at[lax.rem(q, 2)]
    for base, h_ref, sum_ref in ((0, ha_ref, own_ref), (rows, hb_ref, got_ref)):
        at = slice(base, base + rows)
        pair = dot(h_ref[...], w[:, : 2 * half])
        lifted = pair[:, :half] * suv_ref[0:1, :]
        gated = pair[:, half:] * suv_ref[1:2, :]
        act = (lifted * gated * jax.nn.sigmoid(gated)).astype(bf16)
        uv_ref[at, :] = pair.astype(bf16)
        act_ref[at, :] = act
        sum_ref[...] += dot_t(act, w[:, 2 * half : 3 * half])


def mlp_fwd(ha, hb, slots, suv, first, carry):
    rows, width = ha.shape
    parts, _, half = suv.shape
    take = lambda n: pl.BlockSpec((None, 2 * rows, n), lambda q: (first + q, 0, 0))
    whole = full_spec((rows, width))
    anywhere = pl.BlockSpec(memory_space=pl.ANY)
    flat = [p for slot in slots for p in slot]
    ins = [*flat, ha, hb, suv]
    in_specs = [anywhere] * len(flat) + [
        whole,
        whole,
        pl.BlockSpec((None, 2, half), lambda q: (first + q, 0, 0)),
    ]
    alias = {}
    if carry:
        act, uv, own, got = carry
        ins += [own, got, act, uv]
        in_specs += [whole, whole, anywhere, anywhere]
        alias = {len(ins) - 2: 0, len(ins) - 1: 1}
    return pl.pallas_call(
        functools.partial(
            mlp_fwd_kernel, half=half, counts=[len(s) for s in slots], carried=bool(carry)
        ),
        grid=(len(slots),),
        in_specs=in_specs,
        out_specs=[take(half), take(2 * half), whole, whole],
        out_shape=[
            jax.ShapeDtypeStruct((parts, 2 * rows, half), bf16),
            jax.ShapeDtypeStruct((parts, 2 * rows, 2 * half), bf16),
            jax.ShapeDtypeStruct((rows, width), f32),
            jax.ShapeDtypeStruct((rows, width), f32),
        ],
        scratch_shapes=[
            pltpu.VMEM((2, width, 3 * half), bf16),
            pltpu.SemaphoreType.DMA((2, max(len(s) for s in slots))),
        ],
        input_output_aliases=alias,
        compiler_params=params(),
    )(*ins)


def mlp_bwd_kernel(*refs, half, counts):
    total = sum(counts)
    flat, refs = refs[:total], refs[total:]
    slots, at = [], 0
    for n in counts:
        slots.append(flat[at : at + n])
        at += n
    da_ref, db_ref, uv_ref, suv_ref, duv_ref, own_ref, got_ref, gs_ref, acc, wbuf, sems = refs
    rows = da_ref.shape[0]
    q = pl.program_id(0)

    @pl.when(q == 0)
    def _():
        own_ref[...] = jnp.zeros_like(own_ref)
        acc[...] = jnp.zeros_like(acc)

    gs_ref[...] = jnp.zeros_like(gs_ref)
    fetch_weights(q, slots, wbuf, sems)
    w = wbuf.at[lax.rem(q, 2)]
    for base, d_ref, sum_ref in ((0, da_ref, own_ref), (rows, db_ref, acc)):
        at = slice(base, base + rows)
        grad = dot(d_ref[...], w[:, 2 * half : 3 * half])
        up = uv_ref[at, :half].astype(f32)
        gate = uv_ref[at, half:].astype(f32)
        su = suv_ref[0:1, :]
        sv = suv_ref[1:2, :]
        lifted = up * su
        gated = gate * sv
        sigma = jax.nn.sigmoid(gated)
        da = grad * gated * sigma
        db = grad * lifted * sigma * (1.0 + gated * (1.0 - sigma))
        gs_ref[0:1, :] += jnp.sum(da * up, axis=0, keepdims=True)
        gs_ref[1:2, :] += jnp.sum(db * gate, axis=0, keepdims=True)
        duv_ref[at, :half] = (da * su).astype(bf16)
        duv_ref[at, half:] = (db * sv).astype(bf16)
        sum_ref[...] += dot_t(duv_ref[at, :], w[:, : 2 * half])

    @pl.when(q == pl.num_programs(0) - 1)
    def _():
        got_ref[...] = acc[...].astype(bf16)


def mlp_bwd(da, db, slots, uv, suv):
    rows, width = da.shape
    parts, _, half = suv.shape
    take = lambda n: pl.BlockSpec((None, 2 * rows, n), lambda q: (q, 0, 0))
    whole = full_spec((rows, width))
    anywhere = pl.BlockSpec(memory_space=pl.ANY)
    flat = [p for slot in slots for p in slot]
    return pl.pallas_call(
        functools.partial(mlp_bwd_kernel, half=half, counts=[len(s) for s in slots]),
        grid=(parts,),
        in_specs=[anywhere] * len(flat)
        + [
            whole,
            whole,
            take(2 * half),
            pl.BlockSpec((None, 2, half), lambda q: (q, 0, 0)),
        ],
        out_specs=[
            take(2 * half),
            whole,
            whole,
            pl.BlockSpec((None, 8, half), lambda q: (q, 0, 0)),
        ],
        out_shape=[
            jax.ShapeDtypeStruct((parts, 2 * rows, 2 * half), bf16),
            jax.ShapeDtypeStruct((rows, width), f32),
            jax.ShapeDtypeStruct((rows, width), bf16),
            jax.ShapeDtypeStruct((parts, 8, half), f32),
        ],
        scratch_shapes=[
            pltpu.VMEM((rows, width), f32),
            pltpu.VMEM((2, width, 3 * half), bf16),
            pltpu.SemaphoreType.DMA((2, max(len(s) for s in slots))),
        ],
        compiler_params=params(),
    )(*flat, da, db, uv, suv)


EXTRA = 16


def grad_kernel(*refs, count, chunk, more):
    ha, hb = refs[:count], refs[count : 2 * count]
    refs = refs[2 * count :]
    if more:
        oa, ob = refs[:count], refs[count : 2 * count]
        ya_ref, yb_ref, extra_ref = refs[2 * count : 2 * count + 3]
        refs = refs[2 * count + 3 :]
        val_ref, out_ref, turned, turned_o = refs
    else:
        val_ref, out_ref, turned = refs
    rows = ha[0].shape[0]

    @pl.when(pl.program_id(0) == 0)
    def _():
        for j in range(count):
            at = slice(j * chunk, (j + 1) * chunk)
            turned[at, :rows] = ha[j][...].T
            turned[at, rows:] = hb[j][...].T
            if more:
                turned_o[at, :rows] = oa[j][...].T
                turned_o[at, rows:] = ob[j][...].T

    value = dot(turned[...], val_ref[...]).astype(bf16)
    size = value.shape[1]
    for j in range(count):
        at = slice(j * chunk, (j + 1) * chunk)
        out_ref[j, :chunk, :size] = value[at, :]
        if more:
            out_ref[j, :chunk, size:] = (
                dot(turned_o[at, :rows], ya_ref[...]) + dot(turned_o[at, rows:], yb_ref[...])
            ).astype(bf16)
            out_ref[j, chunk:, :] = extra_ref[...].astype(bf16)


def weight_grads(which, parts, chips, hs, value, os=None, ys=None, extra=None):
    rows, width = hs[0].shape
    chunk = width // chips
    size = value.shape[2]
    more = os is not None
    lo, count, nw = parts[0], len(parts), len(which)
    hc = ys[0].shape[1] // value.shape[0] if more else 0
    tall = chunk + (EXTRA if more else 0)
    if chunk % 128:
        cut = lambda pair: jnp.concatenate(
            [jnp.concatenate(pair, axis=0)[:, r * chunk : (r + 1) * chunk] for r in which], axis=1
        )
        found = []
        for k in parts:
            one = t_dot(cut(hs), value[k])
            if more:
                y = jnp.concatenate(ys, axis=0)[:, k * hc : (k + 1) * hc]
                one = jnp.concatenate([one, t_dot(cut(os), y)], axis=1)
            one = one.reshape(nw, chunk, size + hc)
            if more:
                wide = jnp.broadcast_to(extra[k][None], (nw, EXTRA, size + hc))
                one = jnp.concatenate([one, wide], axis=1)
            found.append(one.astype(bf16))
        return jnp.stack(found)
    columns = [pl.BlockSpec((rows, chunk), lambda k, r=r: (0, r)) for r in which]
    ins = [hs[0]] * nw + [hs[1]] * nw
    in_specs = columns * 2
    scratch = [pltpu.VMEM((nw * chunk, 2 * rows), bf16)]
    if more:
        ins += [os[0]] * nw + [os[1]] * nw + [ys[0], ys[1], extra]
        in_specs += columns * 2
        in_specs += [pl.BlockSpec((rows, hc), lambda k: (0, lo + k))] * 2
        in_specs.append(pl.BlockSpec((None, EXTRA, size + hc), lambda k: (lo + k, 0, 0)))
        scratch = scratch * 2
    ins.append(value)
    in_specs.append(pl.BlockSpec((None, 2 * rows, size), lambda k: (lo + k, 0, 0)))
    return pl.pallas_call(
        functools.partial(grad_kernel, count=nw, chunk=chunk, more=more),
        grid=(count,),
        in_specs=in_specs,
        out_specs=pl.BlockSpec((None, nw, tall, size + hc), lambda k: (k, 0, 0, 0)),
        out_shape=jax.ShapeDtypeStruct((count, nw, tall, size + hc), bf16),
        scratch_shapes=scratch,
        compiler_params=params(),
    )(*ins)


def adam_step(weight, grad, first, second):
    first_new = beta_one * first + (1.0 - beta_one) * grad
    second_new = beta_two * second + (1.0 - beta_two) * grad * grad
    moved = weight - learn_rate * (first_new / bias_one) / (
        jnp.sqrt(second_new / bias_two) + adam_eps
    )
    return (first_new, second_new, moved)


def after(value, *others):
    return lax.optimization_barrier((value, *others))[0]


def per_device(
    layer_input,
    cotangent,
    positions,
    w_qkv,
    w_out,
    w_up,
    w_down,
    moment_qkv,
    moment_out,
    moment_up,
    moment_down,
    square_qkv,
    square_out,
    square_up,
    square_down,
    s_qk,
    alpha_attn,
    alpha_mlp,
    s_uv,
):
    nz = lax.axis_size("head")
    nb = lax.axis_size("batch")
    z = lax.axis_index("head")
    b = lax.axis_index("batch")
    core = b % 2
    chip = b // 2
    chips = nb // 2
    bits = [1 << n for n in range(int(math.log2(chips)))]
    rows, cols = layer_input.shape
    width = cols * nz
    own = rows // nz
    hid = w_down.shape[0]
    half = hid // 2
    hc = cols // 2
    heads = cols // HEAD_DIM
    span = w_qkv.shape[0]
    chunk = width // chips
    core_s = core.reshape(1).astype(jnp.int32)
    place = jnp.stack([z, chip]).astype(jnp.int32)
    near_first = [
        sorted(range(nz), key=lambda s, at=at: (abs(s - at), (s < at) == (at < nz // 2)))
        for at in range(nz)
    ]

    def swap_batch(value, bit):
        return lax.ppermute(value, "batch", [(i, i ^ bit) for i in range(nb)])

    def swap_core(value):
        return swap_batch(value, 1)

    def swap_chip(value, bit):
        return swap_batch(value, 2 * bit)

    def turn(value, k):
        return lax.ppermute(value, "head", [(i, (i - k) % nz) for i in range(nz)])

    def from_left(value):
        return lax.ppermute(value, "head", [(i, i + 1) for i in range(nz - 1)])

    def from_right(value):
        return lax.ppermute(value, "head", [(i + 1, i) for i in range(nz - 1)])

    def pick(pair, index):
        return jnp.where(index == 0, pair[0], pair[1])

    def relative(value):
        return jnp.concatenate(
            [
                lax.dynamic_slice_in_dim(value, (chip ^ r) * chunk, chunk, value.ndim - 1)
                for r in range(chips)
            ],
            axis=-1,
        )

    lefts, rights = [from_right(layer_input)], [from_left(layer_input)]
    mine, theirs, qkv_own, out_own = pack(core_s, w_up, w_down, w_out, w_qkv)
    qkv_full = lax.all_gather(qkv_own, "batch", axis=0, tiled=True)
    theirs = swap_core(theirs)
    packet = jnp.concatenate([pick((mine, theirs), core), pick((theirs, mine), core)], axis=0)

    def spread(value):
        if len(bits) == 2:
            return [value, swap_chip(value, 1), swap_chip(value, 2)]
        for bit in bits:
            value = jnp.concatenate([value, swap_chip(value, bit)], axis=0)
        return [value]

    def spread_more(found, *wait):
        if len(bits) == 2:
            near, far = found[1:]
            middle = near.shape[0] // 2
            top, bottom = far[:middle], near[middle:]
            if wait:
                top, bottom, *_ = lax.optimization_barrier((top, bottom, *wait))
            found = found + [swap_chip(top, 1), swap_chip(bottom, 2)]
        return found

    for _ in range(nz - 2):
        lefts.append(from_right(lefts[-1]))
        rights.append(from_left(rights[-1]))
    slots = [spread_more(spread(packet))]

    suv_parts = [s_uv.reshape(2, 2, half)]
    for k in range(1, nz):
        suv_parts.append(turn(suv_parts[0], k))
    suv_all = jnp.stack(suv_parts)
    suv_all = pick((suv_all[:, :, 0], suv_all[:, :, 1]), core)
    order_z = jnp.asarray(near_first, jnp.int32)[z]
    suv = jnp.take(suv_all, (order_z - z) % nz, axis=0)

    freqs = jnp.exp(
        jnp.arange(HEAD_DIM // 2, dtype=f32) * (-2.0 * math.log(10000.0) / HEAD_DIM)
    )
    phase = positions.astype(f32)[:, None] * freqs[None, :]
    cosine, sine = jnp.cos(phase), jnp.sin(phase)
    cosine = jnp.tile(cosine, (1, 2 * heads))
    sine = jnp.tile(jnp.concatenate([-sine, sine], axis=1), (1, heads))
    lane = jnp.arange(cols) // HEAD_DIM
    ones = (lane[:, None] == lane[None, :]).astype(bf16)
    gain = s_qk.reshape(1, cols)
    is_long = (positions[SHORT : SHORT + 1] != 0).astype(jnp.int32)
    attn_gain = relative(alpha_attn[None])
    mlp_gain = relative(alpha_mlp[None])

    packet_z, out_own, lefts[-1], rights[-1] = lax.optimization_barrier(
        (packet, out_own, lefts[-1], rights[-1])
    )
    hops = [[from_right(packet_z)], [from_left(packet_z)]]
    out_full = lax.all_gather(out_own, ("head", "batch"), axis=0, tiled=True)
    out_full = out_full.reshape(nz, width, cols)

    def slot_value(k):
        value = None
        for at in range(nz):
            s = near_first[at][k]
            one = hops[0][s - at - 1] if s > at else hops[1][at - s - 1]
            value = one if value is None else jnp.where(z == at, one, value)
        return value

    tokens_full, q, k, v, rho_q, rho_k = qkv_project(
        place, lefts, layer_input, rights, qkv_full, cosine, sine, gain, ones
    )
    waits = [q]
    held = []

    def next_hop():
        hops[0][-1], hops[1][-1], *_ = lax.optimization_barrier((hops[0][-1], hops[1][-1], *waits))
        count = len(hops[0])
        if count < nz - 1:
            hops[0].append(from_right(hops[0][-1]))
            hops[1].append(from_left(hops[1][-1]))
        held.append(spread(slot_value(count)))

    attended, logs = attn_fwd(is_long, q, k, v)
    next_hop()

    def to_tokens(value):
        parts = []
        for n in range(nz):
            part = lax.dynamic_slice_in_dim(value, ((z - n) % nz) * own, own, 0)
            parts.append(part if n == 0 else turn(part, n))
        return parts

    def natural_z(parts, axis):
        size = parts[0].shape[axis]
        out = jnp.concatenate(parts, axis=axis)
        return jnp.concatenate(
            [
                lax.dynamic_slice_in_dim(out, ((n - z) % nz) * size, size, axis)
                for n in range(nz)
            ],
            axis=axis,
        )

    def to_columns(value):
        parts = []
        for n in range(nz):
            part = lax.dynamic_slice_in_dim(value, ((z - n) % nz) * cols, cols, 1)
            parts.append(part if n == 0 else turn(part, n))
        return natural_z(parts, 0)

    y_parts = to_tokens(attended)
    waits = [attended]
    for _ in range(nz - 3):
        next_hop()
    if len(held) > 0:
        slots.append(spread_more(held[0], attended))
    start = relative(lax.dynamic_slice_in_dim(tokens_full, z * own, own, 0))
    hA, h1, h_own, stat = attn_out(place, y_parts, out_full, start, attn_gain, chips)
    h_got = swap_core(h_own)
    waits = [h_own]
    next_hop()
    for found in held[1 : nz - 2]:
        slots.append(spread_more(found, h_own))
    cot_parts = to_tokens(after(cotangent, h_own))

    some = mlp_fwd(h_own, h_got, slots, suv, 0, None)
    slots.append(spread_more(held[nz - 2]))
    act, uv, mo_own, mo_other = mlp_fwd(h_own, h_got, slots[nz - 1 :], suv, nz - 1, some)
    cot = relative(natural_z(cot_parts, 1))
    hidden, d_own, base, ga_mlp = loss(
        mo_own, swap_core(mo_other.astype(bf16)), h1, cot, mlp_gain
    )
    d_got = swap_core(d_own)
    hidden_t = to_columns(relative(hidden))

    groups = [(list(range(nz // 2)), bits), (list(range(nz // 2, nz)), bits[::-1])]
    sides = lambda order: (
        [r for r in range(chips) if r & order[0]],
        [r for r in range(chips) if not r & order[0]],
    )

    def first_sent(*args):
        made = [weight_grads(sides(order)[0], parts, chips, *args) for parts, order in groups]
        return made, [swap_chip(one, order[0]) for one, (_, order) in zip(made, groups)]

    def first_kept(*args):
        return [weight_grads(sides(order)[1], parts, chips, *args) for parts, order in groups]

    def second(kept, sent):
        found = []
        for (_, order), got, keep in zip(groups, sent, kept):
            left = sides(order)[1]
            for bit in order[1:]:
                send_at = [n for n, r in enumerate(left) if r & bit]
                keep_at = [n for n, r in enumerate(left) if not r & bit]
                left = [left[n] for n in keep_at]
                cut = lambda v, at: jnp.concatenate([v[:, n : n + 1] for n in at], axis=1).astype(f32)
                send = (cut(keep, send_at) + cut(got, send_at)).astype(bf16)
                keep = cut(keep, keep_at) + cut(got, keep_at)
                got = swap_chip(send, bit)
            found.append((keep, got))
        return found

    slot_of = [[near_first[at].index(s) for s in range(nz)] for at in range(nz)]
    slot_of = jnp.asarray(slot_of, jnp.int32)[z]

    def along_z(found):
        pieces = jnp.concatenate([keep[:, 0] + got[:, 0].astype(f32) for keep, got in found], axis=0)
        total = pieces[0]
        low = pieces[1:].astype(bf16)
        for n in range(1, nz):
            at = slot_of[(z + n) % nz] - 1
            one = lax.dynamic_index_in_dim(low, at, 0, keepdims=False)
            total = total + turn(one, nz - n).astype(f32)
        return total

    down_made, down_sent = first_sent((d_own, d_got), act)
    d_own, d_got, *_ = lax.optimization_barrier((d_own, d_got, *down_made))
    duv, dh_own, dh_other, gsuv = mlp_bwd(d_own, d_got, slots, uv, suv)
    dh_got = swap_core(dh_other)
    down_kept = first_kept((after(d_own, dh_other), d_got), act)
    do_own, through, ga_attn, *dy_parts = first_back(
        place, dh_own, dh_got, base, h1, hA, start, stat, attn_gain, out_full, chips
    )
    down_sent = [after(one, do_own) for one in down_sent]
    down_part = second(down_kept, down_sent)
    do_got = swap_core(do_own)
    y_mine = jnp.concatenate([pick((p[:, :hc], p[:, hc:]), core) for p in y_parts], axis=1)
    y_other = jnp.concatenate([pick((p[:, hc:], p[:, :hc]), core) for p in y_parts], axis=1)
    y_got = swap_core(y_other)
    in_slots = lambda value: jnp.concatenate(
        [
            lax.dynamic_slice_in_dim(value, ((order_z[n] - z) % nz) * hc, hc, 1)
            for n in range(nz)
        ],
        axis=1,
    )
    ys = (in_slots(y_mine), in_slots(y_got))

    dy_parts = [p if n == 0 else turn(p, nz - n) for n, p in enumerate(dy_parts)]
    dy = natural_z([dy_parts[(nz - n) % nz] for n in range(nz)], 0)

    alphas = [relative(ga_attn[0:1]), relative(ga_mlp[0:1])]
    extra = []
    wide = 2 * half + hc
    fill = lambda r: jnp.pad(r, ((0, 0), (0, wide - r.shape[1])))
    for n in range(nz):
        at = order_z[n] * cols
        line = jnp.concatenate([lax.dynamic_slice_in_dim(g, at, cols, 1) for g in alphas], axis=1)
        first = gsuv[n, :2].reshape(1, 2 * half)
        extra.append(jnp.pad(jnp.concatenate([fill(first), fill(line)]), ((0, EXTRA - 2), (0, 0))))
    extra = jnp.stack(extra)
    up_args = ((h_own, h_got), duv, (do_own, do_got), ys, extra)
    up_made, up_sent = first_sent(*up_args)
    up_kept = first_kept(*up_args)

    blocks = rows // 512
    middle = blocks // 2
    dy = after(dy, *up_made)
    common = (is_long, q, k, v, dy, attended, logs, rho_q, rho_k, cosine, sine, gain, ones)
    sum_down_t = along_z([(keep, after(got, dy)) for keep, got in down_part])
    dqkv_b, dk_part, dv_part, sqk_b = attn_bwd(*common, middle, blocks - middle, None)

    through = relative(through).astype(f32)
    where_rows = (z % (nz // 2)) * own

    def input_part(dqkv, side):
        part = dot_t(dqkv, qkv_full)
        here = lax.dynamic_slice_in_dim(part, where_rows, own, 0)
        here = here + jnp.where(z // (nz // 2) == side, through, 0.0)
        part = lax.dynamic_update_slice_in_dim(part.astype(bf16), here.astype(bf16), where_rows, 0)
        return lax.psum_scatter(part, "head", scatter_dimension=1, tiled=True)

    input_b = input_part(dqkv_b, 1)
    up_part = second(up_kept, [after(one, dqkv_b) for one in up_sent])
    dqkv_a, sqk_a = attn_bwd(*common, 0, middle, [dk_part, dv_part])
    input_a = input_part(dqkv_a, 0)
    input_grad = jnp.concatenate([input_a, input_b], axis=0).astype(f32)
    sum_up_t = along_z([(keep, after(got, dqkv_a)) for keep, got in up_part])

    dqkv = jnp.concatenate([dqkv_a, dqkv_b], axis=0)
    grad_qkv = t_dot(tokens_full, dqkv).astype(bf16)
    sqk = jnp.pad((sqk_a + sqk_b), ((0, EXTRA - 8), (0, 2 * cols)))
    shard = [lax.dynamic_slice_in_dim(grad_qkv, (b ^ r) * span, span, 0) for r in range(nb)]
    shard = [jnp.concatenate([s, sqk.astype(bf16)], axis=0) for s in shard]
    qbits = [1 << n for n in range(int(math.log2(nb)))]
    held = {r: shard[r] for r in range(nb)}
    for bit in qbits:
        send_at = [r for r in held if r & bit]
        send = jnp.concatenate([held[r] for r in send_at], axis=0).astype(bf16)
        got = swap_batch(send, bit)
        size = span + EXTRA
        held = {
            r ^ bit: held[r ^ bit].astype(f32) + got[n * size : (n + 1) * size].astype(f32)
            for n, r in enumerate(send_at)
        }
    sum_qkv = held[0][:span].reshape(span, 3, cols)
    cell = width // (nz * nb)
    sum_sqk = lax.dynamic_slice_in_dim(held[0][span, :cols], b * cell, cell, 0)

    def both_halves(total):
        two = (total[:span], total[span : 2 * span])
        here = jnp.concatenate([pick(two, core), total[2 * span :]], axis=0)
        there = jnp.concatenate([pick(two, 1 - core), total[2 * span :]], axis=0)
        there = swap_core(there.astype(bf16)).astype(f32)
        return [pick((here, there), core), pick((there, here), core)]

    join = lambda halves, at, size: jnp.concatenate([p[:span, at : at + size] for p in halves], axis=1)
    halves = both_halves(sum_down_t)
    sum_down = join(halves, 0, half).T
    halves = both_halves(sum_up_t)
    sum_up = jnp.stack([join(halves, c * half, half) for c in range(2)], axis=1)
    sum_out = join(halves, 2 * half, hc).T
    suv_rows = jnp.stack(
        [jnp.concatenate([p[span, c * half : (c + 1) * half] for p in halves]) for c in range(2)]
    )
    sum_suv = lax.dynamic_slice_in_dim(suv_rows, b * (hid // nb), hid // nb, 1)
    alphas = halves[0][span + 1] + halves[1][span + 1]
    sum_attn = lax.dynamic_slice_in_dim(alphas[:cols], b * cell, cell, 0)
    sum_mlp = lax.dynamic_slice_in_dim(alphas[cols : 2 * cols], b * cell, cell, 0)

    hidden = hidden_t.astype(f32)

    first_a, second_a, moved_a = adam_step(w_qkv, sum_qkv, moment_qkv, square_qkv)
    first_b, second_b, moved_b = adam_step(w_out, sum_out, moment_out, square_out)
    first_c, second_c, moved_c = adam_step(w_up, sum_up, moment_up, square_up)
    first_d, second_d, moved_d = adam_step(w_down, sum_down, moment_down, square_down)
    squares = [
        jnp.sum(moved_a * moved_a, axis=0).reshape(-1),
        jnp.sum(moved_b * moved_b, axis=1),
        jnp.sum(moved_c * moved_c, axis=0).reshape(-1),
        jnp.sum(moved_d * moved_d, axis=1),
    ]
    sizes = [s.shape[0] for s in squares]
    norms = jnp.concatenate(squares).reshape(-1, 128)
    for bit in qbits:
        norms = norms + swap_batch(norms, bit)
    norms = norms.reshape(-1)
    ends = [sum(sizes[: n + 1]) for n in range(4)]
    norm_a = norms[: ends[0]].reshape(3, cols)
    norm_b = norms[ends[0] : ends[1]]
    norm_c = norms[ends[1] : ends[2]].reshape(2, hid)
    norm_d = norms[ends[2] :]
    new_qkv = moved_a * lax.rsqrt(norm_a / width + layer_eps)[None]
    new_out = moved_b * lax.rsqrt(norm_b / width + layer_eps)[:, None]
    new_up = moved_c * lax.rsqrt(norm_c / width + layer_eps)[None]
    new_down = moved_d * lax.rsqrt(norm_d / width + layer_eps)[:, None]
    return (
        hidden,
        input_grad,
        sum_qkv,
        sum_out,
        sum_up,
        sum_down,
        first_a,
        first_b,
        first_c,
        first_d,
        second_a,
        second_b,
        second_c,
        second_d,
        new_qkv,
        new_out,
        new_up,
        new_down,
        sum_sqk,
        sum_attn,
        sum_mlp,
        sum_suv,
    )


def solution(mesh):
    tokens = P("batch", "head")
    wide = P("batch", None, "head")
    tall = P("head", "batch")
    flat = P(("head", "batch"))
    weights = (wide, tall, wide, tall)
    return jax.shard_map(
        per_device,
        mesh=mesh,
        in_specs=(tokens, tokens, P("batch"))
        + weights * 3
        + (P("head"), P(), P(), P(None, "head")),
        out_specs=(tokens, tokens) + weights * 4 + (flat, flat, flat, P(None, ("head", "batch"))),
        check_vma=False,
    )
```

time: 1470 us -> 755 us (0.51)
  waiting for transfers between devices: 967 us -> 236 us
  Pallas kernels: 0 us -> 203 us
  matrix products: 208 us -> 10 us
  starting transfers between devices: 0.66 us -> 119 us
  blocking collectives: 115 us -> 0 us
  other arithmetic: 107 us -> 66.4 us
  local copies, waits for them, and re-layouts: 48.1 us -> 85.6 us
    reduce_scatter x8 -> x2, waiting for transfers between devices: 643 us -> 0.01 us  [input_part(): return lax.psum_scatter(part, 'head', scatter_dimension=1, tiled=True)]
    all_gather x7 -> x2, waiting for transfers between devices: 323 us -> 0.01 us  [the longest x1 0.01 us: per_device(): qkv_full = lax.all_gather(qkv_own, 'batch', axis=0, tiled=True)]
    ppermute x0 -> x72, waiting for transfers between devices: none -> 236 us  [the longest x21 121 us: turn(): return lax.ppermute(value, 'head', [(i, (i - k) % nz) for i in range(nz)])]
    pallas_call x0 -> x19, Pallas kernels: none -> 203 us  [the longest x8 46.2 us: weight_grads(): pl.pallas_call(functools.partial(grad_kernel, count=nw, chunk=chunk, more...]
    dot_general x36 -> x3, matrix products: 208 us -> 10 us  [the longest x2 6.49 us: dot_t(): lax.dot_general(a, b, (((1,), (1,)), ((), ())), preferred_element_type=f32)]
    ppermute x0 -> x72, starting transfers between devices: none -> 119 us  [the longest x39 40 us: swap_batch(): return lax.ppermute(value, 'batch', [(i, i ^ bit) for i in range(nb)])]
    psum x9 -> x0, blocking collectives: 102 us -> none  [the longest x4 39.9 us: row_total(): return lax.psum(jnp.sum(values * values, axis=1), 'head')]
    reduce_sum x15 -> x2, other arithmetic: 43.9 us -> 3.33 us  [the longest x1 2.29 us: per_device(): jnp.sum(moved_c * moved_c, axis=0).reshape(-1)]
  transfers between devices with their start and end apart: 16 -> 76, of which waited for: 14 -> 32; matrix products, arithmetic and copies ran while one was open for 15% -> 19% of each run, Pallas kernels for 0% -> 25%
where the time goes in v1:
time: 755 us; the launch traced here: 746 us
  waiting for transfers between devices  236 us (31%)
  Pallas kernels  203 us (27%)
  starting transfers between devices  119 us (16%)
  local copies, waits for them, and re-layouts  85.6 us (11%)
  other arithmetic  66.4 us (9%)
  between operations  25.6 us (3%)
  matrix products  10 us (1%)
    ppermute x21, waiting for transfers between devices, turn(): return lax.ppermute(value, 'head', [(i, (i - k) % nz) for i in range(nz)])  121 us
    ppermute x39, waiting for transfers between devices, swap_batch(): return lax.ppermute(value, 'batch', [(i, i ^ bit) for i in range(nb)])  63.8 us
    ppermute x6, waiting for transfers between devices, from_right(): return lax.ppermute(value, 'head', [(i + 1, i) for i in range(nz - 1)])  50 us
    unnamed x196, local copies, waits for them, and re-layouts  48.8 us
    pallas_call x8, Pallas kernels, weight_grads(): pl.pallas_call(functools.partial(grad_kernel, count=nw, chunk=chunk, more...  46.2 us
    pallas_call x2, Pallas kernels, attn_bwd(): pl.pallas_call(inner, grid_spec=pltpu.PrefetchScalarGridSpec(num_scalar_p...  45.8 us
    ppermute x39, starting transfers between devices, swap_batch(): return lax.ppermute(value, 'batch', [(i, i ^ bit) for i in range(nb)])  40 us
    ppermute x21, starting transfers between devices, turn(): return lax.ppermute(value, 'head', [(i, (i - k) % nz) for i in range(nz)])  37.5 us
  transfers between devices with their start and end apart: 76, of which 32 were waited for; matrix products, arithmetic and copies ran while one was open for 19% of the time, Pallas kernels for 25%

profile of v1, /device:TPU:0, one launch (start us, length us, event | category | flops | bytes accessed | tf_op | source)
XLA Modules:
  0.0 745.6 jit_solution(13189546720003315989)
XLA Ops:
  8.5 5.6 collective-permute-start.4
  21.3 14.2 %collective-permute-done.1.refs_0_ = bf16[2048,256]{1,0:T(8,128)(2,1)S(1)} collective-permute-done((bf16[2048,256]{1,0:T(8,128)(2,1)}, bf16[2048,256]{1,0:T(8,128)(2,1)S(1)}, u32[]{:S(2)}, u32[]{:S(2)}) %collective-permute-start.1) | collective-permute-done | bytes 1048608 | tf_op jit(solution)/shard_map/ppermute | solution.py:867
  36.8 5.6 collective-permute-start.5
  42.4 19.3 %collective-permute-done.2.refs_1_ = bf16[2048,256]{1,0:T(8,128)(2,1)S(1)} collective-permute-done((bf16[2048,256]{1,0:T(8,128)(2,1)S(1)}, bf16[2048,256]{1,0:T(8,128)(2,1)S(1)}, u32[]{:S(2)}, u32[]{:S(2)}) %collective-permute-start.2) | collective-permute-done | bytes 1048608 | tf_op jit(solution)/shard_map/ppermute | solution.py:867
  63.1 5.6 collective-permute-start.6
  70.7 16.5 %collective-permute-done.3.refs_2_ = bf16[2048,256]{1,0:T(8,128)(2,1)} collective-permute-done((bf16[2048,256]{1,0:T(8,128)(2,1)S(1)}, bf16[2048,256]{1,0:T(8,128)(2,1)}, u32[]{:S(2)}, u32[]{:S(2)}) %collective-permute-start.3) | collective-permute-done | bytes 1048608 | tf_op jit(solution)/shard_map/ppermute | solution.py:867
  90.0 5.9 collective-permute-start.8
  102.4 12.6 %shard_map.373 = (bf16[2048,1024]{1,0:T(8,128)(2,1)}, bf16[2048,256]{1,0:T(8,128)(2,1)}, bf16[2048,256]{1,0:T(8,128)(2,1)}, bf16[2048,256]{1,0:T(8,128)(2,1)}, f32[2048,256]{1,0:T(8,128)}, /*index=5*/f32[2048,256]{1,0:T(8,128)}) custom-call(s32[2]{0:T(128)} %pad_add_fusion.z_ref.place_ref, bf16[2048,256]{1,0:T(8,128)(2,1)} %copy-done.40, ...), custom_call_target="tpu_custom_call" | custom-call | tf_op jit(solution)/shard_map/pallas_call | solution.py:102
  123.0 17.9 %shard_map.374 = (bf16[2048,256]{1,0:T(8,128)(2,1)}, f32[2048,128]{1,0:T(8,128)}) custom-call(s32[1]{0:T(128)S(6)} %convert_element_type.210.long_ref.r_0_, bf16[2048,256]{1,0:T(8,128)(2,1)} %get-tuple-element.101.q_ref.r_1_, bf16[2048,256]{1,0:T(8,128)(2,1)} %get-tuple-element.104.k_ref.r_2_.r_6_, bf16[2048,256]{1,0:T(8,128)(2,1)} %get-tuple-element.105.v_ref.r_7_), custom_call_target="tpu_custom_call" | custom-call | tf_op jit(solution)/shard_map/pallas_call | solution.py:192
  142.2 5.5 collective-permute-start.12
  157.8 12.7 %collective-permute-done.13.refs_1_ = bf16[512,256]{1,0:T(8,128)(2,1)S(1)} collective-permute-done((bf16[512,256]{1,0:T(8,128)(2,1)S(1)}, bf16[512,256]{1,0:T(8,128)(2,1)S(1)}, u32[]{:S(2)}, u32[]{:S(2)}) %collective-permute-start.13) | collective-permute-done | bytes 262176 | tf_op jit(solution)/shard_map/ppermute | solution.py:861
  171.9 11.1 %collective-permute-done.14.refs_2_ = bf16[512,256]{1,0:T(8,128)(2,1)S(1)} collective-permute-done((bf16[512,256]{1,0:T(8,128)(2,1)S(1)}, bf16[512,256]{1,0:T(8,128)(2,1)S(1)}, u32[]{:S(2)}, u32[]{:S(2)}) %collective-permute-start.14) | collective-permute-done | bytes 262176 | tf_op jit(solution)/shard_map/ppermute | solution.py:861
  186.1 6.7 shard_map.375
  239.9 14.4 %collective-permute-done.17.refs_2_.refs_17_ = bf16[256,1536]{1,0:T(8,128)(2,1)} collective-permute-done((bf16[256,1536]{1,0:T(8,128)(2,1)S(1)}, bf16[256,1536]{1,0:T(8,128)(2,1)}, u32[]{:S(2)}, u32[]{:S(2)}) %collective-permute-start.17) | collective-permute-done | bytes 786464 | tf_op jit(solution)/shard_map/ppermute | solution.py:852
  280.2 17.1 %shard_map.376 = (bf16[4,1024,512]{2,1,0:T(8,128)(2,1)}, bf16[4,1024,1024]{2,1,0:T(8,128)(2,1)}, f32[512,1024]{1,0:T(8,128)}, f32[512,1024]{1,0:T(8,128)}) custom-call(bf16[256,1536]{1,0:T(8,128)(2,1)} %pad_maximum_fusion.9.refs_0_, bf16[256,1536]{1,0:T(8,128)(2,1)} %copy-done.10, bf16[256,1536]{1,0:T(8,128)(2,1)} %collective-permute-done.25.refs_2_, ...), custom_call_target="tpu_custom_call" | custom-call | tf_op jit(solution)/shard_map/pallas_call | solution.py:607
  298.2 11.0 %shard_map.377 = (bf16[4,1024,512]{2,1,0:T(8,128)(2,1)}, bf16[4,1024,1024]{2,1,0:T(8,128)(2,1)}, f32[512,1024]{1,0:T(8,128)}, f32[512,1024]{1,0:T(8,128)}) custom-call(bf16[256,1536]{1,0:T(8,128)(2,1)} %copy-done.8, bf16[256,1536]{1,0:T(8,128)(2,1)} %collective-permute-done.16.refs_1_.refs_16_, ...), custom_call_target="tpu_custom_call", output_to_operand_aliasing={{0}: (10, {}), {1}: (11, {})} | custom-call | tf_op jit(solution)/shard_map/pallas_call | solution.py:607
  322.7 10.1 %collective-permute-done.38 = bf16[512,256]{1,0:T(8,128)(2,1)} collective-permute-done((bf16[512,256]{1,0:T(8,128)(2,1)S(1)}, bf16[512,256]{1,0:T(8,128)(2,1)}, u32[]{:S(2)}, u32[]{:S(2)}) %collective-permute-start.38) | collective-permute-done | bytes 262176 | tf_op jit(solution)/shard_map/ppermute | solution.py:861
  336.5 5.6 shard_map.378
  354.2 26.0 %shard_map.381 = (bf16[4,1024,1024]{2,1,0:T(8,128)(2,1)}, f32[512,1024]{1,0:T(8,128)}, bf16[512,1024]{1,0:T(8,128)(2,1)}, f32[4,8,512]{2,1,0:T(8,128)}) custom-call(bf16[256,1536]{1,0:T(8,128)(2,1)} %pad_maximum_fusion.9.refs_0_, bf16[256,1536]{1,0:T(8,128)(2,1)} %copy-done.10, bf16[256,1536]{1,0:T(8,128)(2,1)} %collective-permute-done.25.refs_2_, ...), custom_call_target="tpu_custom_call" | custom-call | tf_op jit(solution)/shard_map/pallas_call | solution.py:678
  380.7 5.8 collective-permute-start.42
  393.2 10.7 %collective-permute-done.41 = bf16[512,256]{1,0:T(8,128)(2,1)S(1)} collective-permute-done((bf16[512,256]{1,0:T(8,128)(2,1)S(1)}, bf16[512,256]{1,0:T(8,128)(2,1)S(1)}, u32[]{:S(2)}, u32[]{:S(2)}) %collective-permute-start.41) | collective-permute-done | bytes 262176 | tf_op jit(solution)/shard_map/ppermute | solution.py:861
  408.6 8.8 %shard_map.382 = (bf16[512,1024]{1,0:T(8,128)(2,1)}, bf16[512,1024]{1,0:T(8,128)(2,1)}, f32[8,1024]{1,0:T(8,128)}, bf16[512,256]{1,0:T(8,128)(2,1)}, bf16[512,25...) custom-call(s32[2]{0:T(128)} %pad_add_fusion.z_ref.place_ref, ...), custom_call_target="tpu_custom_call" | custom-call | tf_op jit(solution)/shard_map/pallas_call | solution.py:506
  417.4 8.7 %collective-permute-start.45 = (bf16[512,256]{1,0:T(8,128)(2,1)}, bf16[512,256]{1,0:T(8,128)(2,1)S(1)}, u32[]{:S(2)}, u32[]{:S(2)}) collective-permute-start(bf16[512,256]{1,0:T(8,128)(2,1)} %get-tuple-element.138), channel_id=1, source_target_pairs={{0,24},{8,0},{16,8},{24,16},{1,25},{9,1},{17,9},{25,17},{2,26},{10... | collective-permute-start | bytes 786440 | tf_op jit(solution)/shard_map/ppermute | solution.py:861
  434.5 13.5 %collective-permute-done.46 = bf16[512,256]{1,0:T(8,128)(2,1)S(1)} collective-permute-done((bf16[512,256]{1,0:T(8,128)(2,1)}, bf16[512,256]{1,0:T(8,128)(2,1)S(1)}, u32[]{:S(2)}, u32[]{:S(2)}) %collective-permute-start.46) | collective-permute-done | bytes 262176 | tf_op jit(solution)/shard_map/ppermute | solution.py:861
  451.2 7.2 shard_map.383
  458.4 7.3 shard_map.384
  465.7 28.9 %shard_map.385 = (bf16[1024,768]{1,0:T(8,128)(2,1)}, f32[1024,256]{1,0:T(8,128)}, f32[1024,256]{1,0:T(8,128)}, f32[8,256]{1,0:T(8,128)}) custom-call(s32[1]{0:T(128)S(6)} %convert_element_type.210.long_ref.r_0_, bf16[2048,256]{1,0:T(8,128)(2,1)} %get-tuple-element.101.q_ref.r_1_, bf16[2048,256]{1,0:T(8,128)(2,1)} %get-tuple-element.104.k_ref.r_2_.r_6_, ...), custom_call_target="tpu_custom_call" | custom-call | tf_op jit(solution)/shard_map/pallas_call | solution.py:334
  494.5 16.9 %shard_map.386 = (bf16[1024,768]{1,0:T(8,128)(2,1)}, f32[8,256]{1,0:T(8,128)}) custom-call(s32[1]{0:T(128)S(6)} %convert_element_type.210.long_ref.r_0_, bf16[2048,256]{1,0:T(8,128)(2,1)} %get-tuple-element.101.q_ref.r_1_, bf16[2048,256]{1,0:T(8,128)(2,1)} %get-tuple-element.104.k_ref.r_2_.r_6_, bf16[2048,256]{1,0:T(8,128)(2,1)} %pad_maximum_fusion.6.r_3_, ...), custom_call_target="tpu_custom_call" | custom-call | tf_op jit(solution)/shard_map/pallas_call | solution.py:334
  578.6 7.4 shard_map.387
  586.0 7.3 shard_map.388
  621.5 15.4 %collective-permute-done.52 = bf16[144,768]{1,0:T(8,128)(2,1)} collective-permute-done((bf16[144,768]{1,0:T(8,128)(2,1)}, bf16[144,768]{1,0:T(8,128)(2,1)}, u32[]{:S(2)}, u32[]{:S(2)}) %collective-permute-start.52) | collective-permute-done | bytes 221216 | tf_op jit(solution)/shard_map/ppermute | solution.py:852
  662.7 40.0 %collective-permute-done.58 = bf16[272,1152]{1,0:T(8,128)(2,1)} collective-permute-done((bf16[272,1152]{1,0:T(8,128)(2,1)}, bf16[272,1152]{1,0:T(8,128)(2,1)}, u32[]{:S(2)}, u32[]{:S(2)}) %collective-permute-start.58) | collective-permute-done | bytes 626720 | tf_op jit(solution)/shard_map/ppermute | solution.py:861
  (500 shorter events, 318.9 us)
Async XLA Ops:
  7.2 95.3 %all-gather.3.cloned.1.call-start = ((), (), s32[]{:S(2)}) async-start(), calls=%async_computation.2 | async-start | bytes 1769472 | tf_op jit(solution)/shard_map/all_gather | solution.py:883
  7.2 28.3 %collective-permute-start.1 = (bf16[2048,256]{1,0:T(8,128)(2,1)}, bf16[2048,256]{1,0:T(8,128)(2,1)S(1)}, u32[]{:S(2)}, u32[]{:S(2)}) collective-permute-start(bf16[2048,256]{1,0:T(8,128)(2,1)} %refs_3_.1), channel_id=1, source_target_pairs={{8,0},{16,8},{24,16},{9,1},{17,9},{25,17},{10,2},{18,10},{26,18},{... | collective-permute-start | bytes 3145736 | tf_op jit(solution)/shard_map/ppermute | solution.py:867
  8.5 28.3 %collective-permute-start.4 = (bf16[2048,256]{1,0:T(8,128)(2,1)}, bf16[2048,256]{1,0:T(8,128)(2,1)S(1)}, u32[]{:S(2)}, u32[]{:S(2)}) collective-permute-start(bf16[2048,256]{1,0:T(8,128)(2,1)} %refs_3_.1), channel_id=1, source_target_pairs={{0,8},{8,16},{16,24},{1,9},{9,17},{17,25},{2,10},{10,18},{18,26},{... | collective-permute-start | bytes 3145736 | tf_op jit(solution)/shard_map/ppermute | solution.py:864
  21.3 164.1 %all-gather.5.cloned.1.call-start = ((), (), s32[]{:S(2)}) async-start(), calls=%async_computation.3 | async-start | bytes 2162688 | tf_op jit(solution)/shard_map/all_gather | solution.py:935
  88.6 569.2 %reduce-scatter.5.cloned.1.call-start = ((), (), s32[]{:S(2)}) async-start(), calls=%async_computation.5 | async-start | bytes 2621440 | tf_op jit(solution)/shard_map/reduce_scatter | solution.py:1109
  88.7 26.4 %collective-permute-start.7 = (bf16[256,1536]{1,0:T(8,128)(2,1)}, bf16[256,1536]{1,0:T(8,128)(2,1)}, u32[]{:S(2)}, u32[]{:S(2)}) collective-permute-start(bf16[256,1536]{1,0:T(8,128)(2,1)} %pad_maximum_fusion.9.refs_0_), channel_id=1, source_target_pairs={{8,0},{16,8},{24,16},{9,1},{17,9},{25,17},{10,2},{18,10},{26,18},{... | collective-permute-start | bytes 2359304 | tf_op jit(solution)/shard_map/ppermute | solution.py:867
  140.9 51.9 %collective-permute-start.11 = (bf16[256,1536]{1,0:T(8,128)(2,1)S(1)}, bf16[256,1536]{1,0:T(8,128)(2,1)}, u32[]{:S(2)}, u32[]{:S(2)}) collective-permute-start(bf16[256,1536]{1,0:T(8,128)(2,1)S(1)} %collective-permute-done.9), channel_id=1, source_target_pairs={{8,0},{16,8},{24,16},{9,1},{17,9},{25,17},{10,2},{18,10},{26,18},{... | collective-permute-start | bytes 2359304 | tf_op jit(solution)/shard_map/ppermute | solution.py:867
  142.2 50.6 %collective-permute-start.12 = (bf16[256,1536]{1,0:T(8,128)(2,1)}, bf16[256,1536]{1,0:T(8,128)(2,1)}, u32[]{:S(2)}, u32[]{:S(2)}) collective-permute-start(bf16[256,1536]{1,0:T(8,128)(2,1)} %collective-permute-done.10), channel_id=1, source_target_pairs={{0,8},{8,16},{16,24},{1,9},{9,17},{17,25},{2,10},{10,18},{18,26},{... | collective-permute-start | bytes 2359304 | tf_op jit(solution)/shard_map/ppermute | solution.py:864
  151.2 31.8 %collective-permute-start.14 = (bf16[512,256]{1,0:T(8,128)(2,1)S(1)}, bf16[512,256]{1,0:T(8,128)(2,1)S(1)}, u32[]{:S(2)}, u32[]{:S(2)}) collective-permute-start(bf16[512,256]{1,0:T(8,128)(2,1)S(1)} %get-tuple-element.286), channel_id=1, source_target_pairs={{0,16},{8,24},{16,0},{24,8},{1,17},{9,25},{17,1},{25,9},{2,18},{10... | collective-permute-start | bytes 786440 | tf_op jit(solution)/shard_map/ppermute | solution.py:861
  153.0 32.4 %collective-permute-start.15 = (bf16[512,256]{1,0:T(8,128)(2,1)S(1)}, bf16[512,256]{1,0:T(8,128)(2,1)S(1)}, u32[]{:S(2)}, u32[]{:S(2)}) collective-permute-start(bf16[512,256]{1,0:T(8,128)(2,1)S(1)} %get-tuple-element.285), channel_id=1, source_target_pairs={{0,8},{8,16},{16,24},{24,0},{1,9},{9,17},{17,25},{25,1},{2,10},{10... | collective-permute-start | bytes 786440 | tf_op jit(solution)/shard_map/ppermute | solution.py:861
  170.5 41.6 %collective-permute-start.24 = (bf16[256,1536]{1,0:T(8,128)(2,1)}, bf16[256,1536]{1,0:T(8,128)(2,1)S(1)}, u32[]{:S(2)}, u32[]{:S(2)}) collective-permute-start(bf16[256,1536]{1,0:T(8,128)(2,1)} %pad_maximum_fusion.9.refs_0_), channel_id=1, source_target_pairs={{0,2},{1,3},{2,0},{3,1},{4,6},{5,7},{6,4},{7,5},{8,10},{9,11},{10,... | collective-permute-start | bytes 2359304 | tf_op jit(solution)/shard_map/ppermute | solution.py:852
  183.0 31.0 %collective-permute-start.25 = (bf16[256,1536]{1,0:T(8,128)(2,1)}, bf16[256,1536]{1,0:T(8,128)(2,1)}, u32[]{:S(2)}, u32[]{:S(2)}) collective-permute-start(bf16[256,1536]{1,0:T(8,128)(2,1)} %pad_maximum_fusion.9.refs_0_), channel_id=1, source_target_pairs={{0,4},{1,5},{2,6},{3,7},{4,0},{5,1},{6,2},{7,3},{8,12},{9,13},{10,... | collective-permute-start | bytes 2359304 | tf_op jit(solution)/shard_map/ppermute | solution.py:852
  214.0 40.3 %collective-permute-start.17 = (bf16[256,1536]{1,0:T(8,128)(2,1)S(1)}, bf16[256,1536]{1,0:T(8,128)(2,1)}, u32[]{:S(2)}, u32[]{:S(2)}) collective-permute-start(bf16[256,1536]{1,0:T(8,128)(2,1)S(1)} %get-tuple-element.244.refs_0_.refs_15_), channel_id=1, source_target_pairs={{0,4},{1,5},{2,6},{3,7},{4,0},{5,1},{6,2},{7,3},{8,12},{9,13},{10,... | collective-permute-start | bytes 2359304 | tf_op jit(solution)/shard_map/ppermute | solution.py:852
  217.0 49.5 %collective-permute-start.20 = (bf16[512,1024]{1,0:T(8,128)(2,1)S(1)}, bf16[512,1024]{1,0:T(8,128)(2,1)S(1)}, u32[]{:S(2)}, u32[]{:S(2)}) collective-permute-start(bf16[512,1024]{1,0:T(8,128)(2,1)S(1)} %copy-done), channel_id=1, source_target_pairs={{0,1},{1,0},{2,3},{3,2},{4,5},{5,4},{6,7},{7,6},{8,9},{9,8},{10,11... | collective-permute-start | bytes 3145736 | tf_op jit(solution)/shard_map/ppermute | solution.py:852
  220.6 42.0 %collective-permute-start.16 = (bf16[256,1536]{1,0:T(8,128)(2,1)S(1)}, bf16[256,1536]{1,0:T(8,128)(2,1)}, u32[]{:S(2)}, u32[]{:S(2)}) collective-permute-start(bf16[256,1536]{1,0:T(8,128)(2,1)S(1)} %get-tuple-element.244.refs_0_.refs_15_), channel_id=1, source_target_pairs={{0,2},{1,3},{2,0},{3,1},{4,6},{5,7},{6,4},{7,5},{8,10},{9,11},{10,... | collective-permute-start | bytes 2359304 | tf_op jit(solution)/shard_map/ppermute | solution.py:852
  233.8 31.9 %collective-permute-start.26 = (bf16[128,1536]{1,0:T(8,128)(2,1)}, bf16[128,1536]{1,0:T(8,128)(2,1)S(1)}, u32[]{:S(2)}, u32[]{:S(2)}) collective-permute-start(bf16[128,1536]{1,0:T(8,128)(2,1)} %slice.357), channel_id=1, source_target_pairs={{0,2},{1,3},{2,0},{3,1},{4,6},{5,7},{6,4},{7,5},{8,10},{9,11},{10,... | collective-permute-start | bytes 1179656 | tf_op jit(solution)/shard_map/ppermute | solution.py:852
  237.5 29.1 %collective-permute-start.27 = (bf16[128,1536]{1,0:T(8,128)(2,1)}, bf16[128,1536]{1,0:T(8,128)(2,1)}, u32[]{:S(2)}, u32[]{:S(2)}) collective-permute-start(bf16[128,1536]{1,0:T(8,128)(2,1)} %slice.358), channel_id=1, source_target_pairs={{0,4},{1,5},{2,6},{3,7},{4,0},{5,1},{6,2},{7,3},{8,12},{9,13},{10,... | collective-permute-start | bytes 1179656 | tf_op jit(solution)/shard_map/ppermute | solution.py:852
  266.5 30.8 %collective-permute-start.18 = (bf16[128,1536]{1,0:T(8,128)(2,1)}, bf16[128,1536]{1,0:T(8,128)(2,1)S(1)}, u32[]{:S(2)}, u32[]{:S(2)}) collective-permute-start(bf16[128,1536]{1,0:T(8,128)(2,1)} %slice.353), channel_id=1, source_target_pairs={{0,2},{1,3},{2,0},{3,1},{4,6},{5,7},{6,4},{7,5},{8,10},{9,11},{10,... | collective-permute-start | bytes 1179656 | tf_op jit(solution)/shard_map/ppermute | solution.py:852
  268.4 28.9 %collective-permute-start.19 = (bf16[128,1536]{1,0:T(8,128)(2,1)}, bf16[128,1536]{1,0:T(8,128)(2,1)S(1)}, u32[]{:S(2)}, u32[]{:S(2)}) collective-permute-start(bf16[128,1536]{1,0:T(8,128)(2,1)} %slice.354), channel_id=1, source_target_pairs={{0,4},{1,5},{2,6},{3,7},{4,0},{5,1},{6,2},{7,3},{8,12},{9,13},{10,... | collective-permute-start | bytes 1179656 | tf_op jit(solution)/shard_map/ppermute | solution.py:852
  342.4 46.6 %collective-permute-start.49 = (bf16[512,512]{1,0:T(8,128)(2,1)S(1)}, bf16[512,512]{1,0:T(8,128)(2,1)S(1)}, u32[]{:S(2)}, u32[]{:S(2)}) collective-permute-start(bf16[512,512]{1,0:T(8,128)(2,1)S(1)} %pad_maximum_fusion.14), channel_id=1, source_target_pairs={{0,1},{1,0},{2,3},{3,2},{4,5},{5,4},{6,7},{7,6},{8,9},{9,8},{10,11... | collective-permute-start | bytes 1572872 | tf_op jit(solution)/shard_map/ppermute | solution.py:852
  380.2 27.4 %collective-permute-start.44 = (bf16[512,1024]{1,0:T(8,128)(2,1)}, bf16[512,1024]{1,0:T(8,128)(2,1)S(1)}, u32[]{:S(2)}, u32[]{:S(2)}) collective-permute-start(bf16[512,1024]{1,0:T(8,128)(2,1)} %get-tuple-element.133), channel_id=1, source_target_pairs={{0,1},{1,0},{2,3},{3,2},{4,5},{5,4},{6,7},{7,6},{8,9},{9,8},{10,11... | collective-permute-start | bytes 3145736 | tf_op jit(solution)/shard_map/ppermute | solution.py:852
  405.0 127.1 %collective-permute-start.63 = (bf16[2,2,256,512]{3,2,1,0:T(8,128)(2,1)}, bf16[2,2,256,512]{3,2,1,0:T(8,128)(2,1)}, u32[]{:S(2)}, u32[]{:S(2)}) collective-permute-start(bf16[2,2,256,512]{3,2,1,0:T(8,128)(2,1)} %shard_map.380), channel_id=1, source_target_pairs={{0,4},{1,5},{2,6},{3,7},{4,0},{5,1},{6,2},{7,3},{8,12},{9,13},{10,... | collective-permute-start | bytes 3145736 | tf_op jit(solution)/shard_map/ppermute | solution.py:852
  433.3 96.7 %collective-permute-start.61 = (bf16[2,2,256,512]{3,2,0,1:T(8,128)(2,1)}, bf16[2,2,256,512]{3,2,0,1:T(8,128)(2,1)}, u32[]{:S(2)}, u32[]{:S(2)}) collective-permute-start(bf16[2,2,256,512]{3,2,0,1:T(8,128)(2,1)} %copy.89), channel_id=1, source_target_pairs={{0,2},{1,3},{2,0},{3,1},{4,6},{5,7},{6,4},{7,5},{8,10},{9,11},{10,... | collective-permute-start | bytes 3145736 | tf_op jit(solution)/shard_map/ppermute | solution.py:852
  521.2 136.6 %reduce-scatter.3.cloned.1.call-start = ((), (), s32[]{:S(2)}) async-start(), calls=%async_computation.4 | async-start | bytes 2621440 | tf_op jit(solution)/shard_map/reduce_scatter | solution.py:1109
  541.4 64.2 %collective-permute-start.55 = (bf16[2,2,272,1152]{3,2,1,0:T(8,128)(2,1)}, bf16[2,2,272,1152]{3,2,1,0:T(8,128)(2,1)}, u32[]{:S(2)}, u32[]{:S(2)}) collective-permute-start(bf16[2,2,272,1152]{3,2,1,0:T(8,128)(2,1)} %shard_map.384), channel_id=1, source_target_pairs={{0,4},{1,5},{2,6},{3,7},{4,0},{5,1},{6,2},{7,3},{8,12},{9,13},{10,... | collective-permute-start | bytes 7520264 | tf_op jit(solution)/shard_map/ppermute | solution.py:852
  543.4 58.3 %collective-permute-start.53 = (bf16[2,2,272,1152]{3,2,0,1:T(8,128)(2,1)}, bf16[2,2,272,1152]{3,2,0,1:T(8,128)(2,1)}, u32[]{:S(2)}, u32[]{:S(2)}) collective-permute-start(bf16[2,2,272,1152]{3,2,0,1:T(8,128)(2,1)} %copy.86), channel_id=1, source_target_pairs={{0,2},{1,3},{2,0},{3,1},{4,6},{5,7},{6,4},{7,5},{8,10},{9,11},{10,... | collective-permute-start | bytes 7520264 | tf_op jit(solution)/shard_map/ppermute | solution.py:852
  562.0 32.8 %collective-permute-start.50 = (bf16[576,768]{1,0:T(8,128)(2,1)}, bf16[576,768]{1,0:T(8,128)(2,1)}, u32[]{:S(2)}, u32[]{:S(2)}) collective-permute-start(bf16[576,768]{1,0:T(8,128)(2,1)} %get-tuple-element.328), channel_id=1, source_target_pairs={{0,1},{1,0},{2,3},{3,2},{4,5},{5,4},{6,7},{7,6},{8,9},{9,8},{10,11... | collective-permute-start | bytes 2654216 | tf_op jit(solution)/shard_map/ppermute | solution.py:852
  562.0 31.3 %collective-permute-start.66 = (bf16[256,512]{1,0:T(8,128)(2,1)}, bf16[256,512]{1,0:T(8,128)(2,1)}, u32[]{:S(2)}, u32[]{:S(2)}) collective-permute-start(bf16[256,512]{1,0:T(8,128)(2,1)} %get-tuple-element.247), channel_id=1, source_target_pairs={{0,16},{8,24},{16,0},{24,8},{1,17},{9,25},{17,1},{25,9},{2,18},{10... | collective-permute-start | bytes 786440 | tf_op jit(solution)/shard_map/ppermute | solution.py:861
  604.4 35.1 %collective-permute-start.54 = (bf16[2,1,272,1152]{3,2,0,1:T(8,128)(2,1)}, bf16[2,1,272,1152]{3,2,0,1:T(8,128)(2,1)}, u32[]{:S(2)}, u32[]{:S(2)}) collective-permute-start(bf16[2,1,272,1152]{3,2,0,1:T(8,128)(2,1)} %add_convert_fusion.2), channel_id=1, source_target_pairs={{0,4},{1,5},{2,6},{3,7},{4,0},{5,1},{6,2},{7,3},{8,12},{9,13},{10,... | collective-permute-start | bytes 3760136 | tf_op jit(solution)/shard_map/ppermute | solution.py:852
  608.2 31.2 %collective-permute-start.56 = (bf16[2,1,272,1152]{3,2,1,0:T(8,128)(2,1)}, bf16[2,1,272,1152]{3,2,1,0:T(8,128)(2,1)}, u32[]{:S(2)}, u32[]{:S(2)}) collective-permute-start(bf16[2,1,272,1152]{3,2,1,0:T(8,128)(2,1)} %add_convert_fusion.1), channel_id=1, source_target_pairs={{0,2},{1,3},{2,0},{3,1},{4,6},{5,7},{6,4},{7,5},{8,10},{9,11},{10,... | collective-permute-start | bytes 3760136 | tf_op jit(solution)/shard_map/ppermute | solution.py:852
  647.7 54.9 %collective-permute-start.58 = (bf16[272,1152]{1,0:T(8,128)(2,1)}, bf16[272,1152]{1,0:T(8,128)(2,1)}, u32[]{:S(2)}, u32[]{:S(2)}) collective-permute-start(bf16[272,1152]{1,0:T(8,128)(2,1)} %get-tuple-element.235), channel_id=1, source_target_pairs={{0,16},{8,24},{16,0},{24,8},{1,17},{9,25},{17,1},{25,9},{2,18},{10... | collective-permute-start | bytes 1880072 | tf_op jit(solution)/shard_map/ppermute | solution.py:861
  651.0 51.7 %collective-permute-start.57 = (bf16[272,1152]{1,0:T(8,128)(2,1)}, bf16[272,1152]{1,0:T(8,128)(2,1)}, u32[]{:S(2)}, u32[]{:S(2)}) collective-permute-start(bf16[272,1152]{1,0:T(8,128)(2,1)} %get-tuple-element.234), channel_id=1, source_target_pairs={{0,8},{8,16},{16,24},{24,0},{1,9},{9,17},{17,25},{25,1},{2,10},{10... | collective-permute-start | bytes 1880072 | tf_op jit(solution)/shard_map/ppermute | solution.py:861
  (121 other events, 1597.5 us)
Sparse Core Ops, SparseCore 0:
  21.4 26.3 all-gather.2
  88.7 60.5 all-gather.4
  521.3 44.8 reduce-scatter.4
  578.7 43.2 reduce-scatter.2

commit v2 on v1

v2 whole, which is shorter than its diff:
```python
import functools
import math

import jax
import jax.numpy as jnp
from jax import lax
from jax.experimental import pallas as pl
from jax.experimental.pallas import tpu as pltpu
from jax.sharding import PartitionSpec as P

HEAD_DIM = 64
SHORT = 1024

layer_eps = 1e-06
learn_rate = 0.008
beta_one = 0.9
beta_two = 0.95
adam_eps = 1e-08
bias_one = 1.0 - math.exp(100.0 * math.log(0.9))
bias_two = 1.0 - math.exp(100.0 * math.log(0.95))
score_scale = 8.0
LOG2E = math.log2(math.e)
LN2 = math.log(2.0)

bf16 = jnp.bfloat16
f32 = jnp.float32
VMEM_LIMIT = 56 * 1024 * 1024


def dot(a, b):
    return jnp.dot(a, b, preferred_element_type=f32)


def dot_t(a, b):
    return lax.dot_general(a, b, (((1,), (1,)), ((), ())), preferred_element_type=f32)


def t_dot(a, b):
    return lax.dot_general(a, b, (((0,), (0,)), ((), ())), preferred_element_type=f32)


def params():
    return pltpu.CompilerParams(vmem_limit_bytes=VMEM_LIMIT)


def full_spec(shape):
    return pl.BlockSpec(shape, lambda *_: (0,) * len(shape))


def head_sum(value, ones):
    high = value.astype(bf16)
    low = (value - high.astype(f32)).astype(bf16)
    return dot(high, ones) + dot(low, ones)


def widen(value, cols):
    return jnp.concatenate([value] * (cols // value.shape[1]), axis=1)


def swap_halves(value):
    cols = value.shape[-1]
    half = HEAD_DIM // 2
    lane = lax.broadcasted_iota(jnp.int32, value.shape, 1)
    first = (lane % HEAD_DIM) < half
    up = pltpu.roll(value, cols - half, 1)
    down = pltpu.roll(value, half, 1)
    return jnp.where(first, up, down)


def qkv_kernel(place_ref, *refs, parts):
    tokens = refs[:parts]
    w_ref, cos_ref, sin_ref, gain_ref, ones_ref, x_ref, q_ref, k_ref, v_ref, rho_ref = refs[parts:]
    cols = v_ref.shape[1]
    z = place_ref[0]
    for n in range(parts):
        at = pl.multiple_of(lax.rem(z + parts - n, parts) * cols, cols)
        x_ref[:, pl.ds(at, cols)] = tokens[n][...]
    proj = dot(x_ref[...], w_ref[...])
    cosine = widen(cos_ref[...], cols)
    sine = widen(sin_ref[...], cols)
    ones = ones_ref[...]
    gain = gain_ref[...]
    heads = cols // HEAD_DIM
    lane = lax.broadcasted_iota(jnp.int32, rho_ref.shape, 1)
    stats = jnp.zeros(rho_ref.shape, f32)
    for c, (out, scale) in enumerate(((q_ref, score_scale * LOG2E), (k_ref, 1.0))):
        part = proj[:, c * cols : (c + 1) * cols]
        rho = lax.rsqrt(head_sum(part * part, ones) + layer_eps)
        rot = part * cosine + swap_halves(part) * sine
        out[...] = (rot * rho * (gain * scale)).astype(bf16)
        for h in range(heads):
            stats = jnp.where(lane == c * heads + h, rho[:, h * HEAD_DIM : h * HEAD_DIM + 1], stats)
    rho_ref[...] = stats
    v_ref[...] = proj[:, 2 * cols :].astype(bf16)


def qkv_project(place, tokens, w, cosine, sine, gain, ones):
    rows, cols = tokens[0].shape
    parts = len(tokens)
    width = parts * cols
    blk = 512
    row = lambda n: pl.BlockSpec((blk, n), lambda i, s: (i, 0))
    return pl.pallas_call(
        functools.partial(qkv_kernel, parts=parts),
        grid_spec=pltpu.PrefetchScalarGridSpec(
            num_scalar_prefetch=1,
            grid=(rows // blk,),
            in_specs=[row(cols)] * parts
            + [full_spec((width, 3 * cols)), row(128), row(128)]
            + [full_spec((1, cols)), full_spec((cols, cols))],
            out_specs=[row(width)] + [row(cols)] * 3 + [row(128)],
        ),
        out_shape=[jax.ShapeDtypeStruct((rows, width), bf16)]
        + [jax.ShapeDtypeStruct((rows, cols), bf16)] * 3
        + [jax.ShapeDtypeStruct((rows, 128), f32)],
        compiler_params=params(),
    )(place, *tokens, w, cosine, sine, gain, ones)


def head_masks(cols, heads):
    lane = lax.broadcasted_iota(jnp.int32, (1, cols), 1) // HEAD_DIM
    return [(lane == h) for h in range(heads)]


def masked(value, mask):
    return jnp.where(mask, value, jnp.zeros_like(value))


def attn_fwd_kernel(long_ref, q_ref, k_ref, v_ref, y_ref, l_ref, acc, mass, *, heads, blk, sub, first):
    i = first + pl.program_id(0)
    cols = q_ref.shape[1]
    masks = head_masks(cols, heads)
    per = SHORT // blk
    low = jnp.where(long_ref[0] != 0, 0, (i // per) * per)
    acc[...] = jnp.zeros_like(acc)
    mass[...] = jnp.zeros_like(mass)

    def lanes(p):
        total = p[:, 0:128]
        for n in range(1, p.shape[1] // 128):
            total = total + p[:, n * 128 : (n + 1) * 128]
        return total

    def body(j, carry):
        start = pl.multiple_of(j * blk, blk)
        keys = k_ref[pl.ds(start, blk), :]
        vals = v_ref[pl.ds(start, blk), :]
        q = q_ref[...]
        total = jnp.zeros(acc.shape, f32)
        for h in range(heads):
            p = jnp.exp2(dot_t(masked(q, masks[h]), keys))
            mass[h] += lanes(p)
            total += dot(p.astype(bf16), masked(vals, masks[h]))
        acc[...] += total
        return carry

    lax.fori_loop(low, i, body, 0)
    start = pl.multiple_of(i * blk, blk)
    causal = lax.broadcasted_iota(jnp.int32, (sub, sub), 0) >= lax.broadcasted_iota(
        jnp.int32, (sub, sub), 1
    )
    for a in range(blk // sub):
        rows = slice(a * sub, (a + 1) * sub)
        q = q_ref[rows, :]
        for b in range(a + 1):
            at = pl.multiple_of(start + b * sub, sub)
            keys = k_ref[pl.ds(at, sub), :]
            vals = v_ref[pl.ds(at, sub), :]
            total = jnp.zeros((sub, cols), f32)
            for h in range(heads):
                p = jnp.exp2(dot_t(masked(q, masks[h]), keys))
                if a == b:
                    p = jnp.where(causal, p, 0.0)
                mass[h, rows, :] += lanes(p)
                total += dot(p.astype(bf16), masked(vals, masks[h]))
            acc[rows, :] += total
    inverse = jnp.zeros(acc.shape, f32)
    logs = jnp.zeros(l_ref.shape, f32)
    lane = lax.broadcasted_iota(jnp.int32, l_ref.shape, 1)
    for h in range(heads):
        column = jnp.sum(mass[h], axis=1, keepdims=True)
        inverse = jnp.where(masks[h], 1.0 / column, inverse)
        logs = jnp.where(lane == h, jnp.log2(column), logs)
    y_ref[...] = (acc[...] * inverse).astype(bf16)
    l_ref[...] = logs


def attn_fwd(is_long, q, k, v, first, count):
    rows, cols = q.shape
    heads = cols // HEAD_DIM
    blk, sub = 512, 256
    row = lambda n: pl.BlockSpec((blk, n), lambda i, s: (i, 0))
    whole = pl.BlockSpec(((first + count) * blk, cols), lambda i, s: (0, 0))
    return pl.pallas_call(
        functools.partial(attn_fwd_kernel, heads=heads, blk=blk, sub=sub, first=first),
        grid_spec=pltpu.PrefetchScalarGridSpec(
            num_scalar_prefetch=1,
            grid=(count,),
            in_specs=[pl.BlockSpec((blk, cols), lambda i, s: (first + i, 0)), whole, whole],
            out_specs=[row(cols), row(128)],
            scratch_shapes=[pltpu.VMEM((blk, cols), f32), pltpu.VMEM((heads, blk, 128), f32)],
        ),
        out_shape=[
            jax.ShapeDtypeStruct((count * blk, cols), bf16),
            jax.ShapeDtypeStruct((count * blk, 128), f32),
        ],
        compiler_params=params(),
    )(is_long, q, k, v)


def attn_bwd_kernel(
    long_ref, q_ref, qk_ref, dy_ref, y_ref, l_ref, k_ref, v_ref, rho_ref, cos_ref, sin_ref, gain_ref,
    ones_ref, dk_in, dv_in, out_ref, dk_out, dv_out, s_ref, acc, dk_acc, dv_acc, stats, *, heads, blk, sub, first, count
):
    step = pl.program_id(0)
    local = count - 1 - step
    i = first + local
    cols = q_ref.shape[1]
    masks = head_masks(cols, heads)
    per = SHORT // blk
    low = jnp.where(long_ref[0] != 0, 0, (i // per) * per)
    ones = ones_ref[...]
    gain = gain_ref[...]

    @pl.when(step == 0)
    def _():
        dk_acc[...] = jnp.zeros_like(dk_acc)
        dv_acc[...] = jnp.zeros_like(dv_acc)
        s_ref[...] = jnp.zeros_like(s_ref)
        if dk_in is not None:
            dk_acc[...] = dk_in[...]
            dv_acc[...] = dv_in[...]

    acc[...] = jnp.zeros_like(acc)
    prod = dy_ref[...].astype(f32) * y_ref[...].astype(f32)
    high = prod.astype(bf16)
    rest = (prod - high.astype(f32)).astype(bf16)
    pickers = (
        lax.broadcasted_iota(jnp.int32, (8, cols), 1) // HEAD_DIM
        == lax.broadcasted_iota(jnp.int32, (8, cols), 0)
    ).astype(bf16)
    stats[0:8, :] = dot_t(pickers, high) + dot_t(pickers, rest)
    stats[8:16, :] = l_ref[...].T[0:8, :]

    def piece(at, size, rows, causal):
        keys = k_ref[pl.ds(at, size), :]
        vals = v_ref[pl.ds(at, size), :]
        q = q_ref[rows, :]
        dy = dy_ref[rows, :]
        total_q = jnp.zeros(q.shape, f32)
        total_k = jnp.zeros(keys.shape, f32)
        total_v = jnp.zeros(keys.shape, f32)
        for h in range(heads):
            qm = masked(q, masks[h])
            dym = masked(dy, masks[h])
            p = jnp.exp2(dot_t(keys, qm) - stats[8 + h : 9 + h, rows])
            if causal is not None:
                p = jnp.where(causal, p, 0.0)
            ds = (p * (dot_t(vals, dym) - stats[h : h + 1, rows])).astype(bf16)
            total_v += dot(p.astype(bf16), dym)
            total_k += dot(ds, qm)
            total_q += t_dot(ds, masked(keys, masks[h]))
        acc[rows, :] += total_q
        dk_acc[pl.ds(at, size), :] += total_k
        dv_acc[pl.ds(at, size), :] += total_v

    def body(j, carry):
        piece(pl.multiple_of(j * blk, blk), blk, slice(0, blk), None)
        return carry

    lax.fori_loop(low, i, body, 0)
    start = pl.multiple_of(i * blk, blk)
    causal = lax.broadcasted_iota(jnp.int32, (sub, sub), 0) <= lax.broadcasted_iota(
        jnp.int32, (sub, sub), 1
    )
    for a in range(blk // sub):
        for b in range(a + 1):
            piece(
                pl.multiple_of(start + b * sub, sub),
                sub,
                slice(a * sub, (a + 1) * sub),
                causal if a == b else None,
            )
    cosine = widen(cos_ref[...], cols)
    sine = widen(sin_ref[...], cols)
    total = jnp.zeros((1, cols), f32)
    here = pl.ds(start, blk)
    for c, (value, unit, up, scale) in enumerate(
        (
            (acc[...], q_ref[...], score_scale, score_scale * LOG2E),
            (dk_acc[here, :], k_ref[here, :], LN2, 1.0),
        )
    ):
        rho = jnp.zeros(value.shape, f32)
        for h in range(heads):
            at = c * heads + h
            rho = jnp.where(masks[h], rho_ref[:, at : at + 1], rho)
        grad = value * up
        unit = unit.astype(f32) * (1.0 / (gain * scale))
        total += jnp.sum(grad * unit, axis=0, keepdims=True)
        grad = grad * gain
        back = rho * (grad - unit * head_sum(grad * unit, ones))
        turned = back * cosine - swap_halves(back) * sine
        out_ref[:, c * cols : (c + 1) * cols] = turned.astype(bf16)
    out_ref[:, 2 * cols :] = dv_acc[here, :].astype(bf16)
    s_ref[0:1, :] += total
    if dk_out is not None:
        @pl.when(step == count - 1)
        def _():
            dk_out[...] = dk_acc[0 : first * blk, :]
            dv_out[...] = dv_acc[0 : first * blk, :]


def attn_bwd(is_long, q, k, v, dy, y, logs, rho, cosine, sine, gain, ones, first, count, carry):
    rows, cols = q.shape
    heads = cols // HEAD_DIM
    blk, sub = 512, 256
    top = (first + count) * blk
    at = lambda s: first + count - 1 - s
    row = lambda n: pl.BlockSpec((blk, n), lambda s, m: (at(s), 0))
    whole = pl.BlockSpec((top, cols), lambda s, m: (0, 0))
    ins = [q, k, dy, y, logs, k, v, rho, cosine, sine, gain, ones]
    mine = lambda n: pl.BlockSpec((blk, n), lambda s, m: (count - 1 - s, 0))
    in_specs = [row(cols)] * 2 + [mine(cols)] * 2 + [mine(128), whole, whole] + [row(128)] * 3
    in_specs += [full_spec((1, cols)), full_spec((cols, cols))]
    body = functools.partial(
        attn_bwd_kernel, heads=heads, blk=blk, sub=sub, first=first, count=count
    )
    outs = [jax.ShapeDtypeStruct((count * blk, 3 * cols), bf16)]
    out_specs = [pl.BlockSpec((blk, 3 * cols), lambda s, m: (count - 1 - s, 0))]
    if first:
        outs += [jax.ShapeDtypeStruct((first * blk, cols), f32)] * 2
        out_specs += [full_spec((first * blk, cols))] * 2
        inner = lambda *r: body(*r[:13], None, None, *r[13:])
    else:
        ins += carry
        in_specs += [full_spec((top, cols))] * 2
        inner = lambda *r: body(*r[:16], None, None, *r[16:])
    outs.append(jax.ShapeDtypeStruct((8, cols), f32))
    out_specs.append(full_spec((8, cols)))
    return pl.pallas_call(
        inner,
        grid_spec=pltpu.PrefetchScalarGridSpec(
            num_scalar_prefetch=1,
            grid=(count,),
            in_specs=in_specs,
            out_specs=out_specs,
            scratch_shapes=[
                pltpu.VMEM((blk, cols), f32),
                pltpu.VMEM((top, cols), f32),
                pltpu.VMEM((top, cols), f32),
                pltpu.VMEM((16, blk), f32),
            ],
        ),
        out_shape=outs,
        compiler_params=params(),
    )(is_long, *ins)


def row_norm(value):
    return lax.rsqrt(jnp.mean(value * value, axis=1, keepdims=True) + layer_eps)


def norm_back(scale, result, grad):
    return scale * (grad - result * jnp.mean(grad * result, axis=1, keepdims=True))


def pack_kernel(core_ref, up_ref, down_ref, out_ref, qkv_ref, mine_ref, theirs_ref, q_ref):
    half = up_ref.shape[2] // 2
    low = core_ref[0] == 0
    down = down_ref[...].astype(bf16).T
    out = out_ref[...].astype(bf16).T
    for ref, first in ((mine_ref, low), (theirs_ref, jnp.logical_not(low))):
        for c in range(2):
            ref[:, c * half : (c + 1) * half] = jnp.where(
                first, up_ref[:, c, :half], up_ref[:, c, half:]
            ).astype(bf16)
        ref[:, 2 * half : 3 * half] = jnp.where(first, down[:, :half], down[:, half:])
        ref[:, 3 * half :] = out
    cols = qkv_ref.shape[2]
    for c in range(3):
        q_ref[:, c * cols : (c + 1) * cols] = qkv_ref[:, c, :].astype(bf16)


def pack(core, w_up, w_down, w_out, w_qkv):
    span, _, hid = w_up.shape
    cols = w_qkv.shape[2]
    vmem = pl.BlockSpec(memory_space=pltpu.VMEM)
    return pl.pallas_call(
        pack_kernel,
        in_specs=[pl.BlockSpec(memory_space=pltpu.SMEM)] + [vmem] * 4,
        out_specs=[vmem] * 3,
        out_shape=[jax.ShapeDtypeStruct((span, 3 * hid // 2 + cols), bf16)] * 2
        + [jax.ShapeDtypeStruct((span, 3 * cols), bf16)],
        compiler_params=params(),
    )(core, w_up, w_down, w_out, w_qkv)


def place_of(r, chip, chunk):
    return pl.ds(pl.multiple_of((r ^ chip) * chunk, chunk), chunk)


def put_relative(ref, chip, chips, fast):
    if not fast:
        return ref[...]
    if len(ref.shape) == 3:
        return jnp.concatenate([ref[r ^ chip] for r in range(chips)], axis=1)
    chunk = ref.shape[1] // chips
    return jnp.concatenate([ref[:, place_of(r, chip, chunk)] for r in range(chips)], axis=1)


def put_natural(ref, value, chip, chips, fast):
    if not fast:
        ref[...] = value
        return
    chunk = value.shape[1] // chips
    for r in range(chips):
        part = value[:, r * chunk : (r + 1) * chunk]
        if len(ref.shape) == 3:
            ref[r ^ chip] = part
        else:
            ref[:, place_of(r, chip, chunk)] = part


def attn_out_kernel(place_ref, *refs, counts, chips, fast):
    total = sum(counts)
    flat, refs = refs[:total], refs[total:]
    ya_ref, yb_ref, x_ref, alpha_ref, ha_ref, h1_ref, hb_ref, stat_ref, acc = refs
    z, chip = place_ref[0], place_ref[1]
    parts = len(counts)
    early = pl.program_id(0) == 0
    index = 0
    for n in range(parts):
        at = lax.rem(z + parts - n, parts)
        y = jnp.where(early, ya_ref[at], yb_ref[at])
        column = 0
        for piece in flat[index : index + counts[n]]:
            part = slice(column, column + piece.shape[0])
            if n == 0:
                acc[:, part] = dot_t(y, piece[...])
            else:
                acc[:, part] += dot_t(y, piece[...])
            column += piece.shape[0]
        index += counts[n]
    total = acc[...]
    norm = row_norm(total)
    hidden = total * norm
    start = put_relative(x_ref, chip, chips, fast).astype(f32)
    mixed = start + alpha_ref[...] * (hidden - start)
    first_norm = row_norm(mixed)
    out = mixed * first_norm
    ha_ref[...] = hidden
    h1_ref[...] = out
    hb_ref[...] = out.astype(bf16)
    lane = lax.broadcasted_iota(jnp.int32, stat_ref.shape, 1)
    stat_ref[...] = jnp.where(lane == 0, norm, first_norm)


def own_rows(blk, parts, width, fast):
    if fast:
        return pl.BlockSpec((blk, width), lambda i, s: (i * parts + s[0], 0))
    return pl.BlockSpec((blk, width), lambda i, s: (i, 0))


def out_weights(slots, cols):
    flat = [p for slot in slots for p in slot]
    last = flat[0].shape[1] // cols - 1
    return flat, [pl.BlockSpec((p.shape[0], cols), lambda i, s: (0, last)) for p in flat]


def attn_out(place, ya, yb, slots, x, alpha, chips, fast):
    parts, blk, cols = ya.shape
    width = x.shape[1]
    rows = 2 * blk
    row = lambda n: pl.BlockSpec((blk, n), lambda i, s: (i, 0))
    flat, specs = out_weights(slots, cols)
    return pl.pallas_call(
        functools.partial(attn_out_kernel, counts=[len(t) for t in slots], chips=chips, fast=fast),
        grid_spec=pltpu.PrefetchScalarGridSpec(
            num_scalar_prefetch=1,
            grid=(2,),
            in_specs=specs
            + [full_spec(ya.shape)] * 2
            + [own_rows(blk, parts, width, fast), full_spec((1, width))],
            out_specs=[row(width)] * 3 + [row(128)],
            scratch_shapes=[pltpu.VMEM((blk, width), f32)],
        ),
        out_shape=[jax.ShapeDtypeStruct((rows, width), d) for d in (f32, f32, bf16)]
        + [jax.ShapeDtypeStruct((rows, 128), f32)],
        compiler_params=params(),
    )(place, *flat, ya, yb, x, alpha)


def loss_kernel(place_ref, own_ref, got_ref, h1_ref, cot_ref, alpha_ref, hidden_ref, dmo_ref, base_ref, ga_ref, *, chips, fast):
    chip = place_ref[1]
    total = own_ref[...] + got_ref[...].astype(f32)
    alpha = alpha_ref[...]
    norm = row_norm(total)
    inner = total * norm
    h1 = h1_ref[...]
    mixed = h1 + alpha * (inner - h1)
    last = row_norm(mixed)
    hidden = mixed * last
    grad = norm_back(last, hidden, put_relative(cot_ref, chip, chips, fast).astype(f32))
    put_natural(hidden_ref, hidden.astype(bf16), chip, chips, fast)
    base_ref[...] = (1.0 - alpha) * grad
    dmo_ref[...] = norm_back(norm, inner, alpha * grad).astype(bf16)

    @pl.when(pl.program_id(0) == 0)
    def _():
        ga_ref[...] = jnp.zeros_like(ga_ref)

    ga_ref[0:1, :] += jnp.sum(grad * (inner - h1), axis=0, keepdims=True)


def loss(place, own, got, h1, cot, alpha, chips, fast):
    rows, width = own.shape
    blk = rows // 2
    row = pl.BlockSpec((blk, width), lambda i, s: (i, 0))
    part = row
    if fast:
        part = pl.BlockSpec((chips, blk, width // chips), lambda i, s: (0, i, 0))
    return pl.pallas_call(
        functools.partial(loss_kernel, chips=chips, fast=fast),
        grid_spec=pltpu.PrefetchScalarGridSpec(
            num_scalar_prefetch=1,
            grid=(rows // blk,),
            in_specs=[row] * 3 + [part, full_spec((1, width))],
            out_specs=[part] + [row] * 2 + [full_spec((8, width))],
        ),
        out_shape=[jax.ShapeDtypeStruct(cot.shape, bf16)]
        + [jax.ShapeDtypeStruct((rows, width), d) for d in (bf16, f32)]
        + [jax.ShapeDtypeStruct((8, width), f32)],
        compiler_params=params(),
    )(place, own, got, h1, cot, alpha)


def first_back_kernel(place_ref, *refs, counts, chips, fast):
    total = sum(counts)
    flat, refs = refs[:total], refs[total:]
    own_ref, got_ref, base_ref, h1_ref, ha_ref, x_ref, stat_ref, alpha_ref = refs[:8]
    do_ref, through_ref, ga_ref, dya_ref, dyb_ref = refs[8:]
    z, chip = place_ref[0], place_ref[1]
    alpha = alpha_ref[...]
    grad = base_ref[...] + own_ref[...] + got_ref[...].astype(f32)
    grad = norm_back(stat_ref[:, 1:2], h1_ref[...], grad)
    ha = ha_ref[...]
    put_natural(through_ref, ((1.0 - alpha) * grad).astype(bf16), chip, chips, fast)
    back = norm_back(stat_ref[:, 0:1], ha, alpha * grad).astype(bf16)
    do_ref[...] = back
    parts = len(counts)
    step = pl.program_id(0)
    index = 0
    for n in range(parts):
        at = lax.rem(z + parts - n, parts)
        part = jnp.zeros(dya_ref.shape[1:], f32)
        column = 0
        for piece in flat[index : index + counts[n]]:
            part += dot(do_ref[:, column : column + piece.shape[0]], piece[...])
            column += piece.shape[0]
        index += counts[n]
        part = part.astype(bf16)
        for side, ref in enumerate((dya_ref, dyb_ref)):

            @pl.when(step == side)
            def _(ref=ref, part=part, at=at):
                ref[at] = part

    @pl.when(step == 0)
    def _():
        ga_ref[...] = jnp.zeros_like(ga_ref)

    start = put_relative(x_ref, chip, chips, fast).astype(f32)
    ga_ref[0:1, :] += jnp.sum(grad * (ha - start), axis=0, keepdims=True)


def first_back(place, own, got, base, h1, ha, x, stat, alpha, slots, chips, fast, cols):
    rows, width = own.shape
    parts = len(slots)
    blk = rows // 2
    row = lambda n: pl.BlockSpec((blk, n), lambda i, s: (i, 0))
    flat, specs = out_weights(slots, cols)
    return pl.pallas_call(
        functools.partial(first_back_kernel, counts=[len(t) for t in slots], chips=chips, fast=fast),
        grid_spec=pltpu.PrefetchScalarGridSpec(
            num_scalar_prefetch=1,
            grid=(2,),
            in_specs=specs
            + [row(width)] * 5
            + [own_rows(blk, parts, width, fast), row(128), full_spec((1, width))],
            out_specs=[row(width)] * 2
            + [full_spec((8, width))]
            + [full_spec((parts, blk, cols))] * 2,
        ),
        out_shape=[jax.ShapeDtypeStruct((rows, width), bf16)] * 2
        + [jax.ShapeDtypeStruct((8, width), f32)]
        + [jax.ShapeDtypeStruct((parts, blk, cols), bf16)] * 2,
        compiler_params=params(),
    )(place, *flat, own, got, base, h1, ha, x, stat, alpha)


def fetch_weights(q, slots, wbuf, sems):
    def copies(j):
        at = 0
        found = []
        for p, piece in enumerate(slots[j]):
            size = piece.shape[0]
            found.append(
                pltpu.make_async_copy(
                    piece.at[:, : wbuf.shape[2]], wbuf.at[j % 2, at : at + size, :], sems.at[j % 2, p]
                )
            )
            at += size
        return found

    for j in range(len(slots)):

        @pl.when(q == j)
        def _(j=j):
            if j == 0:
                for copy in copies(0):
                    copy.start()
            if j + 1 < len(slots):
                for copy in copies(j + 1):
                    copy.start()
            for copy in copies(j):
                copy.wait()


def mlp_fwd_kernel(*refs, half, counts):
    total = sum(counts)
    flat, refs = refs[:total], refs[total:]
    slots, at = [], 0
    for n in counts:
        slots.append(flat[at : at + n])
        at += n
    ha_ref, hb_ref, suv_ref, act_ref, uv_ref, own_ref, got_ref, acc, wbuf, sems = refs
    rows = ha_ref.shape[0]
    q = pl.program_id(0)

    @pl.when(q == 0)
    def _():
        own_ref[...] = jnp.zeros_like(own_ref)
        acc[...] = jnp.zeros_like(acc)

    fetch_weights(q, slots, wbuf, sems)
    w = wbuf.at[lax.rem(q, 2)]
    for base, h_ref, sum_ref in ((0, ha_ref, own_ref), (rows, hb_ref, acc)):
        at = slice(base, base + rows)
        pair = dot(h_ref[...], w[:, : 2 * half])
        lifted = pair[:, :half] * suv_ref[0:1, :]
        gated = pair[:, half:] * suv_ref[1:2, :]
        act = (lifted * gated * jax.nn.sigmoid(gated)).astype(bf16)
        uv_ref[at, :] = pair.astype(bf16)
        act_ref[at, :] = act
        sum_ref[...] += dot_t(act, w[:, 2 * half : 3 * half])

    @pl.when(q == pl.num_programs(0) - 1)
    def _():
        got_ref[...] = acc[...].astype(bf16)


def mlp_fwd(ha, hb, slots, suv):
    rows, width = ha.shape
    parts, _, half = suv.shape
    take = lambda n: pl.BlockSpec((None, 2 * rows, n), lambda q: (q, 0, 0))
    whole = full_spec((rows, width))
    anywhere = pl.BlockSpec(memory_space=pl.ANY)
    flat = [p for slot in slots for p in slot]
    return pl.pallas_call(
        functools.partial(mlp_fwd_kernel, half=half, counts=[len(s) for s in slots]),
        grid=(parts,),
        in_specs=[anywhere] * len(flat)
        + [whole, whole, pl.BlockSpec((None, 2, half), lambda q: (q, 0, 0))],
        out_specs=[take(half), take(2 * half), whole, whole],
        out_shape=[
            jax.ShapeDtypeStruct((parts, 2 * rows, half), bf16),
            jax.ShapeDtypeStruct((parts, 2 * rows, 2 * half), bf16),
            jax.ShapeDtypeStruct((rows, width), f32),
            jax.ShapeDtypeStruct((rows, width), bf16),
        ],
        scratch_shapes=[
            pltpu.VMEM((rows, width), f32),
            pltpu.VMEM((2, width, 3 * half), bf16),
            pltpu.SemaphoreType.DMA((2, max(len(s) for s in slots))),
        ],
        compiler_params=params(),
    )(*flat, ha, hb, suv)


def mlp_bwd_kernel(*refs, half, counts):
    total = sum(counts)
    flat, refs = refs[:total], refs[total:]
    slots, at = [], 0
    for n in counts:
        slots.append(flat[at : at + n])
        at += n
    da_ref, db_ref, uv_ref, suv_ref, duv_ref, own_ref, got_ref, gs_ref, acc, wbuf, sems = refs
    rows = da_ref.shape[0]
    q = pl.program_id(0)

    @pl.when(q == 0)
    def _():
        own_ref[...] = jnp.zeros_like(own_ref)
        acc[...] = jnp.zeros_like(acc)

    gs_ref[...] = jnp.zeros_like(gs_ref)
    fetch_weights(q, slots, wbuf, sems)
    w = wbuf.at[lax.rem(q, 2)]
    for base, d_ref, sum_ref in ((0, da_ref, own_ref), (rows, db_ref, acc)):
        at = slice(base, base + rows)
        grad = dot(d_ref[...], w[:, 2 * half : 3 * half])
        up = uv_ref[at, :half].astype(f32)
        gate = uv_ref[at, half:].astype(f32)
        su = suv_ref[0:1, :]
        sv = suv_ref[1:2, :]
        lifted = up * su
        gated = gate * sv
        sigma = jax.nn.sigmoid(gated)
        da = grad * gated * sigma
        db = grad * lifted * sigma * (1.0 + gated * (1.0 - sigma))
        gs_ref[0:1, :] += jnp.sum(da * up, axis=0, keepdims=True)
        gs_ref[1:2, :] += jnp.sum(db * gate, axis=0, keepdims=True)
        duv_ref[at, :half] = (da * su).astype(bf16)
        duv_ref[at, half:] = (db * sv).astype(bf16)
        sum_ref[...] += dot_t(duv_ref[at, :], w[:, : 2 * half])

    @pl.when(q == pl.num_programs(0) - 1)
    def _():
        got_ref[...] = acc[...].astype(bf16)


def mlp_bwd(da, db, slots, uv, suv):
    rows, width = da.shape
    parts, _, half = suv.shape
    take = lambda n: pl.BlockSpec((None, 2 * rows, n), lambda q: (q, 0, 0))
    whole = full_spec((rows, width))
    anywhere = pl.BlockSpec(memory_space=pl.ANY)
    flat = [p for slot in slots for p in slot]
    return pl.pallas_call(
        functools.partial(mlp_bwd_kernel, half=half, counts=[len(s) for s in slots]),
        grid=(parts,),
        in_specs=[anywhere] * len(flat)
        + [
            whole,
            whole,
            take(2 * half),
            pl.BlockSpec((None, 2, half), lambda q: (q, 0, 0)),
        ],
        out_specs=[
            take(2 * half),
            whole,
            whole,
            pl.BlockSpec((None, 8, half), lambda q: (q, 0, 0)),
        ],
        out_shape=[
            jax.ShapeDtypeStruct((parts, 2 * rows, 2 * half), bf16),
            jax.ShapeDtypeStruct((rows, width), f32),
            jax.ShapeDtypeStruct((rows, width), bf16),
            jax.ShapeDtypeStruct((parts, 8, half), f32),
        ],
        scratch_shapes=[
            pltpu.VMEM((rows, width), f32),
            pltpu.VMEM((2, width, 3 * half), bf16),
            pltpu.SemaphoreType.DMA((2, max(len(s) for s in slots))),
        ],
        compiler_params=params(),
    )(*flat, da, db, uv, suv)


EXTRA = 16


def grad_kernel(place_ref, *refs, orders, parts, chunk, more):
    ha_ref, hb_ref = refs[:2]
    refs = refs[2:]
    if more:
        oa_ref, ob_ref, ya_ref, yb_ref, extra_ref = refs[:5]
        refs = refs[5:]
    val_ref, *outs = refs[:5]
    turned = refs[5]
    rows = ha_ref.shape[0]
    k = pl.program_id(0)

    @pl.when(k == 0)
    def _():
        turned[:, :rows] = ha_ref[...].T
        turned[:, rows:] = hb_ref[...].T
        if more:
            refs[6][:, :rows] = oa_ref[...].T
            refs[6][:, rows:] = ob_ref[...].T

    for side in range(2):

        @pl.when((k < parts // 2) == (side == 0))
        def _(side=side):
            for which, ref in zip(orders[side], outs[2 * side : 2 * side + 2]):
                for j, r in enumerate(which):
                    at = slice(r * chunk, (r + 1) * chunk)
                    value = dot(turned[at, :], val_ref[...]).astype(bf16)
                    size = value.shape[1]
                    ref[j, :chunk, :size] = value
                    if more:
                        ref[j, :chunk, size:] = (
                            dot(refs[6][at, :rows], ya_ref[...]) + dot(refs[6][at, rows:], yb_ref[...])
                        ).astype(bf16)
                        ref[j, chunk:, :] = extra_ref[...].astype(bf16)


def weight_grads(place, sends, keeps, chips, hs, value, os=None, ys=None, extra=None):
    rows, width = hs[0].shape
    chunk = width // chips
    parts, _, size = value.shape
    more = os is not None
    hc = ys[1].shape[2] if more else 0
    tall = chunk + (EXTRA if more else 0)
    middle = parts // 2
    if chunk % 128:
        result = []
        for which, lo in ((sends[0], 0), (keeps[0], 0), (sends[1], middle), (keeps[1], middle)):
            cut = lambda pair: jnp.concatenate(
                [jnp.concatenate(pair, axis=0)[:, r * chunk : (r + 1) * chunk] for r in which], axis=1
            )
            found = []
            for k in range(lo, lo + middle):
                one = t_dot(cut(hs), value[k])
                if more:
                    at = (place[0] - k) % parts
                    y = lax.dynamic_index_in_dim(ys[0], at, 0, keepdims=False)
                    y = lax.dynamic_slice_in_dim(y, place[2] * hc, hc, 1)
                    y = jnp.concatenate([y, lax.dynamic_index_in_dim(ys[1], at, 0, keepdims=False)])
                    one = jnp.concatenate([one, t_dot(cut(os), y)], axis=1)
                one = one.reshape(len(which), chunk, size + hc)
                if more:
                    wide = jnp.broadcast_to(extra[k][None], (len(which), EXTRA, size + hc))
                    one = jnp.concatenate([one, wide], axis=1)
                found.append(one.astype(bf16))
            result.append(jnp.stack(found, axis=1))
        return [result[0], result[2]], [result[1], result[3]]
    whole = full_spec((rows, width))
    ins = list(hs)
    in_specs = [whole] * 2
    scratch = [pltpu.VMEM((width, 2 * rows), bf16)]
    if more:
        slot = lambda k, p: lax.rem(p[0] + parts - k, parts)
        ins += [*os, ys[0], ys[1], extra]
        in_specs += [whole] * 2
        in_specs += [
            pl.BlockSpec((None, rows, hc), lambda k, p: (slot(k, p), 0, p[2])),
            pl.BlockSpec((None, rows, hc), lambda k, p: (slot(k, p), 0, 0)),
            pl.BlockSpec((None, EXTRA, size + hc), lambda k, p: (k, 0, 0)),
        ]
        scratch = scratch * 2
    ins.append(value)
    in_specs.append(pl.BlockSpec((None, 2 * rows, size), lambda k, p: (k, 0, 0)))
    lists = [sends[0], keeps[0], sends[1], keeps[1]]
    block = lambda one: (len(one), None, tall, size + hc)
    early = lambda k, p: (0, jnp.minimum(k, middle - 1), 0, 0)
    late = lambda k, p: (0, jnp.maximum(k - middle, 0), 0, 0)
    out = pl.pallas_call(
        functools.partial(
            grad_kernel, orders=(lists[:2], lists[2:]), parts=parts, chunk=chunk, more=more
        ),
        grid_spec=pltpu.PrefetchScalarGridSpec(
            num_scalar_prefetch=1,
            grid=(parts,),
            in_specs=in_specs,
            out_specs=[
                pl.BlockSpec(block(one), early if n < 2 else late) for n, one in enumerate(lists)
            ],
            scratch_shapes=scratch,
        ),
        out_shape=[
            jax.ShapeDtypeStruct((len(one), middle, tall, size + hc), bf16) for one in lists
        ],
        compiler_params=params(),
    )(place, *ins)
    return [out[0], out[2]], [out[1], out[3]]


def adam_values(weight, grad, first, second):
    first_new = beta_one * first + (1.0 - beta_one) * grad
    second_new = beta_two * second + (1.0 - beta_two) * grad * grad
    moved = weight - learn_rate * (first_new / bias_one) / (
        jnp.sqrt(second_new / bias_two) + adam_eps
    )
    return first_new, second_new, moved


def lane_sums(value):
    ones = jnp.ones((8, value.shape[1]), bf16)
    high = value.astype(bf16)
    low = (value - high.astype(f32)).astype(bf16)
    return dot_t(ones, high) + dot_t(ones, low)


def adam_wide_kernel(w_ref, g_ref, m_ref, v_ref, g_out, m_out, v_out, n_out, s_out):
    cols = w_ref.shape[2]
    for c in range(w_ref.shape[1]):
        grad = g_ref[:, c * cols : (c + 1) * cols]
        first, second, moved = adam_values(w_ref[:, c, :], grad, m_ref[:, c, :], v_ref[:, c, :])
        g_out[:, c, :] = grad
        m_out[:, c, :] = first
        v_out[:, c, :] = second
        n_out[:, c, :] = moved
        s_out[c : c + 1, :] = jnp.sum(moved * moved, axis=0, keepdims=True)


def adam_wide(w, g, m, v):
    vmem = pl.BlockSpec(memory_space=pltpu.VMEM)
    return pl.pallas_call(
        adam_wide_kernel,
        in_specs=[vmem] * 4,
        out_specs=[vmem] * 5,
        out_shape=[jax.ShapeDtypeStruct(w.shape, f32)] * 4
        + [jax.ShapeDtypeStruct(w.shape[1:], f32)],
        compiler_params=params(),
    )(w, g, m, v)


def adam_tall_kernel(w_ref, g_ref, m_ref, v_ref, g_out, m_out, v_out, n_out, s_out):
    grad = g_ref[...].T
    first, second, moved = adam_values(w_ref[...], grad, m_ref[...], v_ref[...])
    g_out[...] = grad
    m_out[...] = first
    v_out[...] = second
    n_out[...] = moved
    s_out[...] = lane_sums(moved * moved)


def adam_tall(w, g, m, v):
    vmem = pl.BlockSpec(memory_space=pltpu.VMEM)
    return pl.pallas_call(
        adam_tall_kernel,
        in_specs=[vmem] * 4,
        out_specs=[vmem] * 5,
        out_shape=[jax.ShapeDtypeStruct(w.shape, f32)] * 4
        + [jax.ShapeDtypeStruct((8, w.shape[0]), f32)],
        compiler_params=params(),
    )(w, g, m, v)


def scale_kernel(na_ref, nb_ref, nc_ref, nd_ref, a_ref, b_ref, c_ref, d_ref, ao_ref, bo_ref, co_ref, do_ref, *, width):
    factor = lambda value: lax.rsqrt(value / width + layer_eps)
    for norm, ref, out in ((na_ref, a_ref, ao_ref), (nc_ref, c_ref, co_ref)):
        for c in range(ref.shape[1]):
            out[:, c, :] = ref[:, c, :] * factor(norm[c : c + 1, :])
    for norm, ref, out in ((nb_ref, b_ref, bo_ref), (nd_ref, d_ref, do_ref)):
        out[...] = ref[...] * factor(norm[...]).T[:, 0:1]


def scale_weights(norms, weights, width):
    vmem = pl.BlockSpec(memory_space=pltpu.VMEM)
    return pl.pallas_call(
        functools.partial(scale_kernel, width=width),
        in_specs=[vmem] * 8,
        out_specs=[vmem] * 4,
        out_shape=[jax.ShapeDtypeStruct(w.shape, f32) for w in weights],
        compiler_params=params(),
    )(*norms, *weights)


def after(value, *others):
    return lax.optimization_barrier((value, *others))[0]


def per_device(
    layer_input,
    cotangent,
    positions,
    w_qkv,
    w_out,
    w_up,
    w_down,
    moment_qkv,
    moment_out,
    moment_up,
    moment_down,
    square_qkv,
    square_out,
    square_up,
    square_down,
    s_qk,
    alpha_attn,
    alpha_mlp,
    s_uv,
):
    nz = lax.axis_size("head")
    nb = lax.axis_size("batch")
    z = lax.axis_index("head")
    b = lax.axis_index("batch")
    core = b % 2
    chip = b // 2
    chips = nb // 2
    bits = [1 << n for n in range(int(math.log2(chips)))]
    rows, cols = layer_input.shape
    width = cols * nz
    own = rows // nz
    hid = w_down.shape[0]
    half = hid // 2
    hc = cols // 2
    heads = cols // HEAD_DIM
    span = w_qkv.shape[0]
    chunk = width // chips
    core_s = core.reshape(1).astype(jnp.int32)
    place = jnp.stack([z, chip, core]).astype(jnp.int32)
    fast = chunk == cols and chunk % 128 == 0

    def swap_batch(value, bit):
        return lax.ppermute(value, "batch", [(i, i ^ bit) for i in range(nb)])

    def swap_core(value):
        return swap_batch(value, 1)

    def swap_chip(value, bit):
        return swap_batch(value, 2 * bit)

    def onward(value, k=1):
        return lax.ppermute(value, "head", [(i, (i + k) % nz) for i in range(nz)])

    def exchange(value):
        return lax.all_to_all(value, "head", split_axis=0, concat_axis=0)

    def pick(pair, index):
        return jnp.where(index == 0, pair[0], pair[1])

    def relative(value):
        return jnp.concatenate(
            [
                lax.dynamic_slice_in_dim(value, (chip ^ r) * chunk, chunk, value.ndim - 1)
                for r in range(chips)
            ],
            axis=-1,
        )

    def spread(value):
        if chips <= 4:
            return [value] + [swap_chip(value, r) for r in range(1, chips)]
        for bit in bits:
            value = jnp.concatenate([value, swap_chip(value, bit)], axis=0)
        return [value]

    tokens = [layer_input, onward(layer_input)]
    mine, theirs, qkv_own = pack(core_s, w_up, w_down, w_out, w_qkv)
    qkv_full = lax.all_gather(qkv_own, "batch", axis=0, tiled=True)
    theirs = swap_core(theirs)
    packet = jnp.concatenate([pick((mine, theirs), core), pick((theirs, mine), core)], axis=0)
    tokens[1], packet, places, s_uv, alpha_attn, alpha_mlp = lax.optimization_barrier(
        (tokens[1], packet, positions, s_uv, alpha_attn, alpha_mlp)
    )

    suv_own = pick((s_uv[:, :half], s_uv[:, half:]), core)
    freqs = jnp.exp(
        (jnp.arange(128) % (HEAD_DIM // 2)).astype(f32) * (-2.0 * math.log(10000.0) / HEAD_DIM)
    )
    phase = places.astype(f32)[:, None] * freqs[None, :]
    side = jnp.where(jnp.arange(128) % HEAD_DIM < HEAD_DIM // 2, -1.0, 1.0).astype(f32)
    cosine, sine = jnp.cos(phase), jnp.sin(phase) * side[None, :]
    lane = jnp.arange(cols) // HEAD_DIM
    ones = (lane[:, None] == lane[None, :]).astype(bf16)
    gain = s_qk.reshape(1, cols)
    is_long = (places[SHORT : SHORT + 1] != 0).astype(jnp.int32)
    attn_gain = relative(alpha_attn[None])
    mlp_gain = relative(alpha_mlp[None])

    suv = jnp.stack([suv_own] + [onward(suv_own, n) for n in range(1, nz)])
    hops = [packet]
    slots = [spread(packet)]
    for n in range(2, nz):
        tokens.append(onward(tokens[-1]))
        hops.append(onward(hops[-1]))
        tokens[-1], hops[-1], cosine, sine, ones, attn_gain, mlp_gain, suv, *last = lax.optimization_barrier(
            (tokens[-1], hops[-1], cosine, sine, ones, attn_gain, mlp_gain, suv, *slots[-1])
        )
        slots[-1] = list(last)
        slots.append(spread(hops[-1]))
    hops.append(onward(hops[-1]))

    blocks = rows // 512
    middle = blocks // 2
    tokens_full, q, k, v, rho = qkv_project(place, tokens, qkv_full, cosine, sine, gain, ones)
    y_a, logs_a = attn_fwd(is_long, q, k, v, 0, middle)
    q_b, hops[-1] = lax.optimization_barrier((after(q, y_a), hops[-1]))
    y_b, logs_b = attn_fwd(is_long, q_b, k, v, middle, blocks - middle)
    y_one = exchange(y_a.reshape(nz, own // 2, cols))
    y_in, y_one = lax.optimization_barrier((y_b, y_one))
    y_two = exchange(y_in.reshape(nz, own // 2, cols))
    hop = after(hops[-1], y_b)
    slots.append(spread(hop))
    flat = lambda value: value.transpose(1, 0, 2).reshape(own, width)
    start = tokens_full
    if not fast:
        start = jnp.concatenate(
            [
                lax.dynamic_slice_in_dim(tokens_full, h * (rows // 2) + z * (own // 2), own // 2, 0)
                for h in range(2)
            ]
        )
        start = relative(start)
    hA, h1, h_own, stat = attn_out(place, y_one, y_two, slots, start, attn_gain, chips, fast)
    h_got = swap_core(h_own)
    cot = after(cotangent, h_own).reshape(2, nz, own // 2, cols).transpose(1, 0, 2, 3)
    cot = exchange(cot.reshape(nz, own, cols))

    act, uv, mo_own, mo_other = mlp_fwd(h_own, h_got, slots, suv)
    mo_got = swap_core(mo_other)
    if not fast:
        cot = relative(flat(cot))
    hidden, d_own, base, ga_mlp = loss(place, mo_own, mo_got, h1, cot, mlp_gain, chips, fast)
    d_got = swap_core(d_own)
    if not fast:
        hidden = relative(hidden).reshape(own, nz, cols).transpose(1, 0, 2)
    hidden = exchange(hidden)

    orders = [bits, bits[::-1]]
    sent_at = [[r for r in range(chips) if r & order[0]] for order in orders]
    kept_at = [[r for r in range(chips) if not r & order[0]] for order in orders]

    def second(kept, sent):
        found, sends = [], []
        for order, left, got, keep in zip(orders, kept_at, sent, kept):
            for bit in order[1:]:
                send_at = [n for n, r in enumerate(left) if r & bit]
                keep_at = [n for n, r in enumerate(left) if not r & bit]
                left = [left[n] for n in keep_at]
                cut = lambda v, at: jnp.concatenate([v[n : n + 1] for n in at], axis=0).astype(f32)
                send = (cut(keep, send_at) + cut(got, send_at)).astype(bf16)
                keep = cut(keep, keep_at) + cut(got, keep_at)
                got = swap_chip(send, bit)
                sends.append(send)
            found.append((keep, got))
        return found, sends

    def slot_sums(found):
        return [(keep[0, n] + got[0, n].astype(f32)) for keep, got in found for n in range(nz // 2)]

    down_made, down_kept = weight_grads(place, sent_at, kept_at, chips, (d_own, d_got), act)
    down_sent = [swap_chip(one, order[0]) for one, order in zip(down_made, orders)]
    d_own, d_got, *_ = lax.optimization_barrier((d_own, d_got, *down_made))
    duv, dh_own, dh_other, gsuv = mlp_bwd(d_own, d_got, slots, uv, suv)
    dh_got = swap_core(dh_other)
    dh_own, hidden, *down_sent = lax.optimization_barrier((dh_own, hidden, *down_sent))
    do_own, through, ga_attn, dy_a, dy_b = first_back(
        place, dh_own, dh_got, base, h1, hA, start, stat, attn_gain, slots, chips, fast, cols
    )
    dy_b = exchange(dy_b)
    do_got = swap_core(do_own)
    y_mine = jnp.concatenate([y_one, y_two], axis=1)
    y_got = swap_core(lax.dynamic_slice_in_dim(after(y_mine, h_own), (1 - core) * hc, hc, 2))
    down_sent = [after(one, do_own) for one in down_sent]
    down_part, down_next = second(down_kept, down_sent)

    alphas = [relative(ga_attn[0:1]), relative(ga_mlp[0:1])]
    extra = []
    wide = 2 * half + hc
    fill = lambda r: jnp.pad(r, ((0, 0), (0, wide - r.shape[1])))
    for n in range(nz):
        at = ((z - n) % nz) * cols
        line = jnp.concatenate([lax.dynamic_slice_in_dim(g, at, cols, 1) for g in alphas], axis=1)
        first = gsuv[n, :2].reshape(1, 2 * half)
        extra.append(jnp.pad(jnp.concatenate([fill(first), fill(line)]), ((0, EXTRA - 2), (0, 0))))
    extra = jnp.stack(extra)
    h_own, *_ = lax.optimization_barrier((h_own, *down_next))
    up_made, up_kept = weight_grads(
        place, sent_at, kept_at, chips, (h_own, h_got), duv, (do_own, do_got), (y_mine, y_got), extra
    )
    dy_b, dy_a, *up_made = lax.optimization_barrier((dy_b, dy_a, *up_made))
    up_sent = [swap_chip(one, order[0]) for one, order in zip(up_made, orders)]

    dy_a = exchange(dy_a)
    common = lambda dy, y, logs: (
        is_long, q, k, v, dy.reshape(y.shape), y, logs, rho, cosine, sine, gain, ones
    )
    dqkv_b, dk_part, dv_part, sqk_b = attn_bwd(
        *common(dy_b, y_b, logs_b), middle, blocks - middle, None
    )

    if not fast:
        through = relative(through)
    through = through.astype(f32)

    def input_part(dqkv, side):
        part = dot_t(dqkv, qkv_full)
        mine_at = z * (own // 2)
        here = lax.dynamic_slice_in_dim(part, mine_at, own // 2, 0)
        here = here + through[side * (own // 2) : (side + 1) * (own // 2)]
        return lax.dynamic_update_slice_in_dim(part.astype(bf16), here.astype(bf16), mine_at, 0)

    dqkv_b, dk_part, dy_a = lax.optimization_barrier((dqkv_b, dk_part, dy_a))
    part_b = input_part(dqkv_b, 1)
    cut = lambda n: lax.dynamic_slice_in_dim(part_b, ((z + n) % nz) * cols, cols, 1)
    part_cuts = [cut(n) for n in range(nz)]
    down_part = [(keep, after(got, dqkv_b)) for keep, got in down_part]
    down_slots = slot_sums(down_part)
    up_part, up_next = second(up_kept, [after(one, dqkv_b) for one in up_sent])
    part_got = [onward(part_cuts[n], n) for n in range(1, nz)]
    dk_part, dy_a, *_ = lax.optimization_barrier((dk_part, dy_a, *up_next, *part_cuts, *down_slots))
    dqkv_a, sqk_a = attn_bwd(*common(dy_a, y_a, logs_a), 0, middle, [dk_part, dv_part])
    part_got = [after(one, dqkv_a) for one in part_got]
    input_b = part_cuts[0].astype(f32) + sum(one.astype(f32) for one in part_got)
    up_part = [(keep, after(got, dqkv_a)) for keep, got in up_part]
    input_a = lax.psum_scatter(input_part(dqkv_a, 0), "head", scatter_dimension=1, tiled=True)
    down_along = [onward(after(down_slots[n].astype(bf16), input_b), nz - n) for n in range(1, nz)]
    sum_down_t = down_slots[0] + sum(one.astype(f32) for one in down_along)
    up_slots = slot_sums(up_part)
    passed = onward(up_slots[1].astype(bf16))
    for n in range(2, nz):
        passed = onward((up_slots[n] + passed.astype(f32)).astype(bf16))
    sum_up_t = up_slots[0] + passed.astype(f32)
    input_grad = jnp.concatenate([input_a.astype(f32), input_b], axis=0)
    hidden_t = hidden.reshape(nz, 2, own // 2, cols).transpose(1, 0, 2, 3).reshape(rows, cols)

    dqkv = jnp.concatenate([dqkv_a, dqkv_b], axis=0)
    grad_qkv = t_dot(tokens_full, dqkv).astype(bf16)
    sqk = jnp.pad((sqk_a + sqk_b), ((0, EXTRA - 8), (0, 2 * cols)))
    shard = [lax.dynamic_slice_in_dim(grad_qkv, (b ^ r) * span, span, 0) for r in range(nb)]
    shard = [jnp.concatenate([s, sqk.astype(bf16)], axis=0) for s in shard]
    qbits = [1 << n for n in range(int(math.log2(nb)))]
    held = {r: shard[r] for r in range(nb)}
    for bit in qbits:
        send_at = [r for r in held if r & bit]
        send = jnp.concatenate([held[r] for r in send_at], axis=0).astype(bf16)
        got = swap_batch(send, bit)
        size = span + EXTRA
        held = {
            r ^ bit: held[r ^ bit].astype(f32) + got[n * size : (n + 1) * size].astype(f32)
            for n, r in enumerate(send_at)
        }
    cell = width // (nz * nb)
    sum_sqk = lax.dynamic_slice_in_dim(held[0][span, :cols], b * cell, cell, 0)
    qkv_new = adam_wide(w_qkv, held[0][:span], moment_qkv, square_qkv)

    def both_halves(total):
        two = (total[:span], total[span : 2 * span])
        here = jnp.concatenate([pick(two, core), total[2 * span :]], axis=0)
        there = jnp.concatenate([pick(two, 1 - core), total[2 * span :]], axis=0)
        there = swap_core(there.astype(bf16)).astype(f32)
        return [pick((here, there), core), pick((there, here), core)]

    join = lambda halves, at, size: [p[:span, at : at + size] for p in halves]
    halves = both_halves(sum_down_t)
    down_new = adam_tall(w_down, jnp.concatenate(join(halves, 0, half), axis=1), moment_down, square_down)
    halves = both_halves(sum_up_t)
    grad_up = jnp.concatenate(join(halves, 0, half) + join(halves, half, half), axis=1)
    up_new = adam_wide(w_up, grad_up, moment_up, square_up)
    out_new = adam_tall(w_out, jnp.concatenate(join(halves, 2 * half, hc), axis=1), moment_out, square_out)
    suv_rows = jnp.stack(
        [jnp.concatenate([p[span, c * half : (c + 1) * half] for p in halves]) for c in range(2)]
    )
    sum_suv = lax.dynamic_slice_in_dim(suv_rows, b * (hid // nb), hid // nb, 1)
    alphas = halves[0][span + 1] + halves[1][span + 1]
    sum_attn = lax.dynamic_slice_in_dim(alphas[:cols], b * cell, cell, 0)
    sum_mlp = lax.dynamic_slice_in_dim(alphas[cols : 2 * cols], b * cell, cell, 0)

    hidden = hidden_t.astype(f32)

    squares = [qkv_new[4], out_new[4][:1], up_new[4], down_new[4][:1]]
    sizes = [t.size for t in squares]
    norms = jnp.concatenate([t.reshape(-1) for t in squares]).reshape(-1, 128)
    for bit in qbits:
        norms = norms + swap_batch(norms, bit)
    norms = norms.reshape(-1)
    ends = [0] + [sum(sizes[: n + 1]) for n in range(4)]
    back = lambda n, shape: norms[ends[n] : ends[n + 1]].reshape(shape)
    eight = lambda value: jnp.broadcast_to(value, (8, value.shape[1]))
    new_qkv, new_out, new_up, new_down = scale_weights(
        [back(0, (3, cols)), eight(back(1, (1, cols))), back(2, (2, hid)), eight(back(3, (1, hid)))],
        [qkv_new[3], out_new[3], up_new[3], down_new[3]],
        width,
    )
    sum_qkv, first_a, second_a = qkv_new[:3]
    sum_out, first_b, second_b = out_new[:3]
    sum_up, first_c, second_c = up_new[:3]
    sum_down, first_d, second_d = down_new[:3]
    return (
        hidden,
        input_grad,
        sum_qkv,
        sum_out,
        sum_up,
        sum_down,
        first_a,
        first_b,
        first_c,
        first_d,
        second_a,
        second_b,
        second_c,
        second_d,
        new_qkv,
        new_out,
        new_up,
        new_down,
        sum_sqk,
        sum_attn,
        sum_mlp,
        sum_suv,
    )


def solution(mesh):
    tokens = P("batch", "head")
    wide = P("batch", None, "head")
    tall = P("head", "batch")
    flat = P(("head", "batch"))
    weights = (wide, tall, wide, tall)
    return jax.shard_map(
        per_device,
        mesh=mesh,
        in_specs=(tokens, tokens, P("batch"))
        + weights * 3
        + (P("head"), P(), P(), P(None, "head")),
        out_specs=(tokens, tokens) + weights * 4 + (flat, flat, flat, P(None, ("head", "batch"))),
        check_vma=False,
    )
```

time: 755 us -> 666 us (0.88)
  local copies, waits for them, and re-layouts: 85.6 us -> 43.1 us
  Pallas kernels: 203 us -> 182 us
  other arithmetic: 66.4 us -> 52.2 us
  starting transfers between devices: 119 us -> 105 us
  waiting for transfers between devices: 236 us -> 248 us
  between operations: 25.6 us -> 16.4 us
    ppermute x33 -> x18, starting transfers between devices: 78.9 us -> 41.5 us  [onward(): return lax.ppermute(value, 'head', [(i, (i + k) % nz) for i in range(nz)])]
    ppermute x39 -> x35, waiting for transfers between devices: 63.8 us -> 98 us  [swap_batch(): return lax.ppermute(value, 'batch', [(i, i ^ bit) for i in range(nb)])]
    all_to_all x0 -> x6, starting transfers between devices: none -> 27.8 us  [exchange(): return lax.all_to_all(value, 'head', split_axis=0, concat_axis=0)]
    ppermute x33 -> x18, waiting for transfers between devices: 172 us -> 146 us  [onward(): return lax.ppermute(value, 'head', [(i, (i + k) % nz) for i in range(nz)])]
    unnamed x196 -> x130, local copies, waits for them, and re-layouts: 48.8 us -> 24.1 us
    pallas_call x2, Pallas kernels: 45.8 us -> 33 us  [attn_bwd(): pl.pallas_call(inner, grid_spec=pltpu.PrefetchScalarGridSpec(num_scalar_p...]
    slice x16 -> x10, local copies, waits for them, and re-layouts: 15.6 us -> 3.46 us  [the longest x2 2.05 us: per_device(): squares = [qkv_new[4], out_new[4][:1], up_new[4], down_new[4][:1]]]
    add x6 -> x10, other arithmetic: 11.8 us -> 23 us  [the longest x4 13.1 us: second(): keep = cut(keep, keep_at) + cut(got, keep_at)]
  transfers between devices with their start and end apart: 76 -> 61, of which waited for: 32 -> 14; matrix products, arithmetic and copies ran while one was open for 19% -> 14% of each run, Pallas kernels for 25% -> 25%
where the time goes in v2:
time: 666 us; the launch traced here: 657 us
  waiting for transfers between devices  248 us (37%)
  Pallas kernels  182 us (27%)
  starting transfers between devices  105 us (16%)
  other arithmetic  52.2 us (8%)
  local copies, waits for them, and re-layouts  43.1 us (6%)
  between operations  16.4 us (2%)
  matrix products  10.4 us (2%)
    ppermute x18, waiting for transfers between devices, onward(): return lax.ppermute(value, 'head', [(i, (i + k) % nz) for i in range(nz)])  146 us
    ppermute x35, waiting for transfers between devices, swap_batch(): return lax.ppermute(value, 'batch', [(i, i ^ bit) for i in range(nb)])  98 us
    ppermute x18, starting transfers between devices, onward(): return lax.ppermute(value, 'head', [(i, (i + k) % nz) for i in range(nz)])  41.5 us
    ppermute x35, starting transfers between devices, swap_batch(): return lax.ppermute(value, 'batch', [(i, i ^ bit) for i in range(nb)])  35.2 us
    pallas_call x2, Pallas kernels, attn_bwd(): pl.pallas_call(inner, grid_spec=pltpu.PrefetchScalarGridSpec(num_scalar_p...  33 us
    pallas_call x2, Pallas kernels, weight_grads(): pl.pallas_call(functools.partial(grad_kernel, orders=(lists[:2], lists[2:...  29.3 us
    all_to_all x6, starting transfers between devices, exchange(): return lax.all_to_all(value, 'head', split_axis=0, concat_axis=0)  27.8 us
    pallas_call x1, Pallas kernels, mlp_bwd(): pl.pallas_call(functools.partial(mlp_bwd_kernel, half=half, counts=[len(s...  26.2 us
  transfers between devices with their start and end apart: 61, of which 14 were waited for; matrix products, arithmetic and copies ran while one was open for 14% of the time, Pallas kernels for 25%

profile of v2, /device:TPU:0, one launch (start us, length us, event | category | flops | bytes accessed | tf_op | source)
XLA Modules:
  0.0 656.6 jit_solution(9739271049405049249)
XLA Ops:
  9.4 5.0 shard_map.354
  19.6 23.9 %collective-permute-done.refs_1_ = bf16[2048,256]{1,0:T(8,128)(2,1)} collective-permute-done((bf16[2048,256]{1,0:T(8,128)(2,1)S(1)}, bf16[2048,256]{1,0:T(8,128)(2,1)}, u32[]{:S(2)}, u32[]{:S(2)}) %collective-permute-start) | collective-permute-done | bytes 1048608 | tf_op jit(solution)/shard_map/ppermute | solution.py:1019
  54.8 5.5 fusion.16
  61.0 32.4 %collective-permute-done.3.refs_4_ = bf16[256,1792]{1,0:T(8,128)(2,1)S(1)} collective-permute-done((bf16[256,1792]{1,0:T(8,128)(2,1)S(1)}, bf16[256,1792]{1,0:T(8,128)(2,1)S(1)}, u32[]{:S(2)}, u32[]{:S(2)}) %collective-permute-start.3) | collective-permute-done | bytes 917536 | tf_op jit(solution)/shard_map/ppermute | solution.py:1019
  98.4 40.1 %collective-permute-done.11.refs_8_ = bf16[256,1792]{1,0:T(8,128)(2,1)} collective-permute-done((bf16[256,1792]{1,0:T(8,128)(2,1)S(1)}, bf16[256,1792]{1,0:T(8,128)(2,1)}, u32[]{:S(2)}, u32[]{:S(2)}) %collective-permute-start.11) | collective-permute-done | bytes 917536 | tf_op jit(solution)/shard_map/ppermute | solution.py:1019
  143.4 11.6 %shard_map.355 = (bf16[2048,1024]{1,0:T(8,128)(2,1)}, bf16[2048,256]{1,0:T(8,128)(2,1)}, bf16[2048,256]{1,0:T(8,128)(2,1)}, bf16[2048,256]{1,0:T(8,128)(2,1)}, f32[2048,128]{1,0:T(8,128)}) custom-call(s32[3]{0:T(128)} %pad_add_fusion.place_ref, bf16[2048,256]{1,0:T(8,128)(2,1)} %refs_0_.1, bf16[2048,256]{1,0:T(8,128)(2,1)} %collective-permute-done.refs_1_, ...), custom_call_target="tpu_custom_call" | custom-call | tf_op jit(solution)/shard_map/pallas_call | solution.py:103
  155.0 6.4 shard_map.356
  167.4 6.8 %shard_map.357 = (bf16[1024,256]{1,0:T(8,128)(2,1)}, f32[1024,128]{1,0:T(8,128)}) custom-call(s32[1]{0:T(128)S(6)} %convert_element_type.267.long_ref.r_0_, bf16[2048,256]{1,0:T(8,128)(2,1)} %get-tuple-element.197.q_ref.r_1_, bf16[2048,256]{1,0:T(8,128)(2,1)} %get-tuple-element.192.k_ref.r_2_.r_6_, bf16[2048,256]{1,0:T(8,128)(2,1)} %get-tuple-element.193.v_ref.r_7_), custom_call_target="tpu_custom_call" | custom-call | tf_op jit(solution)/shard_map/pallas_call | solution.py:194
  174.2 7.9 %collective-permute-start.19 = (bf16[256,1792]{1,0:T(8,128)(2,1)}, bf16[256,1792]{1,0:T(8,128)(2,1)S(1)}, u32[]{:S(2)}, u32[]{:S(2)}) collective-permute-start(bf16[256,1792]{1,0:T(8,128)(2,1)} %collective-permute-done.18.refs_12_), channel_id=1, source_target_pairs={{0,2},{1,3},{2,0},{3,1},{4,6},{5,7},{6,4},{7,5},{8,10},{9,11},{10,... | collective-permute-start | bytes 2752520 | tf_op jit(solution)/shard_map/ppermute | solution.py:1010
  183.6 5.1 all-to-all-start.1
  188.7 37.6 %collective-permute-done.16.refs_10_ = bf16[256,1792]{1,0:T(8,128)(2,1)S(1)} collective-permute-done((bf16[256,1792]{1,0:T(8,128)(2,1)}, bf16[256,1792]{1,0:T(8,128)(2,1)S(1)}, u32[]{:S(2)}, u32[]{:S(2)}) %collective-permute-start.16) | collective-permute-done | bytes 917536 | tf_op jit(solution)/shard_map/ppermute | solution.py:1010
  226.3 17.4 %collective-permute-done.20.refs_14_ = bf16[256,1792]{1,0:T(8,128)(2,1)} collective-permute-done((bf16[256,1792]{1,0:T(8,128)(2,1)}, bf16[256,1792]{1,0:T(8,128)(2,1)}, u32[]{:S(2)}, u32[]{:S(2)}) %collective-permute-start.20) | collective-permute-done | bytes 917536 | tf_op jit(solution)/shard_map/ppermute | solution.py:1010
  243.8 6.7 %shard_map.358 = (f32[512,1024]{1,0:T(8,128)}, f32[512,1024]{1,0:T(8,128)}, bf16[512,1024]{1,0:T(8,128)(2,1)}, f32[512,128]{1,0:T(8,128)}) custom-call(s32[3]{0:T(128)} %pad_add_fusion.place_ref, bf16[256,1792]{1,0:T(8,128)(2,1)} %copy-done, bf16[256,1792]{1,0:T(8,128)(2,1)} %copy-done.3, bf16[256,1792]{1,0:T(8,128)(2,1)} %copy-done.4, ...), custom_call_target="tpu_custom_call" | custom-call | tf_op jit(solution)/shard_map/pallas_call | solution.py:477
  251.6 4.8 all-to-all-start.2
  257.4 21.1 %shard_map.359 = (bf16[4,1024,512]{2,1,0:T(8,128)(2,1)}, bf16[4,1024,1024]{2,1,0:T(8,128)(2,1)}, f32[512,1024]{1,0:T(8,128)}, bf16[512,1024]{1,0:T(8,128)(2,1)}) custom-call(bf16[256,1792]{1,0:T(8,128)(2,1)} %copy-done, bf16[256,1792]{1,0:T(8,128)(2,1)} %copy-done.3, bf16[256,1792]{1,0:T(8,128)(2,1)} %copy-done.4, bf16[256,1792]{1,0:T(8,128)(2,1)} %copy-done.5, ...), custom_call_target="tpu_custom_call" | custom-call | tf_op jit(solution)/shard_map/pallas_call | solution.py:670
  284.2 6.4 shard_map.360
  295.3 9.9 %shard_map.361 = (bf16[2,2,256,512]{3,2,1,0:T(8,128)(2,1)}, bf16[2,2,256,512]{3,2,1,0:T(8,128)(2,1)}, bf16[2,2,256,512]{3,2,1,0:T(8,128)(2,1)}, bf16[2,2,256,512]{3,2,1,0:T(8,128)(2,1)}) custom-call(s32[3]{0:T(128)} %pad_add_fusion.place_ref, bf16[512,1024]{1,0:T(8,128)(2,1)} %get-tuple-element.215.refs_0_.refs_16_, bf16[512,1024]{1,0:T(8,128)(2,1)} %copy-done.22, ...), custom_call_target="tpu_custom_call" | custom-call | tf_op jit(solution)/shard_map/pallas_call | solution.py:860
  307.3 26.2 %shard_map.362 = (bf16[4,1024,1024]{2,1,0:T(8,128)(2,1)}, f32[512,1024]{1,0:T(8,128)}, bf16[512,1024]{1,0:T(8,128)(2,1)}, f32[4,8,512]{2,1,0:T(8,128)}) custom-call(bf16[256,1792]{1,0:T(8,128)(2,1)} %copy-done, bf16[256,1792]{1,0:T(8,128)(2,1)} %copy-done.3, bf16[256,1792]{1,0:T(8,128)(2,1)} %copy-done.4, bf16[256,1792]{1,0:T(8,128)(2,1)} %copy-done.5, ...), custom_call_target="tpu_custom_call" | custom-call | tf_op jit(solution)/shard_map/pallas_call | solution.py:740
  337.9 11.1 %shard_map.363 = (bf16[512,1024]{1,0:T(8,128)(2,1)}, bf16[512,1024]{1,0:T(8,128)(2,1)}, f32[8,1024]{1,0:T(8,128)}, bf16[4,256,256]{2,1,0:T(8,128)(2,1)}, bf16[4,256,256]{2,1,0:T(8,128)(2,1)}) custom-call(s32[3]{0:T(128)} %pad_add_fusion.place_ref, bf16[256,1792]{1,0:T(8,128)(2,1)} %copy-done, bf16[256,1792]{1,0:T(8,128)(2,1)} %copy-done.3, ...), custom_call_target="tpu_custom_call" | custom-call | tf_op jit(solution)/shard_map/pallas_call | solution.py:583
  350.1 5.5 all-to-all-start.4
  363.2 19.3 %shard_map.364 = (bf16[2,2,272,1152]{3,2,1,0:T(8,128)(2,1)}, bf16[2,2,272,1152]{3,2,1,0:T(8,128)(2,1)}, bf16[2,2,272,1152]{3,2,1,0:T(8,128)(2,1)}, bf16[2,2,272,1152]{3,2,1,0:T(8,128)(2,1)}) custom-call(s32[3]{0:T(128)} %pad_add_fusion.place_ref, bf16[512,1024]{1,0:T(8,128)(2,1)} %get-tuple-element.235.refs_16_.refs_0_, bf16[512,1024]{1,0:T(8,128)(2,1)} %copy-done.17, ...), custom_call_target="tpu_custom_call" | custom-call | tf_op jit(solution)/shard_map/pallas_call | solution.py:860
  384.6 5.1 all-to-all-start.5
  397.6 16.6 %shard_map.365 = (bf16[1024,768]{1,0:T(8,128)(2,1)}, f32[1024,256]{1,0:T(8,128)}, f32[1024,256]{1,0:T(8,128)}, f32[8,256]{1,0:T(8,128)}) custom-call(s32[1]{0:T(128)S(6)} %convert_element_type.267.long_ref.r_0_, bf16[2048,256]{1,0:T(8,128)(2,1)} %get-tuple-element.197.q_ref.r_1_, bf16[2048,256]{1,0:T(8,128)(2,1)} %get-tuple-element.192.k_ref.r_2_.r_6_, ...), custom_call_target="tpu_custom_call" | custom-call | tf_op jit(solution)/shard_map/pallas_call | solution.py:341
  414.3 37.0 %collective-permute-done.33 = bf16[1,2,256,512]{3,2,1,0:T(8,128)(2,1)} collective-permute-done((bf16[1,2,256,512]{3,2,1,0:T(8,128)(2,1)}, bf16[1,2,256,512]{3,2,1,0:T(8,128)(2,1)}, u32[]{:S(2)}, u32[]{:S(2)}) %collective-permute-start.33) | collective-permute-done | bytes 524320 | tf_op jit(solution)/shard_map/ppermute | solution.py:1010
  467.7 4.2 convert_add_fusion
  477.8 16.4 %shard_map.366 = (bf16[1024,768]{1,0:T(8,128)(2,1)}, f32[8,256]{1,0:T(8,128)}) custom-call(s32[1]{0:T(128)S(6)} %convert_element_type.267.long_ref.r_0_, bf16[2048,256]{1,0:T(8,128)(2,1)} %get-tuple-element.197.q_ref.r_1_, bf16[2048,256]{1,0:T(8,128)(2,1)} %get-tuple-element.192.k_ref.r_2_.r_6_, bf16[1024,256]{1,0:T(8,128)(2,1)} %bitcast.33.r_3_, ...), custom_call_target="tpu_custom_call" | custom-call | tf_op jit(solution)/shard_map/pallas_call | solution.py:341
  501.0 11.7 %collective-permute-start.46 = (bf16[256,512]{1,0:T(8,128)(2,1)}, bf16[256,512]{1,0:T(8,128)(2,1)}, u32[]{:S(2)}, u32[]{:S(2)}) collective-permute-start(bf16[256,512]{1,0:T(8,128)(2,1)} %fusion.24), channel_id=1, source_target_pairs={{0,24},{8,0},{16,8},{24,16},{1,25},{9,1},{17,9},{25,17},{2,26},{10... | collective-permute-start | bytes 786440 | tf_op jit(solution)/shard_map/ppermute | solution.py:1019
  530.7 18.8 %collective-permute-done.42 = bf16[272,1152]{1,0:T(8,128)(2,1)} collective-permute-done((bf16[272,1152]{1,0:T(8,128)(2,1)}, bf16[272,1152]{1,0:T(8,128)(2,1)}, u32[]{:S(2)}, u32[]{:S(2)}) %collective-permute-start.42) | collective-permute-done | bytes 626720 | tf_op jit(solution)/shard_map/ppermute | solution.py:1019
  551.4 5.3 collective-permute-start.43
  563.5 27.0 %collective-permute-done.43 = bf16[272,1152]{1,0:T(8,128)(2,1)S(1)} collective-permute-done((bf16[272,1152]{1,0:T(8,128)(2,1)S(1)}, bf16[272,1152]{1,0:T(8,128)(2,1)S(1)}, u32[]{:S(2)}, u32[]{:S(2)}) %collective-permute-start.43) | collective-permute-done | bytes 626720 | tf_op jit(solution)/shard_map/ppermute | solution.py:1019
  592.6 4.8 collective-permute-start.44
  620.1 5.7 shard_map.369
  (352 shorter events, 176.9 us)
Async XLA Ops:
  7.2 136.2 %all-gather.2.cloned.1.call-start = ((), (), s32[]{:S(2)}) async-start(), calls=%async_computation.7 | async-start | bytes 1769472 | tf_op jit(solution)/shard_map/all_gather | solution.py:1045
  47.4 46.1 %collective-permute-start.2 = (bf16[2048,256]{1,0:T(8,128)(2,1)}, bf16[2048,256]{1,0:T(8,128)(2,1)S(1)}, u32[]{:S(2)}, u32[]{:S(2)}) collective-permute-start(bf16[2048,256]{1,0:T(8,128)(2,1)} %collective-permute-done.refs_1_), channel_id=1, source_target_pairs={{0,8},{8,16},{16,24},{24,0},{1,9},{9,17},{17,25},{25,1},{2,10},{10... | collective-permute-start | bytes 3145736 | tf_op jit(solution)/shard_map/ppermute | solution.py:1019
  48.0 45.5 %collective-permute-start.3 = (bf16[256,1792]{1,0:T(8,128)(2,1)S(1)}, bf16[256,1792]{1,0:T(8,128)(2,1)S(1)}, u32[]{:S(2)}, u32[]{:S(2)}) collective-permute-start(bf16[256,1792]{1,0:T(8,128)(2,1)S(1)} %pad_maximum_fusion.2.refs_0_), channel_id=1, source_target_pairs={{0,8},{8,16},{16,24},{24,0},{1,9},{9,17},{17,25},{25,1},{2,10},{10... | collective-permute-start | bytes 2752520 | tf_op jit(solution)/shard_map/ppermute | solution.py:1019
  50.7 42.7 %collective-permute-start.7 = (bf16[256,1792]{1,0:T(8,128)(2,1)S(1)}, bf16[256,1792]{1,0:T(8,128)(2,1)S(1)}, u32[]{:S(2)}, u32[]{:S(2)}) collective-permute-start(bf16[256,1792]{1,0:T(8,128)(2,1)S(1)} %pad_maximum_fusion.2.refs_0_), channel_id=1, source_target_pairs={{0,2},{1,3},{2,0},{3,1},{4,6},{5,7},{6,4},{7,5},{8,10},{9,11},{10,... | collective-permute-start | bytes 2752520 | tf_op jit(solution)/shard_map/ppermute | solution.py:1010
  52.2 41.2 %collective-permute-start.8 = (bf16[256,1792]{1,0:T(8,128)(2,1)S(1)}, bf16[256,1792]{1,0:T(8,128)(2,1)S(1)}, u32[]{:S(2)}, u32[]{:S(2)}) collective-permute-start(bf16[256,1792]{1,0:T(8,128)(2,1)S(1)} %pad_maximum_fusion.2.refs_0_), channel_id=1, source_target_pairs={{0,4},{1,5},{2,6},{3,7},{4,0},{5,1},{6,2},{7,3},{8,12},{9,13},{10,... | collective-permute-start | bytes 2752520 | tf_op jit(solution)/shard_map/ppermute | solution.py:1010
  53.8 39.7 %collective-permute-start.9 = (bf16[256,1792]{1,0:T(8,128)(2,1)S(1)}, bf16[256,1792]{1,0:T(8,128)(2,1)S(1)}, u32[]{:S(2)}, u32[]{:S(2)}) collective-permute-start(bf16[256,1792]{1,0:T(8,128)(2,1)S(1)} %pad_maximum_fusion.2.refs_0_), channel_id=1, source_target_pairs={{0,6},{1,7},{2,4},{3,5},{4,2},{5,3},{6,0},{7,1},{8,14},{9,15},{10,... | collective-permute-start | bytes 2752520 | tf_op jit(solution)/shard_map/ppermute | solution.py:1010
  93.5 45.1 %collective-permute-start.10 = (bf16[2048,256]{1,0:T(8,128)(2,1)S(1)}, bf16[2048,256]{1,0:T(8,128)(2,1)S(1)}, u32[]{:S(2)}, u32[]{:S(2)}) collective-permute-start(bf16[2048,256]{1,0:T(8,128)(2,1)S(1)} %collective-permute-done.2.refs_2_), channel_id=1, source_target_pairs={{0,8},{8,16},{16,24},{24,0},{1,9},{9,17},{17,25},{25,1},{2,10},{10... | collective-permute-start | bytes 3145736 | tf_op jit(solution)/shard_map/ppermute | solution.py:1019
  93.6 45.0 %collective-permute-start.11 = (bf16[256,1792]{1,0:T(8,128)(2,1)S(1)}, bf16[256,1792]{1,0:T(8,128)(2,1)}, u32[]{:S(2)}, u32[]{:S(2)}) collective-permute-start(bf16[256,1792]{1,0:T(8,128)(2,1)S(1)} %collective-permute-done.3.refs_4_), channel_id=1, source_target_pairs={{0,8},{8,16},{16,24},{24,0},{1,9},{9,17},{17,25},{25,1},{2,10},{10... | collective-permute-start | bytes 2752520 | tf_op jit(solution)/shard_map/ppermute | solution.py:1019
  94.9 43.6 %collective-permute-start.12 = (bf16[256,1792]{1,0:T(8,128)(2,1)S(1)}, bf16[256,1792]{1,0:T(8,128)(2,1)S(1)}, u32[]{:S(2)}, u32[]{:S(2)}) collective-permute-start(bf16[256,1792]{1,0:T(8,128)(2,1)S(1)} %collective-permute-done.3.refs_4_), channel_id=1, source_target_pairs={{0,2},{1,3},{2,0},{3,1},{4,6},{5,7},{6,4},{7,5},{8,10},{9,11},{10,... | collective-permute-start | bytes 2752520 | tf_op jit(solution)/shard_map/ppermute | solution.py:1010
  96.1 42.4 %collective-permute-start.13 = (bf16[256,1792]{1,0:T(8,128)(2,1)S(1)}, bf16[256,1792]{1,0:T(8,128)(2,1)S(1)}, u32[]{:S(2)}, u32[]{:S(2)}) collective-permute-start(bf16[256,1792]{1,0:T(8,128)(2,1)S(1)} %collective-permute-done.3.refs_4_), channel_id=1, source_target_pairs={{0,4},{1,5},{2,6},{3,7},{4,0},{5,1},{6,2},{7,3},{8,12},{9,13},{10,... | collective-permute-start | bytes 2752520 | tf_op jit(solution)/shard_map/ppermute | solution.py:1010
  97.0 41.6 %collective-permute-start.14 = (bf16[256,1792]{1,0:T(8,128)(2,1)S(1)}, bf16[256,1792]{1,0:T(8,128)(2,1)S(1)}, u32[]{:S(2)}, u32[]{:S(2)}) collective-permute-start(bf16[256,1792]{1,0:T(8,128)(2,1)S(1)} %collective-permute-done.3.refs_4_), channel_id=1, source_target_pairs={{0,6},{1,7},{2,4},{3,5},{4,2},{5,3},{6,0},{7,1},{8,14},{9,15},{10,... | collective-permute-start | bytes 2752520 | tf_op jit(solution)/shard_map/ppermute | solution.py:1010
  140.4 43.2 %collective-permute-start.15 = (bf16[256,1792]{1,0:T(8,128)(2,1)}, bf16[256,1792]{1,0:T(8,128)(2,1)}, u32[]{:S(2)}, u32[]{:S(2)}) collective-permute-start(bf16[256,1792]{1,0:T(8,128)(2,1)} %collective-permute-done.11.refs_8_), channel_id=1, source_target_pairs={{0,2},{1,3},{2,0},{3,1},{4,6},{5,7},{6,4},{7,5},{8,10},{9,11},{10,... | collective-permute-start | bytes 2752520 | tf_op jit(solution)/shard_map/ppermute | solution.py:1010
  165.1 61.2 %collective-permute-start.16 = (bf16[256,1792]{1,0:T(8,128)(2,1)}, bf16[256,1792]{1,0:T(8,128)(2,1)S(1)}, u32[]{:S(2)}, u32[]{:S(2)}) collective-permute-start(bf16[256,1792]{1,0:T(8,128)(2,1)} %collective-permute-done.11.refs_8_), channel_id=1, source_target_pairs={{0,4},{1,5},{2,6},{3,7},{4,0},{5,1},{6,2},{7,3},{8,12},{9,13},{10,... | collective-permute-start | bytes 2752520 | tf_op jit(solution)/shard_map/ppermute | solution.py:1010
  166.7 59.6 %collective-permute-start.17 = (bf16[256,1792]{1,0:T(8,128)(2,1)}, bf16[256,1792]{1,0:T(8,128)(2,1)S(1)}, u32[]{:S(2)}, u32[]{:S(2)}) collective-permute-start(bf16[256,1792]{1,0:T(8,128)(2,1)} %collective-permute-done.11.refs_8_), channel_id=1, source_target_pairs={{0,6},{1,7},{2,4},{3,5},{4,2},{5,3},{6,0},{7,1},{8,14},{9,15},{10,... | collective-permute-start | bytes 2752520 | tf_op jit(solution)/shard_map/ppermute | solution.py:1010
  174.2 52.1 %collective-permute-start.19 = (bf16[256,1792]{1,0:T(8,128)(2,1)}, bf16[256,1792]{1,0:T(8,128)(2,1)S(1)}, u32[]{:S(2)}, u32[]{:S(2)}) collective-permute-start(bf16[256,1792]{1,0:T(8,128)(2,1)} %collective-permute-done.18.refs_12_), channel_id=1, source_target_pairs={{0,2},{1,3},{2,0},{3,1},{4,6},{5,7},{6,4},{7,5},{8,10},{9,11},{10,... | collective-permute-start | bytes 2752520 | tf_op jit(solution)/shard_map/ppermute | solution.py:1010
  182.1 61.7 %collective-permute-start.20 = (bf16[256,1792]{1,0:T(8,128)(2,1)}, bf16[256,1792]{1,0:T(8,128)(2,1)}, u32[]{:S(2)}, u32[]{:S(2)}) collective-permute-start(bf16[256,1792]{1,0:T(8,128)(2,1)} %collective-permute-done.18.refs_12_), channel_id=1, source_target_pairs={{0,4},{1,5},{2,6},{3,7},{4,0},{5,1},{6,2},{7,3},{8,12},{9,13},{10,... | collective-permute-start | bytes 2752520 | tf_op jit(solution)/shard_map/ppermute | solution.py:1010
  183.6 60.1 %collective-permute-start.21 = (bf16[256,1792]{1,0:T(8,128)(2,1)}, bf16[256,1792]{1,0:T(8,128)(2,1)}, u32[]{:S(2)}, u32[]{:S(2)}) collective-permute-start(bf16[256,1792]{1,0:T(8,128)(2,1)} %collective-permute-done.18.refs_12_), channel_id=1, source_target_pairs={{0,6},{1,7},{2,4},{3,5},{4,2},{5,3},{6,0},{7,1},{8,14},{9,15},{10,... | collective-permute-start | bytes 2752520 | tf_op jit(solution)/shard_map/ppermute | solution.py:1010
  183.6 42.7 %all-to-all-start.1 = ((bf16[4,256,256]{2,1,0:T(8,128)(2,1)}), bf16[4,256,256]{2,1,0:T(8,128)(2,1)}, u32[]{:S(2)}, u32[]{:S(2)}) async-start(bf16[4,256,256]{2,1,0:T(8,128)(2,1)} %bitcast.111), calls=%async_computation.1 | async-start | bytes 1048576 | tf_op jit(solution)/shard_map/all_to_all | solution.py:1022
  290.6 47.3 %all-to-all-start.3 = ((bf16[4,512,256]{2,1,0:T(8,128)(2,1)}), bf16[4,512,256]{2,1,0:T(8,128)(2,1)S(1)}, u32[]{:S(2)}, u32[]{:S(2)}) async-start(bf16[4,512,256]{2,1,0:T(8,128)(2,1)} %get-tuple-element.219), calls=%async_computation.3 | async-start | bytes 2097152 | tf_op jit(solution)/shard_map/all_to_all | solution.py:1022
  382.6 85.1 %collective-permute-start.31 = (bf16[2,2,272,1152]{3,2,1,0:T(8,128)(2,1)}, bf16[2,2,272,1152]{3,2,1,0:T(8,128)(2,1)}, u32[]{:S(2)}, u32[]{:S(2)}) collective-permute-start(bf16[2,2,272,1152]{3,2,1,0:T(8,128)(2,1)} %get-tuple-element.256), channel_id=1, source_target_pairs={{0,4},{1,5},{2,6},{3,7},{4,0},{5,1},{6,2},{7,3},{8,12},{9,13},{10,... | collective-permute-start | bytes 7520264 | tf_op jit(solution)/shard_map/ppermute | solution.py:1010
  383.5 84.2 %collective-permute-start.30 = (bf16[2,2,272,1152]{3,2,1,0:T(8,128)(2,1)}, bf16[2,2,272,1152]{3,2,1,0:T(8,128)(2,1)}, u32[]{:S(2)}, u32[]{:S(2)}) collective-permute-start(bf16[2,2,272,1152]{3,2,1,0:T(8,128)(2,1)} %get-tuple-element.252), channel_id=1, source_target_pairs={{0,2},{1,3},{2,0},{3,1},{4,6},{5,7},{6,4},{7,5},{8,10},{9,11},{10,... | collective-permute-start | bytes 7520264 | tf_op jit(solution)/shard_map/ppermute | solution.py:1010
  389.7 257.0 %reduce-scatter.2.cloned.1.call-start = ((), (), s32[]{:S(2)}) async-start(), calls=%async_computation.8 | async-start | bytes 2621440 | tf_op jit(solution)/shard_map/reduce_scatter | solution.py:1202
  389.9 61.4 %collective-permute-start.33 = (bf16[1,2,256,512]{3,2,1,0:T(8,128)(2,1)}, bf16[1,2,256,512]{3,2,1,0:T(8,128)(2,1)}, u32[]{:S(2)}, u32[]{:S(2)}) collective-permute-start(bf16[1,2,256,512]{3,2,1,0:T(8,128)(2,1)} %get-tuple-element.327), channel_id=1, source_target_pairs={{0,2},{1,3},{2,0},{3,1},{4,6},{5,7},{6,4},{7,5},{8,10},{9,11},{10,... | collective-permute-start | bytes 1572872 | tf_op jit(solution)/shard_map/ppermute | solution.py:1010
  390.9 60.4 %collective-permute-start.32 = (bf16[1,2,256,512]{3,2,1,0:T(8,128)(2,1)}, bf16[1,2,256,512]{3,2,1,0:T(8,128)(2,1)}, u32[]{:S(2)}, u32[]{:S(2)}) collective-permute-start(bf16[1,2,256,512]{3,2,1,0:T(8,128)(2,1)} %get-tuple-element.329), channel_id=1, source_target_pairs={{0,4},{1,5},{2,6},{3,7},{4,0},{5,1},{6,2},{7,3},{8,12},{9,13},{10,... | collective-permute-start | bytes 1572872 | tf_op jit(solution)/shard_map/ppermute | solution.py:1010
  456.4 37.8 %collective-permute-start.34 = (bf16[1024,256]{1,0:T(8,128)(2,1)}, bf16[1024,256]{1,0:T(8,128)(2,1)S(1)}, u32[]{:S(2)}, u32[]{:S(2)}) collective-permute-start(bf16[1024,256]{1,0:T(8,128)(2,1)} %get-tuple-element.332), channel_id=1, source_target_pairs={{0,8},{8,16},{16,24},{24,0},{1,9},{9,17},{17,25},{25,1},{2,10},{10... | collective-permute-start | bytes 1572872 | tf_op jit(solution)/shard_map/ppermute | solution.py:1019
  458.2 36.0 %collective-permute-start.35 = (bf16[1024,256]{1,0:T(8,128)(2,1)}, bf16[1024,256]{1,0:T(8,128)(2,1)S(1)}, u32[]{:S(2)}, u32[]{:S(2)}) collective-permute-start(bf16[1024,256]{1,0:T(8,128)(2,1)} %get-tuple-element.330), channel_id=1, source_target_pairs={{0,16},{8,24},{16,0},{24,8},{1,17},{9,25},{17,1},{25,9},{2,18},{10... | collective-permute-start | bytes 1572872 | tf_op jit(solution)/shard_map/ppermute | solution.py:1019
  471.9 57.5 %collective-permute-start.41 = (bf16[1,2,272,1152]{3,2,1,0:T(8,128)(2,1)}, bf16[1,2,272,1152]{3,2,1,0:T(8,128)(2,1)}, u32[]{:S(2)}, u32[]{:S(2)}) collective-permute-start(bf16[1,2,272,1152]{3,2,1,0:T(8,128)(2,1)} %get-tuple-element.323), channel_id=1, source_target_pairs={{0,2},{1,3},{2,0},{3,1},{4,6},{5,7},{6,4},{7,5},{8,10},{9,11},{10,... | collective-permute-start | bytes 3760136 | tf_op jit(solution)/shard_map/ppermute | solution.py:1010
  476.3 45.1 %collective-permute-start.40 = (bf16[1,2,272,1152]{3,2,1,0:T(8,128)(2,1)}, bf16[1,2,272,1152]{3,2,1,0:T(8,128)(2,1)}, u32[]{:S(2)}, u32[]{:S(2)}) collective-permute-start(bf16[1,2,272,1152]{3,2,1,0:T(8,128)(2,1)} %get-tuple-element.325), channel_id=1, source_target_pairs={{0,4},{1,5},{2,6},{3,7},{4,0},{5,1},{6,2},{7,3},{8,12},{9,13},{10,... | collective-permute-start | bytes 3760136 | tf_op jit(solution)/shard_map/ppermute | solution.py:1010
  501.0 55.8 %collective-permute-start.46 = (bf16[256,512]{1,0:T(8,128)(2,1)}, bf16[256,512]{1,0:T(8,128)(2,1)}, u32[]{:S(2)}, u32[]{:S(2)}) collective-permute-start(bf16[256,512]{1,0:T(8,128)(2,1)} %fusion.24), channel_id=1, source_target_pairs={{0,24},{8,0},{16,8},{24,16},{1,25},{9,1},{17,9},{25,17},{2,26},{10... | collective-permute-start | bytes 786440 | tf_op jit(solution)/shard_map/ppermute | solution.py:1019
  512.7 44.1 %collective-permute-start.47 = (bf16[256,512]{1,0:T(8,128)(2,1)}, bf16[256,512]{1,0:T(8,128)(2,1)}, u32[]{:S(2)}, u32[]{:S(2)}) collective-permute-start(bf16[256,512]{1,0:T(8,128)(2,1)} %get-tuple-element.277), channel_id=1, source_target_pairs={{0,16},{8,24},{16,0},{24,8},{1,17},{9,25},{17,1},{25,9},{2,18},{10... | collective-permute-start | bytes 786440 | tf_op jit(solution)/shard_map/ppermute | solution.py:1019
  551.4 39.1 %collective-permute-start.43 = (bf16[272,1152]{1,0:T(8,128)(2,1)S(1)}, bf16[272,1152]{1,0:T(8,128)(2,1)S(1)}, u32[]{:S(2)}, u32[]{:S(2)}) collective-permute-start(bf16[272,1152]{1,0:T(8,128)(2,1)S(1)} %fusion.10), channel_id=1, source_target_pairs={{0,8},{8,16},{16,24},{24,0},{1,9},{9,17},{17,25},{25,1},{2,10},{10... | collective-permute-start | bytes 1880072 | tf_op jit(solution)/shard_map/ppermute | solution.py:1019
  562.7 40.3 %collective-permute-start.39 = (bf16[144,768]{1,0:T(8,128)(2,1)S(1)}, bf16[144,768]{1,0:T(8,128)(2,1)S(1)}, u32[]{:S(2)}, u32[]{:S(2)}) collective-permute-start(bf16[144,768]{1,0:T(8,128)(2,1)S(1)} %add_convert_fusion.4), channel_id=1, source_target_pairs={{0,4},{1,5},{2,6},{3,7},{4,0},{5,1},{6,2},{7,3},{8,12},{9,13},{10,... | collective-permute-start | bytes 663560 | tf_op jit(solution)/shard_map/ppermute | solution.py:1010
  (84 other events, 1587.7 us)
Sparse Core Ops, SparseCore 0:
  17.8 25.9 all-gather.1
  525.3 72.2 reduce-scatter.1

commit v3 on v2

--- a/solution.py
+++ b/solution.py
@@ -1045,9 +1045,12 @@
     qkv_full = lax.all_gather(qkv_own, "batch", axis=0, tiled=True)
     theirs = swap_core(theirs)
     packet = jnp.concatenate([pick((mine, theirs), core), pick((theirs, mine), core)], axis=0)
-    tokens[1], packet, places, s_uv, alpha_attn, alpha_mlp = lax.optimization_barrier(
-        (tokens[1], packet, positions, s_uv, alpha_attn, alpha_mlp)
+    hops = [packet, onward(packet)]
+    slots = [spread(packet)]
+    tokens[1], hops[1], places, s_uv, alpha_attn, alpha_mlp, *last = lax.optimization_barrier(
+        (tokens[1], hops[1], positions, s_uv, alpha_attn, alpha_mlp, *slots[0])
     )
+    slots[0] = list(last)
 
     suv_own = pick((s_uv[:, :half], s_uv[:, half:]), core)
     freqs = jnp.exp(
@@ -1063,30 +1066,32 @@
     attn_gain = relative(alpha_attn[None])
     mlp_gain = relative(alpha_mlp[None])
 
+    for n in range(2, nz):
+        slots.append(spread(hops[-1]))
+        tokens.append(onward(tokens[-1]))
+        if n < nz - 1:
+            hops.append(onward(hops[-1]))
+            tokens[-1], hops[-1], cosine, sine, ones, attn_gain, mlp_gain, suv_own, *last = (
+                lax.optimization_barrier(
+                    (tokens[-1], hops[-1], cosine, sine, ones, attn_gain, mlp_gain, suv_own, *slots[-1])
+                )
+            )
+            slots[-1] = list(last)
+    last_hop, tokens[-1] = lax.optimization_barrier((hops[-1], tokens[-1]))
+    hops.append(onward(last_hop))
     suv = jnp.stack([suv_own] + [onward(suv_own, n) for n in range(1, nz)])
-    hops = [packet]
-    slots = [spread(packet)]
-    for n in range(2, nz):
-        tokens.append(onward(tokens[-1]))
-        hops.append(onward(hops[-1]))
-        tokens[-1], hops[-1], cosine, sine, ones, attn_gain, mlp_gain, suv, *last = lax.optimization_barrier(
-            (tokens[-1], hops[-1], cosine, sine, ones, attn_gain, mlp_gain, suv, *slots[-1])
-        )
-        slots[-1] = list(last)
-        slots.append(spread(hops[-1]))
-    hops.append(onward(hops[-1]))
 
     blocks = rows // 512
     middle = blocks // 2
     tokens_full, q, k, v, rho = qkv_project(place, tokens, qkv_full, cosine, sine, gain, ones)
     y_a, logs_a = attn_fwd(is_long, q, k, v, 0, middle)
-    q_b, hops[-1] = lax.optimization_barrier((after(q, y_a), hops[-1]))
+    q_b, suv, hops[-1], *last = lax.optimization_barrier((after(q, y_a), suv, hops[-1], *slots[-1]))
+    slots[-1] = list(last)
+    slots.append(spread(hops[-1]))
     y_b, logs_b = attn_fwd(is_long, q_b, k, v, middle, blocks - middle)
     y_one = exchange(y_a.reshape(nz, own // 2, cols))
     y_in, y_one = lax.optimization_barrier((y_b, y_one))
     y_two = exchange(y_in.reshape(nz, own // 2, cols))
-    hop = after(hops[-1], y_b)
-    slots.append(spread(hop))
     flat = lambda value: value.transpose(1, 0, 2).reshape(own, width)
     start = tokens_full
     if not fast:
@@ -1164,7 +1169,12 @@
     up_made, up_kept = weight_grads(
         place, sent_at, kept_at, chips, (h_own, h_got), duv, (do_own, do_got), (y_mine, y_got), extra
     )
-    dy_b, dy_a, *up_made = lax.optimization_barrier((dy_b, dy_a, *up_made))
+    down_keep, down_got = [p[0] for p in down_part], [p[1] for p in down_part]
+    down_got = [after(one, *up_kept) for one in down_got]
+    down_slots = slot_sums(list(zip(down_keep, down_got)))
+    dy_b, dy_a, *both = lax.optimization_barrier((dy_b, dy_a, *up_made, *down_slots))
+    up_made, down_slots = both[: len(up_made)], both[len(up_made) :]
+    down_along = [onward(down_slots[n].astype(bf16), nz - n) for n in range(1, nz)]
     up_sent = [swap_chip(one, order[0]) for one, order in zip(up_made, orders)]
 
     dy_a = exchange(dy_a)
@@ -1190,23 +1200,23 @@
     part_b = input_part(dqkv_b, 1)
     cut = lambda n: lax.dynamic_slice_in_dim(part_b, ((z + n) % nz) * cols, cols, 1)
     part_cuts = [cut(n) for n in range(nz)]
-    down_part = [(keep, after(got, dqkv_b)) for keep, got in down_part]
-    down_slots = slot_sums(down_part)
+    down_along = [after(one, dqkv_b) for one in down_along]
+    sum_down_t = down_slots[0] + sum(one.astype(f32) for one in down_along)
     up_part, up_next = second(up_kept, [after(one, dqkv_b) for one in up_sent])
     part_got = [onward(part_cuts[n], n) for n in range(1, nz)]
-    dk_part, dy_a, *_ = lax.optimization_barrier((dk_part, dy_a, *up_next, *part_cuts, *down_slots))
+    dk_part, dy_a, *_ = lax.optimization_barrier((dk_part, dy_a, *up_next, *part_cuts, sum_down_t))
     dqkv_a, sqk_a = attn_bwd(*common(dy_a, y_a, logs_a), 0, middle, [dk_part, dv_part])
     part_got = [after(one, dqkv_a) for one in part_got]
     input_b = part_cuts[0].astype(f32) + sum(one.astype(f32) for one in part_got)
     up_part = [(keep, after(got, dqkv_a)) for keep, got in up_part]
-    input_a = lax.psum_scatter(input_part(dqkv_a, 0), "head", scatter_dimension=1, tiled=True)
-    down_along = [onward(after(down_slots[n].astype(bf16), input_b), nz - n) for n in range(1, nz)]
-    sum_down_t = down_slots[0] + sum(one.astype(f32) for one in down_along)
+    part_a = input_part(dqkv_a, 0)
     up_slots = slot_sums(up_part)
     passed = onward(up_slots[1].astype(bf16))
     for n in range(2, nz):
         passed = onward((up_slots[n] + passed.astype(f32)).astype(bf16))
+    passed, part_a = lax.optimization_barrier((passed, part_a))
     sum_up_t = up_slots[0] + passed.astype(f32)
+    input_a = lax.psum_scatter(part_a, "head", scatter_dimension=1, tiled=True)
     input_grad = jnp.concatenate([input_a.astype(f32), input_b], axis=0)
     hidden_t = hidden.reshape(nz, 2, own // 2, cols).transpose(1, 0, 2, 3).reshape(rows, cols)
 

time: 666 us -> 591 us (0.89)
  waiting for transfers between devices: 248 us -> 173 us
  starting transfers between devices: 105 us -> 78.8 us
  Pallas kernels: 182 us -> 201 us
  blocking collectives: 0 us -> 14.5 us
    ppermute x35, waiting for transfers between devices: 98 us -> 49.3 us  [swap_batch(): return lax.ppermute(value, 'batch', [(i, i ^ bit) for i in range(nb)])]
    ppermute x18, waiting for transfers between devices: 146 us -> 108 us  [onward(): return lax.ppermute(value, 'head', [(i, (i + k) % nz) for i in range(nz)])]
    ppermute x18, starting transfers between devices: 41.5 us -> 25.4 us  [onward(): return lax.ppermute(value, 'head', [(i, (i + k) % nz) for i in range(nz)])]
    all_to_all x0 -> x1, blocking collectives: none -> 14.5 us  [exchange(): return lax.all_to_all(value, 'head', split_axis=0, concat_axis=0)]
    pallas_call x2, Pallas kernels: 33 us -> 44.9 us  [attn_bwd(): pl.pallas_call(inner, grid_spec=pltpu.PrefetchScalarGridSpec(num_scalar_p...]
    reduce_scatter x1, waiting for transfers between devices: 0.01 us -> 11.8 us  [per_device(): input_a = lax.psum_scatter(part_a, 'head', scatter_dimension=1, tiled=True)]
    pallas_call x2, Pallas kernels: 13.2 us -> 19.9 us  [attn_fwd(): pl.pallas_call(functools.partial(attn_fwd_kernel, heads=heads, blk=blk, s...]
    all_to_all x6 -> x5, starting transfers between devices: 27.8 us -> 23.2 us  [exchange(): return lax.all_to_all(value, 'head', split_axis=0, concat_axis=0)]
  transfers between devices with their start and end apart: 61 -> 60, of which waited for: 14 -> 24; matrix products, arithmetic and copies ran while one was open for 14% -> 14% of each run, Pallas kernels for 25% -> 31%
where the time goes in v3:
time: 591 us; the launch traced here: 581 us
  Pallas kernels  201 us (34%)
  waiting for transfers between devices  173 us (29%)
  starting transfers between devices  78.8 us (13%)
  other arithmetic  47.4 us (8%)
  local copies, waits for them, and re-layouts  38.1 us (6%)
  between operations  16.4 us (3%)
  blocking collectives  14.5 us (2%)
  matrix products  11.8 us (2%)
    ppermute x18, waiting for transfers between devices, onward(): return lax.ppermute(value, 'head', [(i, (i + k) % nz) for i in range(nz)])  108 us
    ppermute x35, waiting for transfers between devices, swap_batch(): return lax.ppermute(value, 'batch', [(i, i ^ bit) for i in range(nb)])  49.3 us
    pallas_call x2, Pallas kernels, attn_bwd(): pl.pallas_call(inner, grid_spec=pltpu.PrefetchScalarGridSpec(num_scalar_p...  44.9 us
    ppermute x35, starting transfers between devices, swap_batch(): return lax.ppermute(value, 'batch', [(i, i ^ bit) for i in range(nb)])  30.1 us
    pallas_call x2, Pallas kernels, weight_grads(): pl.pallas_call(functools.partial(grad_kernel, orders=(lists[:2], lists[2:...  29.2 us
    pallas_call x1, Pallas kernels, mlp_bwd(): pl.pallas_call(functools.partial(mlp_bwd_kernel, half=half, counts=[len(s...  26.2 us
    ppermute x18, starting transfers between devices, onward(): return lax.ppermute(value, 'head', [(i, (i + k) % nz) for i in range(nz)])  25.4 us
    all_to_all x5, starting transfers between devices, exchange(): return lax.all_to_all(value, 'head', split_axis=0, concat_axis=0)  23.2 us
  transfers between devices with their start and end apart: 60, of which 24 were waited for; matrix products, arithmetic and copies ran while one was open for 14% of the time, Pallas kernels for 31%

profile of v3, /device:TPU:0, one launch (start us, length us, event | category | flops | bytes accessed | tf_op | source)
XLA Modules:
  0.0 581.0 jit_solution(3121573313648461102)
XLA Ops:
  9.3 5.0 shard_map.354
  25.0 18.8 %collective-permute-done.refs_1_ = bf16[2048,256]{1,0:T(8,128)(2,1)} collective-permute-done((bf16[2048,256]{1,0:T(8,128)(2,1)}, bf16[2048,256]{1,0:T(8,128)(2,1)}, u32[]{:S(2)}, u32[]{:S(2)}) %collective-permute-start) | collective-permute-done | bytes 1048608 | tf_op jit(solution)/shard_map/ppermute | solution.py:1019
  43.9 19.3 %collective-permute-done.2.refs_4_ = bf16[256,1792]{1,0:T(8,128)(2,1)S(1)} collective-permute-done((bf16[256,1792]{1,0:T(8,128)(2,1)S(1)}, bf16[256,1792]{1,0:T(8,128)(2,1)S(1)}, u32[]{:S(2)}, u32[]{:S(2)}) %collective-permute-start.2) | collective-permute-done | bytes 917536 | tf_op jit(solution)/shard_map/ppermute | solution.py:1019
  63.2 6.7 %collective-permute-done.5.refs_3_ = bf16[256,1792]{1,0:T(8,128)(2,1)} collective-permute-done((bf16[256,1792]{1,0:T(8,128)(2,1)S(1)}, bf16[256,1792]{1,0:T(8,128)(2,1)}, u32[]{:S(2)}, u32[]{:S(2)}) %collective-permute-start.5) | collective-permute-done | bytes 917536 | tf_op jit(solution)/shard_map/ppermute | solution.py:1010
  77.9 5.5 fusion.16
  83.4 10.7 %collective-permute-done.10.refs_7_ = bf16[256,1792]{1,0:T(8,128)(2,1)S(1)} collective-permute-done((bf16[256,1792]{1,0:T(8,128)(2,1)S(1)}, bf16[256,1792]{1,0:T(8,128)(2,1)S(1)}, u32[]{:S(2)}, u32[]{:S(2)}) %collective-permute-start.10) | collective-permute-done | bytes 917536 | tf_op jit(solution)/shard_map/ppermute | solution.py:1010
  96.5 14.2 %collective-permute-done.8.refs_5_ = bf16[256,1792]{1,0:T(8,128)(2,1)S(1)} collective-permute-done((bf16[256,1792]{1,0:T(8,128)(2,1)S(1)}, bf16[256,1792]{1,0:T(8,128)(2,1)S(1)}, u32[]{:S(2)}, u32[]{:S(2)}) %collective-permute-start.8) | collective-permute-done | bytes 917536 | tf_op jit(solution)/shard_map/ppermute | solution.py:1010
  121.0 21.1 %collective-permute-done.11.refs_3_ = bf16[2048,256]{1,0:T(8,128)(2,1)S(1)} collective-permute-done((bf16[2048,256]{1,0:T(8,128)(2,1)S(1)}, bf16[2048,256]{1,0:T(8,128)(2,1)S(1)}, u32[]{:S(2)}, u32[]{:S(2)}) %collective-permute-start.11) | collective-permute-done | bytes 1048608 | tf_op jit(solution)/shard_map/ppermute | solution.py:1019
  144.8 11.6 %shard_map.355 = (bf16[2048,1024]{1,0:T(8,128)(2,1)}, bf16[2048,256]{1,0:T(8,128)(2,1)}, bf16[2048,256]{1,0:T(8,128)(2,1)}, bf16[2048,256]{1,0:T(8,128)(2,1)}, f32[2048,128]{1,0:T(8,128)}) custom-call(s32[3]{0:T(128)} %pad_add_fusion.place_ref, bf16[2048,256]{1,0:T(8,128)(2,1)} %refs_0_.1, bf16[2048,256]{1,0:T(8,128)(2,1)} %collective-permute-done.refs_1_, ...), custom_call_target="tpu_custom_call" | custom-call | tf_op jit(solution)/shard_map/pallas_call | solution.py:103
  156.4 6.4 %shard_map.356 = (bf16[1024,256]{1,0:T(8,128)(2,1)}, f32[1024,128]{1,0:T(8,128)}) custom-call(s32[1]{0:T(128)S(6)} %convert_element_type.267.long_ref.r_0_, bf16[2048,256]{1,0:T(8,128)(2,1)} %get-tuple-element.200.q_ref.r_1_, bf16[2048,256]{1,0:T(8,128)(2,1)} %get-tuple-element.189.k_ref.r_2_.r_6_, bf16[2048,256]{1,0:T(8,128)(2,1)} %get-tuple-element.190.v_ref.r_7_), custom_call_target="tpu_custom_call" | custom-call | tf_op jit(solution)/shard_map/pallas_call | solution.py:194
  162.8 5.1 all-to-all-start
  170.0 7.9 %collective-permute-done.12 = f32[2,512]{1,0:T(2,128)S(1)} collective-permute-done((f32[2,512]{1,0:T(2,128)S(1)}, f32[2,512]{1,0:T(2,128)S(1)}, u32[]{:S(2)}, u32[]{:S(2)}) %collective-permute-start.12) | collective-permute-done | bytes 4128 | tf_op jit(solution)/shard_map/ppermute | solution.py:1019
  190.3 13.5 %shard_map.357 = (bf16[1024,256]{1,0:T(8,128)(2,1)}, f32[1024,128]{1,0:T(8,128)}) custom-call(s32[1]{0:T(128)S(6)} %convert_element_type.267.long_ref.r_0_, bf16[2048,256]{1,0:T(8,128)(2,1)} %get-tuple-element.200.q_ref.r_1_, bf16[2048,256]{1,0:T(8,128)(2,1)} %get-tuple-element.189.k_ref.r_2_.r_6_, bf16[2048,256]{1,0:T(8,128)(2,1)} %get-tuple-element.190.v_ref.r_7_), custom_call_target="tpu_custom_call" | custom-call | tf_op jit(solution)/shard_map/pallas_call | solution.py:194
  203.8 14.5 %all_to_all.30.refs_17_ = bf16[4,256,256]{2,1,0:T(8,128)(2,1)} all-to-all(bf16[4,256,256]{2,1,0:T(8,128)(2,1)} %bitcast.110), channel_id=1, replica_groups=mesh['head'=4,'batch'=8] {'head'}, dimensions={0} | all-to-all | bytes 1048576 | tf_op jit(solution)/shard_map/all_to_all | solution.py:1022
  218.3 5.6 collective-permute-done.20.refs_14_
  226.5 6.7 %shard_map.358 = (f32[512,1024]{1,0:T(8,128)}, f32[512,1024]{1,0:T(8,128)}, bf16[512,1024]{1,0:T(8,128)(2,1)}, f32[512,128]{1,0:T(8,128)}) custom-call(s32[3]{0:T(128)} %pad_add_fusion.place_ref, bf16[256,1792]{1,0:T(8,128)(2,1)} %copy-done, bf16[256,1792]{1,0:T(8,128)(2,1)} %copy-done.3, bf16[256,1792]{1,0:T(8,128)(2,1)} %collective-permute-done.4.refs_2_, ...), custom_call_target="tpu_custom_call" | custom-call | tf_op jit(solution)/shard_map/pallas_call | solution.py:477
  239.2 21.1 %shard_map.359 = (bf16[4,1024,512]{2,1,0:T(8,128)(2,1)}, bf16[4,1024,1024]{2,1,0:T(8,128)(2,1)}, f32[512,1024]{1,0:T(8,128)}, bf16[512,1024]{1,0:T(8,128)(2,1)}) custom-call(bf16[256,1792]{1,0:T(8,128)(2,1)} %copy-done, bf16[256,1792]{1,0:T(8,128)(2,1)} %copy-done.3, bf16[256,1792]{1,0:T(8,128)(2,1)} %collective-permute-done.4.refs_2_, ...), custom_call_target="tpu_custom_call" | custom-call | tf_op jit(solution)/shard_map/pallas_call | solution.py:670
  266.0 6.3 %shard_map.360 = (bf16[4,512,256]{2,1,0:T(8,128)(2,1)}, bf16[512,1024]{1,0:T(8,128)(2,1)}, f32[512,1024]{1,0:T(8,128)}, f32[8,1024]{1,0:T(8,128)}) custom-call(s32[3]{0:T(128)} %pad_add_fusion.place_ref, f32[512,1024]{1,0:T(8,128)} %get-tuple-element.208.own_ref, bf16[512,1024]{1,0:T(8,128)(2,1)} %copy-done.35, ...), custom_call_target="tpu_custom_call" | custom-call | tf_op jit(solution)/shard_map/pallas_call | solution.py:523
  277.1 10.0 %shard_map.361 = (bf16[2,2,256,512]{3,2,1,0:T(8,128)(2,1)}, bf16[2,2,256,512]{3,2,1,0:T(8,128)(2,1)}, bf16[2,2,256,512]{3,2,1,0:T(8,128)(2,1)}, bf16[2,2,256,512]{3,2,1,0:T(8,128)(2,1)}) custom-call(s32[3]{0:T(128)} %pad_add_fusion.place_ref, bf16[512,1024]{1,0:T(8,128)(2,1)} %get-tuple-element.217.refs_0_.refs_16_, bf16[512,1024]{1,0:T(8,128)(2,1)} %copy-done.21, ...), custom_call_target="tpu_custom_call" | custom-call | tf_op jit(solution)/shard_map/pallas_call | solution.py:860
  289.7 26.2 %shard_map.362 = (bf16[4,1024,1024]{2,1,0:T(8,128)(2,1)}, f32[512,1024]{1,0:T(8,128)}, bf16[512,1024]{1,0:T(8,128)(2,1)}, f32[4,8,512]{2,1,0:T(8,128)}) custom-call(bf16[256,1792]{1,0:T(8,128)(2,1)} %copy-done, bf16[256,1792]{1,0:T(8,128)(2,1)} %copy-done.3, bf16[256,1792]{1,0:T(8,128)(2,1)} %collective-permute-done.4.refs_2_, ...), custom_call_target="tpu_custom_call" | custom-call | tf_op jit(solution)/shard_map/pallas_call | solution.py:740
  319.3 11.3 %shard_map.363 = (bf16[512,1024]{1,0:T(8,128)(2,1)}, bf16[512,1024]{1,0:T(8,128)(2,1)}, f32[8,1024]{1,0:T(8,128)}, bf16[4,256,256]{2,1,0:T(8,128)(2,1)}, bf16[4,256,256]{2,1,0:T(8,128)(2,1)}) custom-call(s32[3]{0:T(128)} %pad_add_fusion.place_ref, bf16[256,1792]{1,0:T(8,128)(2,1)} %copy-done, bf16[256,1792]{1,0:T(8,128)(2,1)} %copy-done.3, ...), custom_call_target="tpu_custom_call" | custom-call | tf_op jit(solution)/shard_map/pallas_call | solution.py:583
  336.6 5.5 all-to-all-start.4
  343.0 19.2 %shard_map.364 = (bf16[2,2,272,1152]{3,2,1,0:T(8,128)(2,1)}, bf16[2,2,272,1152]{3,2,1,0:T(8,128)(2,1)}, bf16[2,2,272,1152]{3,2,1,0:T(8,128)(2,1)}, bf16[2,2,272,1152]{3,2,1,0:T(8,128)(2,1)}) custom-call(s32[3]{0:T(128)} %pad_add_fusion.place_ref, bf16[512,1024]{1,0:T(8,128)(2,1)} %get-tuple-element.235.refs_16_.refs_0_, bf16[512,1024]{1,0:T(8,128)(2,1)} %copy-done.18, ...), custom_call_target="tpu_custom_call" | custom-call | tf_op jit(solution)/shard_map/pallas_call | solution.py:860
  368.8 5.1 all-to-all-start.5
  386.1 28.5 %shard_map.365 = (bf16[1024,768]{1,0:T(8,128)(2,1)}, f32[1024,256]{1,0:T(8,128)}, f32[1024,256]{1,0:T(8,128)}, f32[8,256]{1,0:T(8,128)}) custom-call(s32[1]{0:T(128)S(6)} %convert_element_type.267.long_ref.r_0_, bf16[2048,256]{1,0:T(8,128)(2,1)} %get-tuple-element.200.q_ref.r_1_, bf16[2048,256]{1,0:T(8,128)(2,1)} %get-tuple-element.189.k_ref.r_2_.r_6_, ...), custom_call_target="tpu_custom_call" | custom-call | tf_op jit(solution)/shard_map/pallas_call | solution.py:341
  430.2 5.2 collective-permute-done.34
  440.6 16.3 %shard_map.366 = (bf16[1024,768]{1,0:T(8,128)(2,1)}, f32[8,256]{1,0:T(8,128)}) custom-call(s32[1]{0:T(128)S(6)} %convert_element_type.267.long_ref.r_0_, bf16[2048,256]{1,0:T(8,128)(2,1)} %get-tuple-element.200.q_ref.r_1_, bf16[2048,256]{1,0:T(8,128)(2,1)} %get-tuple-element.189.k_ref.r_2_.r_6_, bf16[1024,256]{1,0:T(8,128)(2,1)} %bitcast.111, ...), custom_call_target="tpu_custom_call" | custom-call | tf_op jit(solution)/shard_map/pallas_call | solution.py:341
  457.0 5.4 fusion.4
  475.9 12.9 %collective-permute-done.39 = bf16[272,1152]{1,0:T(8,128)(2,1)S(1)} collective-permute-done((bf16[272,1152]{1,0:T(8,128)(2,1)S(1)}, bf16[272,1152]{1,0:T(8,128)(2,1)S(1)}, u32[]{:S(2)}, u32[]{:S(2)}) %collective-permute-start.39) | collective-permute-done | bytes 626720 | tf_op jit(solution)/shard_map/ppermute | solution.py:1019
  496.4 11.2 %collective-permute-done.40 = bf16[272,1152]{1,0:T(8,128)(2,1)S(1)} collective-permute-done((bf16[272,1152]{1,0:T(8,128)(2,1)S(1)}, bf16[272,1152]{1,0:T(8,128)(2,1)S(1)}, u32[]{:S(2)}, u32[]{:S(2)}) %collective-permute-start.40) | collective-permute-done | bytes 626720 | tf_op jit(solution)/shard_map/ppermute | solution.py:1019
  532.2 6.1 %shard_map.369 = (f32[128,2,1024]{2,1,0:T(2,128)}, f32[128,2,1024]{2,1,0:T(2,128)}, f32[128,2,1024]{2,1,0:T(2,128)}, f32[128,2,1024]{2,1,0:T(2,128)}, f32[2,1024]{1,0:T(2,128)}) custom-call(f32[128,2,1024]{2,1,0:T(2,128)} %w_ref.5, f32[128,2048]{1,0:T(8,128)} %pad_maximum_fusion.1.g_ref, f32[128,2,1024]{2,1,0:T(2,128)} %m_ref.5, f32[128,2,1024]{2,1,0:T(2,128)} %v_ref.5), custom_call_target="tpu_custom_call" | custom-call | tf_op jit(solution)/shard_map/pallas_call | solution.py:911
  559.3 11.8 %reduce-scatter.2.cloned.1.call-done = bf16[1024,256]{1,0:T(8,128)(2,1)} async-done(((bf16[1024,1024]{1,0:T(8,128)(2,1)}), bf16[1024,256]{1,0:T(8,128)(2,1)}) %reduce-scatter.2.cloned.1.call-update) | async-done | bytes 524304 | tf_op jit(solution)/shard_map/reduce_scatter | solution.py:1219
  (347 shorter events, 189.8 us)
Async XLA Ops:
  7.2 137.6 %all-gather.2.cloned.1.call-start = ((), (), s32[]{:S(2)}) async-start(), calls=%async_computation.7 | async-start | bytes 1769472 | tf_op jit(solution)/shard_map/all_gather | solution.py:1045
  18.7 44.5 %collective-permute-start.2 = (bf16[256,1792]{1,0:T(8,128)(2,1)S(1)}, bf16[256,1792]{1,0:T(8,128)(2,1)S(1)}, u32[]{:S(2)}, u32[]{:S(2)}) collective-permute-start(bf16[256,1792]{1,0:T(8,128)(2,1)S(1)} %pad_maximum_fusion.2.refs_0_), channel_id=1, source_target_pairs={{0,8},{8,16},{16,24},{24,0},{1,9},{9,17},{17,25},{25,1},{2,10},{10... | collective-permute-start | bytes 2752520 | tf_op jit(solution)/shard_map/ppermute | solution.py:1019
  20.7 42.5 %collective-permute-start.3 = (bf16[256,1792]{1,0:T(8,128)(2,1)S(1)}, bf16[256,1792]{1,0:T(8,128)(2,1)S(1)}, u32[]{:S(2)}, u32[]{:S(2)}) collective-permute-start(bf16[256,1792]{1,0:T(8,128)(2,1)S(1)} %pad_maximum_fusion.2.refs_0_), channel_id=1, source_target_pairs={{0,2},{1,3},{2,0},{3,1},{4,6},{5,7},{6,4},{7,5},{8,10},{9,11},{10,... | collective-permute-start | bytes 2752520 | tf_op jit(solution)/shard_map/ppermute | solution.py:1010
  22.2 41.0 %collective-permute-start.4 = (bf16[256,1792]{1,0:T(8,128)(2,1)S(1)}, bf16[256,1792]{1,0:T(8,128)(2,1)}, u32[]{:S(2)}, u32[]{:S(2)}) collective-permute-start(bf16[256,1792]{1,0:T(8,128)(2,1)S(1)} %pad_maximum_fusion.2.refs_0_), channel_id=1, source_target_pairs={{0,4},{1,5},{2,6},{3,7},{4,0},{5,1},{6,2},{7,3},{8,12},{9,13},{10,... | collective-permute-start | bytes 2752520 | tf_op jit(solution)/shard_map/ppermute | solution.py:1010
  23.7 46.2 %collective-permute-start.5 = (bf16[256,1792]{1,0:T(8,128)(2,1)S(1)}, bf16[256,1792]{1,0:T(8,128)(2,1)}, u32[]{:S(2)}, u32[]{:S(2)}) collective-permute-start(bf16[256,1792]{1,0:T(8,128)(2,1)S(1)} %pad_maximum_fusion.2.refs_0_), channel_id=1, source_target_pairs={{0,6},{1,7},{2,4},{3,5},{4,2},{5,3},{6,0},{7,1},{8,14},{9,15},{10,... | collective-permute-start | bytes 2752520 | tf_op jit(solution)/shard_map/ppermute | solution.py:1010
  72.9 37.8 %collective-permute-start.8 = (bf16[256,1792]{1,0:T(8,128)(2,1)S(1)}, bf16[256,1792]{1,0:T(8,128)(2,1)S(1)}, u32[]{:S(2)}, u32[]{:S(2)}) collective-permute-start(bf16[256,1792]{1,0:T(8,128)(2,1)S(1)} %collective-permute-done.2.refs_4_), channel_id=1, source_target_pairs={{0,2},{1,3},{2,0},{3,1},{4,6},{5,7},{6,4},{7,5},{8,10},{9,11},{10,... | collective-permute-start | bytes 2752520 | tf_op jit(solution)/shard_map/ppermute | solution.py:1010
  73.5 38.2 %collective-permute-start.9 = (bf16[256,1792]{1,0:T(8,128)(2,1)S(1)}, bf16[256,1792]{1,0:T(8,128)(2,1)S(1)}, u32[]{:S(2)}, u32[]{:S(2)}) collective-permute-start(bf16[256,1792]{1,0:T(8,128)(2,1)S(1)} %collective-permute-done.2.refs_4_), channel_id=1, source_target_pairs={{0,4},{1,5},{2,6},{3,7},{4,0},{5,1},{6,2},{7,3},{8,12},{9,13},{10,... | collective-permute-start | bytes 2752520 | tf_op jit(solution)/shard_map/ppermute | solution.py:1010
  75.0 41.5 %collective-permute-start.6 = (bf16[2048,256]{1,0:T(8,128)(2,1)}, bf16[2048,256]{1,0:T(8,128)(2,1)S(1)}, u32[]{:S(2)}, u32[]{:S(2)}) collective-permute-start(bf16[2048,256]{1,0:T(8,128)(2,1)} %collective-permute-done.refs_1_), channel_id=1, source_target_pairs={{0,8},{8,16},{16,24},{24,0},{1,9},{9,17},{17,25},{25,1},{2,10},{10... | collective-permute-start | bytes 3145736 | tf_op jit(solution)/shard_map/ppermute | solution.py:1019
  117.5 69.2 %collective-permute-start.16 = (bf16[256,1792]{1,0:T(8,128)(2,1)}, bf16[256,1792]{1,0:T(8,128)(2,1)}, u32[]{:S(2)}, u32[]{:S(2)}) collective-permute-start(bf16[256,1792]{1,0:T(8,128)(2,1)} %collective-permute-done.7.refs_8_), channel_id=1, source_target_pairs={{0,2},{1,3},{2,0},{3,1},{4,6},{5,7},{6,4},{7,5},{8,10},{9,11},{10,... | collective-permute-start | bytes 2752520 | tf_op jit(solution)/shard_map/ppermute | solution.py:1010
  118.0 68.7 %collective-permute-start.17 = (bf16[256,1792]{1,0:T(8,128)(2,1)}, bf16[256,1792]{1,0:T(8,128)(2,1)}, u32[]{:S(2)}, u32[]{:S(2)}) collective-permute-start(bf16[256,1792]{1,0:T(8,128)(2,1)} %collective-permute-done.7.refs_8_), channel_id=1, source_target_pairs={{0,4},{1,5},{2,6},{3,7},{4,0},{5,1},{6,2},{7,3},{8,12},{9,13},{10,... | collective-permute-start | bytes 2752520 | tf_op jit(solution)/shard_map/ppermute | solution.py:1010
  119.5 67.2 %collective-permute-start.18 = (bf16[256,1792]{1,0:T(8,128)(2,1)}, bf16[256,1792]{1,0:T(8,128)(2,1)}, u32[]{:S(2)}, u32[]{:S(2)}) collective-permute-start(bf16[256,1792]{1,0:T(8,128)(2,1)} %collective-permute-done.7.refs_8_), channel_id=1, source_target_pairs={{0,6},{1,7},{2,4},{3,5},{4,2},{5,3},{6,0},{7,1},{8,14},{9,15},{10,... | collective-permute-start | bytes 2752520 | tf_op jit(solution)/shard_map/ppermute | solution.py:1010
  143.0 43.7 %collective-permute-start.15 = (bf16[256,1792]{1,0:T(8,128)(2,1)}, bf16[256,1792]{1,0:T(8,128)(2,1)}, u32[]{:S(2)}, u32[]{:S(2)}) collective-permute-start(bf16[256,1792]{1,0:T(8,128)(2,1)} %collective-permute-done.7.refs_8_), channel_id=1, source_target_pairs={{0,8},{8,16},{16,24},{24,0},{1,9},{9,17},{17,25},{25,1},{2,10},{10... | collective-permute-start | bytes 2752520 | tf_op jit(solution)/shard_map/ppermute | solution.py:1019
  162.8 40.9 %all-to-all-start = ((bf16[4,256,256]{2,1,0:T(8,128)(2,1)}), bf16[4,256,256]{2,1,0:T(8,128)(2,1)S(1)}, u32[]{:S(2)}, u32[]{:S(2)}) async-start(bf16[4,256,256]{2,1,0:T(8,128)(2,1)} %bitcast.109), calls=%async_computation | async-start | bytes 1048576 | tf_op jit(solution)/shard_map/all_to_all | solution.py:1022
  186.8 31.5 %collective-permute-start.19 = (bf16[256,1792]{1,0:T(8,128)(2,1)}, bf16[256,1792]{1,0:T(8,128)(2,1)S(1)}, u32[]{:S(2)}, u32[]{:S(2)}) collective-permute-start(bf16[256,1792]{1,0:T(8,128)(2,1)} %collective-permute-done.15.refs_12_), channel_id=1, source_target_pairs={{0,2},{1,3},{2,0},{3,1},{4,6},{5,7},{6,4},{7,5},{8,10},{9,11},{10,... | collective-permute-start | bytes 2752520 | tf_op jit(solution)/shard_map/ppermute | solution.py:1010
  187.4 36.5 %collective-permute-start.20 = (bf16[256,1792]{1,0:T(8,128)(2,1)}, bf16[256,1792]{1,0:T(8,128)(2,1)S(1)}, u32[]{:S(2)}, u32[]{:S(2)}) collective-permute-start(bf16[256,1792]{1,0:T(8,128)(2,1)} %collective-permute-done.15.refs_12_), channel_id=1, source_target_pairs={{0,4},{1,5},{2,6},{3,7},{4,0},{5,1},{6,2},{7,3},{8,12},{9,13},{10,... | collective-permute-start | bytes 2752520 | tf_op jit(solution)/shard_map/ppermute | solution.py:1010
  188.9 36.7 %collective-permute-start.21 = (bf16[256,1792]{1,0:T(8,128)(2,1)}, bf16[256,1792]{1,0:T(8,128)(2,1)S(1)}, u32[]{:S(2)}, u32[]{:S(2)}) collective-permute-start(bf16[256,1792]{1,0:T(8,128)(2,1)} %collective-permute-done.15.refs_12_), channel_id=1, source_target_pairs={{0,6},{1,7},{2,4},{3,5},{4,2},{5,3},{6,0},{7,1},{8,14},{9,15},{10,... | collective-permute-start | bytes 2752520 | tf_op jit(solution)/shard_map/ppermute | solution.py:1010
  234.4 30.2 %all-to-all-start.2 = ((bf16[4,512,256]{2,1,0:T(8,128)(2,1)}), bf16[4,512,256]{2,1,0:T(8,128)(2,1)S(1)}, u32[]{:S(2)}, u32[]{:S(2)}) async-start(bf16[4,512,256]{2,1,0:T(8,128)(2,1)} %bitcast.20), calls=%async_computation.2 | async-start | bytes 2097152 | tf_op jit(solution)/shard_map/all_to_all | solution.py:1022
  272.4 46.9 %all-to-all-start.3 = ((bf16[4,512,256]{2,1,0:T(8,128)(2,1)}), bf16[4,512,256]{2,1,0:T(8,128)(2,1)S(1)}, u32[]{:S(2)}, u32[]{:S(2)}) async-start(bf16[4,512,256]{2,1,0:T(8,128)(2,1)} %get-tuple-element.221), calls=%async_computation.3 | async-start | bytes 2097152 | tf_op jit(solution)/shard_map/all_to_all | solution.py:1022
  287.1 32.2 %collective-permute-start.25 = (bf16[2,2,256,512]{3,2,1,0:T(8,128)(2,1)}, bf16[2,2,256,512]{3,2,1,0:T(8,128)(2,1)S(1)}, u32[]{:S(2)}, u32[]{:S(2)}) collective-permute-start(bf16[2,2,256,512]{3,2,1,0:T(8,128)(2,1)} %get-tuple-element.215), channel_id=1, source_target_pairs={{0,2},{1,3},{2,0},{3,1},{4,6},{5,7},{6,4},{7,5},{8,10},{9,11},{10,... | collective-permute-start | bytes 3145736 | tf_op jit(solution)/shard_map/ppermute | solution.py:1010
  288.0 31.3 %collective-permute-start.26 = (bf16[2,2,256,512]{3,2,1,0:T(8,128)(2,1)}, bf16[2,2,256,512]{3,2,1,0:T(8,128)(2,1)}, u32[]{:S(2)}, u32[]{:S(2)}) collective-permute-start(bf16[2,2,256,512]{3,2,1,0:T(8,128)(2,1)} %get-tuple-element.216), channel_id=1, source_target_pairs={{0,4},{1,5},{2,6},{3,7},{4,0},{5,1},{6,2},{7,3},{8,12},{9,13},{10,... | collective-permute-start | bytes 3145736 | tf_op jit(solution)/shard_map/ppermute | solution.py:1010
  336.6 31.2 %all-to-all-start.4 = ((bf16[4,256,256]{2,1,0:T(8,128)(2,1)}), bf16[4,256,256]{2,1,0:T(8,128)(2,1)}, u32[]{:S(2)}, u32[]{:S(2)}) async-start(bf16[4,256,256]{2,1,0:T(8,128)(2,1)} %get-tuple-element.242), calls=%async_computation.4 | async-start | bytes 1048576 | tf_op jit(solution)/shard_map/all_to_all | solution.py:1022
  367.8 58.1 %collective-permute-start.32 = (bf16[2,2,272,1152]{3,2,1,0:T(8,128)(2,1)}, bf16[2,2,272,1152]{3,2,1,0:T(8,128)(2,1)}, u32[]{:S(2)}, u32[]{:S(2)}) collective-permute-start(bf16[2,2,272,1152]{3,2,1,0:T(8,128)(2,1)} %get-tuple-element.249), channel_id=1, source_target_pairs={{0,4},{1,5},{2,6},{3,7},{4,0},{5,1},{6,2},{7,3},{8,12},{9,13},{10,... | collective-permute-start | bytes 7520264 | tf_op jit(solution)/shard_map/ppermute | solution.py:1010
  368.8 45.9 %all-to-all-start.5 = ((bf16[4,256,256]{2,1,0:T(8,128)(2,1)}), bf16[4,256,256]{2,1,0:T(8,128)(2,1)S(1)}, u32[]{:S(2)}, u32[]{:S(2)}) async-start(bf16[4,256,256]{2,1,0:T(8,128)(2,1)} %get-tuple-element.255), calls=%async_computation.5 | async-start | bytes 1048576 | tf_op jit(solution)/shard_map/all_to_all | solution.py:1022
  373.8 197.3 %reduce-scatter.2.cloned.1.call-start = ((), (), s32[]{:S(2)}) async-start(), calls=%async_computation.8 | async-start | bytes 2621440 | tf_op jit(solution)/shard_map/reduce_scatter | solution.py:1219
  376.0 38.6 %collective-permute-start.35 = (bf16[256,512]{1,0:T(8,128)(2,1)}, bf16[256,512]{1,0:T(8,128)(2,1)S(1)}, u32[]{:S(2)}, u32[]{:S(2)}) collective-permute-start(bf16[256,512]{1,0:T(8,128)(2,1)} %fusion.24), channel_id=1, source_target_pairs={{0,24},{8,0},{16,8},{24,16},{1,25},{9,1},{17,9},{25,17},{2,26},{10... | collective-permute-start | bytes 786440 | tf_op jit(solution)/shard_map/ppermute | solution.py:1019
  379.8 34.8 %collective-permute-start.36 = (bf16[256,512]{1,0:T(8,128)(2,1)}, bf16[256,512]{1,0:T(8,128)(2,1)}, u32[]{:S(2)}, u32[]{:S(2)}) collective-permute-start(bf16[256,512]{1,0:T(8,128)(2,1)} %get-tuple-element.266), channel_id=1, source_target_pairs={{0,16},{8,24},{16,0},{24,8},{1,17},{9,25},{17,1},{25,9},{2,18},{10... | collective-permute-start | bytes 786440 | tf_op jit(solution)/shard_map/ppermute | solution.py:1019
  379.9 34.8 %collective-permute-start.37 = (bf16[256,512]{1,0:T(8,128)(2,1)}, bf16[256,512]{1,0:T(8,128)(2,1)}, u32[]{:S(2)}, u32[]{:S(2)}) collective-permute-start(bf16[256,512]{1,0:T(8,128)(2,1)} %get-tuple-element.268), channel_id=1, source_target_pairs={{0,8},{8,16},{16,24},{24,0},{1,9},{9,17},{17,25},{25,1},{2,10},{10... | collective-permute-start | bytes 786440 | tf_op jit(solution)/shard_map/ppermute | solution.py:1019
  381.1 54.3 %collective-permute-start.34 = (bf16[2,2,272,1152]{3,2,1,0:T(8,128)(2,1)}, bf16[2,2,272,1152]{3,2,1,0:T(8,128)(2,1)}, u32[]{:S(2)}, u32[]{:S(2)}) collective-permute-start(bf16[2,2,272,1152]{3,2,1,0:T(8,128)(2,1)} %get-tuple-element.260), channel_id=1, source_target_pairs={{0,2},{1,3},{2,0},{3,1},{4,6},{5,7},{6,4},{7,5},{8,10},{9,11},{10,... | collective-permute-start | bytes 7520264 | tf_op jit(solution)/shard_map/ppermute | solution.py:1010
  421.1 42.3 %collective-permute-start.42 = (bf16[1024,256]{1,0:T(8,128)(2,1)}, bf16[1024,256]{1,0:T(8,128)(2,1)S(1)}, u32[]{:S(2)}, u32[]{:S(2)}) collective-permute-start(bf16[1024,256]{1,0:T(8,128)(2,1)} %get-tuple-element.336), channel_id=1, source_target_pairs={{0,8},{8,16},{16,24},{24,0},{1,9},{9,17},{17,25},{25,1},{2,10},{10... | collective-permute-start | bytes 1572872 | tf_op jit(solution)/shard_map/ppermute | solution.py:1019
  423.5 45.5 %collective-permute-start.43 = (bf16[1024,256]{1,0:T(8,128)(2,1)}, bf16[1024,256]{1,0:T(8,128)(2,1)}, u32[]{:S(2)}, u32[]{:S(2)}) collective-permute-start(bf16[1024,256]{1,0:T(8,128)(2,1)} %get-tuple-element.334), channel_id=1, source_target_pairs={{0,16},{8,24},{16,0},{24,8},{1,17},{9,25},{17,1},{25,9},{2,18},{10... | collective-permute-start | bytes 1572872 | tf_op jit(solution)/shard_map/ppermute | solution.py:1019
  424.3 44.7 %collective-permute-start.44 = (bf16[1024,256]{1,0:T(8,128)(2,1)}, bf16[1024,256]{1,0:T(8,128)(2,1)}, u32[]{:S(2)}, u32[]{:S(2)}) collective-permute-start(bf16[1024,256]{1,0:T(8,128)(2,1)} %get-tuple-element.335), channel_id=1, source_target_pairs={{0,24},{8,0},{16,8},{24,16},{1,25},{9,1},{17,9},{25,17},{2,26},{10... | collective-permute-start | bytes 1572872 | tf_op jit(solution)/shard_map/ppermute | solution.py:1019
  438.6 37.2 %collective-permute-start.33 = (bf16[1,2,272,1152]{3,2,1,0:T(8,128)(2,1)}, bf16[1,2,272,1152]{3,2,1,0:T(8,128)(2,1)}, u32[]{:S(2)}, u32[]{:S(2)}) collective-permute-start(bf16[1,2,272,1152]{3,2,1,0:T(8,128)(2,1)} %get-tuple-element.333), channel_id=1, source_target_pairs={{0,2},{1,3},{2,0},{3,1},{4,6},{5,7},{6,4},{7,5},{8,10},{9,11},{10,... | collective-permute-start | bytes 3760136 | tf_op jit(solution)/shard_map/ppermute | solution.py:1010
  (82 other events, 1416.4 us)
Sparse Core Ops, SparseCore 0:
  24.3 47.2 all-gather.1
  529.4 41.6 reduce-scatter.1

commit v4 on v3

--- a/solution.py
+++ b/solution.py
@@ -365,7 +365,7 @@
     return scale * (grad - result * jnp.mean(grad * result, axis=1, keepdims=True))
 
 
-def pack_kernel(core_ref, up_ref, down_ref, out_ref, qkv_ref, mine_ref, theirs_ref, q_ref):
+def pack_kernel(core_ref, up_ref, down_ref, out_ref, mine_ref, theirs_ref):
     half = up_ref.shape[2] // 2
     low = core_ref[0] == 0
     down = down_ref[...].astype(bf16).T
@@ -377,23 +377,19 @@
             ).astype(bf16)
         ref[:, 2 * half : 3 * half] = jnp.where(first, down[:, :half], down[:, half:])
         ref[:, 3 * half :] = out
-    cols = qkv_ref.shape[2]
-    for c in range(3):
-        q_ref[:, c * cols : (c + 1) * cols] = qkv_ref[:, c, :].astype(bf16)
-
-
-def pack(core, w_up, w_down, w_out, w_qkv):
+
+
+def pack(core, w_up, w_down, w_out):
     span, _, hid = w_up.shape
-    cols = w_qkv.shape[2]
+    cols = w_out.shape[0]
     vmem = pl.BlockSpec(memory_space=pltpu.VMEM)
     return pl.pallas_call(
         pack_kernel,
-        in_specs=[pl.BlockSpec(memory_space=pltpu.SMEM)] + [vmem] * 4,
-        out_specs=[vmem] * 3,
-        out_shape=[jax.ShapeDtypeStruct((span, 3 * hid // 2 + cols), bf16)] * 2
-        + [jax.ShapeDtypeStruct((span, 3 * cols), bf16)],
+        in_specs=[pl.BlockSpec(memory_space=pltpu.SMEM)] + [vmem] * 3,
+        out_specs=[vmem] * 2,
+        out_shape=[jax.ShapeDtypeStruct((span, 3 * hid // 2 + cols), bf16)] * 2,
         compiler_params=params(),
-    )(core, w_up, w_down, w_out, w_qkv)
+    )(core, w_up, w_down, w_out)
 
 
 def place_of(r, chip, chunk):
@@ -775,8 +771,8 @@
     ha_ref, hb_ref = refs[:2]
     refs = refs[2:]
     if more:
-        oa_ref, ob_ref, ya_ref, yb_ref, extra_ref = refs[:5]
-        refs = refs[5:]
+        oa_ref, ob_ref, ya_ref, yb_ref, gs_ref, g1_ref, g2_ref = refs[:7]
+        refs = refs[7:]
     val_ref, *outs = refs[:5]
     turned = refs[5]
     rows = ha_ref.shape[0]
@@ -789,6 +785,14 @@
         if more:
             refs[6][:, :rows] = oa_ref[...].T
             refs[6][:, rows:] = ob_ref[...].T
+
+    if more:
+        size = outs[0].shape[2]
+        fill = lambda row: jnp.concatenate([row, jnp.zeros((1, size - row.shape[1]), f32)], axis=1)
+        line = lax.broadcasted_iota(jnp.int32, (EXTRA, size), 0)
+        units = fill(jnp.concatenate([gs_ref[0:1, :], gs_ref[1:2, :]], axis=1))
+        steps = fill(jnp.concatenate([g1_ref[0:1, :], g2_ref[0:1, :]], axis=1))
+        extra = jnp.where(line == 0, units, jnp.where(line == 1, steps, 0.0)).astype(bf16)
 
     for side in range(2):
 
@@ -804,7 +808,7 @@
                         ref[j, :chunk, size:] = (
                             dot(refs[6][at, :rows], ya_ref[...]) + dot(refs[6][at, rows:], yb_ref[...])
                         ).astype(bf16)
-                        ref[j, chunk:, :] = extra_ref[...].astype(bf16)
+                        ref[j, chunk:, :] = extra
 
 
 def weight_grads(place, sends, keeps, chips, hs, value, os=None, ys=None, extra=None):
@@ -843,12 +847,16 @@
     scratch = [pltpu.VMEM((width, 2 * rows), bf16)]
     if more:
         slot = lambda k, p: lax.rem(p[0] + parts - k, parts)
-        ins += [*os, ys[0], ys[1], extra]
+        cols = ys[0].shape[2]
+        part = pl.BlockSpec((8, cols), lambda k, p: (0, slot(k, p) ^ p[1]))
+        ins += [*os, ys[0], ys[1], *extra]
         in_specs += [whole] * 2
         in_specs += [
             pl.BlockSpec((None, rows, hc), lambda k, p: (slot(k, p), 0, p[2])),
             pl.BlockSpec((None, rows, hc), lambda k, p: (slot(k, p), 0, 0)),
-            pl.BlockSpec((None, EXTRA, size + hc), lambda k, p: (k, 0, 0)),
+            pl.BlockSpec((None, 8, size // 2), lambda k, p: (k, 0, 0)),
+            part,
+            part,
         ]
         scratch = scratch * 2
     ins.append(value)
@@ -1041,18 +1049,20 @@
         return [value]
 
     tokens = [layer_input, onward(layer_input)]
-    mine, theirs, qkv_own = pack(core_s, w_up, w_down, w_out, w_qkv)
+    mine, theirs = pack(core_s, w_up, w_down, w_out)
+    qkv_own = after(w_qkv, mine).reshape(span, 3 * cols).astype(bf16)
     qkv_full = lax.all_gather(qkv_own, "batch", axis=0, tiled=True)
     theirs = swap_core(theirs)
     packet = jnp.concatenate([pick((mine, theirs), core), pick((theirs, mine), core)], axis=0)
     hops = [packet, onward(packet)]
     slots = [spread(packet)]
-    tokens[1], hops[1], places, s_uv, alpha_attn, alpha_mlp, *last = lax.optimization_barrier(
-        (tokens[1], hops[1], positions, s_uv, alpha_attn, alpha_mlp, *slots[0])
+    suv_own = after(pick((s_uv[:, :half], s_uv[:, half:]), core), tokens[1])
+    suv = jnp.stack([suv_own] + [onward(suv_own, n) for n in range(1, nz)])
+    tokens[1], hops[1], places, suv, alpha_attn, alpha_mlp, *last = lax.optimization_barrier(
+        (tokens[1], hops[1], positions, suv, alpha_attn, alpha_mlp, *slots[0])
     )
     slots[0] = list(last)
 
-    suv_own = pick((s_uv[:, :half], s_uv[:, half:]), core)
     freqs = jnp.exp(
         (jnp.arange(128) % (HEAD_DIM // 2)).astype(f32) * (-2.0 * math.log(10000.0) / HEAD_DIM)
     )
@@ -1071,21 +1081,20 @@
         tokens.append(onward(tokens[-1]))
         if n < nz - 1:
             hops.append(onward(hops[-1]))
-            tokens[-1], hops[-1], cosine, sine, ones, attn_gain, mlp_gain, suv_own, *last = (
+            tokens[-1], hops[-1], cosine, sine, ones, attn_gain, mlp_gain, *last = (
                 lax.optimization_barrier(
-                    (tokens[-1], hops[-1], cosine, sine, ones, attn_gain, mlp_gain, suv_own, *slots[-1])
+                    (tokens[-1], hops[-1], cosine, sine, ones, attn_gain, mlp_gain, *slots[-1])
                 )
             )
             slots[-1] = list(last)
     last_hop, tokens[-1] = lax.optimization_barrier((hops[-1], tokens[-1]))
     hops.append(onward(last_hop))
-    suv = jnp.stack([suv_own] + [onward(suv_own, n) for n in range(1, nz)])
 
     blocks = rows // 512
     middle = blocks // 2
     tokens_full, q, k, v, rho = qkv_project(place, tokens, qkv_full, cosine, sine, gain, ones)
     y_a, logs_a = attn_fwd(is_long, q, k, v, 0, middle)
-    q_b, suv, hops[-1], *last = lax.optimization_barrier((after(q, y_a), suv, hops[-1], *slots[-1]))
+    q_b, hops[-1], *last = lax.optimization_barrier((after(q, y_a), hops[-1], *slots[-1]))
     slots[-1] = list(last)
     slots.append(spread(hops[-1]))
     y_b, logs_b = attn_fwd(is_long, q_b, k, v, middle, blocks - middle)
@@ -1102,6 +1111,9 @@
             ]
         )
         start = relative(start)
+    y_mine = jnp.concatenate([y_one, y_two], axis=1)
+    y_got = swap_core(lax.dynamic_slice_in_dim(y_mine, (1 - core) * hc, hc, 2))
+    y_one, y_two, y_mine, y_got = lax.optimization_barrier((y_one, y_two, y_mine, y_got))
     hA, h1, h_own, stat = attn_out(place, y_one, y_two, slots, start, attn_gain, chips, fast)
     h_got = swap_core(h_own)
     cot = after(cotangent, h_own).reshape(2, nz, own // 2, cols).transpose(1, 0, 2, 3)
@@ -1124,56 +1136,59 @@
     def second(kept, sent):
         found, sends = [], []
         for order, left, got, keep in zip(orders, kept_at, sent, kept):
+            terms = [keep, got]
             for bit in order[1:]:
                 send_at = [n for n, r in enumerate(left) if r & bit]
                 keep_at = [n for n, r in enumerate(left) if not r & bit]
                 left = [left[n] for n in keep_at]
-                cut = lambda v, at: jnp.concatenate([v[n : n + 1] for n in at], axis=0).astype(f32)
-                send = (cut(keep, send_at) + cut(got, send_at)).astype(bf16)
-                keep = cut(keep, keep_at) + cut(got, keep_at)
-                got = swap_chip(send, bit)
+                cut = lambda v, at: jnp.concatenate([v[n : n + 1] for n in at], axis=0)
+                send = sum(cut(t, send_at).astype(f32) for t in terms).astype(bf16)
+                terms = [cut(t, keep_at) for t in terms] + [swap_chip(send, bit)]
                 sends.append(send)
-            found.append((keep, got))
+            found.append(terms)
         return found, sends
 
     def slot_sums(found):
-        return [(keep[0, n] + got[0, n].astype(f32)) for keep, got in found for n in range(nz // 2)]
+        return [sum(t[0, n].astype(f32) for t in terms) for terms in found for n in range(nz // 2)]
+
+    def wait_last(found, *others):
+        return [terms[:-1] + [after(terms[-1], *others)] for terms in found]
 
     down_made, down_kept = weight_grads(place, sent_at, kept_at, chips, (d_own, d_got), act)
     down_sent = [swap_chip(one, order[0]) for one, order in zip(down_made, orders)]
     d_own, d_got, *_ = lax.optimization_barrier((d_own, d_got, *down_made))
     duv, dh_own, dh_other, gsuv = mlp_bwd(d_own, d_got, slots, uv, suv)
     dh_got = swap_core(dh_other)
-    dh_own, hidden, *down_sent = lax.optimization_barrier((dh_own, hidden, *down_sent))
+    down_sent = [after(one, dh_other) for one in down_sent]
+    down_part, down_next = second(down_kept, down_sent)
+    dh_own, hidden, *_ = lax.optimization_barrier((dh_own, hidden, *down_next))
     do_own, through, ga_attn, dy_a, dy_b = first_back(
         place, dh_own, dh_got, base, h1, hA, start, stat, attn_gain, slots, chips, fast, cols
     )
     dy_b = exchange(dy_b)
     do_got = swap_core(do_own)
-    y_mine = jnp.concatenate([y_one, y_two], axis=1)
-    y_got = swap_core(lax.dynamic_slice_in_dim(after(y_mine, h_own), (1 - core) * hc, hc, 2))
-    down_sent = [after(one, do_own) for one in down_sent]
-    down_part, down_next = second(down_kept, down_sent)
-
-    alphas = [relative(ga_attn[0:1]), relative(ga_mlp[0:1])]
-    extra = []
-    wide = 2 * half + hc
-    fill = lambda r: jnp.pad(r, ((0, 0), (0, wide - r.shape[1])))
-    for n in range(nz):
-        at = ((z - n) % nz) * cols
-        line = jnp.concatenate([lax.dynamic_slice_in_dim(g, at, cols, 1) for g in alphas], axis=1)
-        first = gsuv[n, :2].reshape(1, 2 * half)
-        extra.append(jnp.pad(jnp.concatenate([fill(first), fill(line)]), ((0, EXTRA - 2), (0, 0))))
-    extra = jnp.stack(extra)
-    h_own, *_ = lax.optimization_barrier((h_own, *down_next))
+
+    extra = (gsuv, ga_attn, ga_mlp)
+    if not fast:
+        alphas = [relative(ga_attn[0:1]), relative(ga_mlp[0:1])]
+        extra = []
+        wide = 2 * half + hc
+        fill = lambda r: jnp.pad(r, ((0, 0), (0, wide - r.shape[1])))
+        for n in range(nz):
+            at = ((z - n) % nz) * cols
+            line = [lax.dynamic_slice_in_dim(g, at, cols, 1) for g in alphas]
+            lines = [gsuv[n, :2].reshape(1, 2 * half), jnp.concatenate(line, axis=1)]
+            lines = jnp.concatenate([fill(r) for r in lines])
+            extra.append(jnp.pad(lines, ((0, EXTRA - 2), (0, 0))))
+        extra = jnp.stack(extra)
     up_made, up_kept = weight_grads(
         place, sent_at, kept_at, chips, (h_own, h_got), duv, (do_own, do_got), (y_mine, y_got), extra
     )
-    down_keep, down_got = [p[0] for p in down_part], [p[1] for p in down_part]
-    down_got = [after(one, *up_kept) for one in down_got]
-    down_slots = slot_sums(list(zip(down_keep, down_got)))
-    dy_b, dy_a, *both = lax.optimization_barrier((dy_b, dy_a, *up_made, *down_slots))
-    up_made, down_slots = both[: len(up_made)], both[len(up_made) :]
+    down_part = wait_last(down_part, *up_kept)
+    down_last = [terms[-1] for terms in down_part]
+    dy_b, dy_a, *both = lax.optimization_barrier((dy_b, dy_a, *up_made, *down_last))
+    up_made, down_last = both[: len(up_made)], both[len(up_made) :]
+    down_slots = slot_sums([t[:-1] + [last] for t, last in zip(down_part, down_last)])
     down_along = [onward(down_slots[n].astype(bf16), nz - n) for n in range(1, nz)]
     up_sent = [swap_chip(one, order[0]) for one, order in zip(up_made, orders)]
 
@@ -1197,24 +1212,28 @@
         return lax.dynamic_update_slice_in_dim(part.astype(bf16), here.astype(bf16), mine_at, 0)
 
     dqkv_b, dk_part, dy_a = lax.optimization_barrier((dqkv_b, dk_part, dy_a))
-    part_b = input_part(dqkv_b, 1)
-    cut = lambda n: lax.dynamic_slice_in_dim(part_b, ((z + n) % nz) * cols, cols, 1)
-    part_cuts = [cut(n) for n in range(nz)]
+    part_b = jnp.einsum(
+        "tn,zcn->ztc", dqkv_b, qkv_full.reshape(nz, cols, 3 * cols), preferred_element_type=f32
+    )
+    mine_at = z * (own // 2)
+    here = lax.dynamic_slice_in_dim(part_b, mine_at, own // 2, 1)
+    here = here + through[own // 2 :].reshape(own // 2, nz, cols).transpose(1, 0, 2)
+    part_b = lax.dynamic_update_slice_in_dim(part_b.astype(bf16), here.astype(bf16), mine_at, 1)
     down_along = [after(one, dqkv_b) for one in down_along]
     sum_down_t = down_slots[0] + sum(one.astype(f32) for one in down_along)
     up_part, up_next = second(up_kept, [after(one, dqkv_b) for one in up_sent])
-    part_got = [onward(part_cuts[n], n) for n in range(1, nz)]
-    dk_part, dy_a, *_ = lax.optimization_barrier((dk_part, dy_a, *up_next, *part_cuts, sum_down_t))
+    part_got = exchange(part_b)
+    dk_part, dy_a, *_ = lax.optimization_barrier((dk_part, dy_a, *up_next, part_b, sum_down_t))
     dqkv_a, sqk_a = attn_bwd(*common(dy_a, y_a, logs_a), 0, middle, [dk_part, dv_part])
-    part_got = [after(one, dqkv_a) for one in part_got]
-    input_b = part_cuts[0].astype(f32) + sum(one.astype(f32) for one in part_got)
-    up_part = [(keep, after(got, dqkv_a)) for keep, got in up_part]
+    input_b = jnp.sum(after(part_got, dqkv_a).astype(f32), axis=0)
+    up_part = wait_last(up_part, dqkv_a)
     part_a = input_part(dqkv_a, 0)
     up_slots = slot_sums(up_part)
     passed = onward(up_slots[1].astype(bf16))
     for n in range(2, nz):
+        if n == nz - 1:
+            passed, part_a = lax.optimization_barrier((passed, part_a))
         passed = onward((up_slots[n] + passed.astype(f32)).astype(bf16))
-    passed, part_a = lax.optimization_barrier((passed, part_a))
     sum_up_t = up_slots[0] + passed.astype(f32)
     input_a = lax.psum_scatter(part_a, "head", scatter_dimension=1, tiled=True)
     input_grad = jnp.concatenate([input_a.astype(f32), input_b], axis=0)
@@ -1248,7 +1267,7 @@
         return [pick((here, there), core), pick((there, here), core)]
 
     join = lambda halves, at, size: [p[:span, at : at + size] for p in halves]
-    halves = both_halves(sum_down_t)
+    halves = both_halves(after(sum_down_t, part_a))
     down_new = adam_tall(w_down, jnp.concatenate(join(halves, 0, half), axis=1), moment_down, square_down)
     halves = both_halves(sum_up_t)
     grad_up = jnp.concatenate(join(halves, 0, half) + join(halves, half, half), axis=1)

time: 591 us -> 574 us (0.971)
  waiting for transfers between devices: 173 us -> 198 us
  Pallas kernels: 201 us -> 182 us
  blocking collectives: 14.5 us -> 0 us
    ppermute x18 -> x15, waiting for transfers between devices: 108 us -> 128 us  [onward(): return lax.ppermute(value, 'head', [(i, (i + k) % nz) for i in range(nz)])]
    add x8 -> x0, other arithmetic: 18 us -> none  [the longest x4 10.8 us: second(): keep = cut(keep, keep_at) + cut(got, keep_at)]
    all_to_all x1 -> x0, blocking collectives: 14.5 us -> none  [exchange(): return lax.all_to_all(value, 'head', split_axis=0, concat_axis=0)]
    convert_element_type x0 -> x7, other arithmetic: none -> 13 us  [the longest x4 7.96 us: second(): send = sum((cut(t, send_at).astype(f32) for t in terms)).astype(bf16)]
    pallas_call x2, Pallas kernels: 44.9 us -> 33.2 us  [attn_bwd(): pl.pallas_call(inner, grid_spec=pltpu.PrefetchScalarGridSpec(num_scalar_p...]
    ppermute x18 -> x15, starting transfers between devices: 25.4 us -> 13.8 us  [onward(): return lax.ppermute(value, 'head', [(i, (i + k) % nz) for i in range(nz)])]
    all_to_all x5 -> x7, waiting for transfers between devices: 4.04 us -> 15.2 us  [exchange(): return lax.all_to_all(value, 'head', split_axis=0, concat_axis=0)]
    all_to_all x5 -> x7, starting transfers between devices: 23.2 us -> 32.3 us  [exchange(): return lax.all_to_all(value, 'head', split_axis=0, concat_axis=0)]
  transfers between devices with their start and end apart: 60 -> 59, of which waited for: 24 -> 25; matrix products, arithmetic and copies ran while one was open for 14% -> 15% of each run, Pallas kernels for 31% -> 25%
where the time goes in v4:
time: 574 us; the launch traced here: 568 us
  waiting for transfers between devices  198 us (34%)
  Pallas kernels  182 us (32%)
  starting transfers between devices  77.2 us (13%)
  other arithmetic  47.3 us (8%)
  local copies, waits for them, and re-layouts  35.2 us (6%)
  between operations  16.1 us (3%)
  matrix products  12.3 us (2%)
    ppermute x15, waiting for transfers between devices, onward(): return lax.ppermute(value, 'head', [(i, (i + k) % nz) for i in range(nz)])  128 us
    ppermute x35, waiting for transfers between devices, swap_batch(): return lax.ppermute(value, 'batch', [(i, i ^ bit) for i in range(nb)])  45.9 us
    pallas_call x2, Pallas kernels, attn_bwd(): pl.pallas_call(inner, grid_spec=pltpu.PrefetchScalarGridSpec(num_scalar_p...  33.2 us
    all_to_all x7, starting transfers between devices, exchange(): return lax.all_to_all(value, 'head', split_axis=0, concat_axis=0)  32.3 us
    ppermute x35, starting transfers between devices, swap_batch(): return lax.ppermute(value, 'batch', [(i, i ^ bit) for i in range(nb)])  31.1 us
    pallas_call x2, Pallas kernels, weight_grads(): pl.pallas_call(functools.partial(grad_kernel, orders=(lists[:2], lists[2:...  29.4 us
    pallas_call x1, Pallas kernels, mlp_bwd(): pl.pallas_call(functools.partial(mlp_bwd_kernel, half=half, counts=[len(s...  26.4 us
    pallas_call x1, Pallas kernels, mlp_fwd(): pl.pallas_call(functools.partial(mlp_fwd_kernel, half=half, counts=[len(s...  21.1 us
  transfers between devices with their start and end apart: 59, of which 25 were waited for; matrix products, arithmetic and copies ran while one was open for 15% of the time, Pallas kernels for 25%

profile of v4, /device:TPU:0, one launch (start us, length us, event | category | flops | bytes accessed | tf_op | source)
XLA Modules:
  0.0 568.1 jit_solution(7252565753760710384)
XLA Ops:
  7.2 4.2 shard_map.354
  22.3 18.5 %collective-permute-done.refs_1_ = bf16[2048,256]{1,0:T(8,128)(2,1)} collective-permute-done((bf16[2048,256]{1,0:T(8,128)(2,1)}, bf16[2048,256]{1,0:T(8,128)(2,1)}, u32[]{:S(2)}, u32[]{:S(2)}) %collective-permute-start) | collective-permute-done | bytes 1048608 | tf_op jit(solution)/shard_map/ppermute | solution.py:1027
  40.9 19.5 %collective-permute-done.3 = f32[2,512]{1,0:T(2,128)S(1)} collective-permute-done((f32[2,512]{1,0:T(2,128)S(1)}, f32[2,512]{1,0:T(2,128)S(1)}, u32[]{:S(2)}, u32[]{:S(2)}) %collective-permute-start.3) | collective-permute-done | bytes 4128 | tf_op jit(solution)/shard_map/ppermute | solution.py:1027
  76.0 5.5 fusion.11
  81.6 32.9 %collective-permute-done.10.refs_8_ = bf16[256,1792]{1,0:T(8,128)(2,1)} collective-permute-done((bf16[256,1792]{1,0:T(8,128)(2,1)S(1)}, bf16[256,1792]{1,0:T(8,128)(2,1)}, u32[]{:S(2)}, u32[]{:S(2)}) %collective-permute-start.10) | collective-permute-done | bytes 917536 | tf_op jit(solution)/shard_map/ppermute | solution.py:1027
  119.8 21.1 %collective-permute-done.14.refs_3_ = bf16[2048,256]{1,0:T(8,128)(2,1)} collective-permute-done((bf16[2048,256]{1,0:T(8,128)(2,1)}, bf16[2048,256]{1,0:T(8,128)(2,1)}, u32[]{:S(2)}, u32[]{:S(2)}) %collective-permute-start.14) | collective-permute-done | bytes 1048608 | tf_op jit(solution)/shard_map/ppermute | solution.py:1027
  142.8 11.5 %shard_map.355 = (bf16[2048,1024]{1,0:T(8,128)(2,1)}, bf16[2048,256]{1,0:T(8,128)(2,1)}, bf16[2048,256]{1,0:T(8,128)(2,1)}, bf16[2048,256]{1,0:T(8,128)(2,1)}, f32[2048,128]{1,0:T(8,128)}) custom-call(s32[3]{0:T(128)} %pad_add_fusion.place_ref, bf16[2048,256]{1,0:T(8,128)(2,1)} %refs_0_.1, bf16[2048,256]{1,0:T(8,128)(2,1)} %collective-permute-done.refs_1_, ...), custom_call_target="tpu_custom_call" | custom-call | tf_op jit(solution)/shard_map/pallas_call | solution.py:103
  154.3 6.4 %shard_map.356 = (bf16[1024,256]{1,0:T(8,128)(2,1)}, f32[1024,128]{1,0:T(8,128)}) custom-call(s32[1]{0:T(128)S(6)} %convert_element_type.303.long_ref.r_0_, bf16[2048,256]{1,0:T(8,128)(2,1)} %get-tuple-element.195.q_ref.r_1_, bf16[2048,256]{1,0:T(8,128)(2,1)} %get-tuple-element.185.k_ref.r_2_.r_6_, bf16[2048,256]{1,0:T(8,128)(2,1)} %get-tuple-element.186.v_ref.r_7_), custom_call_target="tpu_custom_call" | custom-call | tf_op jit(solution)/shard_map/pallas_call | solution.py:194
  160.7 5.3 all-to-all-start
  166.0 6.8 %shard_map.357 = (bf16[1024,256]{1,0:T(8,128)(2,1)}, f32[1024,128]{1,0:T(8,128)}) custom-call(s32[1]{0:T(128)S(6)} %convert_element_type.303.long_ref.r_0_, bf16[2048,256]{1,0:T(8,128)(2,1)} %get-tuple-element.195.q_ref.r_1_, bf16[2048,256]{1,0:T(8,128)(2,1)} %get-tuple-element.185.k_ref.r_2_.r_6_, bf16[2048,256]{1,0:T(8,128)(2,1)} %get-tuple-element.186.v_ref.r_7_), custom_call_target="tpu_custom_call" | custom-call | tf_op jit(solution)/shard_map/pallas_call | solution.py:194
  188.2 7.0 %all-to-all-done.1.refs_17_ = bf16[4,256,256]{2,1,0:T(8,128)(2,1)} async-done(((bf16[4,256,256]{2,1,0:T(8,128)(2,1)}), bf16[4,256,256]{2,1,0:T(8,128)(2,1)}, u32[]{:S(2)}, u32[]{:S(2)}) %all-to-all-start.1) | async-done | bytes 524320 | tf_op jit(solution)/shard_map/all_to_all | solution.py:1030
  200.1 4.6 collective-permute-done.19.refs_13_
  207.7 15.1 %collective-permute-done.21.refs_15_ = bf16[256,1792]{1,0:T(8,128)(2,1)S(1)} collective-permute-done((bf16[256,1792]{1,0:T(8,128)(2,1)}, bf16[256,1792]{1,0:T(8,128)(2,1)S(1)}, u32[]{:S(2)}, u32[]{:S(2)}) %collective-permute-start.21) | collective-permute-done | bytes 917536 | tf_op jit(solution)/shard_map/ppermute | solution.py:1018
  223.7 6.7 %shard_map.358 = (f32[512,1024]{1,0:T(8,128)}, f32[512,1024]{1,0:T(8,128)}, bf16[512,1024]{1,0:T(8,128)(2,1)}, f32[512,128]{1,0:T(8,128)}) custom-call(s32[3]{0:T(128)} %pad_add_fusion.place_ref, bf16[256,1792]{1,0:T(8,128)(2,1)} %copy-done, bf16[256,1792]{1,0:T(8,128)(2,1)} %copy-done.3, bf16[256,1792]{1,0:T(8,128)(2,1)} %collective-permute-done.7.refs_2_, ...), custom_call_target="tpu_custom_call" | custom-call | tf_op jit(solution)/shard_map/pallas_call | solution.py:473
  231.6 4.8 all-to-all-start.2
  237.3 21.1 %shard_map.359 = (bf16[4,1024,512]{2,1,0:T(8,128)(2,1)}, bf16[4,1024,1024]{2,1,0:T(8,128)(2,1)}, f32[512,1024]{1,0:T(8,128)}, bf16[512,1024]{1,0:T(8,128)(2,1)}) custom-call(bf16[256,1792]{1,0:T(8,128)(2,1)} %copy-done, bf16[256,1792]{1,0:T(8,128)(2,1)} %copy-done.3, bf16[256,1792]{1,0:T(8,128)(2,1)} %collective-permute-done.7.refs_2_, ...), custom_call_target="tpu_custom_call" | custom-call | tf_op jit(solution)/shard_map/pallas_call | solution.py:666
  264.1 6.4 %shard_map.360 = (bf16[4,512,256]{2,1,0:T(8,128)(2,1)}, bf16[512,1024]{1,0:T(8,128)(2,1)}, f32[512,1024]{1,0:T(8,128)}, f32[8,1024]{1,0:T(8,128)}) custom-call(s32[3]{0:T(128)} %pad_add_fusion.place_ref, f32[512,1024]{1,0:T(8,128)} %get-tuple-element.205.own_ref, bf16[512,1024]{1,0:T(8,128)(2,1)} %copy-done.30, ...), custom_call_target="tpu_custom_call" | custom-call | tf_op jit(solution)/shard_map/pallas_call | solution.py:519
  274.4 10.0 %shard_map.361 = (bf16[2,2,256,512]{3,2,1,0:T(8,128)(2,1)}, bf16[2,2,256,512]{3,2,1,0:T(8,128)(2,1)}, bf16[2,2,256,512]{3,2,1,0:T(8,128)(2,1)}, bf16[2,2,256,512]{3,2,1,0:T(8,128)(2,1)}) custom-call(s32[3]{0:T(128)} %pad_add_fusion.place_ref, bf16[512,1024]{1,0:T(8,128)(2,1)} %get-tuple-element.214.refs_0_.refs_16_, bf16[512,1024]{1,0:T(8,128)(2,1)} %copy-done.15, ...), custom_call_target="tpu_custom_call" | custom-call | tf_op jit(solution)/shard_map/pallas_call | solution.py:868
  290.7 26.4 %shard_map.362 = (bf16[4,1024,1024]{2,1,0:T(8,128)(2,1)}, f32[512,1024]{1,0:T(8,128)}, bf16[512,1024]{1,0:T(8,128)(2,1)}, f32[4,8,512]{2,1,0:T(8,128)}) custom-call(bf16[256,1792]{1,0:T(8,128)(2,1)} %copy-done, bf16[256,1792]{1,0:T(8,128)(2,1)} %copy-done.3, bf16[256,1792]{1,0:T(8,128)(2,1)} %collective-permute-done.7.refs_2_, ...), custom_call_target="tpu_custom_call" | custom-call | tf_op jit(solution)/shard_map/pallas_call | solution.py:736
  320.2 11.1 %shard_map.363 = (bf16[512,1024]{1,0:T(8,128)(2,1)}, bf16[512,1024]{1,0:T(8,128)(2,1)}, f32[8,1024]{1,0:T(8,128)}, bf16[4,256,256]{2,1,0:T(8,128)(2,1)}, bf16[4,256,256]{2,1,0:T(8,128)(2,1)}) custom-call(s32[3]{0:T(128)} %pad_add_fusion.place_ref, bf16[256,1792]{1,0:T(8,128)(2,1)} %copy-done, bf16[256,1792]{1,0:T(8,128)(2,1)} %copy-done.3, ...), custom_call_target="tpu_custom_call" | custom-call | tf_op jit(solution)/shard_map/pallas_call | solution.py:579
  331.5 5.5 all-to-all-start.4
  339.4 19.4 %shard_map.364 = (bf16[2,2,272,1152]{3,2,1,0:T(8,128)(2,1)}, bf16[2,2,272,1152]{3,2,1,0:T(8,128)(2,1)}, bf16[2,2,272,1152]{3,2,1,0:T(8,128)(2,1)}, bf16[2,2,272,1152]{3,2,1,0:T(8,128)(2,1)}) custom-call(s32[3]{0:T(128)} %pad_add_fusion.place_ref, bf16[512,1024]{1,0:T(8,128)(2,1)} %get-tuple-element.203.refs_16_.refs_0_, bf16[512,1024]{1,0:T(8,128)(2,1)} %copy-done.14, ...), custom_call_target="tpu_custom_call" | custom-call | tf_op jit(solution)/shard_map/pallas_call | solution.py:868
  366.0 5.2 all-to-all-start.5
  383.1 16.6 %shard_map.365 = (bf16[1024,768]{1,0:T(8,128)(2,1)}, f32[1024,256]{1,0:T(8,128)}, f32[1024,256]{1,0:T(8,128)}, f32[8,256]{1,0:T(8,128)}) custom-call(s32[1]{0:T(128)S(6)} %convert_element_type.303.long_ref.r_0_, bf16[2048,256]{1,0:T(8,128)(2,1)} %get-tuple-element.195.q_ref.r_1_, bf16[2048,256]{1,0:T(8,128)(2,1)} %get-tuple-element.185.k_ref.r_2_.r_6_, ...), custom_call_target="tpu_custom_call" | custom-call | tf_op jit(solution)/shard_map/pallas_call | solution.py:341
  399.8 7.6 %collective-permute-done.36 = bf16[256,512]{1,0:T(8,128)(2,1)S(1)} collective-permute-done((bf16[256,512]{1,0:T(8,128)(2,1)}, bf16[256,512]{1,0:T(8,128)(2,1)S(1)}, u32[]{:S(2)}, u32[]{:S(2)}) %collective-permute-start.36) | collective-permute-done | bytes 262176 | tf_op jit(solution)/shard_map/ppermute | solution.py:1027
  422.7 8.4 %collective-permute-done.34 = bf16[2,2,272,1152]{3,2,1,0:T(8,128)(2,1)} collective-permute-done((bf16[2,2,272,1152]{3,2,1,0:T(8,128)(2,1)}, bf16[2,2,272,1152]{3,2,1,0:T(8,128)(2,1)}, u32[]{:S(2)}, u32[]{:S(2)}) %collective-permute-start.34) | collective-permute-done | bytes 2506784 | tf_op jit(solution)/shard_map/ppermute | solution.py:1018
  436.4 16.6 %shard_map.366 = (bf16[1024,768]{1,0:T(8,128)(2,1)}, f32[8,256]{1,0:T(8,128)}) custom-call(s32[1]{0:T(128)S(6)} %convert_element_type.303.long_ref.r_0_, bf16[2048,256]{1,0:T(8,128)(2,1)} %get-tuple-element.195.q_ref.r_1_, bf16[2048,256]{1,0:T(8,128)(2,1)} %get-tuple-element.185.k_ref.r_2_.r_6_, bf16[1024,256]{1,0:T(8,128)(2,1)} %bitcast.102, ...), custom_call_target="tpu_custom_call" | custom-call | tf_op jit(solution)/shard_map/pallas_call | solution.py:341
  453.0 5.4 fusion.4
  468.2 11.8 %collective-permute-done.39 = bf16[272,1152]{1,0:T(8,128)(2,1)S(1)} collective-permute-done((bf16[272,1152]{1,0:T(8,128)(2,1)S(1)}, bf16[272,1152]{1,0:T(8,128)(2,1)S(1)}, u32[]{:S(2)}, u32[]{:S(2)}) %collective-permute-start.39) | collective-permute-done | bytes 626720 | tf_op jit(solution)/shard_map/ppermute | solution.py:1027
  487.4 11.4 %collective-permute-done.40 = bf16[272,1152]{1,0:T(8,128)(2,1)} collective-permute-done((bf16[272,1152]{1,0:T(8,128)(2,1)}, bf16[272,1152]{1,0:T(8,128)(2,1)}, u32[]{:S(2)}, u32[]{:S(2)}) %collective-permute-start.40) | collective-permute-done | bytes 626720 | tf_op jit(solution)/shard_map/ppermute | solution.py:1027
  522.8 5.7 shard_map.369
  549.4 8.8 %reduce-scatter.2.cloned.1.call-done = bf16[1024,256]{1,0:T(8,128)(2,1)} async-done(((bf16[1024,1024]{1,0:T(8,128)(2,1)}), bf16[1024,256]{1,0:T(8,128)(2,1)}) %reduce-scatter.2.cloned.1.call-update) | async-done | bytes 524304 | tf_op jit(solution)/shard_map/reduce_scatter | solution.py:1238
  (317 shorter events, 184.8 us)
Async XLA Ops:
  7.2 135.6 %all-gather.2.cloned.1.call-start = ((), (), s32[]{:S(2)}) async-start(), calls=%async_computation.8 | async-start | bytes 1769472 | tf_op jit(solution)/shard_map/all_gather | solution.py:1054
  11.9 28.9 %collective-permute-start = (bf16[2048,256]{1,0:T(8,128)(2,1)}, bf16[2048,256]{1,0:T(8,128)(2,1)}, u32[]{:S(2)}, u32[]{:S(2)}) collective-permute-start(bf16[2048,256]{1,0:T(8,128)(2,1)} %refs_0_.1), channel_id=1, source_target_pairs={{0,8},{8,16},{16,24},{24,0},{1,9},{9,17},{17,25},{25,1},{2,10},{10... | collective-permute-start | bytes 3145736 | tf_op jit(solution)/shard_map/ppermute | solution.py:1027
  15.7 53.3 %collective-permute-start.2 = (bf16[256,1792]{1,0:T(8,128)(2,1)S(1)}, bf16[256,1792]{1,0:T(8,128)(2,1)S(1)}, u32[]{:S(2)}, u32[]{:S(2)}) collective-permute-start(bf16[256,1792]{1,0:T(8,128)(2,1)S(1)} %pad_maximum_fusion.2.refs_0_), channel_id=1, source_target_pairs={{0,8},{8,16},{16,24},{24,0},{1,9},{9,17},{17,25},{25,1},{2,10},{10... | collective-permute-start | bytes 2752520 | tf_op jit(solution)/shard_map/ppermute | solution.py:1027
  17.8 51.3 %collective-permute-start.6 = (bf16[256,1792]{1,0:T(8,128)(2,1)S(1)}, bf16[256,1792]{1,0:T(8,128)(2,1)S(1)}, u32[]{:S(2)}, u32[]{:S(2)}) collective-permute-start(bf16[256,1792]{1,0:T(8,128)(2,1)S(1)} %pad_maximum_fusion.2.refs_0_), channel_id=1, source_target_pairs={{0,2},{1,3},{2,0},{3,1},{4,6},{5,7},{6,4},{7,5},{8,10},{9,11},{10,... | collective-permute-start | bytes 2752520 | tf_op jit(solution)/shard_map/ppermute | solution.py:1018
  19.3 49.8 %collective-permute-start.7 = (bf16[256,1792]{1,0:T(8,128)(2,1)S(1)}, bf16[256,1792]{1,0:T(8,128)(2,1)}, u32[]{:S(2)}, u32[]{:S(2)}) collective-permute-start(bf16[256,1792]{1,0:T(8,128)(2,1)S(1)} %pad_maximum_fusion.2.refs_0_), channel_id=1, source_target_pairs={{0,4},{1,5},{2,6},{3,7},{4,0},{5,1},{6,2},{7,3},{8,12},{9,13},{10,... | collective-permute-start | bytes 2752520 | tf_op jit(solution)/shard_map/ppermute | solution.py:1018
  20.8 48.3 %collective-permute-start.8 = (bf16[256,1792]{1,0:T(8,128)(2,1)S(1)}, bf16[256,1792]{1,0:T(8,128)(2,1)}, u32[]{:S(2)}, u32[]{:S(2)}) collective-permute-start(bf16[256,1792]{1,0:T(8,128)(2,1)S(1)} %pad_maximum_fusion.2.refs_0_), channel_id=1, source_target_pairs={{0,6},{1,7},{2,4},{3,5},{4,2},{5,3},{6,0},{7,1},{8,14},{9,15},{10,... | collective-permute-start | bytes 2752520 | tf_op jit(solution)/shard_map/ppermute | solution.py:1018
  69.1 46.3 %collective-permute-start.9 = (bf16[2048,256]{1,0:T(8,128)(2,1)}, bf16[2048,256]{1,0:T(8,128)(2,1)}, u32[]{:S(2)}, u32[]{:S(2)}) collective-permute-start(bf16[2048,256]{1,0:T(8,128)(2,1)} %collective-permute-done.refs_1_), channel_id=1, source_target_pairs={{0,8},{8,16},{16,24},{24,0},{1,9},{9,17},{17,25},{25,1},{2,10},{10... | collective-permute-start | bytes 3145736 | tf_op jit(solution)/shard_map/ppermute | solution.py:1027
  70.2 44.2 %collective-permute-start.10 = (bf16[256,1792]{1,0:T(8,128)(2,1)S(1)}, bf16[256,1792]{1,0:T(8,128)(2,1)}, u32[]{:S(2)}, u32[]{:S(2)}) collective-permute-start(bf16[256,1792]{1,0:T(8,128)(2,1)S(1)} %collective-permute-done.2.refs_4_), channel_id=1, source_target_pairs={{0,8},{8,16},{16,24},{24,0},{1,9},{9,17},{17,25},{25,1},{2,10},{10... | collective-permute-start | bytes 2752520 | tf_op jit(solution)/shard_map/ppermute | solution.py:1027
  71.2 43.2 %collective-permute-start.11 = (bf16[256,1792]{1,0:T(8,128)(2,1)S(1)}, bf16[256,1792]{1,0:T(8,128)(2,1)S(1)}, u32[]{:S(2)}, u32[]{:S(2)}) collective-permute-start(bf16[256,1792]{1,0:T(8,128)(2,1)S(1)} %collective-permute-done.2.refs_4_), channel_id=1, source_target_pairs={{0,2},{1,3},{2,0},{3,1},{4,6},{5,7},{6,4},{7,5},{8,10},{9,11},{10,... | collective-permute-start | bytes 2752520 | tf_op jit(solution)/shard_map/ppermute | solution.py:1018
  72.7 41.7 %collective-permute-start.12 = (bf16[256,1792]{1,0:T(8,128)(2,1)S(1)}, bf16[256,1792]{1,0:T(8,128)(2,1)S(1)}, u32[]{:S(2)}, u32[]{:S(2)}) collective-permute-start(bf16[256,1792]{1,0:T(8,128)(2,1)S(1)} %collective-permute-done.2.refs_4_), channel_id=1, source_target_pairs={{0,4},{1,5},{2,6},{3,7},{4,0},{5,1},{6,2},{7,3},{8,12},{9,13},{10,... | collective-permute-start | bytes 2752520 | tf_op jit(solution)/shard_map/ppermute | solution.py:1018
  74.2 40.2 %collective-permute-start.13 = (bf16[256,1792]{1,0:T(8,128)(2,1)S(1)}, bf16[256,1792]{1,0:T(8,128)(2,1)S(1)}, u32[]{:S(2)}, u32[]{:S(2)}) collective-permute-start(bf16[256,1792]{1,0:T(8,128)(2,1)S(1)} %collective-permute-done.2.refs_4_), channel_id=1, source_target_pairs={{0,6},{1,7},{2,4},{3,5},{4,2},{5,3},{6,0},{7,1},{8,14},{9,15},{10,... | collective-permute-start | bytes 2752520 | tf_op jit(solution)/shard_map/ppermute | solution.py:1018
  116.4 49.6 %collective-permute-start.16 = (bf16[256,1792]{1,0:T(8,128)(2,1)}, bf16[256,1792]{1,0:T(8,128)(2,1)}, u32[]{:S(2)}, u32[]{:S(2)}) collective-permute-start(bf16[256,1792]{1,0:T(8,128)(2,1)} %collective-permute-done.10.refs_8_), channel_id=1, source_target_pairs={{0,2},{1,3},{2,0},{3,1},{4,6},{5,7},{6,4},{7,5},{8,10},{9,11},{10,... | collective-permute-start | bytes 2752520 | tf_op jit(solution)/shard_map/ppermute | solution.py:1018
  117.7 48.4 %collective-permute-start.17 = (bf16[256,1792]{1,0:T(8,128)(2,1)}, bf16[256,1792]{1,0:T(8,128)(2,1)}, u32[]{:S(2)}, u32[]{:S(2)}) collective-permute-start(bf16[256,1792]{1,0:T(8,128)(2,1)} %collective-permute-done.10.refs_8_), channel_id=1, source_target_pairs={{0,4},{1,5},{2,6},{3,7},{4,0},{5,1},{6,2},{7,3},{8,12},{9,13},{10,... | collective-permute-start | bytes 2752520 | tf_op jit(solution)/shard_map/ppermute | solution.py:1018
  118.9 47.1 %collective-permute-start.18 = (bf16[256,1792]{1,0:T(8,128)(2,1)}, bf16[256,1792]{1,0:T(8,128)(2,1)}, u32[]{:S(2)}, u32[]{:S(2)}) collective-permute-start(bf16[256,1792]{1,0:T(8,128)(2,1)} %collective-permute-done.10.refs_8_), channel_id=1, source_target_pairs={{0,6},{1,7},{2,4},{3,5},{4,2},{5,3},{6,0},{7,1},{8,14},{9,15},{10,... | collective-permute-start | bytes 2752520 | tf_op jit(solution)/shard_map/ppermute | solution.py:1018
  141.0 25.0 %collective-permute-start.15 = (bf16[256,1792]{1,0:T(8,128)(2,1)}, bf16[256,1792]{1,0:T(8,128)(2,1)}, u32[]{:S(2)}, u32[]{:S(2)}) collective-permute-start(bf16[256,1792]{1,0:T(8,128)(2,1)} %collective-permute-done.10.refs_8_), channel_id=1, source_target_pairs={{0,8},{8,16},{16,24},{24,0},{1,9},{9,17},{17,25},{25,1},{2,10},{10... | collective-permute-start | bytes 2752520 | tf_op jit(solution)/shard_map/ppermute | solution.py:1027
  182.3 25.4 %collective-permute-start.20 = (bf16[256,1792]{1,0:T(8,128)(2,1)}, bf16[256,1792]{1,0:T(8,128)(2,1)S(1)}, u32[]{:S(2)}, u32[]{:S(2)}) collective-permute-start(bf16[256,1792]{1,0:T(8,128)(2,1)} %collective-permute-done.15.refs_12_), channel_id=1, source_target_pairs={{0,4},{1,5},{2,6},{3,7},{4,0},{5,1},{6,2},{7,3},{8,12},{9,13},{10,... | collective-permute-start | bytes 2752520 | tf_op jit(solution)/shard_map/ppermute | solution.py:1018
  185.9 36.9 %collective-permute-start.21 = (bf16[256,1792]{1,0:T(8,128)(2,1)}, bf16[256,1792]{1,0:T(8,128)(2,1)S(1)}, u32[]{:S(2)}, u32[]{:S(2)}) collective-permute-start(bf16[256,1792]{1,0:T(8,128)(2,1)} %collective-permute-done.15.refs_12_), channel_id=1, source_target_pairs={{0,6},{1,7},{2,4},{3,5},{4,2},{5,3},{6,0},{7,1},{8,14},{9,15},{10,... | collective-permute-start | bytes 2752520 | tf_op jit(solution)/shard_map/ppermute | solution.py:1018
  231.6 31.2 %all-to-all-start.2 = ((bf16[4,512,256]{2,1,0:T(8,128)(2,1)}), bf16[4,512,256]{2,1,0:T(8,128)(2,1)S(1)}, u32[]{:S(2)}, u32[]{:S(2)}) async-start(bf16[4,512,256]{2,1,0:T(8,128)(2,1)} %bitcast.21), calls=%async_computation.2 | async-start | bytes 2097152 | tf_op jit(solution)/shard_map/all_to_all | solution.py:1030
  284.4 32.8 %collective-permute-start.27 = (bf16[2,2,256,512]{3,2,1,0:T(8,128)(2,1)}, bf16[2,2,256,512]{3,2,1,0:T(8,128)(2,1)S(1)}, u32[]{:S(2)}, u32[]{:S(2)}) collective-permute-start(bf16[2,2,256,512]{3,2,1,0:T(8,128)(2,1)} %get-tuple-element.213), channel_id=1, source_target_pairs={{0,4},{1,5},{2,6},{3,7},{4,0},{5,1},{6,2},{7,3},{8,12},{9,13},{10,... | collective-permute-start | bytes 3145736 | tf_op jit(solution)/shard_map/ppermute | solution.py:1018
  285.3 31.9 %collective-permute-start.26 = (bf16[2,2,256,512]{3,2,1,0:T(8,128)(2,1)}, bf16[2,2,256,512]{3,2,1,0:T(8,128)(2,1)S(1)}, u32[]{:S(2)}, u32[]{:S(2)}) collective-permute-start(bf16[2,2,256,512]{3,2,1,0:T(8,128)(2,1)} %get-tuple-element.212), channel_id=1, source_target_pairs={{0,2},{1,3},{2,0},{3,1},{4,6},{5,7},{6,4},{7,5},{8,10},{9,11},{10,... | collective-permute-start | bytes 3145736 | tf_op jit(solution)/shard_map/ppermute | solution.py:1018
  287.0 32.3 %all-to-all-start.3 = ((bf16[4,512,256]{2,1,0:T(8,128)(2,1)}), bf16[4,512,256]{2,1,0:T(8,128)(2,1)S(1)}, u32[]{:S(2)}, u32[]{:S(2)}) async-start(bf16[4,512,256]{2,1,0:T(8,128)(2,1)} %get-tuple-element.218), calls=%async_computation.3 | async-start | bytes 2097152 | tf_op jit(solution)/shard_map/all_to_all | solution.py:1030
  331.5 28.2 %all-to-all-start.4 = ((bf16[4,256,256]{2,1,0:T(8,128)(2,1)}), bf16[4,256,256]{2,1,0:T(8,128)(2,1)S(1)}, u32[]{:S(2)}, u32[]{:S(2)}) async-start(bf16[4,256,256]{2,1,0:T(8,128)(2,1)} %get-tuple-element.237), calls=%async_computation.4 | async-start | bytes 1048576 | tf_op jit(solution)/shard_map/all_to_all | solution.py:1030
  359.6 59.9 %collective-permute-start.32 = (bf16[2,2,272,1152]{3,2,1,0:T(8,128)(2,1)}, bf16[2,2,272,1152]{3,2,1,0:T(8,128)(2,1)}, u32[]{:S(2)}, u32[]{:S(2)}) collective-permute-start(bf16[2,2,272,1152]{3,2,1,0:T(8,128)(2,1)} %get-tuple-element.244), channel_id=1, source_target_pairs={{0,4},{1,5},{2,6},{3,7},{4,0},{5,1},{6,2},{7,3},{8,12},{9,13},{10,... | collective-permute-start | bytes 7520264 | tf_op jit(solution)/shard_map/ppermute | solution.py:1018
  366.0 33.7 %all-to-all-start.5 = ((bf16[4,256,256]{2,1,0:T(8,128)(2,1)}), bf16[4,256,256]{2,1,0:T(8,128)(2,1)S(1)}, u32[]{:S(2)}, u32[]{:S(2)}) async-start(bf16[4,256,256]{2,1,0:T(8,128)(2,1)} %get-tuple-element.250), calls=%async_computation.5 | async-start | bytes 1048576 | tf_op jit(solution)/shard_map/all_to_all | solution.py:1030
  372.5 27.3 %collective-permute-start.35 = (bf16[256,512]{1,0:T(8,128)(2,1)S(1)}, bf16[256,512]{1,0:T(8,128)(2,1)}, u32[]{:S(2)}, u32[]{:S(2)}) collective-permute-start(bf16[256,512]{1,0:T(8,128)(2,1)S(1)} %fusion.17), channel_id=1, source_target_pairs={{0,24},{8,0},{16,8},{24,16},{1,25},{9,1},{17,9},{25,17},{2,26},{10... | collective-permute-start | bytes 786440 | tf_op jit(solution)/shard_map/ppermute | solution.py:1027
  376.3 54.7 %collective-permute-start.34 = (bf16[2,2,272,1152]{3,2,1,0:T(8,128)(2,1)}, bf16[2,2,272,1152]{3,2,1,0:T(8,128)(2,1)}, u32[]{:S(2)}, u32[]{:S(2)}) collective-permute-start(bf16[2,2,272,1152]{3,2,1,0:T(8,128)(2,1)} %get-tuple-element.255), channel_id=1, source_target_pairs={{0,2},{1,3},{2,0},{3,1},{4,6},{5,7},{6,4},{7,5},{8,10},{9,11},{10,... | collective-permute-start | bytes 7520264 | tf_op jit(solution)/shard_map/ppermute | solution.py:1018
  380.2 27.2 %collective-permute-start.36 = (bf16[256,512]{1,0:T(8,128)(2,1)}, bf16[256,512]{1,0:T(8,128)(2,1)S(1)}, u32[]{:S(2)}, u32[]{:S(2)}) collective-permute-start(bf16[256,512]{1,0:T(8,128)(2,1)} %get-tuple-element.366), channel_id=1, source_target_pairs={{0,16},{8,24},{16,0},{24,8},{1,17},{9,25},{17,1},{25,9},{2,18},{10... | collective-permute-start | bytes 786440 | tf_op jit(solution)/shard_map/ppermute | solution.py:1027
  380.2 27.2 %collective-permute-start.37 = (bf16[256,512]{1,0:T(8,128)(2,1)}, bf16[256,512]{1,0:T(8,128)(2,1)S(1)}, u32[]{:S(2)}, u32[]{:S(2)}) collective-permute-start(bf16[256,512]{1,0:T(8,128)(2,1)} %get-tuple-element.367), channel_id=1, source_target_pairs={{0,8},{8,16},{16,24},{24,0},{1,9},{9,17},{17,25},{25,1},{2,10},{10... | collective-permute-start | bytes 786440 | tf_op jit(solution)/shard_map/ppermute | solution.py:1027
  413.6 73.0 %all-to-all-start.6 = ((bf16[4,1024,256]{1,2,0:T(8,128)(2,1)}), bf16[4,1024,256]{1,2,0:T(8,128)(2,1)S(1)}, u32[]{:S(2)}, u32[]{:S(2)}) async-start(bf16[4,1024,256]{1,2,0:T(8,128)(2,1)} %fusion.15), calls=%async_computation.7 | async-start | bytes 4194304 | tf_op jit(solution)/shard_map/all_to_all | solution.py:1030
  417.3 140.9 %reduce-scatter.2.cloned.1.call-start = ((), (), s32[]{:S(2)}) async-start(), calls=%async_computation.9 | async-start | bytes 2621440 | tf_op jit(solution)/shard_map/reduce_scatter | solution.py:1238
  433.9 34.4 %collective-permute-start.33 = (bf16[1,2,272,1152]{3,2,1,0:T(8,128)(2,1)}, bf16[1,2,272,1152]{3,2,1,0:T(8,128)(2,1)}, u32[]{:S(2)}, u32[]{:S(2)}) collective-permute-start(bf16[1,2,272,1152]{3,2,1,0:T(8,128)(2,1)} %add_convert_fusion.1), channel_id=1, source_target_pairs={{0,2},{1,3},{2,0},{3,1},{4,6},{5,7},{6,4},{7,5},{8,10},{9,11},{10,... | collective-permute-start | bytes 3760136 | tf_op jit(solution)/shard_map/ppermute | solution.py:1018
  435.5 26.6 %collective-permute-start.38 = (bf16[1,2,272,1152]{3,2,1,0:T(8,128)(2,1)}, bf16[1,2,272,1152]{3,2,1,0:T(8,128)(2,1)S(1)}, u32[]{:S(2)}, u32[]{:S(2)}) collective-permute-start(bf16[1,2,272,1152]{3,2,1,0:T(8,128)(2,1)} %add_convert_fusion), channel_id=1, source_target_pairs={{0,4},{1,5},{2,6},{3,7},{4,0},{5,1},{6,2},{7,3},{8,12},{9,13},{10,... | collective-permute-start | bytes 3760136 | tf_op jit(solution)/shard_map/ppermute | solution.py:1018
  (78 other events, 1204.0 us)
Sparse Core Ops, SparseCore 0:
  22.4 46.2 all-gather.1
  513.1 45.0 reduce-scatter.1

commit v5 on v4

--- a/solution.py
+++ b/solution.py
@@ -24,7 +24,6 @@
 
 bf16 = jnp.bfloat16
 f32 = jnp.float32
-VMEM_LIMIT = 56 * 1024 * 1024
 
 
 def dot(a, b):
@@ -39,8 +38,8 @@
     return lax.dot_general(a, b, (((0,), (0,)), ((), ())), preferred_element_type=f32)
 
 
-def params():
-    return pltpu.CompilerParams(vmem_limit_bytes=VMEM_LIMIT)
+def params(mib):
+    return pltpu.CompilerParams(vmem_limit_bytes=mib * 1024 * 1024)
 
 
 def full_spec(shape):
@@ -113,7 +112,7 @@
         out_shape=[jax.ShapeDtypeStruct((rows, width), bf16)]
         + [jax.ShapeDtypeStruct((rows, cols), bf16)] * 3
         + [jax.ShapeDtypeStruct((rows, 128), f32)],
-        compiler_params=params(),
+        compiler_params=params(24),
     )(place, *tokens, w, cosine, sine, gain, ones)
 
 
@@ -204,7 +203,7 @@
             jax.ShapeDtypeStruct((count * blk, cols), bf16),
             jax.ShapeDtypeStruct((count * blk, 128), f32),
         ],
-        compiler_params=params(),
+        compiler_params=params(20),
     )(is_long, q, k, v)
 
 
@@ -353,7 +352,7 @@
             ],
         ),
         out_shape=outs,
-        compiler_params=params(),
+        compiler_params=params(28),
     )(is_long, *ins)
 
 
@@ -365,31 +364,32 @@
     return scale * (grad - result * jnp.mean(grad * result, axis=1, keepdims=True))
 
 
-def pack_kernel(core_ref, up_ref, down_ref, out_ref, mine_ref, theirs_ref):
+def pack_kernel(core_ref, up_ref, gain_ref, down_ref, out_ref, mine_ref, theirs_ref):
     half = up_ref.shape[2] // 2
     low = core_ref[0] == 0
     down = down_ref[...].astype(bf16).T
     out = out_ref[...].astype(bf16).T
     for ref, first in ((mine_ref, low), (theirs_ref, jnp.logical_not(low))):
         for c in range(2):
+            gain = gain_ref[c : c + 1, :]
             ref[:, c * half : (c + 1) * half] = jnp.where(
-                first, up_ref[:, c, :half], up_ref[:, c, half:]
+                first, up_ref[:, c, :half] * gain[:, :half], up_ref[:, c, half:] * gain[:, half:]
             ).astype(bf16)
         ref[:, 2 * half : 3 * half] = jnp.where(first, down[:, :half], down[:, half:])
         ref[:, 3 * half :] = out
 
 
-def pack(core, w_up, w_down, w_out):
+def pack(core, w_up, gain, w_down, w_out):
     span, _, hid = w_up.shape
     cols = w_out.shape[0]
     vmem = pl.BlockSpec(memory_space=pltpu.VMEM)
     return pl.pallas_call(
         pack_kernel,
-        in_specs=[pl.BlockSpec(memory_space=pltpu.SMEM)] + [vmem] * 3,
+        in_specs=[pl.BlockSpec(memory_space=pltpu.SMEM)] + [vmem] * 4,
         out_specs=[vmem] * 2,
         out_shape=[jax.ShapeDtypeStruct((span, 3 * hid // 2 + cols), bf16)] * 2,
-        compiler_params=params(),
-    )(core, w_up, w_down, w_out)
+        compiler_params=params(16),
+    )(core, w_up, gain, w_down, w_out)
 
 
 def place_of(r, chip, chunk):
@@ -421,14 +421,17 @@
 def attn_out_kernel(place_ref, *refs, counts, chips, fast):
     total = sum(counts)
     flat, refs = refs[:total], refs[total:]
-    ya_ref, yb_ref, x_ref, alpha_ref, ha_ref, h1_ref, hb_ref, stat_ref, acc = refs
-    z, chip = place_ref[0], place_ref[1]
+    ya_ref, yb_ref, x_ref, alpha_ref, ha_ref, h1_ref, hb_ref, stat_ref, all_ref, half_ref, acc = refs
+    z, chip, low = place_ref[0], place_ref[1], place_ref[2] == 0
     parts = len(counts)
     early = pl.program_id(0) == 0
     index = 0
     for n in range(parts):
         at = lax.rem(z + parts - n, parts)
         y = jnp.where(early, ya_ref[at], yb_ref[at])
+        hc = y.shape[1] // 2
+        all_ref[at] = y
+        half_ref[at] = jnp.where(low, y[:, hc:], y[:, :hc])
         column = 0
         for piece in flat[index : index + counts[n]]:
             part = slice(column, column + piece.shape[0])
@@ -478,12 +481,15 @@
             in_specs=specs
             + [full_spec(ya.shape)] * 2
             + [own_rows(blk, parts, width, fast), full_spec((1, width))],
-            out_specs=[row(width)] * 3 + [row(128)],
+            out_specs=[row(width)] * 3
+            + [row(128)]
+            + [pl.BlockSpec((parts, blk, n), lambda i, s: (0, i, 0)) for n in (cols, cols // 2)],
             scratch_shapes=[pltpu.VMEM((blk, width), f32)],
         ),
         out_shape=[jax.ShapeDtypeStruct((rows, width), d) for d in (f32, f32, bf16)]
-        + [jax.ShapeDtypeStruct((rows, 128), f32)],
-        compiler_params=params(),
+        + [jax.ShapeDtypeStruct((rows, 128), f32)]
+        + [jax.ShapeDtypeStruct((parts, rows, n), bf16) for n in (cols, cols // 2)],
+        compiler_params=params(24),
     )(place, *flat, ya, yb, x, alpha)
 
 
@@ -527,7 +533,7 @@
         out_shape=[jax.ShapeDtypeStruct(cot.shape, bf16)]
         + [jax.ShapeDtypeStruct((rows, width), d) for d in (bf16, f32)]
         + [jax.ShapeDtypeStruct((8, width), f32)],
-        compiler_params=params(),
+        compiler_params=params(24),
     )(place, own, got, h1, cot, alpha)
 
 
@@ -591,7 +597,7 @@
         out_shape=[jax.ShapeDtypeStruct((rows, width), bf16)] * 2
         + [jax.ShapeDtypeStruct((8, width), f32)]
         + [jax.ShapeDtypeStruct((parts, blk, cols), bf16)] * 2,
-        compiler_params=params(),
+        compiler_params=params(30),
     )(place, *flat, own, got, base, h1, ha, x, stat, alpha)
 
 
@@ -630,7 +636,7 @@
     for n in counts:
         slots.append(flat[at : at + n])
         at += n
-    ha_ref, hb_ref, suv_ref, act_ref, uv_ref, own_ref, got_ref, acc, wbuf, sems = refs
+    ha_ref, hb_ref, act_ref, uv_ref, own_ref, got_ref, acc, wbuf, sems = refs
     rows = ha_ref.shape[0]
     q = pl.program_id(0)
 
@@ -644,8 +650,8 @@
     for base, h_ref, sum_ref in ((0, ha_ref, own_ref), (rows, hb_ref, acc)):
         at = slice(base, base + rows)
         pair = dot(h_ref[...], w[:, : 2 * half])
-        lifted = pair[:, :half] * suv_ref[0:1, :]
-        gated = pair[:, half:] * suv_ref[1:2, :]
+        lifted = pair[:, :half]
+        gated = pair[:, half:]
         act = (lifted * gated * jax.nn.sigmoid(gated)).astype(bf16)
         uv_ref[at, :] = pair.astype(bf16)
         act_ref[at, :] = act
@@ -656,9 +662,9 @@
         got_ref[...] = acc[...].astype(bf16)
 
 
-def mlp_fwd(ha, hb, slots, suv):
+def mlp_fwd(ha, hb, slots, half):
     rows, width = ha.shape
-    parts, _, half = suv.shape
+    parts = len(slots)
     take = lambda n: pl.BlockSpec((None, 2 * rows, n), lambda q: (q, 0, 0))
     whole = full_spec((rows, width))
     anywhere = pl.BlockSpec(memory_space=pl.ANY)
@@ -667,7 +673,7 @@
         functools.partial(mlp_fwd_kernel, half=half, counts=[len(s) for s in slots]),
         grid=(parts,),
         in_specs=[anywhere] * len(flat)
-        + [whole, whole, pl.BlockSpec((None, 2, half), lambda q: (q, 0, 0))],
+        + [whole, whole],
         out_specs=[take(half), take(2 * half), whole, whole],
         out_shape=[
             jax.ShapeDtypeStruct((parts, 2 * rows, half), bf16),
@@ -680,8 +686,8 @@
             pltpu.VMEM((2, width, 3 * half), bf16),
             pltpu.SemaphoreType.DMA((2, max(len(s) for s in slots))),
         ],
-        compiler_params=params(),
-    )(*flat, ha, hb, suv)
+        compiler_params=params(32),
+    )(*flat, ha, hb)
 
 
 def mlp_bwd_kernel(*refs, half, counts):
@@ -691,7 +697,7 @@
     for n in counts:
         slots.append(flat[at : at + n])
         at += n
-    da_ref, db_ref, uv_ref, suv_ref, duv_ref, own_ref, got_ref, gs_ref, acc, wbuf, sems = refs
+    da_ref, db_ref, uv_ref, duv_ref, own_ref, got_ref, gs_ref, acc, wbuf, sems = refs
     rows = da_ref.shape[0]
     q = pl.program_id(0)
 
@@ -706,19 +712,15 @@
     for base, d_ref, sum_ref in ((0, da_ref, own_ref), (rows, db_ref, acc)):
         at = slice(base, base + rows)
         grad = dot(d_ref[...], w[:, 2 * half : 3 * half])
-        up = uv_ref[at, :half].astype(f32)
-        gate = uv_ref[at, half:].astype(f32)
-        su = suv_ref[0:1, :]
-        sv = suv_ref[1:2, :]
-        lifted = up * su
-        gated = gate * sv
+        lifted = uv_ref[at, :half].astype(f32)
+        gated = uv_ref[at, half:].astype(f32)
         sigma = jax.nn.sigmoid(gated)
         da = grad * gated * sigma
         db = grad * lifted * sigma * (1.0 + gated * (1.0 - sigma))
-        gs_ref[0:1, :] += jnp.sum(da * up, axis=0, keepdims=True)
-        gs_ref[1:2, :] += jnp.sum(db * gate, axis=0, keepdims=True)
-        duv_ref[at, :half] = (da * su).astype(bf16)
-        duv_ref[at, half:] = (db * sv).astype(bf16)
+        gs_ref[0:1, :] += jnp.sum(da * lifted, axis=0, keepdims=True)
+        gs_ref[1:2, :] += jnp.sum(db * gated, axis=0, keepdims=True)
+        duv_ref[at, :half] = da.astype(bf16)
+        duv_ref[at, half:] = db.astype(bf16)
         sum_ref[...] += dot_t(duv_ref[at, :], w[:, : 2 * half])
 
     @pl.when(q == pl.num_programs(0) - 1)
@@ -726,9 +728,9 @@
         got_ref[...] = acc[...].astype(bf16)
 
 
-def mlp_bwd(da, db, slots, uv, suv):
+def mlp_bwd(da, db, slots, uv, half):
     rows, width = da.shape
-    parts, _, half = suv.shape
+    parts = len(slots)
     take = lambda n: pl.BlockSpec((None, 2 * rows, n), lambda q: (q, 0, 0))
     whole = full_spec((rows, width))
     anywhere = pl.BlockSpec(memory_space=pl.ANY)
@@ -741,7 +743,6 @@
             whole,
             whole,
             take(2 * half),
-            pl.BlockSpec((None, 2, half), lambda q: (q, 0, 0)),
         ],
         out_specs=[
             take(2 * half),
@@ -760,8 +761,8 @@
             pltpu.VMEM((2, width, 3 * half), bf16),
             pltpu.SemaphoreType.DMA((2, max(len(s) for s in slots))),
         ],
-        compiler_params=params(),
-    )(*flat, da, db, uv, suv)
+        compiler_params=params(36),
+    )(*flat, da, db, uv)
 
 
 EXTRA = 16
@@ -881,7 +882,7 @@
         out_shape=[
             jax.ShapeDtypeStruct((len(one), middle, tall, size + hc), bf16) for one in lists
         ],
-        compiler_params=params(),
+        compiler_params=params(36),
     )(place, *ins)
     return [out[0], out[2]], [out[1], out[3]]
 
@@ -922,7 +923,7 @@
         out_specs=[vmem] * 5,
         out_shape=[jax.ShapeDtypeStruct(w.shape, f32)] * 4
         + [jax.ShapeDtypeStruct(w.shape[1:], f32)],
-        compiler_params=params(),
+        compiler_params=params(16),
     )(w, g, m, v)
 
 
@@ -944,7 +945,7 @@
         out_specs=[vmem] * 5,
         out_shape=[jax.ShapeDtypeStruct(w.shape, f32)] * 4
         + [jax.ShapeDtypeStruct((8, w.shape[0]), f32)],
-        compiler_params=params(),
+        compiler_params=params(16),
     )(w, g, m, v)
 
 
@@ -964,7 +965,7 @@
         in_specs=[vmem] * 8,
         out_specs=[vmem] * 4,
         out_shape=[jax.ShapeDtypeStruct(w.shape, f32) for w in weights],
-        compiler_params=params(),
+        compiler_params=params(16),
     )(*norms, *weights)
 
 
@@ -1049,17 +1050,15 @@
         return [value]
 
     tokens = [layer_input, onward(layer_input)]
-    mine, theirs = pack(core_s, w_up, w_down, w_out)
+    mine, theirs = pack(core_s, w_up, s_uv, w_down, w_out)
     qkv_own = after(w_qkv, mine).reshape(span, 3 * cols).astype(bf16)
     qkv_full = lax.all_gather(qkv_own, "batch", axis=0, tiled=True)
     theirs = swap_core(theirs)
     packet = jnp.concatenate([pick((mine, theirs), core), pick((theirs, mine), core)], axis=0)
     hops = [packet, onward(packet)]
     slots = [spread(packet)]
-    suv_own = after(pick((s_uv[:, :half], s_uv[:, half:]), core), tokens[1])
-    suv = jnp.stack([suv_own] + [onward(suv_own, n) for n in range(1, nz)])
-    tokens[1], hops[1], places, suv, alpha_attn, alpha_mlp, *last = lax.optimization_barrier(
-        (tokens[1], hops[1], positions, suv, alpha_attn, alpha_mlp, *slots[0])
+    tokens[1], hops[1], places, alpha_attn, alpha_mlp, *last = lax.optimization_barrier(
+        (tokens[1], hops[1], positions, alpha_attn, alpha_mlp, *slots[0])
     )
     slots[0] = list(last)
 
@@ -1111,15 +1110,16 @@
             ]
         )
         start = relative(start)
-    y_mine = jnp.concatenate([y_one, y_two], axis=1)
-    y_got = swap_core(lax.dynamic_slice_in_dim(y_mine, (1 - core) * hc, hc, 2))
-    y_one, y_two, y_mine, y_got = lax.optimization_barrier((y_one, y_two, y_mine, y_got))
-    hA, h1, h_own, stat = attn_out(place, y_one, y_two, slots, start, attn_gain, chips, fast)
+    y_one, y_two, *last = lax.optimization_barrier((y_one, y_two, *slots[-1]))
+    slots[-1] = list(last)
+    hA, h1, h_own, stat, y_mine, y_other = attn_out(place, y_one, y_two, slots, start, attn_gain, chips, fast)
     h_got = swap_core(h_own)
+    y_got = swap_core(y_other)
+    h_got, y_got = lax.optimization_barrier((h_got, y_got))
     cot = after(cotangent, h_own).reshape(2, nz, own // 2, cols).transpose(1, 0, 2, 3)
     cot = exchange(cot.reshape(nz, own, cols))
 
-    act, uv, mo_own, mo_other = mlp_fwd(h_own, h_got, slots, suv)
+    act, uv, mo_own, mo_other = mlp_fwd(h_own, h_got, slots, half)
     mo_got = swap_core(mo_other)
     if not fast:
         cot = relative(flat(cot))
@@ -1157,7 +1157,7 @@
     down_made, down_kept = weight_grads(place, sent_at, kept_at, chips, (d_own, d_got), act)
     down_sent = [swap_chip(one, order[0]) for one, order in zip(down_made, orders)]
     d_own, d_got, *_ = lax.optimization_barrier((d_own, d_got, *down_made))
-    duv, dh_own, dh_other, gsuv = mlp_bwd(d_own, d_got, slots, uv, suv)
+    duv, dh_own, dh_other, gsuv = mlp_bwd(d_own, d_got, slots, uv, half)
     dh_got = swap_core(dh_other)
     down_sent = [after(one, dh_other) for one in down_sent]
     down_part, down_next = second(down_kept, down_sent)
@@ -1271,11 +1271,13 @@
     down_new = adam_tall(w_down, jnp.concatenate(join(halves, 0, half), axis=1), moment_down, square_down)
     halves = both_halves(sum_up_t)
     grad_up = jnp.concatenate(join(halves, 0, half) + join(halves, half, half), axis=1)
+    grad_up = grad_up * s_uv.reshape(1, 2 * hid)
     up_new = adam_wide(w_up, grad_up, moment_up, square_up)
     out_new = adam_tall(w_out, jnp.concatenate(join(halves, 2 * half, hc), axis=1), moment_out, square_out)
     suv_rows = jnp.stack(
         [jnp.concatenate([p[span, c * half : (c + 1) * half] for p in halves]) for c in range(2)]
     )
+    suv_rows = suv_rows / s_uv
     sum_suv = lax.dynamic_slice_in_dim(suv_rows, b * (hid // nb), hid // nb, 1)
     alphas = halves[0][span + 1] + halves[1][span + 1]
     sum_attn = lax.dynamic_slice_in_dim(alphas[:cols], b * cell, cell, 0)

time: 574 us -> 603 us (1.051)
  local copies, waits for them, and re-layouts: 35.2 us -> 106 us
  waiting for transfers between devices: 198 us -> 153 us
  Pallas kernels: 182 us -> 159 us
  blocking collectives: 0 us -> 15.5 us
  starting transfers between devices: 77.2 us -> 85.5 us
    unnamed x117 -> x265, local copies, waits for them, and re-layouts: 19.3 us -> 92 us
    ppermute x15 -> x12, waiting for transfers between devices: 128 us -> 95 us  [onward(): return lax.ppermute(value, 'head', [(i, (i + k) % nz) for i in range(nz)])]
    all_to_all x0 -> x1, blocking collectives: none -> 15.5 us  [exchange(): return lax.all_to_all(value, 'head', split_axis=0, concat_axis=0)]
    all_to_all x7 -> x6, waiting for transfers between devices: 15.2 us -> 0.02 us  [exchange(): return lax.all_to_all(value, 'head', split_axis=0, concat_axis=0)]
    ppermute x35, starting transfers between devices: 31.1 us -> 37.9 us  [swap_batch(): return lax.ppermute(value, 'batch', [(i, i ^ bit) for i in range(nb)])]
    ppermute x15 -> x12, starting transfers between devices: 13.8 us -> 17.3 us  [onward(): return lax.ppermute(value, 'head', [(i, (i + k) % nz) for i in range(nz)])]
    all_to_all x7 -> x6, starting transfers between devices: 32.3 us -> 30.2 us  [exchange(): return lax.all_to_all(value, 'head', split_axis=0, concat_axis=0)]
  transfers between devices with their start and end apart: 59 -> 55, of which waited for: 25 -> 19; matrix products, arithmetic and copies ran while one was open for 15% -> 13% of each run, Pallas kernels for 25% -> 22%
where the time goes in v5:
time: 603 us; the launch traced here: 592 us
  Pallas kernels  159 us (26%)
  waiting for transfers between devices  153 us (25%)
  local copies, waits for them, and re-layouts  106 us (18%)
  starting transfers between devices  85.5 us (14%)
  other arithmetic  46.8 us (8%)
  between operations  16.2 us (3%)
  blocking collectives  15.5 us (3%)
  matrix products  10.4 us (2%)
    ppermute x12, waiting for transfers between devices, onward(): return lax.ppermute(value, 'head', [(i, (i + k) % nz) for i in range(nz)])  95 us
    unnamed x265, local copies, waits for them, and re-layouts  92 us
    ppermute x35, waiting for transfers between devices, swap_batch(): return lax.ppermute(value, 'batch', [(i, i ^ bit) for i in range(nb)])  43.4 us
    ppermute x35, starting transfers between devices, swap_batch(): return lax.ppermute(value, 'batch', [(i, i ^ bit) for i in range(nb)])  37.9 us
    pallas_call x2, Pallas kernels, attn_bwd(): pl.pallas_call(inner, grid_spec=pltpu.PrefetchScalarGridSpec(num_scalar_p...  37.8 us
    all_to_all x6, starting transfers between devices, exchange(): return lax.all_to_all(value, 'head', split_axis=0, concat_axis=0)  30.2 us
    pallas_call x2, Pallas kernels, weight_grads(): pl.pallas_call(functools.partial(grad_kernel, orders=(lists[:2], lists[2:...  24.6 us
    pallas_call x1, Pallas kernels, mlp_bwd(): pl.pallas_call(functools.partial(mlp_bwd_kernel, half=half, counts=[len(s...  23.9 us
  transfers between devices with their start and end apart: 55, of which 19 were waited for; matrix products, arithmetic and copies ran while one was open for 13% of the time, Pallas kernels for 22%

profile of v5, /device:TPU:0, one launch (start us, length us, event | category | flops | bytes accessed | tf_op | source)
XLA Modules:
  0.0 591.9 jit_solution(51127909611417025)
XLA Ops:
  23.0 18.3 %collective-permute-done.refs_1_ = bf16[2048,256]{1,0:T(8,128)(2,1)} collective-permute-done((bf16[2048,256]{1,0:T(8,128)(2,1)}, bf16[2048,256]{1,0:T(8,128)(2,1)}, u32[]{:S(2)}, u32[]{:S(2)}) %collective-permute-start) | collective-permute-done | bytes 1048608 | tf_op jit(solution)/shard_map/ppermute | solution.py:1028
  41.3 19.3 %collective-permute-done.2.refs_4_ = bf16[256,1792]{1,0:T(8,128)(2,1)S(1)} collective-permute-done((bf16[256,1792]{1,0:T(8,128)(2,1)S(1)}, bf16[256,1792]{1,0:T(8,128)(2,1)S(1)}, u32[]{:S(2)}, u32[]{:S(2)}) %collective-permute-start.2) | collective-permute-done | bytes 917536 | tf_op jit(solution)/shard_map/ppermute | solution.py:1028
  61.6 4.6 collective-permute-done.5.refs_3_
  73.2 5.0 fusion.11
  78.2 14.0 %collective-permute-done.10.refs_7_ = bf16[256,1792]{1,0:T(8,128)(2,1)S(1)} collective-permute-done((bf16[256,1792]{1,0:T(8,128)(2,1)S(1)}, bf16[256,1792]{1,0:T(8,128)(2,1)S(1)}, u32[]{:S(2)}, u32[]{:S(2)}) %collective-permute-start.10) | collective-permute-done | bytes 917536 | tf_op jit(solution)/shard_map/ppermute | solution.py:1019
  93.1 18.8 %collective-permute-done.7.refs_8_ = bf16[256,1792]{1,0:T(8,128)(2,1)} collective-permute-done((bf16[256,1792]{1,0:T(8,128)(2,1)S(1)}, bf16[256,1792]{1,0:T(8,128)(2,1)}, u32[]{:S(2)}, u32[]{:S(2)}) %collective-permute-start.7) | collective-permute-done | bytes 917536 | tf_op jit(solution)/shard_map/ppermute | solution.py:1028
  117.3 21.6 %collective-permute-done.11.refs_3_ = bf16[2048,256]{1,0:T(8,128)(2,1)S(1)} collective-permute-done((bf16[2048,256]{1,0:T(8,128)(2,1)}, bf16[2048,256]{1,0:T(8,128)(2,1)S(1)}, u32[]{:S(2)}, u32[]{:S(2)}) %collective-permute-start.11) | collective-permute-done | bytes 1048608 | tf_op jit(solution)/shard_map/ppermute | solution.py:1028
  146.3 9.6 %shard_map.355 = (bf16[2048,1024]{1,0:T(8,128)(2,1)S(1)}, bf16[2048,256]{1,0:T(8,128)(2,1)S(1)}, bf16[2048,256]{1,0:T(8,128)(2,1)S(1)}, bf16[2048,256]{1,0:T(8,128)(2,1)S(1)}, f32[2048,128]{1,0:T(8,128)S(1)}) custom-call(s32[3]{0:T(128)S(1)} %pad_add_fusion.place_ref, bf16[2048,256]{1,0:T(8,128)(2,1)S(1)} %copy-done.74, ...), custom_call_target="tpu_custom_call" | custom-call | tf_op jit(solution)/shard_map/pallas_call | solution.py:102
  157.8 4.4 shard_map.356
  164.9 5.1 all-to-all-start
  176.0 11.1 %shard_map.357 = (bf16[1024,256]{1,0:T(8,128)(2,1)S(1)}, f32[1024,128]{1,0:T(8,128)S(1)}) custom-call(s32[1]{0:T(128)S(6)} %convert_element_type.303.long_ref.r_0_, bf16[2048,256]{1,0:T(8,128)(2,1)S(1)} %copy-done.4, bf16[2048,256]{1,0:T(8,128)(2,1)S(1)} %get-tuple-element.188.k_ref.r_2_.r_6_, bf16[2048,256]{1,0:T(8,128)(2,1)S(1)} %copy-done.8), custom_call_target="tpu_custom_call" | custom-call | tf_op jit(solution)/shard_map/pallas_call | solution.py:193
  188.7 15.5 %all_to_all.35.refs_17_ = bf16[4,256,256]{2,1,0:T(8,128)(2,1)S(1)} all-to-all(bf16[4,256,256]{2,1,0:T(8,128)(2,1)} %bitcast.98), channel_id=1, replica_groups=mesh['head'=4,'batch'=8] {'head'}, dimensions={0} | all-to-all | bytes 1048576 | tf_op jit(solution)/shard_map/all_to_all | solution.py:1031
  204.2 5.9 collective-permute-done.17.refs_14_
  218.2 5.5 shard_map.358
  229.0 4.8 all-to-all-start.2
  239.7 19.6 %shard_map.359 = (bf16[4,1024,512]{2,1,0:T(8,128)(2,1)}, bf16[4,1024,1024]{2,1,0:T(8,128)(2,1)}, f32[512,1024]{1,0:T(8,128)S(1)}, bf16[512,1024]{1,0:T(8,128)(2,1)}) custom-call(bf16[256,1792]{1,0:T(8,128)(2,1)S(1)} %pad_maximum_fusion.1.refs_0_, bf16[256,1792]{1,0:T(8,128)(2,1)S(1)} %copy-done.21, bf16[256,1792]{1,0:T(8,128)(2,1)} %collective-permute-done.4.refs_2_, ...), custom_call_target="tpu_custom_call" | custom-call | tf_op jit(solution)/shard_map/pallas_call | solution.py:672
  266.8 4.5 shard_map.360
  276.2 7.4 %shard_map.361 = (bf16[2,2,256,512]{3,2,1,0:T(8,128)(2,1)}, bf16[2,2,256,512]{3,2,1,0:T(8,128)(2,1)S(1)}, bf16[2,2,256,512]{3,2,1,0:T(8,128)(2,1)}, bf16[2,2,256,512]{3,2,1,0:T(8,128)(2,1)S(1)}) custom-call(s32[3]{0:T(128)S(1)} %pad_add_fusion.place_ref, bf16[512,1024]{1,0:T(8,128)(2,1)S(1)} %get-tuple-element.222.refs_0_.refs_16_, ...), custom_call_target="tpu_custom_call" | custom-call | tf_op jit(solution)/shard_map/pallas_call | solution.py:869
  287.4 5.3 all-to-all-start.3
  301.1 23.9 %shard_map.362 = (bf16[4,1024,1024]{2,1,0:T(8,128)(2,1)}, f32[512,1024]{1,0:T(8,128)}, bf16[512,1024]{1,0:T(8,128)(2,1)}, f32[4,8,512]{2,1,0:T(8,128)S(1)}) custom-call(bf16[256,1792]{1,0:T(8,128)(2,1)S(1)} %pad_maximum_fusion.1.refs_0_, bf16[256,1792]{1,0:T(8,128)(2,1)S(1)} %copy-done.22, bf16[256,1792]{1,0:T(8,128)(2,1)} %collective-permute-done.4.refs_2_, ...), custom_call_target="tpu_custom_call" | custom-call | tf_op jit(solution)/shard_map/pallas_call | solution.py:738
  338.1 8.9 %shard_map.363 = (bf16[512,1024]{1,0:T(8,128)(2,1)}, bf16[512,1024]{1,0:T(8,128)(2,1)S(1)}, f32[8,1024]{1,0:T(8,128)S(1)}, bf16[4,256,256]{2,1,0:T(8,128)(2,1)S(1)}, bf16[4,256,256]{2,1,0:T(8,128)(2,1)S(1)}) custom-call(s32[3]{0:T(128)S(1)} %pad_add_fusion.place_ref, bf16[256,1792]{1,0:T(8,128)(2,1)S(1)} %pad_maximum_fusion.1.refs_0_, ...), custom_call_target="tpu_custom_call" | custom-call | tf_op jit(solution)/shard_map/pallas_call | solution.py:585
  350.1 5.3 all-to-all-start.4
  359.1 17.1 %shard_map.364 = (bf16[2,2,272,1152]{3,2,1,0:T(8,128)(2,1)S(1)}, bf16[2,2,272,1152]{3,2,1,0:T(8,128)(2,1)S(1)}, bf16[2,2,272,1152]{3,2,1,0:T(8,128)(2,1)S(1)}, bf16[2,2,272,1152]{3,2,1,0:T(8,128)(2,1)S(1)}) custom-call(s32[3]{0:T(128)S(1)} %pad_add_fusion.place_ref, bf16[512,1024]{1,0:T(8,128)(2,1)} %get-tuple-element.210.refs_16_.refs_0_, ...), custom_call_target="tpu_custom_call" | custom-call | tf_op jit(solution)/shard_map/pallas_call | solution.py:869
  394.2 5.1 all-to-all-start.5
  414.0 25.3 %shard_map.365 = (bf16[1024,768]{1,0:T(8,128)(2,1)S(1)}, f32[1024,256]{1,0:T(8,128)S(1)}, f32[1024,256]{1,0:T(8,128)S(1)}, f32[8,256]{1,0:T(8,128)S(1)}) custom-call(s32[1]{0:T(128)S(6)} %convert_element_type.303.long_ref.r_0_, bf16[2048,256]{1,0:T(8,128)(2,1)S(1)} %copy-done.5, bf16[2048,256]{1,0:T(8,128)(2,1)S(1)} %get-tuple-element.188.k_ref.r_2_.r_6_, ...), custom_call_target="tpu_custom_call" | custom-call | tf_op jit(solution)/shard_map/pallas_call | solution.py:340
  448.9 4.6 all-to-all-start.6
  462.8 12.5 %shard_map.366 = (bf16[1024,768]{1,0:T(8,128)(2,1)S(1)}, f32[8,256]{1,0:T(8,128)S(1)}) custom-call(s32[1]{0:T(128)S(6)} %convert_element_type.303.long_ref.r_0_, bf16[2048,256]{1,0:T(8,128)(2,1)S(1)} %copy-done.6, bf16[2048,256]{1,0:T(8,128)(2,1)S(1)} %get-tuple-element.188.k_ref.r_2_.r_6_, bf16[1024,256]{1,0:T(8,128)(2,1)S(1)} %bitcast.99, ...), custom_call_target="tpu_custom_call" | custom-call | tf_op jit(solution)/shard_map/pallas_call | solution.py:340
  479.1 8.7 %collective-permute-done.35 = bf16[1,2,272,1152]{3,2,1,0:T(8,128)(2,1)S(1)} collective-permute-done((bf16[1,2,272,1152]{3,2,1,0:T(8,128)(2,1)S(1)}, bf16[1,2,272,1152]{3,2,1,0:T(8,128)(2,1)S(1)}, u32[]{:S(2)}, u32[]{:S(2)}) %collective-permute-start.35) | collective-permute-done | bytes 1253408 | tf_op jit(solution)/shard_map/ppermute | solution.py:1019
  496.0 7.4 %collective-permute-done.36 = bf16[272,1152]{1,0:T(8,128)(2,1)S(1)} collective-permute-done((bf16[272,1152]{1,0:T(8,128)(2,1)S(1)}, bf16[272,1152]{1,0:T(8,128)(2,1)S(1)}, u32[]{:S(2)}, u32[]{:S(2)}) %collective-permute-start.36) | collective-permute-done | bytes 626720 | tf_op jit(solution)/shard_map/ppermute | solution.py:1028
  534.8 5.8 collective-permute-done.41
  556.1 7.2 %collective-permute-start.46 = (f32[32,128]{1,0:T(8,128)S(1)}, f32[32,128]{1,0:T(8,128)S(1)}, u32[]{:S(2)}, u32[]{:S(2)}) collective-permute-start(f32[32,128]{1,0:T(8,128)S(1)} %fusion.42), channel_id=1, source_target_pairs={{0,4},{1,5},{2,6},{3,7},{4,0},{5,1},{6,2},{7,3},{8,12},{9,13},{10,... | collective-permute-start | bytes 49160 | tf_op jit(solution)/shard_map/ppermute | solution.py:1019
  568.2 14.1 %reduce-scatter.2.cloned.1.call-done = bf16[1024,256]{1,0:T(8,128)(2,1)} async-done(((bf16[1024,1024]{1,0:T(8,128)(2,1)}), bf16[1024,256]{1,0:T(8,128)(2,1)}) %reduce-scatter.2.cloned.1.call-update) | async-done | bytes 524304 | tf_op jit(solution)/shard_map/reduce_scatter | solution.py:1238
  (454 shorter events, 229.7 us)
Async XLA Ops:
  7.2 134.0 %all-gather.2.cloned.1.call-start = ((), (), s32[]{:S(2)}) async-start(), calls=%async_computation.8 | async-start | bytes 1769472 | tf_op jit(solution)/shard_map/all_gather | solution.py:1055
  12.3 29.0 %collective-permute-start = (bf16[2048,256]{1,0:T(8,128)(2,1)}, bf16[2048,256]{1,0:T(8,128)(2,1)}, u32[]{:S(2)}, u32[]{:S(2)}) collective-permute-start(bf16[2048,256]{1,0:T(8,128)(2,1)} %refs_0_.1), channel_id=1, source_target_pairs={{0,8},{8,16},{16,24},{24,0},{1,9},{9,17},{17,25},{25,1},{2,10},{10... | collective-permute-start | bytes 3145736 | tf_op jit(solution)/shard_map/ppermute | solution.py:1028
  15.1 45.5 %collective-permute-start.2 = (bf16[256,1792]{1,0:T(8,128)(2,1)S(1)}, bf16[256,1792]{1,0:T(8,128)(2,1)S(1)}, u32[]{:S(2)}, u32[]{:S(2)}) collective-permute-start(bf16[256,1792]{1,0:T(8,128)(2,1)S(1)} %pad_maximum_fusion.1.refs_0_), channel_id=1, source_target_pairs={{0,8},{8,16},{16,24},{24,0},{1,9},{9,17},{17,25},{25,1},{2,10},{10... | collective-permute-start | bytes 2752520 | tf_op jit(solution)/shard_map/ppermute | solution.py:1028
  16.9 43.7 %collective-permute-start.3 = (bf16[256,1792]{1,0:T(8,128)(2,1)S(1)}, bf16[256,1792]{1,0:T(8,128)(2,1)S(1)}, u32[]{:S(2)}, u32[]{:S(2)}) collective-permute-start(bf16[256,1792]{1,0:T(8,128)(2,1)S(1)} %pad_maximum_fusion.1.refs_0_), channel_id=1, source_target_pairs={{0,2},{1,3},{2,0},{3,1},{4,6},{5,7},{6,4},{7,5},{8,10},{9,11},{10,... | collective-permute-start | bytes 2752520 | tf_op jit(solution)/shard_map/ppermute | solution.py:1019
  18.4 43.2 %collective-permute-start.4 = (bf16[256,1792]{1,0:T(8,128)(2,1)S(1)}, bf16[256,1792]{1,0:T(8,128)(2,1)}, u32[]{:S(2)}, u32[]{:S(2)}) collective-permute-start(bf16[256,1792]{1,0:T(8,128)(2,1)S(1)} %pad_maximum_fusion.1.refs_0_), channel_id=1, source_target_pairs={{0,4},{1,5},{2,6},{3,7},{4,0},{5,1},{6,2},{7,3},{8,12},{9,13},{10,... | collective-permute-start | bytes 2752520 | tf_op jit(solution)/shard_map/ppermute | solution.py:1019
  19.9 46.2 %collective-permute-start.5 = (bf16[256,1792]{1,0:T(8,128)(2,1)S(1)}, bf16[256,1792]{1,0:T(8,128)(2,1)}, u32[]{:S(2)}, u32[]{:S(2)}) collective-permute-start(bf16[256,1792]{1,0:T(8,128)(2,1)S(1)} %pad_maximum_fusion.1.refs_0_), channel_id=1, source_target_pairs={{0,6},{1,7},{2,4},{3,5},{4,2},{5,3},{6,0},{7,1},{8,14},{9,15},{10,... | collective-permute-start | bytes 2752520 | tf_op jit(solution)/shard_map/ppermute | solution.py:1019
  66.2 47.7 %collective-permute-start.6 = (bf16[2048,256]{1,0:T(8,128)(2,1)}, bf16[2048,256]{1,0:T(8,128)(2,1)}, u32[]{:S(2)}, u32[]{:S(2)}) collective-permute-start(bf16[2048,256]{1,0:T(8,128)(2,1)} %collective-permute-done.refs_1_), channel_id=1, source_target_pairs={{0,8},{8,16},{16,24},{24,0},{1,9},{9,17},{17,25},{25,1},{2,10},{10... | collective-permute-start | bytes 3145736 | tf_op jit(solution)/shard_map/ppermute | solution.py:1028
  69.4 42.5 %collective-permute-start.7 = (bf16[256,1792]{1,0:T(8,128)(2,1)S(1)}, bf16[256,1792]{1,0:T(8,128)(2,1)}, u32[]{:S(2)}, u32[]{:S(2)}) collective-permute-start(bf16[256,1792]{1,0:T(8,128)(2,1)S(1)} %collective-permute-done.2.refs_4_), channel_id=1, source_target_pairs={{0,8},{8,16},{16,24},{24,0},{1,9},{9,17},{17,25},{25,1},{2,10},{10... | collective-permute-start | bytes 2752520 | tf_op jit(solution)/shard_map/ppermute | solution.py:1028
  71.0 41.0 %collective-permute-start.8 = (bf16[256,1792]{1,0:T(8,128)(2,1)S(1)}, bf16[256,1792]{1,0:T(8,128)(2,1)S(1)}, u32[]{:S(2)}, u32[]{:S(2)}) collective-permute-start(bf16[256,1792]{1,0:T(8,128)(2,1)S(1)} %collective-permute-done.2.refs_4_), channel_id=1, source_target_pairs={{0,2},{1,3},{2,0},{3,1},{4,6},{5,7},{6,4},{7,5},{8,10},{9,11},{10,... | collective-permute-start | bytes 2752520 | tf_op jit(solution)/shard_map/ppermute | solution.py:1019
  71.5 41.4 %collective-permute-start.9 = (bf16[256,1792]{1,0:T(8,128)(2,1)S(1)}, bf16[256,1792]{1,0:T(8,128)(2,1)S(1)}, u32[]{:S(2)}, u32[]{:S(2)}) collective-permute-start(bf16[256,1792]{1,0:T(8,128)(2,1)S(1)} %collective-permute-done.2.refs_4_), channel_id=1, source_target_pairs={{0,4},{1,5},{2,6},{3,7},{4,0},{5,1},{6,2},{7,3},{8,12},{9,13},{10,... | collective-permute-start | bytes 2752520 | tf_op jit(solution)/shard_map/ppermute | solution.py:1019
  113.9 56.1 %collective-permute-start.13 = (bf16[256,1792]{1,0:T(8,128)(2,1)}, bf16[256,1792]{1,0:T(8,128)(2,1)}, u32[]{:S(2)}, u32[]{:S(2)}) collective-permute-start(bf16[256,1792]{1,0:T(8,128)(2,1)} %collective-permute-done.7.refs_8_), channel_id=1, source_target_pairs={{0,2},{1,3},{2,0},{3,1},{4,6},{5,7},{6,4},{7,5},{8,10},{9,11},{10,... | collective-permute-start | bytes 2752520 | tf_op jit(solution)/shard_map/ppermute | solution.py:1019
  115.3 54.7 %collective-permute-start.14 = (bf16[256,1792]{1,0:T(8,128)(2,1)}, bf16[256,1792]{1,0:T(8,128)(2,1)}, u32[]{:S(2)}, u32[]{:S(2)}) collective-permute-start(bf16[256,1792]{1,0:T(8,128)(2,1)} %collective-permute-done.7.refs_8_), channel_id=1, source_target_pairs={{0,4},{1,5},{2,6},{3,7},{4,0},{5,1},{6,2},{7,3},{8,12},{9,13},{10,... | collective-permute-start | bytes 2752520 | tf_op jit(solution)/shard_map/ppermute | solution.py:1019
  115.9 54.1 %collective-permute-start.15 = (bf16[256,1792]{1,0:T(8,128)(2,1)}, bf16[256,1792]{1,0:T(8,128)(2,1)}, u32[]{:S(2)}, u32[]{:S(2)}) collective-permute-start(bf16[256,1792]{1,0:T(8,128)(2,1)} %collective-permute-done.7.refs_8_), channel_id=1, source_target_pairs={{0,6},{1,7},{2,4},{3,5},{4,2},{5,3},{6,0},{7,1},{8,14},{9,15},{10,... | collective-permute-start | bytes 2752520 | tf_op jit(solution)/shard_map/ppermute | solution.py:1019
  139.9 30.1 %collective-permute-start.12 = (bf16[256,1792]{1,0:T(8,128)(2,1)}, bf16[256,1792]{1,0:T(8,128)(2,1)}, u32[]{:S(2)}, u32[]{:S(2)}) collective-permute-start(bf16[256,1792]{1,0:T(8,128)(2,1)} %collective-permute-done.7.refs_8_), channel_id=1, source_target_pairs={{0,8},{8,16},{16,24},{24,0},{1,9},{9,17},{17,25},{25,1},{2,10},{10... | collective-permute-start | bytes 2752520 | tf_op jit(solution)/shard_map/ppermute | solution.py:1028
  170.0 34.2 %collective-permute-start.16 = (bf16[256,1792]{1,0:T(8,128)(2,1)}, bf16[256,1792]{1,0:T(8,128)(2,1)}, u32[]{:S(2)}, u32[]{:S(2)}) collective-permute-start(bf16[256,1792]{1,0:T(8,128)(2,1)} %collective-permute-done.12.refs_12_), channel_id=1, source_target_pairs={{0,2},{1,3},{2,0},{3,1},{4,6},{5,7},{6,4},{7,5},{8,10},{9,11},{10,... | collective-permute-start | bytes 2752520 | tf_op jit(solution)/shard_map/ppermute | solution.py:1019
  171.6 38.5 %collective-permute-start.17 = (bf16[256,1792]{1,0:T(8,128)(2,1)}, bf16[256,1792]{1,0:T(8,128)(2,1)}, u32[]{:S(2)}, u32[]{:S(2)}) collective-permute-start(bf16[256,1792]{1,0:T(8,128)(2,1)} %collective-permute-done.12.refs_12_), channel_id=1, source_target_pairs={{0,4},{1,5},{2,6},{3,7},{4,0},{5,1},{6,2},{7,3},{8,12},{9,13},{10,... | collective-permute-start | bytes 2752520 | tf_op jit(solution)/shard_map/ppermute | solution.py:1019
  172.1 38.0 %collective-permute-start.18 = (bf16[256,1792]{1,0:T(8,128)(2,1)}, bf16[256,1792]{1,0:T(8,128)(2,1)}, u32[]{:S(2)}, u32[]{:S(2)}) collective-permute-start(bf16[256,1792]{1,0:T(8,128)(2,1)} %collective-permute-done.12.refs_12_), channel_id=1, source_target_pairs={{0,6},{1,7},{2,4},{3,5},{4,2},{5,3},{6,0},{7,1},{8,14},{9,15},{10,... | collective-permute-start | bytes 2752520 | tf_op jit(solution)/shard_map/ppermute | solution.py:1019
  229.0 31.6 %all-to-all-start.2 = ((bf16[4,512,256]{2,1,0:T(8,128)(2,1)}), bf16[4,512,256]{2,1,0:T(8,128)(2,1)}, u32[]{:S(2)}, u32[]{:S(2)}) async-start(bf16[4,512,256]{2,1,0:T(8,128)(2,1)} %bitcast.107), calls=%async_computation.2 | async-start | bytes 2097152 | tf_op jit(solution)/shard_map/all_to_all | solution.py:1031
  285.7 39.4 %collective-permute-start.24 = (bf16[2,2,256,512]{3,2,1,0:T(8,128)(2,1)}, bf16[2,2,256,512]{3,2,1,0:T(8,128)(2,1)}, u32[]{:S(2)}, u32[]{:S(2)}) collective-permute-start(bf16[2,2,256,512]{3,2,1,0:T(8,128)(2,1)} %get-tuple-element.221), channel_id=1, source_target_pairs={{0,4},{1,5},{2,6},{3,7},{4,0},{5,1},{6,2},{7,3},{8,12},{9,13},{10,... | collective-permute-start | bytes 3145736 | tf_op jit(solution)/shard_map/ppermute | solution.py:1019
  286.1 38.9 %collective-permute-start.23 = (bf16[2,2,256,512]{3,2,1,0:T(8,128)(2,1)}, bf16[2,2,256,512]{3,2,1,0:T(8,128)(2,1)}, u32[]{:S(2)}, u32[]{:S(2)}) collective-permute-start(bf16[2,2,256,512]{3,2,1,0:T(8,128)(2,1)} %get-tuple-element.220), channel_id=1, source_target_pairs={{0,2},{1,3},{2,0},{3,1},{4,6},{5,7},{6,4},{7,5},{8,10},{9,11},{10,... | collective-permute-start | bytes 3145736 | tf_op jit(solution)/shard_map/ppermute | solution.py:1019
  287.4 41.6 %all-to-all-start.3 = ((bf16[4,512,256]{2,1,0:T(8,128)(2,1)}), bf16[4,512,256]{2,1,0:T(8,128)(2,1)}, u32[]{:S(2)}, u32[]{:S(2)}) async-start(bf16[4,512,256]{2,1,0:T(8,128)(2,1)} %copy-done.83), calls=%async_computation.3 | async-start | bytes 2097152 | tf_op jit(solution)/shard_map/all_to_all | solution.py:1031
  350.1 32.1 %all-to-all-start.4 = ((bf16[4,256,256]{2,1,0:T(8,128)(2,1)}), bf16[4,256,256]{2,1,0:T(8,128)(2,1)}, u32[]{:S(2)}, u32[]{:S(2)}) async-start(bf16[4,256,256]{2,1,0:T(8,128)(2,1)} %copy-done.95), calls=%async_computation.4 | async-start | bytes 1048576 | tf_op jit(solution)/shard_map/all_to_all | solution.py:1031
  355.4 26.7 %collective-permute-start.28 = (bf16[1,2,256,512]{3,2,1,0:T(8,128)(2,1)}, bf16[1,2,256,512]{3,2,1,0:T(8,128)(2,1)}, u32[]{:S(2)}, u32[]{:S(2)}) collective-permute-start(bf16[1,2,256,512]{3,2,1,0:T(8,128)(2,1)} %add_convert_fusion.3), channel_id=1, source_target_pairs={{0,2},{1,3},{2,0},{3,1},{4,6},{5,7},{6,4},{7,5},{8,10},{9,11},{10,... | collective-permute-start | bytes 1572872 | tf_op jit(solution)/shard_map/ppermute | solution.py:1019
  382.2 73.8 %collective-permute-start.29 = (bf16[2,2,272,1152]{3,2,1,0:T(8,128)(2,1)}, bf16[2,2,272,1152]{3,2,1,0:T(8,128)(2,1)}, u32[]{:S(2)}, u32[]{:S(2)}) collective-permute-start(bf16[2,2,272,1152]{3,2,1,0:T(8,128)(2,1)} %copy-done.106), channel_id=1, source_target_pairs={{0,4},{1,5},{2,6},{3,7},{4,0},{5,1},{6,2},{7,3},{8,12},{9,13},{10,... | collective-permute-start | bytes 7520264 | tf_op jit(solution)/shard_map/ppermute | solution.py:1019
  394.2 48.3 %all-to-all-start.5 = ((bf16[4,256,256]{2,1,0:T(8,128)(2,1)}), bf16[4,256,256]{2,1,0:T(8,128)(2,1)S(1)}, u32[]{:S(2)}, u32[]{:S(2)}) async-start(bf16[4,256,256]{2,1,0:T(8,128)(2,1)} %copy-done.94), calls=%async_computation.5 | async-start | bytes 1048576 | tf_op jit(solution)/shard_map/all_to_all | solution.py:1031
  400.5 42.0 %collective-permute-start.32 = (bf16[256,512]{1,0:T(8,128)(2,1)S(1)}, bf16[256,512]{1,0:T(8,128)(2,1)S(1)}, u32[]{:S(2)}, u32[]{:S(2)}) collective-permute-start(bf16[256,512]{1,0:T(8,128)(2,1)S(1)} %fusion.17), channel_id=1, source_target_pairs={{0,24},{8,0},{16,8},{24,16},{1,25},{9,1},{17,9},{25,17},{2,26},{10... | collective-permute-start | bytes 786440 | tf_op jit(solution)/shard_map/ppermute | solution.py:1028
  404.4 54.5 %collective-permute-start.31 = (bf16[2,2,272,1152]{3,2,1,0:T(8,128)(2,1)}, bf16[2,2,272,1152]{3,2,1,0:T(8,128)(2,1)}, u32[]{:S(2)}, u32[]{:S(2)}) collective-permute-start(bf16[2,2,272,1152]{3,2,1,0:T(8,128)(2,1)} %copy-done.105), channel_id=1, source_target_pairs={{0,2},{1,3},{2,0},{3,1},{4,6},{5,7},{6,4},{7,5},{8,10},{9,11},{10,... | collective-permute-start | bytes 7520264 | tf_op jit(solution)/shard_map/ppermute | solution.py:1019
  408.0 34.5 %collective-permute-start.33 = (bf16[256,512]{1,0:T(8,128)(2,1)}, bf16[256,512]{1,0:T(8,128)(2,1)}, u32[]{:S(2)}, u32[]{:S(2)}) collective-permute-start(bf16[256,512]{1,0:T(8,128)(2,1)} %get-tuple-element.374), channel_id=1, source_target_pairs={{0,16},{8,24},{16,0},{24,8},{1,17},{9,25},{17,1},{25,9},{2,18},{10... | collective-permute-start | bytes 786440 | tf_op jit(solution)/shard_map/ppermute | solution.py:1028
  408.0 34.5 %collective-permute-start.34 = (bf16[256,512]{1,0:T(8,128)(2,1)}, bf16[256,512]{1,0:T(8,128)(2,1)}, u32[]{:S(2)}, u32[]{:S(2)}) collective-permute-start(bf16[256,512]{1,0:T(8,128)(2,1)} %get-tuple-element.375), channel_id=1, source_target_pairs={{0,8},{8,16},{16,24},{24,0},{1,9},{9,17},{17,25},{25,1},{2,10},{10... | collective-permute-start | bytes 786440 | tf_op jit(solution)/shard_map/ppermute | solution.py:1028
  448.9 64.6 %all-to-all-start.6 = ((bf16[4,1024,256]{1,2,0:T(8,128)(2,1)}), bf16[4,1024,256]{1,2,0:T(8,128)(2,1)}, u32[]{:S(2)}, u32[]{:S(2)}) async-start(bf16[4,1024,256]{1,2,0:T(8,128)(2,1)} %fusion.15), calls=%async_computation.7 | async-start | bytes 4194304 | tf_op jit(solution)/shard_map/all_to_all | solution.py:1031
  453.5 128.8 %reduce-scatter.2.cloned.1.call-start = ((), (), s32[]{:S(2)}) async-start(), calls=%async_computation.9 | async-start | bytes 2621440 | tf_op jit(solution)/shard_map/reduce_scatter | solution.py:1238
  460.8 35.2 %collective-permute-start.30 = (bf16[1,2,272,1152]{3,2,1,0:T(8,128)(2,1)S(1)}, bf16[1,2,272,1152]{3,2,1,0:T(8,128)(2,1)S(1)}, u32[]{:S(2)}, u32[]{:S(2)}) collective-permute-start(bf16[1,2,272,1152]{3,2,1,0:T(8,128)(2,1)S(1)} %add_convert_fusion.1), channel_id=1, source_target_pairs={{0,2},{1,3},{2,0},{3,1},{4,6},{5,7},{6,4},{7,5},{8,10},{9,11},{10,... | collective-permute-start | bytes 3760136 | tf_op jit(solution)/shard_map/ppermute | solution.py:1019
  (148 other events, 1128.4 us)
Sparse Core Ops, SparseCore 0:
  23.1 44.6 all-gather.1
  531.9 50.3 reduce-scatter.1

commit v6 on v5

--- a/solution.py
+++ b/solution.py
@@ -112,7 +112,7 @@
         out_shape=[jax.ShapeDtypeStruct((rows, width), bf16)]
         + [jax.ShapeDtypeStruct((rows, cols), bf16)] * 3
         + [jax.ShapeDtypeStruct((rows, 128), f32)],
-        compiler_params=params(24),
+        compiler_params=params(56),
     )(place, *tokens, w, cosine, sine, gain, ones)
 
 
@@ -203,7 +203,7 @@
             jax.ShapeDtypeStruct((count * blk, cols), bf16),
             jax.ShapeDtypeStruct((count * blk, 128), f32),
         ],
-        compiler_params=params(20),
+        compiler_params=params(56),
     )(is_long, q, k, v)
 
 
@@ -352,7 +352,7 @@
             ],
         ),
         out_shape=outs,
-        compiler_params=params(28),
+        compiler_params=params(56),
     )(is_long, *ins)
 
 
@@ -489,7 +489,7 @@
         out_shape=[jax.ShapeDtypeStruct((rows, width), d) for d in (f32, f32, bf16)]
         + [jax.ShapeDtypeStruct((rows, 128), f32)]
         + [jax.ShapeDtypeStruct((parts, rows, n), bf16) for n in (cols, cols // 2)],
-        compiler_params=params(24),
+        compiler_params=params(56),
     )(place, *flat, ya, yb, x, alpha)
 
 
@@ -533,7 +533,7 @@
         out_shape=[jax.ShapeDtypeStruct(cot.shape, bf16)]
         + [jax.ShapeDtypeStruct((rows, width), d) for d in (bf16, f32)]
         + [jax.ShapeDtypeStruct((8, width), f32)],
-        compiler_params=params(24),
+        compiler_params=params(56),
     )(place, own, got, h1, cot, alpha)
 
 
@@ -597,7 +597,7 @@
         out_shape=[jax.ShapeDtypeStruct((rows, width), bf16)] * 2
         + [jax.ShapeDtypeStruct((8, width), f32)]
         + [jax.ShapeDtypeStruct((parts, blk, cols), bf16)] * 2,
-        compiler_params=params(30),
+        compiler_params=params(56),
     )(place, *flat, own, got, base, h1, ha, x, stat, alpha)
 
 
@@ -686,7 +686,7 @@
             pltpu.VMEM((2, width, 3 * half), bf16),
             pltpu.SemaphoreType.DMA((2, max(len(s) for s in slots))),
         ],
-        compiler_params=params(32),
+        compiler_params=params(56),
     )(*flat, ha, hb)
 
 
@@ -761,7 +761,7 @@
             pltpu.VMEM((2, width, 3 * half), bf16),
             pltpu.SemaphoreType.DMA((2, max(len(s) for s in slots))),
         ],
-        compiler_params=params(36),
+        compiler_params=params(56),
     )(*flat, da, db, uv)
 
 
@@ -882,7 +882,7 @@
         out_shape=[
             jax.ShapeDtypeStruct((len(one), middle, tall, size + hc), bf16) for one in lists
         ],
-        compiler_params=params(36),
+        compiler_params=params(56),
     )(place, *ins)
     return [out[0], out[2]], [out[1], out[3]]
 
@@ -1202,42 +1202,40 @@
 
     if not fast:
         through = relative(through)
-    through = through.astype(f32)
+
+    mine_at = z * (own // 2)
 
     def input_part(dqkv, side):
-        part = dot_t(dqkv, qkv_full)
-        mine_at = z * (own // 2)
-        here = lax.dynamic_slice_in_dim(part, mine_at, own // 2, 0)
-        here = here + through[side * (own // 2) : (side + 1) * (own // 2)]
-        return lax.dynamic_update_slice_in_dim(part.astype(bf16), here.astype(bf16), mine_at, 0)
+        part = dot_t(dqkv, qkv_full).astype(bf16)
+        here = lax.dynamic_slice_in_dim(part, mine_at, own // 2, 0).astype(f32)
+        here = here + through[side * (own // 2) : (side + 1) * (own // 2)].astype(f32)
+        return lax.dynamic_update_slice_in_dim(part, here.astype(bf16), mine_at, 0)
 
     dqkv_b, dk_part, dy_a = lax.optimization_barrier((dqkv_b, dk_part, dy_a))
     part_b = jnp.einsum(
         "tn,zcn->ztc", dqkv_b, qkv_full.reshape(nz, cols, 3 * cols), preferred_element_type=f32
-    )
-    mine_at = z * (own // 2)
-    here = lax.dynamic_slice_in_dim(part_b, mine_at, own // 2, 1)
-    here = here + through[own // 2 :].reshape(own // 2, nz, cols).transpose(1, 0, 2)
-    part_b = lax.dynamic_update_slice_in_dim(part_b.astype(bf16), here.astype(bf16), mine_at, 1)
+    ).astype(bf16)
+    here = lax.dynamic_slice_in_dim(part_b, mine_at, own // 2, 1).astype(f32)
+    here = here + through[own // 2 :].reshape(own // 2, nz, cols).transpose(1, 0, 2).astype(f32)
+    part_b = lax.dynamic_update_slice_in_dim(part_b, here.astype(bf16), mine_at, 1)
     down_along = [after(one, dqkv_b) for one in down_along]
-    sum_down_t = down_slots[0] + sum(one.astype(f32) for one in down_along)
     up_part, up_next = second(up_kept, [after(one, dqkv_b) for one in up_sent])
     part_got = exchange(part_b)
-    dk_part, dy_a, *_ = lax.optimization_barrier((dk_part, dy_a, *up_next, part_b, sum_down_t))
+    dk_part, dy_a, *_ = lax.optimization_barrier((dk_part, dy_a, *up_next, part_b, *down_along))
     dqkv_a, sqk_a = attn_bwd(*common(dy_a, y_a, logs_a), 0, middle, [dk_part, dv_part])
     input_b = jnp.sum(after(part_got, dqkv_a).astype(f32), axis=0)
-    up_part = wait_last(up_part, dqkv_a)
+    up_part = wait_last(up_part, dqkv_a, *[terms[-1] for terms in up_part])
     part_a = input_part(dqkv_a, 0)
     up_slots = slot_sums(up_part)
     passed = onward(up_slots[1].astype(bf16))
     for n in range(2, nz):
-        if n == nz - 1:
+        if n == nz - 2:
             passed, part_a = lax.optimization_barrier((passed, part_a))
         passed = onward((up_slots[n] + passed.astype(f32)).astype(bf16))
     sum_up_t = up_slots[0] + passed.astype(f32)
     input_a = lax.psum_scatter(part_a, "head", scatter_dimension=1, tiled=True)
     input_grad = jnp.concatenate([input_a.astype(f32), input_b], axis=0)
-    hidden_t = hidden.reshape(nz, 2, own // 2, cols).transpose(1, 0, 2, 3).reshape(rows, cols)
+    hidden_t = after(hidden, part_a).reshape(nz, 2, own // 2, cols).transpose(1, 0, 2, 3).reshape(rows, cols)
 
     dqkv = jnp.concatenate([dqkv_a, dqkv_b], axis=0)
     grad_qkv = t_dot(tokens_full, dqkv).astype(bf16)
@@ -1257,7 +1255,8 @@
         }
     cell = width // (nz * nb)
     sum_sqk = lax.dynamic_slice_in_dim(held[0][span, :cols], b * cell, cell, 0)
-    qkv_new = adam_wide(w_qkv, held[0][:span], moment_qkv, square_qkv)
+    w_late, m_late, v_late, _ = lax.optimization_barrier((w_qkv, moment_qkv, square_qkv, part_a))
+    qkv_new = adam_wide(w_late, held[0][:span], m_late, v_late)
 
     def both_halves(total):
         two = (total[:span], total[span : 2 * span])
@@ -1267,7 +1266,8 @@
         return [pick((here, there), core), pick((there, here), core)]
 
     join = lambda halves, at, size: [p[:span, at : at + size] for p in halves]
-    halves = both_halves(after(sum_down_t, part_a))
+    down_along = [after(one, part_a) for one in down_along]
+    halves = both_halves(down_slots[0] + sum(one.astype(f32) for one in down_along))
     down_new = adam_tall(w_down, jnp.concatenate(join(halves, 0, half), axis=1), moment_down, square_down)
     halves = both_halves(sum_up_t)
     grad_up = jnp.concatenate(join(halves, 0, half) + join(halves, half, half), axis=1)

time: 603 us -> 561 us (0.930)
  local copies, waits for them, and re-layouts: 106 us -> 33.7 us
  waiting for transfers between devices: 153 us -> 179 us
  starting transfers between devices: 85.5 us -> 76.7 us
  Pallas kernels: 159 us -> 166 us
    unnamed x265 -> x137, local copies, waits for them, and re-layouts: 92 us -> 23.6 us
    ppermute x12, waiting for transfers between devices: 95 us -> 129 us  [onward(): return lax.ppermute(value, 'head', [(i, (i + k) % nz) for i in range(nz)])]
    reduce_scatter x1, waiting for transfers between devices: 14.1 us -> 0.01 us  [per_device(): input_a = lax.psum_scatter(part_a, 'head', scatter_dimension=1, tiled=True)]
    ppermute x35, starting transfers between devices: 37.9 us -> 28.3 us  [swap_batch(): return lax.ppermute(value, 'batch', [(i, i ^ bit) for i in range(nb)])]
  transfers between devices with their start and end apart: 55 -> 55, of which waited for: 19 -> 20; matrix products, arithmetic and copies ran while one was open for 13% -> 14% of each run, Pallas kernels for 22% -> 24%
where the time goes in v6:
time: 561 us; the launch traced here: 550 us
  waiting for transfers between devices  179 us (32%)
  Pallas kernels  166 us (30%)
  starting transfers between devices  76.7 us (14%)
  other arithmetic  44.6 us (8%)
  local copies, waits for them, and re-layouts  33.7 us (6%)
  blocking collectives  19.6 us (3%)
  between operations  16.3 us (3%)
  matrix products  14.2 us (3%)
    ppermute x12, waiting for transfers between devices, onward(): return lax.ppermute(value, 'head', [(i, (i + k) % nz) for i in range(nz)])  129 us
    ppermute x35, waiting for transfers between devices, swap_batch(): return lax.ppermute(value, 'batch', [(i, i ^ bit) for i in range(nb)])  44.5 us
    pallas_call x2, Pallas kernels, attn_bwd(): pl.pallas_call(inner, grid_spec=pltpu.PrefetchScalarGridSpec(num_scalar_p...  33.1 us
    all_to_all x6, starting transfers between devices, exchange(): return lax.all_to_all(value, 'head', split_axis=0, concat_axis=0)  31.5 us
    pallas_call x2, Pallas kernels, weight_grads(): pl.pallas_call(functools.partial(grad_kernel, orders=(lists[:2], lists[2:...  29.2 us
    ppermute x35, starting transfers between devices, swap_batch(): return lax.ppermute(value, 'batch', [(i, i ^ bit) for i in range(nb)])  28.3 us
    pallas_call x1, Pallas kernels, mlp_bwd(): pl.pallas_call(functools.partial(mlp_bwd_kernel, half=half, counts=[len(s...  25 us
    unnamed x137, local copies, waits for them, and re-layouts  23.6 us
  transfers between devices with their start and end apart: 55, of which 20 were waited for; matrix products, arithmetic and copies ran while one was open for 14% of the time, Pallas kernels for 24%

profile of v6, /device:TPU:0, one launch (start us, length us, event | category | flops | bytes accessed | tf_op | source)
XLA Modules:
  0.0 550.4 jit_solution(2902880001190136675)
XLA Ops:
  21.5 19.8 %collective-permute-done.refs_1_ = bf16[2048,256]{1,0:T(8,128)(2,1)} collective-permute-done((bf16[2048,256]{1,0:T(8,128)(2,1)}, bf16[2048,256]{1,0:T(8,128)(2,1)}, u32[]{:S(2)}, u32[]{:S(2)}) %collective-permute-start) | collective-permute-done | bytes 1048608 | tf_op jit(solution)/shard_map/ppermute | solution.py:1028
  41.3 19.3 %collective-permute-done.2.refs_4_ = bf16[256,1792]{1,0:T(8,128)(2,1)S(1)} collective-permute-done((bf16[256,1792]{1,0:T(8,128)(2,1)S(1)}, bf16[256,1792]{1,0:T(8,128)(2,1)S(1)}, u32[]{:S(2)}, u32[]{:S(2)}) %collective-permute-start.2) | collective-permute-done | bytes 917536 | tf_op jit(solution)/shard_map/ppermute | solution.py:1028
  60.6 5.6 %collective-permute-done.5.refs_3_ = bf16[256,1792]{1,0:T(8,128)(2,1)} collective-permute-done((bf16[256,1792]{1,0:T(8,128)(2,1)S(1)}, bf16[256,1792]{1,0:T(8,128)(2,1)}, u32[]{:S(2)}, u32[]{:S(2)}) %collective-permute-start.5) | collective-permute-done | bytes 917536 | tf_op jit(solution)/shard_map/ppermute | solution.py:1019
  74.9 5.5 %fusion.10 = (f32[2048,128]{1,0:T(8,128)}, f32[2048,128]{1,0:T(8,128)}) fusion(f32[128]{0:T(128)S(1)} %get-tuple-element.423, f32[128]{0:T(128)S(1)} %get-tuple-element.424, f32[2048]{0:T(1024)S(1)} %convert_element_type.316), kind=kLoop, calls=%fused_computation.21 | loop fusion | flops 524288 | bytes 2106368 | tf_op jit(solution)/shard_map/mul | solution.py:1070
  80.5 12.3 %collective-permute-done.10.refs_7_ = bf16[256,1792]{1,0:T(8,128)(2,1)S(1)} collective-permute-done((bf16[256,1792]{1,0:T(8,128)(2,1)S(1)}, bf16[256,1792]{1,0:T(8,128)(2,1)S(1)}, u32[]{:S(2)}, u32[]{:S(2)}) %collective-permute-start.10) | collective-permute-done | bytes 917536 | tf_op jit(solution)/shard_map/ppermute | solution.py:1019
  92.8 19.2 %collective-permute-done.7.refs_8_ = bf16[256,1792]{1,0:T(8,128)(2,1)} collective-permute-done((bf16[256,1792]{1,0:T(8,128)(2,1)S(1)}, bf16[256,1792]{1,0:T(8,128)(2,1)}, u32[]{:S(2)}, u32[]{:S(2)}) %collective-permute-start.7) | collective-permute-done | bytes 917536 | tf_op jit(solution)/shard_map/ppermute | solution.py:1028
  116.7 21.7 %collective-permute-done.11.refs_3_ = bf16[2048,256]{1,0:T(8,128)(2,1)} collective-permute-done((bf16[2048,256]{1,0:T(8,128)(2,1)}, bf16[2048,256]{1,0:T(8,128)(2,1)}, u32[]{:S(2)}, u32[]{:S(2)}) %collective-permute-start.11) | collective-permute-done | bytes 1048608 | tf_op jit(solution)/shard_map/ppermute | solution.py:1028
  140.2 11.5 %shard_map.355 = (bf16[2048,1024]{1,0:T(8,128)(2,1)}, bf16[2048,256]{1,0:T(8,128)(2,1)}, bf16[2048,256]{1,0:T(8,128)(2,1)}, bf16[2048,256]{1,0:T(8,128)(2,1)}, f32[2048,128]{1,0:T(8,128)}) custom-call(s32[3]{0:T(128)} %pad_add_fusion.place_ref, bf16[2048,256]{1,0:T(8,128)(2,1)} %refs_0_.1, bf16[2048,256]{1,0:T(8,128)(2,1)} %collective-permute-done.refs_1_, ...), custom_call_target="tpu_custom_call" | custom-call | tf_op jit(solution)/shard_map/pallas_call | solution.py:102
  151.8 6.4 %shard_map.356 = (bf16[1024,256]{1,0:T(8,128)(2,1)}, f32[1024,128]{1,0:T(8,128)}) custom-call(s32[1]{0:T(128)S(6)} %convert_element_type.321.long_ref.r_0_, bf16[2048,256]{1,0:T(8,128)(2,1)} %get-tuple-element.203.q_ref.r_1_, bf16[2048,256]{1,0:T(8,128)(2,1)} %get-tuple-element.194.k_ref.r_2_.r_6_, bf16[2048,256]{1,0:T(8,128)(2,1)} %get-tuple-element.195.v_ref.r_7_), custom_call_target="tpu_custom_call" | custom-call | tf_op jit(solution)/shard_map/pallas_call | solution.py:193
  158.2 5.1 all-to-all-start
  166.9 6.7 %shard_map.357 = (bf16[1024,256]{1,0:T(8,128)(2,1)}, f32[1024,128]{1,0:T(8,128)}) custom-call(s32[1]{0:T(128)S(6)} %convert_element_type.321.long_ref.r_0_, bf16[2048,256]{1,0:T(8,128)(2,1)} %get-tuple-element.203.q_ref.r_1_, bf16[2048,256]{1,0:T(8,128)(2,1)} %get-tuple-element.194.k_ref.r_2_.r_6_, bf16[2048,256]{1,0:T(8,128)(2,1)} %get-tuple-element.195.v_ref.r_7_), custom_call_target="tpu_custom_call" | custom-call | tf_op jit(solution)/shard_map/pallas_call | solution.py:193
  174.7 19.6 %all_to_all.35.refs_17_ = bf16[4,256,256]{2,1,0:T(8,128)(2,1)} all-to-all(bf16[4,256,256]{2,1,0:T(8,128)(2,1)} %bitcast.102), channel_id=1, replica_groups=mesh['head'=4,'batch'=8] {'head'}, dimensions={0} | all-to-all | bytes 1048576 | tf_op jit(solution)/shard_map/all_to_all | solution.py:1031
  194.3 8.9 %collective-permute-done.17.refs_14_ = bf16[256,1792]{1,0:T(8,128)(2,1)S(1)} collective-permute-done((bf16[256,1792]{1,0:T(8,128)(2,1)}, bf16[256,1792]{1,0:T(8,128)(2,1)S(1)}, u32[]{:S(2)}, u32[]{:S(2)}) %collective-permute-start.17) | collective-permute-done | bytes 917536 | tf_op jit(solution)/shard_map/ppermute | solution.py:1019
  204.6 6.9 %shard_map.358 = (f32[512,1024]{1,0:T(8,128)}, f32[512,1024]{1,0:T(8,128)}, bf16[512,1024]{1,0:T(8,128)(2,1)}, f32[512,128]{1,0:T(8,128)}, bf16[4,512,256]{2,1,0:T(8,128)(2,1)}, /*index=5*/bf16[4,512,128]{2,1,0:T(8,128)(2,1)}) custom-call(s32[3]{0:T(128)} %pad_add_fusion.place_ref, bf16[256,1792]{1,0:T(8,128)(2,1)} %copy-done.14, ...), custom_call_target="tpu_custom_call" | custom-call | tf_op jit(solution)/shard_map/pallas_call | solution.py:476
  213.2 4.8 all-to-all-start.2
  219.1 20.4 %shard_map.359 = (bf16[4,1024,512]{2,1,0:T(8,128)(2,1)}, bf16[4,1024,1024]{2,1,0:T(8,128)(2,1)}, f32[512,1024]{1,0:T(8,128)}, bf16[512,1024]{1,0:T(8,128)(2,1)}) custom-call(bf16[256,1792]{1,0:T(8,128)(2,1)} %copy-done.14, bf16[256,1792]{1,0:T(8,128)(2,1)} %copy-done.17, bf16[256,1792]{1,0:T(8,128)(2,1)} %collective-permute-done.4.refs_2_, ...), custom_call_target="tpu_custom_call" | custom-call | tf_op jit(solution)/shard_map/pallas_call | solution.py:672
  245.4 6.4 %shard_map.360 = (bf16[4,512,256]{2,1,0:T(8,128)(2,1)}, bf16[512,1024]{1,0:T(8,128)(2,1)}, f32[512,1024]{1,0:T(8,128)}, f32[8,1024]{1,0:T(8,128)}) custom-call(s32[3]{0:T(128)} %pad_add_fusion.place_ref, f32[512,1024]{1,0:T(8,128)} %get-tuple-element.219.own_ref, bf16[512,1024]{1,0:T(8,128)(2,1)} %copy-done.45, ...), custom_call_target="tpu_custom_call" | custom-call | tf_op jit(solution)/shard_map/pallas_call | solution.py:525
  255.7 10.0 %shard_map.361 = (bf16[2,2,256,512]{3,2,1,0:T(8,128)(2,1)}, bf16[2,2,256,512]{3,2,1,0:T(8,128)(2,1)}, bf16[2,2,256,512]{3,2,1,0:T(8,128)(2,1)}, bf16[2,2,256,512]{3,2,1,0:T(8,128)(2,1)}) custom-call(s32[3]{0:T(128)} %pad_add_fusion.place_ref, bf16[512,1024]{1,0:T(8,128)(2,1)} %get-tuple-element.228.refs_0_.refs_16_, bf16[512,1024]{1,0:T(8,128)(2,1)} %copy-done.25, ...), custom_call_target="tpu_custom_call" | custom-call | tf_op jit(solution)/shard_map/pallas_call | solution.py:869
  270.9 25.0 %shard_map.362 = (bf16[4,1024,1024]{2,1,0:T(8,128)(2,1)}, f32[512,1024]{1,0:T(8,128)}, bf16[512,1024]{1,0:T(8,128)(2,1)}, f32[4,8,512]{2,1,0:T(8,128)}) custom-call(bf16[256,1792]{1,0:T(8,128)(2,1)} %copy-done.14, bf16[256,1792]{1,0:T(8,128)(2,1)} %copy-done.17, bf16[256,1792]{1,0:T(8,128)(2,1)} %collective-permute-done.4.refs_2_, ...), custom_call_target="tpu_custom_call" | custom-call | tf_op jit(solution)/shard_map/pallas_call | solution.py:738
  299.6 11.1 %shard_map.363 = (bf16[512,1024]{1,0:T(8,128)(2,1)}, bf16[512,1024]{1,0:T(8,128)(2,1)}, f32[8,1024]{1,0:T(8,128)}, bf16[4,256,256]{2,1,0:T(8,128)(2,1)}, bf16[4,256,256]{2,1,0:T(8,128)(2,1)}) custom-call(s32[3]{0:T(128)} %pad_add_fusion.place_ref, bf16[256,1792]{1,0:T(8,128)(2,1)} %copy-done.14, bf16[256,1792]{1,0:T(8,128)(2,1)} %copy-done.17, ...), custom_call_target="tpu_custom_call" | custom-call | tf_op jit(solution)/shard_map/pallas_call | solution.py:585
  310.8 5.5 %all-to-all-start.4 = ((bf16[4,256,256]{2,1,0:T(8,128)(2,1)}), bf16[4,256,256]{2,1,0:T(8,128)(2,1)S(1)}, u32[]{:S(2)}, u32[]{:S(2)}) async-start(bf16[4,256,256]{2,1,0:T(8,128)(2,1)} %get-tuple-element.251), calls=%async_computation.4 | async-start | bytes 1048576 | tf_op jit(solution)/shard_map/all_to_all | solution.py:1031
  320.0 19.2 %shard_map.364 = (bf16[2,2,272,1152]{3,2,1,0:T(8,128)(2,1)}, bf16[2,2,272,1152]{3,2,1,0:T(8,128)(2,1)}, bf16[2,2,272,1152]{3,2,1,0:T(8,128)(2,1)}, bf16[2,2,272,1152]{3,2,1,0:T(8,128)(2,1)}) custom-call(s32[3]{0:T(128)} %pad_add_fusion.place_ref, bf16[512,1024]{1,0:T(8,128)(2,1)} %get-tuple-element.216.refs_16_.refs_0_, bf16[512,1024]{1,0:T(8,128)(2,1)} %copy-done.30, ...), custom_call_target="tpu_custom_call" | custom-call | tf_op jit(solution)/shard_map/pallas_call | solution.py:869
  340.8 5.1 all-to-all-start.5
  355.9 16.7 %shard_map.365 = (bf16[1024,768]{1,0:T(8,128)(2,1)}, f32[1024,256]{1,0:T(8,128)}, f32[1024,256]{1,0:T(8,128)}, f32[8,256]{1,0:T(8,128)}) custom-call(s32[1]{0:T(128)S(6)} %convert_element_type.321.long_ref.r_0_, bf16[2048,256]{1,0:T(8,128)(2,1)} %get-tuple-element.203.q_ref.r_1_, bf16[2048,256]{1,0:T(8,128)(2,1)} %get-tuple-element.194.k_ref.r_2_.r_6_, ...), custom_call_target="tpu_custom_call" | custom-call | tf_op jit(solution)/shard_map/pallas_call | solution.py:340
  372.6 4.8 collective-permute-done.33
  383.5 7.2 %all-to-all-start.6 = ((bf16[4,1024,256]{1,2,0:T(8,128)(2,1)}), bf16[4,1024,256]{1,2,0:T(8,128)(2,1)S(1)}, u32[]{:S(2)}, u32[]{:S(2)}) async-start(bf16[4,1024,256]{1,2,0:T(8,128)(2,1)} %fusion.14), calls=%async_computation.7 | async-start | bytes 4194304 | tf_op jit(solution)/shard_map/all_to_all | solution.py:1031
  403.1 16.5 %shard_map.366 = (bf16[1024,768]{1,0:T(8,128)(2,1)}, f32[8,256]{1,0:T(8,128)}) custom-call(s32[1]{0:T(128)S(6)} %convert_element_type.321.long_ref.r_0_, bf16[2048,256]{1,0:T(8,128)(2,1)} %get-tuple-element.203.q_ref.r_1_, bf16[2048,256]{1,0:T(8,128)(2,1)} %get-tuple-element.194.k_ref.r_2_.r_6_, bf16[1024,256]{1,0:T(8,128)(2,1)} %bitcast.103, ...), custom_call_target="tpu_custom_call" | custom-call | tf_op jit(solution)/shard_map/pallas_call | solution.py:340
  419.6 5.4 fusion.4
  431.1 5.1 convolution_convert_fusion
  445.4 5.6 %collective-permute-done.38 = bf16[288,768]{1,0:T(8,128)(2,1)} collective-permute-done((bf16[288,768]{1,0:T(8,128)(2,1)}, bf16[288,768]{1,0:T(8,128)(2,1)}, u32[]{:S(2)}, u32[]{:S(2)}) %collective-permute-start.38) | collective-permute-done | bytes 442400 | tf_op jit(solution)/shard_map/ppermute | solution.py:1019
  465.6 20.1 %collective-permute-done.40 = bf16[272,1152]{1,0:T(8,128)(2,1)S(1)} collective-permute-done((bf16[272,1152]{1,0:T(8,128)(2,1)S(1)}, bf16[272,1152]{1,0:T(8,128)(2,1)S(1)}, u32[]{:S(2)}, u32[]{:S(2)}) %collective-permute-start.40) | collective-permute-done | bytes 626720 | tf_op jit(solution)/shard_map/ppermute | solution.py:1028
  500.1 19.4 %collective-permute-done.41 = bf16[272,1152]{1,0:T(8,128)(2,1)} collective-permute-done((bf16[272,1152]{1,0:T(8,128)(2,1)}, bf16[272,1152]{1,0:T(8,128)(2,1)}, u32[]{:S(2)}, u32[]{:S(2)}) %collective-permute-start.41) | collective-permute-done | bytes 626720 | tf_op jit(solution)/shard_map/ppermute | solution.py:1028
  (327 shorter events, 157.1 us)
Async XLA Ops:
  7.2 133.0 %all-gather.2.cloned.1.call-start = ((), (), s32[]{:S(2)}) async-start(), calls=%async_computation.8 | async-start | bytes 1769472 | tf_op jit(solution)/shard_map/all_gather | solution.py:1055
  12.3 29.0 %collective-permute-start = (bf16[2048,256]{1,0:T(8,128)(2,1)}, bf16[2048,256]{1,0:T(8,128)(2,1)}, u32[]{:S(2)}, u32[]{:S(2)}) collective-permute-start(bf16[2048,256]{1,0:T(8,128)(2,1)} %refs_0_.1), channel_id=1, source_target_pairs={{0,8},{8,16},{16,24},{24,0},{1,9},{9,17},{17,25},{25,1},{2,10},{10... | collective-permute-start | bytes 3145736 | tf_op jit(solution)/shard_map/ppermute | solution.py:1028
  15.1 45.5 %collective-permute-start.2 = (bf16[256,1792]{1,0:T(8,128)(2,1)S(1)}, bf16[256,1792]{1,0:T(8,128)(2,1)S(1)}, u32[]{:S(2)}, u32[]{:S(2)}) collective-permute-start(bf16[256,1792]{1,0:T(8,128)(2,1)S(1)} %pad_maximum_fusion.1.refs_0_), channel_id=1, source_target_pairs={{0,8},{8,16},{16,24},{24,0},{1,9},{9,17},{17,25},{25,1},{2,10},{10... | collective-permute-start | bytes 2752520 | tf_op jit(solution)/shard_map/ppermute | solution.py:1028
  16.9 43.7 %collective-permute-start.3 = (bf16[256,1792]{1,0:T(8,128)(2,1)S(1)}, bf16[256,1792]{1,0:T(8,128)(2,1)S(1)}, u32[]{:S(2)}, u32[]{:S(2)}) collective-permute-start(bf16[256,1792]{1,0:T(8,128)(2,1)S(1)} %pad_maximum_fusion.1.refs_0_), channel_id=1, source_target_pairs={{0,2},{1,3},{2,0},{3,1},{4,6},{5,7},{6,4},{7,5},{8,10},{9,11},{10,... | collective-permute-start | bytes 2752520 | tf_op jit(solution)/shard_map/ppermute | solution.py:1019
  18.4 42.2 %collective-permute-start.4 = (bf16[256,1792]{1,0:T(8,128)(2,1)S(1)}, bf16[256,1792]{1,0:T(8,128)(2,1)}, u32[]{:S(2)}, u32[]{:S(2)}) collective-permute-start(bf16[256,1792]{1,0:T(8,128)(2,1)S(1)} %pad_maximum_fusion.1.refs_0_), channel_id=1, source_target_pairs={{0,4},{1,5},{2,6},{3,7},{4,0},{5,1},{6,2},{7,3},{8,12},{9,13},{10,... | collective-permute-start | bytes 2752520 | tf_op jit(solution)/shard_map/ppermute | solution.py:1019
  20.0 46.2 %collective-permute-start.5 = (bf16[256,1792]{1,0:T(8,128)(2,1)S(1)}, bf16[256,1792]{1,0:T(8,128)(2,1)}, u32[]{:S(2)}, u32[]{:S(2)}) collective-permute-start(bf16[256,1792]{1,0:T(8,128)(2,1)S(1)} %pad_maximum_fusion.1.refs_0_), channel_id=1, source_target_pairs={{0,6},{1,7},{2,4},{3,5},{4,2},{5,3},{6,0},{7,1},{8,14},{9,15},{10,... | collective-permute-start | bytes 2752520 | tf_op jit(solution)/shard_map/ppermute | solution.py:1019
  66.2 45.8 %collective-permute-start.6 = (bf16[2048,256]{1,0:T(8,128)(2,1)}, bf16[2048,256]{1,0:T(8,128)(2,1)}, u32[]{:S(2)}, u32[]{:S(2)}) collective-permute-start(bf16[2048,256]{1,0:T(8,128)(2,1)} %collective-permute-done.refs_1_), channel_id=1, source_target_pairs={{0,8},{8,16},{16,24},{24,0},{1,9},{9,17},{17,25},{25,1},{2,10},{10... | collective-permute-start | bytes 3145736 | tf_op jit(solution)/shard_map/ppermute | solution.py:1028
  69.9 42.0 %collective-permute-start.7 = (bf16[256,1792]{1,0:T(8,128)(2,1)S(1)}, bf16[256,1792]{1,0:T(8,128)(2,1)}, u32[]{:S(2)}, u32[]{:S(2)}) collective-permute-start(bf16[256,1792]{1,0:T(8,128)(2,1)S(1)} %collective-permute-done.2.refs_4_), channel_id=1, source_target_pairs={{0,8},{8,16},{16,24},{24,0},{1,9},{9,17},{17,25},{25,1},{2,10},{10... | collective-permute-start | bytes 2752520 | tf_op jit(solution)/shard_map/ppermute | solution.py:1028
  71.5 40.5 %collective-permute-start.8 = (bf16[256,1792]{1,0:T(8,128)(2,1)S(1)}, bf16[256,1792]{1,0:T(8,128)(2,1)S(1)}, u32[]{:S(2)}, u32[]{:S(2)}) collective-permute-start(bf16[256,1792]{1,0:T(8,128)(2,1)S(1)} %collective-permute-done.2.refs_4_), channel_id=1, source_target_pairs={{0,2},{1,3},{2,0},{3,1},{4,6},{5,7},{6,4},{7,5},{8,10},{9,11},{10,... | collective-permute-start | bytes 2752520 | tf_op jit(solution)/shard_map/ppermute | solution.py:1019
  72.1 39.9 %collective-permute-start.9 = (bf16[256,1792]{1,0:T(8,128)(2,1)S(1)}, bf16[256,1792]{1,0:T(8,128)(2,1)S(1)}, u32[]{:S(2)}, u32[]{:S(2)}) collective-permute-start(bf16[256,1792]{1,0:T(8,128)(2,1)S(1)} %collective-permute-done.2.refs_4_), channel_id=1, source_target_pairs={{0,4},{1,5},{2,6},{3,7},{4,0},{5,1},{6,2},{7,3},{8,12},{9,13},{10,... | collective-permute-start | bytes 2752520 | tf_op jit(solution)/shard_map/ppermute | solution.py:1019
  113.2 25.2 %collective-permute-start.11 = (bf16[2048,256]{1,0:T(8,128)(2,1)}, bf16[2048,256]{1,0:T(8,128)(2,1)}, u32[]{:S(2)}, u32[]{:S(2)}) collective-permute-start(bf16[2048,256]{1,0:T(8,128)(2,1)} %collective-permute-done.6.refs_2_), channel_id=1, source_target_pairs={{0,8},{8,16},{16,24},{24,0},{1,9},{9,17},{17,25},{25,1},{2,10},{10... | collective-permute-start | bytes 3145736 | tf_op jit(solution)/shard_map/ppermute | solution.py:1028
  113.2 50.0 %collective-permute-start.13 = (bf16[256,1792]{1,0:T(8,128)(2,1)}, bf16[256,1792]{1,0:T(8,128)(2,1)}, u32[]{:S(2)}, u32[]{:S(2)}) collective-permute-start(bf16[256,1792]{1,0:T(8,128)(2,1)} %collective-permute-done.7.refs_8_), channel_id=1, source_target_pairs={{0,2},{1,3},{2,0},{3,1},{4,6},{5,7},{6,4},{7,5},{8,10},{9,11},{10,... | collective-permute-start | bytes 2752520 | tf_op jit(solution)/shard_map/ppermute | solution.py:1019
  114.7 48.6 %collective-permute-start.14 = (bf16[256,1792]{1,0:T(8,128)(2,1)}, bf16[256,1792]{1,0:T(8,128)(2,1)}, u32[]{:S(2)}, u32[]{:S(2)}) collective-permute-start(bf16[256,1792]{1,0:T(8,128)(2,1)} %collective-permute-done.7.refs_8_), channel_id=1, source_target_pairs={{0,4},{1,5},{2,6},{3,7},{4,0},{5,1},{6,2},{7,3},{8,12},{9,13},{10,... | collective-permute-start | bytes 2752520 | tf_op jit(solution)/shard_map/ppermute | solution.py:1019
  115.2 48.1 %collective-permute-start.15 = (bf16[256,1792]{1,0:T(8,128)(2,1)}, bf16[256,1792]{1,0:T(8,128)(2,1)}, u32[]{:S(2)}, u32[]{:S(2)}) collective-permute-start(bf16[256,1792]{1,0:T(8,128)(2,1)} %collective-permute-done.7.refs_8_), channel_id=1, source_target_pairs={{0,6},{1,7},{2,4},{3,5},{4,2},{5,3},{6,0},{7,1},{8,14},{9,15},{10,... | collective-permute-start | bytes 2752520 | tf_op jit(solution)/shard_map/ppermute | solution.py:1019
  163.3 31.0 %collective-permute-start.16 = (bf16[256,1792]{1,0:T(8,128)(2,1)}, bf16[256,1792]{1,0:T(8,128)(2,1)S(1)}, u32[]{:S(2)}, u32[]{:S(2)}) collective-permute-start(bf16[256,1792]{1,0:T(8,128)(2,1)} %collective-permute-done.12.refs_12_), channel_id=1, source_target_pairs={{0,2},{1,3},{2,0},{3,1},{4,6},{5,7},{6,4},{7,5},{8,10},{9,11},{10,... | collective-permute-start | bytes 2752520 | tf_op jit(solution)/shard_map/ppermute | solution.py:1019
  164.9 38.4 %collective-permute-start.17 = (bf16[256,1792]{1,0:T(8,128)(2,1)}, bf16[256,1792]{1,0:T(8,128)(2,1)S(1)}, u32[]{:S(2)}, u32[]{:S(2)}) collective-permute-start(bf16[256,1792]{1,0:T(8,128)(2,1)} %collective-permute-done.12.refs_12_), channel_id=1, source_target_pairs={{0,4},{1,5},{2,6},{3,7},{4,0},{5,1},{6,2},{7,3},{8,12},{9,13},{10,... | collective-permute-start | bytes 2752520 | tf_op jit(solution)/shard_map/ppermute | solution.py:1019
  165.3 38.0 %collective-permute-start.18 = (bf16[256,1792]{1,0:T(8,128)(2,1)}, bf16[256,1792]{1,0:T(8,128)(2,1)S(1)}, u32[]{:S(2)}, u32[]{:S(2)}) collective-permute-start(bf16[256,1792]{1,0:T(8,128)(2,1)} %collective-permute-done.12.refs_12_), channel_id=1, source_target_pairs={{0,6},{1,7},{2,4},{3,5},{4,2},{5,3},{6,0},{7,1},{8,14},{9,15},{10,... | collective-permute-start | bytes 2752520 | tf_op jit(solution)/shard_map/ppermute | solution.py:1019
  213.2 30.8 %all-to-all-start.2 = ((bf16[4,512,256]{2,1,0:T(8,128)(2,1)}), bf16[4,512,256]{2,1,0:T(8,128)(2,1)S(1)}, u32[]{:S(2)}, u32[]{:S(2)}) async-start(bf16[4,512,256]{2,1,0:T(8,128)(2,1)} %bitcast.17), calls=%async_computation.2 | async-start | bytes 2097152 | tf_op jit(solution)/shard_map/all_to_all | solution.py:1031
  265.7 30.3 %collective-permute-start.24 = (bf16[2,2,256,512]{3,2,1,0:T(8,128)(2,1)}, bf16[2,2,256,512]{3,2,1,0:T(8,128)(2,1)S(1)}, u32[]{:S(2)}, u32[]{:S(2)}) collective-permute-start(bf16[2,2,256,512]{3,2,1,0:T(8,128)(2,1)} %get-tuple-element.227), channel_id=1, source_target_pairs={{0,4},{1,5},{2,6},{3,7},{4,0},{5,1},{6,2},{7,3},{8,12},{9,13},{10,... | collective-permute-start | bytes 3145736 | tf_op jit(solution)/shard_map/ppermute | solution.py:1019
  266.1 29.9 %collective-permute-start.23 = (bf16[2,2,256,512]{3,2,1,0:T(8,128)(2,1)}, bf16[2,2,256,512]{3,2,1,0:T(8,128)(2,1)}, u32[]{:S(2)}, u32[]{:S(2)}) collective-permute-start(bf16[2,2,256,512]{3,2,1,0:T(8,128)(2,1)} %get-tuple-element.226), channel_id=1, source_target_pairs={{0,2},{1,3},{2,0},{3,1},{4,6},{5,7},{6,4},{7,5},{8,10},{9,11},{10,... | collective-permute-start | bytes 3145736 | tf_op jit(solution)/shard_map/ppermute | solution.py:1019
  267.1 32.5 %all-to-all-start.3 = ((bf16[4,512,256]{2,1,0:T(8,128)(2,1)}), bf16[4,512,256]{2,1,0:T(8,128)(2,1)S(1)}, u32[]{:S(2)}, u32[]{:S(2)}) async-start(bf16[4,512,256]{2,1,0:T(8,128)(2,1)} %get-tuple-element.232), calls=%async_computation.3 | async-start | bytes 2097152 | tf_op jit(solution)/shard_map/all_to_all | solution.py:1031
  310.8 28.5 %all-to-all-start.4 = ((bf16[4,256,256]{2,1,0:T(8,128)(2,1)}), bf16[4,256,256]{2,1,0:T(8,128)(2,1)S(1)}, u32[]{:S(2)}, u32[]{:S(2)}) async-start(bf16[4,256,256]{2,1,0:T(8,128)(2,1)} %get-tuple-element.251), calls=%async_computation.4 | async-start | bytes 1048576 | tf_op jit(solution)/shard_map/all_to_all | solution.py:1031
  339.3 56.3 %collective-permute-start.31 = (bf16[2,2,272,1152]{3,2,1,0:T(8,128)(2,1)}, bf16[2,2,272,1152]{3,2,1,0:T(8,128)(2,1)}, u32[]{:S(2)}, u32[]{:S(2)}) collective-permute-start(bf16[2,2,272,1152]{3,2,1,0:T(8,128)(2,1)} %get-tuple-element.269), channel_id=1, source_target_pairs={{0,4},{1,5},{2,6},{3,7},{4,0},{5,1},{6,2},{7,3},{8,12},{9,13},{10,... | collective-permute-start | bytes 7520264 | tf_op jit(solution)/shard_map/ppermute | solution.py:1019
  339.8 58.9 %collective-permute-start.29 = (bf16[2,2,272,1152]{3,2,1,0:T(8,128)(2,1)}, bf16[2,2,272,1152]{3,2,1,0:T(8,128)(2,1)}, u32[]{:S(2)}, u32[]{:S(2)}) collective-permute-start(bf16[2,2,272,1152]{3,2,1,0:T(8,128)(2,1)} %get-tuple-element.258), channel_id=1, source_target_pairs={{0,2},{1,3},{2,0},{3,1},{4,6},{5,7},{6,4},{7,5},{8,10},{9,11},{10,... | collective-permute-start | bytes 7520264 | tf_op jit(solution)/shard_map/ppermute | solution.py:1019
  340.8 31.8 %all-to-all-start.5 = ((bf16[4,256,256]{2,1,0:T(8,128)(2,1)}), bf16[4,256,256]{2,1,0:T(8,128)(2,1)S(1)}, u32[]{:S(2)}, u32[]{:S(2)}) async-start(bf16[4,256,256]{2,1,0:T(8,128)(2,1)} %get-tuple-element.264), calls=%async_computation.5 | async-start | bytes 1048576 | tf_op jit(solution)/shard_map/all_to_all | solution.py:1031
  350.2 27.2 %collective-permute-start.33 = (bf16[256,512]{1,0:T(8,128)(2,1)}, bf16[256,512]{1,0:T(8,128)(2,1)}, u32[]{:S(2)}, u32[]{:S(2)}) collective-permute-start(bf16[256,512]{1,0:T(8,128)(2,1)} %get-tuple-element.387), channel_id=1, source_target_pairs={{0,16},{8,24},{16,0},{24,8},{1,17},{9,25},{17,1},{25,9},{2,18},{10... | collective-permute-start | bytes 786440 | tf_op jit(solution)/shard_map/ppermute | solution.py:1028
  383.5 70.2 %all-to-all-start.6 = ((bf16[4,1024,256]{1,2,0:T(8,128)(2,1)}), bf16[4,1024,256]{1,2,0:T(8,128)(2,1)S(1)}, u32[]{:S(2)}, u32[]{:S(2)}) async-start(bf16[4,1024,256]{1,2,0:T(8,128)(2,1)} %fusion.14), calls=%async_computation.7 | async-start | bytes 4194304 | tf_op jit(solution)/shard_map/all_to_all | solution.py:1031
  390.7 149.8 %reduce-scatter.2.cloned.1.call-start = ((), (), s32[]{:S(2)}) async-start(), calls=%async_computation.9 | async-start | bytes 2621440 | tf_op jit(solution)/shard_map/reduce_scatter | solution.py:1236
  401.3 37.5 %collective-permute-start.35 = (bf16[1,2,272,1152]{3,2,1,0:T(8,128)(2,1)}, bf16[1,2,272,1152]{3,2,1,0:T(8,128)(2,1)}, u32[]{:S(2)}, u32[]{:S(2)}) collective-permute-start(bf16[1,2,272,1152]{3,2,1,0:T(8,128)(2,1)} %add_convert_fusion), channel_id=1, source_target_pairs={{0,2},{1,3},{2,0},{3,1},{4,6},{5,7},{6,4},{7,5},{8,10},{9,11},{10,... | collective-permute-start | bytes 3760136 | tf_op jit(solution)/shard_map/ppermute | solution.py:1019
  401.8 37.0 %collective-permute-start.30 = (bf16[1,2,272,1152]{3,2,1,0:T(8,128)(2,1)}, bf16[1,2,272,1152]{3,2,1,0:T(8,128)(2,1)S(1)}, u32[]{:S(2)}, u32[]{:S(2)}) collective-permute-start(bf16[1,2,272,1152]{3,2,1,0:T(8,128)(2,1)} %add_convert_fusion.1), channel_id=1, source_target_pairs={{0,4},{1,5},{2,6},{3,7},{4,0},{5,1},{6,2},{7,3},{8,12},{9,13},{10,... | collective-permute-start | bytes 3760136 | tf_op jit(solution)/shard_map/ppermute | solution.py:1019
  465.5 31.6 %collective-permute-start.43 = (bf16[128,512]{1,0:T(8,128)(2,1)S(1)}, bf16[128,512]{1,0:T(8,128)(2,1)S(1)}, u32[]{:S(2)}, u32[]{:S(2)}) collective-permute-start(bf16[128,512]{1,0:T(8,128)(2,1)S(1)} %select_convert_fusion.1), channel_id=1, source_target_pairs={{0,1},{1,0},{2,3},{3,2},{4,5},{5,4},{6,7},{7,6},{8,9},{9,8},{10,11... | collective-permute-start | bytes 393224 | tf_op jit(solution)/shard_map/ppermute | solution.py:1019
  488.3 31.1 %collective-permute-start.41 = (bf16[272,1152]{1,0:T(8,128)(2,1)}, bf16[272,1152]{1,0:T(8,128)(2,1)}, u32[]{:S(2)}, u32[]{:S(2)}) collective-permute-start(bf16[272,1152]{1,0:T(8,128)(2,1)} %fusion.9), channel_id=1, source_target_pairs={{0,8},{8,16},{16,24},{24,0},{1,9},{9,17},{17,25},{25,1},{2,10},{10... | collective-permute-start | bytes 1880072 | tf_op jit(solution)/shard_map/ppermute | solution.py:1028
  (85 other events, 1119.6 us)
Sparse Core Ops, SparseCore 0:
  21.6 46.2 all-gather.1
  464.0 63.4 reduce-scatter.1

commit v7 on v6

--- a/solution.py
+++ b/solution.py
@@ -209,7 +209,7 @@
 
 def attn_bwd_kernel(
     long_ref, q_ref, qk_ref, dy_ref, y_ref, l_ref, k_ref, v_ref, rho_ref, cos_ref, sin_ref, gain_ref,
-    ones_ref, dk_in, dv_in, out_ref, dk_out, dv_out, s_ref, acc, dk_acc, dv_acc, stats, *, heads, blk, sub, first, count
+    ones_ref, dk_in, dv_in, out_ref, dk_out, dv_out, s_ref, acc, dk_acc, dv_acc, stats, dys, *, heads, blk, sub, first, count
 ):
     step = pl.program_id(0)
     local = count - 1 - step
@@ -231,7 +231,8 @@
             dv_acc[...] = dv_in[...]
 
     acc[...] = jnp.zeros_like(acc)
-    prod = dy_ref[...].astype(f32) * y_ref[...].astype(f32)
+    dys[...] = dy_ref[...].reshape(dys.shape)
+    prod = dys[...].astype(f32) * y_ref[...].astype(f32)
     high = prod.astype(bf16)
     rest = (prod - high.astype(f32)).astype(bf16)
     pickers = (
@@ -245,7 +246,7 @@
         keys = k_ref[pl.ds(at, size), :]
         vals = v_ref[pl.ds(at, size), :]
         q = q_ref[rows, :]
-        dy = dy_ref[rows, :]
+        dy = dys[rows, :]
         total_q = jnp.zeros(q.shape, f32)
         total_k = jnp.zeros(keys.shape, f32)
         total_v = jnp.zeros(keys.shape, f32)
@@ -320,7 +321,13 @@
     whole = pl.BlockSpec((top, cols), lambda s, m: (0, 0))
     ins = [q, k, dy, y, logs, k, v, rho, cosine, sine, gain, ones]
     mine = lambda n: pl.BlockSpec((blk, n), lambda s, m: (count - 1 - s, 0))
-    in_specs = [row(cols)] * 2 + [mine(cols)] * 2 + [mine(128), whole, whole] + [row(128)] * 3
+    share = dy.shape[2]
+    half_at = 1 if first else 0
+    in_specs = [row(cols)] * 2
+    in_specs.append(
+        pl.BlockSpec((blk // share, None, share, cols), lambda s, m: (count - 1 - s, half_at, 0, 0))
+    )
+    in_specs += [mine(cols), mine(128), whole, whole] + [row(128)] * 3
     in_specs += [full_spec((1, cols)), full_spec((cols, cols))]
     body = functools.partial(
         attn_bwd_kernel, heads=heads, blk=blk, sub=sub, first=first, count=count
@@ -349,6 +356,7 @@
                 pltpu.VMEM((top, cols), f32),
                 pltpu.VMEM((top, cols), f32),
                 pltpu.VMEM((16, blk), f32),
+                pltpu.VMEM((blk, cols), bf16),
             ],
         ),
         out_shape=outs,
@@ -541,7 +549,7 @@
     total = sum(counts)
     flat, refs = refs[:total], refs[total:]
     own_ref, got_ref, base_ref, h1_ref, ha_ref, x_ref, stat_ref, alpha_ref = refs[:8]
-    do_ref, through_ref, ga_ref, dya_ref, dyb_ref = refs[8:]
+    do_ref, through_ref, ga_ref, dy_ref = refs[8:]
     z, chip = place_ref[0], place_ref[1]
     alpha = alpha_ref[...]
     grad = base_ref[...] + own_ref[...] + got_ref[...].astype(f32)
@@ -555,18 +563,13 @@
     index = 0
     for n in range(parts):
         at = lax.rem(z + parts - n, parts)
-        part = jnp.zeros(dya_ref.shape[1:], f32)
+        part = jnp.zeros(dy_ref.shape[1:], f32)
         column = 0
         for piece in flat[index : index + counts[n]]:
-            part += dot(do_ref[:, column : column + piece.shape[0]], piece[...])
+            part += dot(back[:, column : column + piece.shape[0]], piece[...])
             column += piece.shape[0]
         index += counts[n]
-        part = part.astype(bf16)
-        for side, ref in enumerate((dya_ref, dyb_ref)):
-
-            @pl.when(step == side)
-            def _(ref=ref, part=part, at=at):
-                ref[at] = part
+        dy_ref[at] = part.astype(bf16)
 
     @pl.when(step == 0)
     def _():
@@ -591,12 +594,13 @@
             + [row(width)] * 5
             + [own_rows(blk, parts, width, fast), row(128), full_spec((1, width))],
             out_specs=[row(width)] * 2
-            + [full_spec((8, width))]
-            + [full_spec((parts, blk, cols))] * 2,
+            + [full_spec((8, width)), pl.BlockSpec((parts, blk, cols), lambda i, s: (0, i, 0))],
         ),
         out_shape=[jax.ShapeDtypeStruct((rows, width), bf16)] * 2
-        + [jax.ShapeDtypeStruct((8, width), f32)]
-        + [jax.ShapeDtypeStruct((parts, blk, cols), bf16)] * 2,
+        + [
+            jax.ShapeDtypeStruct((8, width), f32),
+            jax.ShapeDtypeStruct((parts, rows, cols), bf16),
+        ],
         compiler_params=params(56),
     )(place, *flat, own, got, base, h1, ha, x, stat, alpha)
 
@@ -887,6 +891,24 @@
     return [out[0], out[2]], [out[1], out[3]]
 
 
+def pair_sum_kernel(ka_ref, ga_ref, kb_ref, gb_ref, a_ref, b_ref):
+    a_ref[...] = (ka_ref[...].astype(f32) + ga_ref[...].astype(f32)).astype(bf16)
+    b_ref[...] = (kb_ref[...].astype(f32) + gb_ref[...].astype(f32)).astype(bf16)
+
+
+def pair_sums(kept, got, at):
+    _, slots, tall, wide = kept[0].shape
+    spec = lambda n: pl.BlockSpec((None, None, tall, wide), lambda k, n=n: (n, k, 0, 0))
+    return pl.pallas_call(
+        pair_sum_kernel,
+        grid=(slots,),
+        in_specs=[spec(at[0]), spec(at[0]), spec(at[1]), spec(at[1])],
+        out_specs=[spec(0)] * 2,
+        out_shape=[jax.ShapeDtypeStruct((1, slots, tall, wide), bf16)] * 2,
+        compiler_params=params(56),
+    )(kept[0], got[0], kept[1], got[1])
+
+
 def adam_values(weight, grad, first, second):
     first_new = beta_one * first + (1.0 - beta_one) * grad
     second_new = beta_two * second + (1.0 - beta_two) * grad * grad
@@ -1135,6 +1157,13 @@
 
     def second(kept, sent):
         found, sends = [], []
+        if chips == 4:
+            at = [[n for n, r in enumerate(left) if r & order[1]] for order, left in zip(orders, kept_at)]
+            sends = pair_sums(kept, sent, [one[0] for one in at])
+            for order, one, keep, got, send in zip(orders, at, kept, sent, sends):
+                cut = lambda t, n=1 - one[0]: t[n : n + 1]
+                found.append([cut(keep), cut(got), swap_chip(send, order[1])])
+            return found, sends
         for order, left, got, keep in zip(orders, kept_at, sent, kept):
             terms = [keep, got]
             for bit in order[1:]:
@@ -1162,10 +1191,10 @@
     down_sent = [after(one, dh_other) for one in down_sent]
     down_part, down_next = second(down_kept, down_sent)
     dh_own, hidden, *_ = lax.optimization_barrier((dh_own, hidden, *down_next))
-    do_own, through, ga_attn, dy_a, dy_b = first_back(
+    do_own, through, ga_attn, dy = first_back(
         place, dh_own, dh_got, base, h1, hA, start, stat, attn_gain, slots, chips, fast, cols
     )
-    dy_b = exchange(dy_b)
+    dy = exchange(dy)
     do_got = swap_core(do_own)
 
     extra = (gsuv, ga_attn, ga_mlp)
@@ -1186,18 +1215,18 @@
     )
     down_part = wait_last(down_part, *up_kept)
     down_last = [terms[-1] for terms in down_part]
-    dy_b, dy_a, *both = lax.optimization_barrier((dy_b, dy_a, *up_made, *down_last))
+    dy, *both = lax.optimization_barrier((dy, *up_made, *down_last))
     up_made, down_last = both[: len(up_made)], both[len(up_made) :]
     down_slots = slot_sums([t[:-1] + [last] for t, last in zip(down_part, down_last)])
     down_along = [onward(down_slots[n].astype(bf16), nz - n) for n in range(1, nz)]
     up_sent = [swap_chip(one, order[0]) for one, order in zip(up_made, orders)]
 
-    dy_a = exchange(dy_a)
-    common = lambda dy, y, logs: (
-        is_long, q, k, v, dy.reshape(y.shape), y, logs, rho, cosine, sine, gain, ones
+    dy = dy.reshape(nz, 2, own // 2, cols)
+    common = lambda y, logs: (
+        is_long, q, k, v, dy, y, logs, rho, cosine, sine, gain, ones
     )
     dqkv_b, dk_part, dv_part, sqk_b = attn_bwd(
-        *common(dy_b, y_b, logs_b), middle, blocks - middle, None
+        *common(y_b, logs_b), middle, blocks - middle, None
     )
 
     if not fast:
@@ -1211,7 +1240,6 @@
         here = here + through[side * (own // 2) : (side + 1) * (own // 2)].astype(f32)
         return lax.dynamic_update_slice_in_dim(part, here.astype(bf16), mine_at, 0)
 
-    dqkv_b, dk_part, dy_a = lax.optimization_barrier((dqkv_b, dk_part, dy_a))
     part_b = jnp.einsum(
         "tn,zcn->ztc", dqkv_b, qkv_full.reshape(nz, cols, 3 * cols), preferred_element_type=f32
     ).astype(bf16)
@@ -1221,15 +1249,18 @@
     down_along = [after(one, dqkv_b) for one in down_along]
     up_part, up_next = second(up_kept, [after(one, dqkv_b) for one in up_sent])
     part_got = exchange(part_b)
-    dk_part, dy_a, *_ = lax.optimization_barrier((dk_part, dy_a, *up_next, part_b, *down_along))
-    dqkv_a, sqk_a = attn_bwd(*common(dy_a, y_a, logs_a), 0, middle, [dk_part, dv_part])
+    dk_part, *_ = lax.optimization_barrier((dk_part, *up_next, part_b, *down_along))
+    dqkv_a, sqk_a = attn_bwd(*common(y_a, logs_a), 0, middle, [dk_part, dv_part])
     input_b = jnp.sum(after(part_got, dqkv_a).astype(f32), axis=0)
     up_part = wait_last(up_part, dqkv_a, *[terms[-1] for terms in up_part])
     part_a = input_part(dqkv_a, 0)
     up_slots = slot_sums(up_part)
-    passed = onward(up_slots[1].astype(bf16))
+    passed = up_slots[1].astype(bf16)
+    part_a, passed = lax.optimization_barrier((part_a, passed))
+    dqkv_late = after(dqkv_a, passed)
+    passed = onward(passed)
     for n in range(2, nz):
-        if n == nz - 2:
+        if n == nz - 1:
             passed, part_a = lax.optimization_barrier((passed, part_a))
         passed = onward((up_slots[n] + passed.astype(f32)).astype(bf16))
     sum_up_t = up_slots[0] + passed.astype(f32)
@@ -1237,7 +1268,7 @@
     input_grad = jnp.concatenate([input_a.astype(f32), input_b], axis=0)
     hidden_t = after(hidden, part_a).reshape(nz, 2, own // 2, cols).transpose(1, 0, 2, 3).reshape(rows, cols)
 
-    dqkv = jnp.concatenate([dqkv_a, dqkv_b], axis=0)
+    dqkv = jnp.concatenate([dqkv_late, dqkv_b], axis=0)
     grad_qkv = t_dot(tokens_full, dqkv).astype(bf16)
     sqk = jnp.pad((sqk_a + sqk_b), ((0, EXTRA - 8), (0, 2 * cols)))
     shard = [lax.dynamic_slice_in_dim(grad_qkv, (b ^ r) * span, span, 0) for r in range(nb)]

time: 561 us -> 562 us (level)
  Pallas kernels: 166 us -> 188 us
  waiting for transfers between devices: 179 us -> 170 us
  other arithmetic: 44.6 us -> 36.2 us
    ppermute x12, waiting for transfers between devices: 129 us -> 102 us  [onward(): return lax.ppermute(value, 'head', [(i, (i + k) % nz) for i in range(nz)])]
    all_to_all x6 -> x5, waiting for transfers between devices: 5.59 us -> 18.5 us  [exchange(): return lax.all_to_all(value, 'head', split_axis=0, concat_axis=0)]
    pallas_call x2, Pallas kernels: 33.1 us -> 44.2 us  [attn_bwd(): pl.pallas_call(inner, grid_spec=pltpu.PrefetchScalarGridSpec(num_scalar_p...]
    convert_element_type x5 -> x1, other arithmetic: 11.4 us -> 1.99 us  [per_device(): passed = up_slots[1].astype(bf16)]
    all_to_all x6 -> x5, starting transfers between devices: 31.5 us -> 22.9 us  [exchange(): return lax.all_to_all(value, 'head', split_axis=0, concat_axis=0)]
    pallas_call x2, Pallas kernels: 13.2 us -> 19.9 us  [attn_fwd(): pl.pallas_call(functools.partial(attn_fwd_kernel, heads=heads, blk=blk, s...]
    ppermute x12, starting transfers between devices: 16.7 us -> 22.7 us  [onward(): return lax.ppermute(value, 'head', [(i, (i + k) % nz) for i in range(nz)])]
    pallas_call x0 -> x2, Pallas kernels: none -> 5.98 us  [pair_sums(): pl.pallas_call(pair_sum_kernel, grid=(slots,), in_specs=[spec(at[0]), spe...]
  transfers between devices with their start and end apart: 55 -> 54, of which waited for: 20 -> 20; matrix products, arithmetic and copies ran while one was open for 14% -> 12% of each run, Pallas kernels for 24% -> 30%
where the time goes in v7:
time: 562 us; the launch traced here: 553 us
  Pallas kernels  188 us (33%)
  waiting for transfers between devices  170 us (30%)
  starting transfers between devices  75.4 us (13%)
  local copies, waits for them, and re-layouts  38.6 us (7%)
  other arithmetic  36.2 us (6%)
  between operations  16.2 us (3%)
  blocking collectives  15.7 us (3%)
  matrix products  12.7 us (2%)
    ppermute x12, waiting for transfers between devices, onward(): return lax.ppermute(value, 'head', [(i, (i + k) % nz) for i in range(nz)])  102 us
    ppermute x35, waiting for transfers between devices, swap_batch(): return lax.ppermute(value, 'batch', [(i, i ^ bit) for i in range(nb)])  49.6 us
    pallas_call x2, Pallas kernels, attn_bwd(): pl.pallas_call(inner, grid_spec=pltpu.PrefetchScalarGridSpec(num_scalar_p...  44.2 us
    ppermute x35, starting transfers between devices, swap_batch(): return lax.ppermute(value, 'batch', [(i, i ^ bit) for i in range(nb)])  29.5 us
    pallas_call x2, Pallas kernels, weight_grads(): pl.pallas_call(functools.partial(grad_kernel, orders=(lists[:2], lists[2:...  29.2 us
    unnamed x139, local copies, waits for them, and re-layouts  26.3 us
    pallas_call x1, Pallas kernels, mlp_bwd(): pl.pallas_call(functools.partial(mlp_bwd_kernel, half=half, counts=[len(s...  25 us
    all_to_all x5, starting transfers between devices, exchange(): return lax.all_to_all(value, 'head', split_axis=0, concat_axis=0)  22.9 us
  transfers between devices with their start and end apart: 54, of which 20 were waited for; matrix products, arithmetic and copies ran while one was open for 12% of the time, Pallas kernels for 30%

profile of v7, /device:TPU:0, one launch (start us, length us, event | category | flops | bytes accessed | tf_op | source)
XLA Modules:
  0.0 552.5 jit_solution(6641016459278588279)
XLA Ops:
  21.5 19.8 %collective-permute-done.refs_1_ = bf16[2048,256]{1,0:T(8,128)(2,1)} collective-permute-done((bf16[2048,256]{1,0:T(8,128)(2,1)}, bf16[2048,256]{1,0:T(8,128)(2,1)}, u32[]{:S(2)}, u32[]{:S(2)}) %collective-permute-start) | collective-permute-done | bytes 1048608 | tf_op jit(solution)/shard_map/ppermute | solution.py:1050
  41.3 19.3 %collective-permute-done.2.refs_4_ = bf16[256,1792]{1,0:T(8,128)(2,1)S(1)} collective-permute-done((bf16[256,1792]{1,0:T(8,128)(2,1)S(1)}, bf16[256,1792]{1,0:T(8,128)(2,1)S(1)}, u32[]{:S(2)}, u32[]{:S(2)}) %collective-permute-start.2) | collective-permute-done | bytes 917536 | tf_op jit(solution)/shard_map/ppermute | solution.py:1050
  60.6 5.6 %collective-permute-done.5.refs_3_ = bf16[256,1792]{1,0:T(8,128)(2,1)} collective-permute-done((bf16[256,1792]{1,0:T(8,128)(2,1)S(1)}, bf16[256,1792]{1,0:T(8,128)(2,1)}, u32[]{:S(2)}, u32[]{:S(2)}) %collective-permute-start.5) | collective-permute-done | bytes 917536 | tf_op jit(solution)/shard_map/ppermute | solution.py:1041
  74.9 5.5 %fusion.10 = (f32[2048,128]{1,0:T(8,128)}, f32[2048,128]{1,0:T(8,128)}) fusion(f32[128]{0:T(128)S(1)} %get-tuple-element.425, f32[128]{0:T(128)S(1)} %get-tuple-element.426, f32[2048]{0:T(1024)S(1)} %convert_element_type.280), kind=kLoop, calls=%fused_computation.19 | loop fusion | flops 524288 | bytes 2106368 | tf_op jit(solution)/shard_map/mul | solution.py:1092
  80.5 12.3 %collective-permute-done.10.refs_7_ = bf16[256,1792]{1,0:T(8,128)(2,1)S(1)} collective-permute-done((bf16[256,1792]{1,0:T(8,128)(2,1)S(1)}, bf16[256,1792]{1,0:T(8,128)(2,1)S(1)}, u32[]{:S(2)}, u32[]{:S(2)}) %collective-permute-start.10) | collective-permute-done | bytes 917536 | tf_op jit(solution)/shard_map/ppermute | solution.py:1041
  92.8 19.2 %collective-permute-done.7.refs_8_ = bf16[256,1792]{1,0:T(8,128)(2,1)} collective-permute-done((bf16[256,1792]{1,0:T(8,128)(2,1)S(1)}, bf16[256,1792]{1,0:T(8,128)(2,1)}, u32[]{:S(2)}, u32[]{:S(2)}) %collective-permute-start.7) | collective-permute-done | bytes 917536 | tf_op jit(solution)/shard_map/ppermute | solution.py:1050
  116.7 21.7 %collective-permute-done.11.refs_3_ = bf16[2048,256]{1,0:T(8,128)(2,1)} collective-permute-done((bf16[2048,256]{1,0:T(8,128)(2,1)}, bf16[2048,256]{1,0:T(8,128)(2,1)}, u32[]{:S(2)}, u32[]{:S(2)}) %collective-permute-start.11) | collective-permute-done | bytes 1048608 | tf_op jit(solution)/shard_map/ppermute | solution.py:1050
  140.2 11.5 %shard_map.355 = (bf16[2048,1024]{1,0:T(8,128)(2,1)}, bf16[2048,256]{1,0:T(8,128)(2,1)}, bf16[2048,256]{1,0:T(8,128)(2,1)}, bf16[2048,256]{1,0:T(8,128)(2,1)}, f32[2048,128]{1,0:T(8,128)}) custom-call(s32[3]{0:T(128)} %pad_add_fusion.place_ref, bf16[2048,256]{1,0:T(8,128)(2,1)} %refs_0_.1, bf16[2048,256]{1,0:T(8,128)(2,1)} %collective-permute-done.refs_1_, ...), custom_call_target="tpu_custom_call" | custom-call | tf_op jit(solution)/shard_map/pallas_call | solution.py:102
  151.7 6.4 %shard_map.356 = (bf16[1024,256]{1,0:T(8,128)(2,1)}, f32[1024,128]{1,0:T(8,128)}) custom-call(s32[1]{0:T(128)S(6)} %convert_element_type.285.long_ref.r_0_, bf16[2048,256]{1,0:T(8,128)(2,1)} %get-tuple-element.204.q_ref.r_1_, bf16[2048,256]{1,0:T(8,128)(2,1)} %get-tuple-element.195.k_ref.r_2_.r_6_, bf16[2048,256]{1,0:T(8,128)(2,1)} %get-tuple-element.196.v_ref.r_7_), custom_call_target="tpu_custom_call" | custom-call | tf_op jit(solution)/shard_map/pallas_call | solution.py:193
  158.2 5.1 all-to-all-start
  166.8 13.4 %shard_map.357 = (bf16[1024,256]{1,0:T(8,128)(2,1)}, f32[1024,128]{1,0:T(8,128)}) custom-call(s32[1]{0:T(128)S(6)} %convert_element_type.285.long_ref.r_0_, bf16[2048,256]{1,0:T(8,128)(2,1)} %get-tuple-element.204.q_ref.r_1_, bf16[2048,256]{1,0:T(8,128)(2,1)} %get-tuple-element.195.k_ref.r_2_.r_6_, bf16[2048,256]{1,0:T(8,128)(2,1)} %get-tuple-element.196.v_ref.r_7_), custom_call_target="tpu_custom_call" | custom-call | tf_op jit(solution)/shard_map/pallas_call | solution.py:193
  180.3 15.7 %all_to_all.30.refs_17_ = bf16[4,256,256]{2,1,0:T(8,128)(2,1)} all-to-all(bf16[4,256,256]{2,1,0:T(8,128)(2,1)} %bitcast.103), channel_id=1, replica_groups=mesh['head'=4,'batch'=8] {'head'}, dimensions={0} | all-to-all | bytes 1048576 | tf_op jit(solution)/shard_map/all_to_all | solution.py:1053
  196.0 7.3 %collective-permute-done.17.refs_14_ = bf16[256,1792]{1,0:T(8,128)(2,1)S(1)} collective-permute-done((bf16[256,1792]{1,0:T(8,128)(2,1)}, bf16[256,1792]{1,0:T(8,128)(2,1)S(1)}, u32[]{:S(2)}, u32[]{:S(2)}) %collective-permute-start.17) | collective-permute-done | bytes 917536 | tf_op jit(solution)/shard_map/ppermute | solution.py:1041
  204.3 6.9 %shard_map.358 = (f32[512,1024]{1,0:T(8,128)}, f32[512,1024]{1,0:T(8,128)}, bf16[512,1024]{1,0:T(8,128)(2,1)}, f32[512,128]{1,0:T(8,128)}, bf16[4,512,256]{2,1,0:T(8,128)(2,1)}, /*index=5*/bf16[4,512,128]{2,1,0:T(8,128)(2,1)}) custom-call(s32[3]{0:T(128)} %pad_add_fusion.place_ref, bf16[256,1792]{1,0:T(8,128)(2,1)} %copy-done.14, ...), custom_call_target="tpu_custom_call" | custom-call | tf_op jit(solution)/shard_map/pallas_call | solution.py:484
  212.9 4.8 all-to-all-start.2
  218.7 20.4 %shard_map.359 = (bf16[4,1024,512]{2,1,0:T(8,128)(2,1)}, bf16[4,1024,1024]{2,1,0:T(8,128)(2,1)}, f32[512,1024]{1,0:T(8,128)}, bf16[512,1024]{1,0:T(8,128)(2,1)}) custom-call(bf16[256,1792]{1,0:T(8,128)(2,1)} %copy-done.14, bf16[256,1792]{1,0:T(8,128)(2,1)} %copy-done.16, bf16[256,1792]{1,0:T(8,128)(2,1)} %collective-permute-done.4.refs_2_, ...), custom_call_target="tpu_custom_call" | custom-call | tf_op jit(solution)/shard_map/pallas_call | solution.py:676
  239.2 4.4 all-to-all-done.2.cot_ref
  245.1 6.4 %shard_map.360 = (bf16[4,512,256]{2,1,0:T(8,128)(2,1)}, bf16[512,1024]{1,0:T(8,128)(2,1)}, f32[512,1024]{1,0:T(8,128)}, f32[8,1024]{1,0:T(8,128)}) custom-call(s32[3]{0:T(128)} %pad_add_fusion.place_ref, f32[512,1024]{1,0:T(8,128)} %get-tuple-element.220.own_ref, bf16[512,1024]{1,0:T(8,128)(2,1)} %copy-done.43, ...), custom_call_target="tpu_custom_call" | custom-call | tf_op jit(solution)/shard_map/pallas_call | solution.py:533
  256.3 10.0 %shard_map.361 = (bf16[2,2,256,512]{3,2,1,0:T(8,128)(2,1)}, bf16[2,2,256,512]{3,2,1,0:T(8,128)(2,1)}, bf16[2,2,256,512]{3,2,1,0:T(8,128)(2,1)}, bf16[2,2,256,512]{3,2,1,0:T(8,128)(2,1)}) custom-call(s32[3]{0:T(128)} %pad_add_fusion.place_ref, bf16[512,1024]{1,0:T(8,128)(2,1)} %get-tuple-element.229.refs_0_.refs_16_, bf16[512,1024]{1,0:T(8,128)(2,1)} %copy-done.25, ...), custom_call_target="tpu_custom_call" | custom-call | tf_op jit(solution)/shard_map/pallas_call | solution.py:873
  267.2 25.0 %shard_map.362 = (bf16[4,1024,1024]{2,1,0:T(8,128)(2,1)}, f32[512,1024]{1,0:T(8,128)}, bf16[512,1024]{1,0:T(8,128)(2,1)}, f32[4,8,512]{2,1,0:T(8,128)}) custom-call(bf16[256,1792]{1,0:T(8,128)(2,1)} %copy-done.14, bf16[256,1792]{1,0:T(8,128)(2,1)} %copy-done.16, bf16[256,1792]{1,0:T(8,128)(2,1)} %collective-permute-done.4.refs_2_, ...), custom_call_target="tpu_custom_call" | custom-call | tf_op jit(solution)/shard_map/pallas_call | solution.py:742
  297.0 9.0 %shard_map.364 = (bf16[512,1024]{1,0:T(8,128)(2,1)}, bf16[512,1024]{1,0:T(8,128)(2,1)}, f32[8,1024]{1,0:T(8,128)}, bf16[4,512,256]{2,1,0:T(8,128)(2,1)}) custom-call(s32[3]{0:T(128)} %pad_add_fusion.place_ref, bf16[256,1792]{1,0:T(8,128)(2,1)} %copy-done.14, bf16[256,1792]{1,0:T(8,128)(2,1)} %copy-done.16, bf16[256,1792]{1,0:T(8,128)(2,1)} %collective-permute-done.4.refs_2_, ...), custom_call_target="tpu_custom_call" | custom-call | tf_op jit(solution)/shard_map/pallas_call | solution.py:588
  306.0 5.6 %all-to-all-start.4 = ((bf16[4,512,256]{2,1,0:T(8,128)(2,1)}), bf16[4,512,256]{2,1,0:T(8,128)(2,1)S(1)}, u32[]{:S(2)}, u32[]{:S(2)}) async-start(bf16[4,512,256]{2,1,0:T(8,128)(2,1)} %get-tuple-element.254), calls=%async_computation.4 | async-start | bytes 2097152 | tf_op jit(solution)/shard_map/all_to_all | solution.py:1053
  316.0 19.3 %shard_map.365 = (bf16[2,2,272,1152]{3,2,1,0:T(8,128)(2,1)}, bf16[2,2,272,1152]{3,2,1,0:T(8,128)(2,1)}, bf16[2,2,272,1152]{3,2,1,0:T(8,128)(2,1)}, bf16[2,2,272,1152]{3,2,1,0:T(8,128)(2,1)}) custom-call(s32[3]{0:T(128)} %pad_add_fusion.place_ref, bf16[512,1024]{1,0:T(8,128)(2,1)} %get-tuple-element.217.refs_16_.refs_0_, bf16[512,1024]{1,0:T(8,128)(2,1)} %copy-done.31, ...), custom_call_target="tpu_custom_call" | custom-call | tf_op jit(solution)/shard_map/pallas_call | solution.py:873
  354.1 28.3 %shard_map.366 = (bf16[1024,768]{1,0:T(8,128)(2,1)}, f32[1024,256]{1,0:T(8,128)}, f32[1024,256]{1,0:T(8,128)}, f32[8,256]{1,0:T(8,128)}) custom-call(s32[1]{0:T(128)S(6)} %convert_element_type.285.long_ref.r_0_, bf16[2048,256]{1,0:T(8,128)(2,1)} %get-tuple-element.204.q_ref.r_1_, bf16[2048,256]{1,0:T(8,128)(2,1)} %get-tuple-element.195.k_ref.r_2_.r_6_, ...), custom_call_target="tpu_custom_call" | custom-call | tf_op jit(solution)/shard_map/pallas_call | solution.py:347
  382.4 11.6 %collective-permute-done.29.gb_ref = bf16[2,2,272,1152]{3,2,1,0:T(8,128)(2,1)} collective-permute-done((bf16[2,2,272,1152]{3,2,1,0:T(8,128)(2,1)}, bf16[2,2,272,1152]{3,2,1,0:T(8,128)(2,1)}, u32[]{:S(2)}, u32[]{:S(2)}) %collective-permute-start.29) | collective-permute-done | bytes 2506784 | tf_op jit(solution)/shard_map/ppermute | solution.py:1041
  411.3 15.8 %shard_map.368 = (bf16[1024,768]{1,0:T(8,128)(2,1)}, f32[8,256]{1,0:T(8,128)}) custom-call(s32[1]{0:T(128)S(6)} %convert_element_type.285.long_ref.r_0_, bf16[2048,256]{1,0:T(8,128)(2,1)} %get-tuple-element.204.q_ref.r_1_, bf16[2048,256]{1,0:T(8,128)(2,1)} %get-tuple-element.195.k_ref.r_2_.r_6_, bf16[4,2,256,256]{3,2,1,0:T(8,128)(2,1)} %bitcast.98, ...), custom_call_target="tpu_custom_call" | custom-call | tf_op jit(solution)/shard_map/pallas_call | solution.py:347
  427.2 4.7 convolution_convert_fusion
  438.0 6.2 %fusion.4 = bf16[1024,768]{1,0:T(8,128)(2,1)S(1)} fusion(bf16[2048,1024]{1,0:T(8,128)(2,1)} %get-tuple-element.215.refs_18_.refs_21_, bf16[1024,768]{1,0:T(8,128)(2,1)S(1)} %copy-done.60, bf16[1024,768]{1,0:T(8,128)(2,1)} %get-tuple-element.289), kind=kOutput, calls=%fused_computation.9 | convolution fusion | flops 3228303360 | bytes 8912896 | tf_op jit(solution)/shard_map/dot_general | solution.py:38
  449.6 11.3 %collective-permute-done.36 = bf16[272,1152]{1,0:T(8,128)(2,1)S(1)} collective-permute-done((bf16[272,1152]{1,0:T(8,128)(2,1)S(1)}, bf16[272,1152]{1,0:T(8,128)(2,1)S(1)}, u32[]{:S(2)}, u32[]{:S(2)}) %collective-permute-start.36) | collective-permute-done | bytes 626720 | tf_op jit(solution)/shard_map/ppermute | solution.py:1050
  463.5 8.9 %collective-permute-start.37 = (bf16[272,1152]{1,0:T(8,128)(2,1)}, bf16[272,1152]{1,0:T(8,128)(2,1)}, u32[]{:S(2)}, u32[]{:S(2)}) collective-permute-start(bf16[272,1152]{1,0:T(8,128)(2,1)} %fusion.9), channel_id=1, source_target_pairs={{0,8},{8,16},{16,24},{24,0},{1,9},{9,17},{17,25},{25,1},{2,10},{10... | collective-permute-start | bytes 1880072 | tf_op jit(solution)/shard_map/ppermute | solution.py:1050
  472.4 12.1 %all-to-all-done.5 = bf16[4,1024,256]{1,2,0:T(8,128)(2,1)S(1)} async-done(((bf16[4,1024,256]{1,2,0:T(8,128)(2,1)}), bf16[4,1024,256]{1,2,0:T(8,128)(2,1)S(1)}, u32[]{:S(2)}, u32[]{:S(2)}) %all-to-all-start.5) | async-done | bytes 2097184 | tf_op jit(solution)/shard_map/all_to_all | solution.py:1053
  511.2 10.5 %collective-permute-done.41 = bf16[272,1152]{1,0:T(8,128)(2,1)} collective-permute-done((bf16[272,1152]{1,0:T(8,128)(2,1)}, bf16[272,1152]{1,0:T(8,128)(2,1)}, u32[]{:S(2)}, u32[]{:S(2)}) %collective-permute-start.41) | collective-permute-done | bytes 626720 | tf_op jit(solution)/shard_map/ppermute | solution.py:1050
  (325 shorter events, 152.2 us)
Async XLA Ops:
  7.2 133.0 %all-gather.2.cloned.1.call-start = ((), (), s32[]{:S(2)}) async-start(), calls=%async_computation.7 | async-start | bytes 1769472 | tf_op jit(solution)/shard_map/all_gather | solution.py:1077
  12.3 29.0 %collective-permute-start = (bf16[2048,256]{1,0:T(8,128)(2,1)}, bf16[2048,256]{1,0:T(8,128)(2,1)}, u32[]{:S(2)}, u32[]{:S(2)}) collective-permute-start(bf16[2048,256]{1,0:T(8,128)(2,1)} %refs_0_.1), channel_id=1, source_target_pairs={{0,8},{8,16},{16,24},{24,0},{1,9},{9,17},{17,25},{25,1},{2,10},{10... | collective-permute-start | bytes 3145736 | tf_op jit(solution)/shard_map/ppermute | solution.py:1050
  15.1 45.5 %collective-permute-start.2 = (bf16[256,1792]{1,0:T(8,128)(2,1)S(1)}, bf16[256,1792]{1,0:T(8,128)(2,1)S(1)}, u32[]{:S(2)}, u32[]{:S(2)}) collective-permute-start(bf16[256,1792]{1,0:T(8,128)(2,1)S(1)} %pad_maximum_fusion.1.refs_0_), channel_id=1, source_target_pairs={{0,8},{8,16},{16,24},{24,0},{1,9},{9,17},{17,25},{25,1},{2,10},{10... | collective-permute-start | bytes 2752520 | tf_op jit(solution)/shard_map/ppermute | solution.py:1050
  16.9 43.7 %collective-permute-start.3 = (bf16[256,1792]{1,0:T(8,128)(2,1)S(1)}, bf16[256,1792]{1,0:T(8,128)(2,1)S(1)}, u32[]{:S(2)}, u32[]{:S(2)}) collective-permute-start(bf16[256,1792]{1,0:T(8,128)(2,1)S(1)} %pad_maximum_fusion.1.refs_0_), channel_id=1, source_target_pairs={{0,2},{1,3},{2,0},{3,1},{4,6},{5,7},{6,4},{7,5},{8,10},{9,11},{10,... | collective-permute-start | bytes 2752520 | tf_op jit(solution)/shard_map/ppermute | solution.py:1041
  18.4 42.2 %collective-permute-start.4 = (bf16[256,1792]{1,0:T(8,128)(2,1)S(1)}, bf16[256,1792]{1,0:T(8,128)(2,1)}, u32[]{:S(2)}, u32[]{:S(2)}) collective-permute-start(bf16[256,1792]{1,0:T(8,128)(2,1)S(1)} %pad_maximum_fusion.1.refs_0_), channel_id=1, source_target_pairs={{0,4},{1,5},{2,6},{3,7},{4,0},{5,1},{6,2},{7,3},{8,12},{9,13},{10,... | collective-permute-start | bytes 2752520 | tf_op jit(solution)/shard_map/ppermute | solution.py:1041
  20.0 46.2 %collective-permute-start.5 = (bf16[256,1792]{1,0:T(8,128)(2,1)S(1)}, bf16[256,1792]{1,0:T(8,128)(2,1)}, u32[]{:S(2)}, u32[]{:S(2)}) collective-permute-start(bf16[256,1792]{1,0:T(8,128)(2,1)S(1)} %pad_maximum_fusion.1.refs_0_), channel_id=1, source_target_pairs={{0,6},{1,7},{2,4},{3,5},{4,2},{5,3},{6,0},{7,1},{8,14},{9,15},{10,... | collective-permute-start | bytes 2752520 | tf_op jit(solution)/shard_map/ppermute | solution.py:1041
  66.2 45.8 %collective-permute-start.6 = (bf16[2048,256]{1,0:T(8,128)(2,1)}, bf16[2048,256]{1,0:T(8,128)(2,1)}, u32[]{:S(2)}, u32[]{:S(2)}) collective-permute-start(bf16[2048,256]{1,0:T(8,128)(2,1)} %collective-permute-done.refs_1_), channel_id=1, source_target_pairs={{0,8},{8,16},{16,24},{24,0},{1,9},{9,17},{17,25},{25,1},{2,10},{10... | collective-permute-start | bytes 3145736 | tf_op jit(solution)/shard_map/ppermute | solution.py:1050
  69.9 42.0 %collective-permute-start.7 = (bf16[256,1792]{1,0:T(8,128)(2,1)S(1)}, bf16[256,1792]{1,0:T(8,128)(2,1)}, u32[]{:S(2)}, u32[]{:S(2)}) collective-permute-start(bf16[256,1792]{1,0:T(8,128)(2,1)S(1)} %collective-permute-done.2.refs_4_), channel_id=1, source_target_pairs={{0,8},{8,16},{16,24},{24,0},{1,9},{9,17},{17,25},{25,1},{2,10},{10... | collective-permute-start | bytes 2752520 | tf_op jit(solution)/shard_map/ppermute | solution.py:1050
  71.5 40.5 %collective-permute-start.8 = (bf16[256,1792]{1,0:T(8,128)(2,1)S(1)}, bf16[256,1792]{1,0:T(8,128)(2,1)S(1)}, u32[]{:S(2)}, u32[]{:S(2)}) collective-permute-start(bf16[256,1792]{1,0:T(8,128)(2,1)S(1)} %collective-permute-done.2.refs_4_), channel_id=1, source_target_pairs={{0,2},{1,3},{2,0},{3,1},{4,6},{5,7},{6,4},{7,5},{8,10},{9,11},{10,... | collective-permute-start | bytes 2752520 | tf_op jit(solution)/shard_map/ppermute | solution.py:1041
  72.1 39.9 %collective-permute-start.9 = (bf16[256,1792]{1,0:T(8,128)(2,1)S(1)}, bf16[256,1792]{1,0:T(8,128)(2,1)S(1)}, u32[]{:S(2)}, u32[]{:S(2)}) collective-permute-start(bf16[256,1792]{1,0:T(8,128)(2,1)S(1)} %collective-permute-done.2.refs_4_), channel_id=1, source_target_pairs={{0,4},{1,5},{2,6},{3,7},{4,0},{5,1},{6,2},{7,3},{8,12},{9,13},{10,... | collective-permute-start | bytes 2752520 | tf_op jit(solution)/shard_map/ppermute | solution.py:1041
  113.2 50.0 %collective-permute-start.13 = (bf16[256,1792]{1,0:T(8,128)(2,1)}, bf16[256,1792]{1,0:T(8,128)(2,1)S(1)}, u32[]{:S(2)}, u32[]{:S(2)}) collective-permute-start(bf16[256,1792]{1,0:T(8,128)(2,1)} %collective-permute-done.7.refs_8_), channel_id=1, source_target_pairs={{0,2},{1,3},{2,0},{3,1},{4,6},{5,7},{6,4},{7,5},{8,10},{9,11},{10,... | collective-permute-start | bytes 2752520 | tf_op jit(solution)/shard_map/ppermute | solution.py:1041
  114.7 48.6 %collective-permute-start.14 = (bf16[256,1792]{1,0:T(8,128)(2,1)}, bf16[256,1792]{1,0:T(8,128)(2,1)}, u32[]{:S(2)}, u32[]{:S(2)}) collective-permute-start(bf16[256,1792]{1,0:T(8,128)(2,1)} %collective-permute-done.7.refs_8_), channel_id=1, source_target_pairs={{0,4},{1,5},{2,6},{3,7},{4,0},{5,1},{6,2},{7,3},{8,12},{9,13},{10,... | collective-permute-start | bytes 2752520 | tf_op jit(solution)/shard_map/ppermute | solution.py:1041
  115.2 48.1 %collective-permute-start.15 = (bf16[256,1792]{1,0:T(8,128)(2,1)}, bf16[256,1792]{1,0:T(8,128)(2,1)}, u32[]{:S(2)}, u32[]{:S(2)}) collective-permute-start(bf16[256,1792]{1,0:T(8,128)(2,1)} %collective-permute-done.7.refs_8_), channel_id=1, source_target_pairs={{0,6},{1,7},{2,4},{3,5},{4,2},{5,3},{6,0},{7,1},{8,14},{9,15},{10,... | collective-permute-start | bytes 2752520 | tf_op jit(solution)/shard_map/ppermute | solution.py:1041
  163.3 32.7 %collective-permute-start.16 = (bf16[256,1792]{1,0:T(8,128)(2,1)}, bf16[256,1792]{1,0:T(8,128)(2,1)S(1)}, u32[]{:S(2)}, u32[]{:S(2)}) collective-permute-start(bf16[256,1792]{1,0:T(8,128)(2,1)} %collective-permute-done.12.refs_12_), channel_id=1, source_target_pairs={{0,2},{1,3},{2,0},{3,1},{4,6},{5,7},{6,4},{7,5},{8,10},{9,11},{10,... | collective-permute-start | bytes 2752520 | tf_op jit(solution)/shard_map/ppermute | solution.py:1041
  164.9 38.4 %collective-permute-start.17 = (bf16[256,1792]{1,0:T(8,128)(2,1)}, bf16[256,1792]{1,0:T(8,128)(2,1)S(1)}, u32[]{:S(2)}, u32[]{:S(2)}) collective-permute-start(bf16[256,1792]{1,0:T(8,128)(2,1)} %collective-permute-done.12.refs_12_), channel_id=1, source_target_pairs={{0,4},{1,5},{2,6},{3,7},{4,0},{5,1},{6,2},{7,3},{8,12},{9,13},{10,... | collective-permute-start | bytes 2752520 | tf_op jit(solution)/shard_map/ppermute | solution.py:1041
  165.3 38.0 %collective-permute-start.18 = (bf16[256,1792]{1,0:T(8,128)(2,1)}, bf16[256,1792]{1,0:T(8,128)(2,1)}, u32[]{:S(2)}, u32[]{:S(2)}) collective-permute-start(bf16[256,1792]{1,0:T(8,128)(2,1)} %collective-permute-done.12.refs_12_), channel_id=1, source_target_pairs={{0,6},{1,7},{2,4},{3,5},{4,2},{5,3},{6,0},{7,1},{8,14},{9,15},{10,... | collective-permute-start | bytes 2752520 | tf_op jit(solution)/shard_map/ppermute | solution.py:1041
  212.9 30.8 %all-to-all-start.2 = ((bf16[4,512,256]{2,1,0:T(8,128)(2,1)}), bf16[4,512,256]{2,1,0:T(8,128)(2,1)S(1)}, u32[]{:S(2)}, u32[]{:S(2)}) async-start(bf16[4,512,256]{2,1,0:T(8,128)(2,1)} %bitcast.17), calls=%async_computation.2 | async-start | bytes 2097152 | tf_op jit(solution)/shard_map/all_to_all | solution.py:1053
  251.5 44.5 %all-to-all-start.3 = ((bf16[4,512,256]{2,1,0:T(8,128)(2,1)}), bf16[4,512,256]{2,1,0:T(8,128)(2,1)S(1)}, u32[]{:S(2)}, u32[]{:S(2)}) async-start(bf16[4,512,256]{2,1,0:T(8,128)(2,1)} %get-tuple-element.233), calls=%async_computation.3 | async-start | bytes 2097152 | tf_op jit(solution)/shard_map/all_to_all | solution.py:1053
  266.2 26.0 %collective-permute-start.24 = (bf16[2,2,256,512]{3,2,1,0:T(8,128)(2,1)}, bf16[2,2,256,512]{3,2,1,0:T(8,128)(2,1)S(1)}, u32[]{:S(2)}, u32[]{:S(2)}) collective-permute-start(bf16[2,2,256,512]{3,2,1,0:T(8,128)(2,1)} %get-tuple-element.228), channel_id=1, source_target_pairs={{0,4},{1,5},{2,6},{3,7},{4,0},{5,1},{6,2},{7,3},{8,12},{9,13},{10,... | collective-permute-start | bytes 3145736 | tf_op jit(solution)/shard_map/ppermute | solution.py:1041
  266.6 25.7 %collective-permute-start.23 = (bf16[2,2,256,512]{3,2,1,0:T(8,128)(2,1)}, bf16[2,2,256,512]{3,2,1,0:T(8,128)(2,1)S(1)}, u32[]{:S(2)}, u32[]{:S(2)}) collective-permute-start(bf16[2,2,256,512]{3,2,1,0:T(8,128)(2,1)} %get-tuple-element.227), channel_id=1, source_target_pairs={{0,2},{1,3},{2,0},{3,1},{4,6},{5,7},{6,4},{7,5},{8,10},{9,11},{10,... | collective-permute-start | bytes 3145736 | tf_op jit(solution)/shard_map/ppermute | solution.py:1041
  306.0 32.0 %all-to-all-start.4 = ((bf16[4,512,256]{2,1,0:T(8,128)(2,1)}), bf16[4,512,256]{2,1,0:T(8,128)(2,1)S(1)}, u32[]{:S(2)}, u32[]{:S(2)}) async-start(bf16[4,512,256]{2,1,0:T(8,128)(2,1)} %get-tuple-element.254), calls=%async_computation.4 | async-start | bytes 2097152 | tf_op jit(solution)/shard_map/all_to_all | solution.py:1053
  338.0 56.0 %collective-permute-start.29 = (bf16[2,2,272,1152]{3,2,1,0:T(8,128)(2,1)}, bf16[2,2,272,1152]{3,2,1,0:T(8,128)(2,1)}, u32[]{:S(2)}, u32[]{:S(2)}) collective-permute-start(bf16[2,2,272,1152]{3,2,1,0:T(8,128)(2,1)} %get-tuple-element.260), channel_id=1, source_target_pairs={{0,4},{1,5},{2,6},{3,7},{4,0},{5,1},{6,2},{7,3},{8,12},{9,13},{10,... | collective-permute-start | bytes 7520264 | tf_op jit(solution)/shard_map/ppermute | solution.py:1041
  339.6 55.6 %collective-permute-start.30 = (bf16[2,2,272,1152]{3,2,1,0:T(8,128)(2,1)}, bf16[2,2,272,1152]{3,2,1,0:T(8,128)(2,1)S(1)}, u32[]{:S(2)}, u32[]{:S(2)}) collective-permute-start(bf16[2,2,272,1152]{3,2,1,0:T(8,128)(2,1)} %get-tuple-element.266), channel_id=1, source_target_pairs={{0,2},{1,3},{2,0},{3,1},{4,6},{5,7},{6,4},{7,5},{8,10},{9,11},{10,... | collective-permute-start | bytes 7520264 | tf_op jit(solution)/shard_map/ppermute | solution.py:1041
  348.2 63.1 %collective-permute-start.34 = (bf16[256,512]{1,0:T(8,128)(2,1)}, bf16[256,512]{1,0:T(8,128)(2,1)}, u32[]{:S(2)}, u32[]{:S(2)}) collective-permute-start(bf16[256,512]{1,0:T(8,128)(2,1)} %get-tuple-element.388), channel_id=1, source_target_pairs={{0,8},{8,16},{16,24},{24,0},{1,9},{9,17},{17,25},{25,1},{2,10},{10... | collective-permute-start | bytes 786440 | tf_op jit(solution)/shard_map/ppermute | solution.py:1050
  348.2 63.1 %collective-permute-start.33 = (bf16[256,512]{1,0:T(8,128)(2,1)}, bf16[256,512]{1,0:T(8,128)(2,1)}, u32[]{:S(2)}, u32[]{:S(2)}) collective-permute-start(bf16[256,512]{1,0:T(8,128)(2,1)} %get-tuple-element.389), channel_id=1, source_target_pairs={{0,16},{8,24},{16,0},{24,8},{1,17},{9,25},{17,1},{25,9},{2,18},{10... | collective-permute-start | bytes 786440 | tf_op jit(solution)/shard_map/ppermute | solution.py:1050
  352.1 59.2 %collective-permute-start.32 = (bf16[256,512]{1,0:T(8,128)(2,1)}, bf16[256,512]{1,0:T(8,128)(2,1)}, u32[]{:S(2)}, u32[]{:S(2)}) collective-permute-start(bf16[256,512]{1,0:T(8,128)(2,1)} %fusion.15), channel_id=1, source_target_pairs={{0,24},{8,0},{16,8},{24,16},{1,25},{9,1},{17,9},{25,17},{2,26},{10... | collective-permute-start | bytes 786440 | tf_op jit(solution)/shard_map/ppermute | solution.py:1050
  400.3 33.7 %collective-permute-start.31 = (bf16[1,2,272,1152]{3,2,1,0:T(8,128)(2,1)}, bf16[1,2,272,1152]{3,2,1,0:T(8,128)(2,1)}, u32[]{:S(2)}, u32[]{:S(2)}) collective-permute-start(bf16[1,2,272,1152]{3,2,1,0:T(8,128)(2,1)} %get-tuple-element.268), channel_id=1, source_target_pairs={{0,2},{1,3},{2,0},{3,1},{4,6},{5,7},{6,4},{7,5},{8,10},{9,11},{10,... | collective-permute-start | bytes 3760136 | tf_op jit(solution)/shard_map/ppermute | solution.py:1041
  401.8 32.1 %collective-permute-start.35 = (bf16[1,2,272,1152]{3,2,1,0:T(8,128)(2,1)}, bf16[1,2,272,1152]{3,2,1,0:T(8,128)(2,1)S(1)}, u32[]{:S(2)}, u32[]{:S(2)}) collective-permute-start(bf16[1,2,272,1152]{3,2,1,0:T(8,128)(2,1)} %get-tuple-element.271), channel_id=1, source_target_pairs={{0,4},{1,5},{2,6},{3,7},{4,0},{5,1},{6,2},{7,3},{8,12},{9,13},{10,... | collective-permute-start | bytes 3760136 | tf_op jit(solution)/shard_map/ppermute | solution.py:1041
  407.4 77.1 %all-to-all-start.5 = ((bf16[4,1024,256]{1,2,0:T(8,128)(2,1)}), bf16[4,1024,256]{1,2,0:T(8,128)(2,1)S(1)}, u32[]{:S(2)}, u32[]{:S(2)}) async-start(bf16[4,1024,256]{1,2,0:T(8,128)(2,1)} %fusion.14), calls=%async_computation.6 | async-start | bytes 4194304 | tf_op jit(solution)/shard_map/all_to_all | solution.py:1053
  411.0 131.6 %reduce-scatter.2.cloned.1.call-start = ((), (), s32[]{:S(2)}) async-start(), calls=%async_computation.8 | async-start | bytes 2621440 | tf_op jit(solution)/shard_map/reduce_scatter | solution.py:1267
  449.6 36.7 %collective-permute-start.38 = (bf16[576,768]{1,0:T(8,128)(2,1)}, bf16[576,768]{1,0:T(8,128)(2,1)}, u32[]{:S(2)}, u32[]{:S(2)}) collective-permute-start(bf16[576,768]{1,0:T(8,128)(2,1)} %get-tuple-element.415), channel_id=1, source_target_pairs={{0,1},{1,0},{2,3},{3,2},{4,5},{5,4},{6,7},{7,6},{8,9},{9,8},{10,11... | collective-permute-start | bytes 2654216 | tf_op jit(solution)/shard_map/ppermute | solution.py:1041
  490.8 30.8 %collective-permute-start.41 = (bf16[272,1152]{1,0:T(8,128)(2,1)}, bf16[272,1152]{1,0:T(8,128)(2,1)}, u32[]{:S(2)}, u32[]{:S(2)}) collective-permute-start(bf16[272,1152]{1,0:T(8,128)(2,1)} %fusion.8), channel_id=1, source_target_pairs={{0,8},{8,16},{16,24},{24,0},{1,9},{9,17},{17,25},{25,1},{2,10},{10... | collective-permute-start | bytes 1880072 | tf_op jit(solution)/shard_map/ppermute | solution.py:1050
  (85 other events, 975.6 us)
Sparse Core Ops, SparseCore 0:
  21.6 46.2 all-gather.1
  488.1 53.9 reduce-scatter.1
